TPU v7x, 32 devices: a whole 2x2x4 slice. The times are simulated.
32 devices in a mesh: pipe: 4 (over z), expert: 8 (over y, x, core).
Axes of the slice: x: 2, y: 2, z: 4, core: 2. Of those that a mesh axis runs over, the one named last changes fastest.
Arguments:
- up_state: bfloat16 [4, 128, 3584], P('pipe', 'expert'), may hold values from -6 to 6
- down_state: bfloat16 [4, 128, 3584], P('pipe', 'expert'), may hold values from -6 to 6
- entering_up: bfloat16 [128, 3584], P('expert'), may hold values from -6 to 6
- entering_down: bfloat16 [128, 3584], P('expert'), may hold values from -6 to 6
- up_route: int32 [2, 4, 128, 1], P(None, 'pipe', 'expert'), may hold values from 0 to 7; in each aligned block of 16 rows (0 to 15, 16 to 31, ..., all dimensions but the last counted through in order) at most 2 rows name the same one
- down_route: int32 [2, 4, 128, 1], P(None, 'pipe', 'expert'), may hold values from 0 to 7; in each aligned block of 16 rows (0 to 15, 16 to 31, ..., all dimensions but the last counted through in order) at most 2 rows name the same one
- norm_gain: float32 [4, 3584], P('pipe'), may hold values from 0.5 to 1.5
- router: bfloat16 [4, 3584, 8], P('pipe'), may hold values from -0.09375 to 0.09375
- w_gate: bfloat16 [4, 3584, 8192], P('pipe', None, 'expert'), may hold values from -0.09375 to 0.09375
- w_up: bfloat16 [4, 3584, 8192], P('pipe', None, 'expert'), may hold values from -0.09375 to 0.09375
- w_down: bfloat16 [4, 8192, 3584], P('pipe', 'expert'), may hold values from -0.1875 to 0.1875
Outputs:
- up_out: bfloat16 [4, 128, 3584], P('pipe', 'expert')
- down_out: bfloat16 [4, 128, 3584], P('pipe', 'expert')
Inputs may be any that keep to these rules, and one draw needn't show every extreme that they name: `up_route`: each row names one expert. Within each aligned block of 16 rows (the rows of one device) every expert is named by exactly 2 rows. `down_route`: as for up_route.
All inputs are finite; a program needn't handle non-finite values.
Results may differ from a plain program's by a relative error of at most 0.0057.
Values may be sent and summed in bfloat16 or wider, within the bound.
No kernel may reach another device: no remote copies, remote signals or barrier semaphores. Data moves between devices by JAX's collectives and lax.ppermute only.
A program may use at most 64 MiB of HBM per device.

v0:
```python
import jax
import jax.numpy as jnp
from jax import lax
from jax.sharding import PartitionSpec as P

TOP = 1
TICKS = 2


norm_eps = 1e-06


def shifted(value, axis, by):
    length = lax.axis_size(axis)
    pairs = [(i, i + by) for i in range(length) if 0 <= i + by < length]
    return lax.ppermute(value, axis, pairs)


def normalize(token_rows, gain_row):
    widened = token_rows.astype(jnp.float32)
    inverse = lax.rsqrt(jnp.mean(widened * widened, axis=1, keepdims=True) + norm_eps)
    return (widened * inverse * gain_row).astype(jnp.bfloat16)


def routing_tables(normed, routing, router_cols, expert_count, slot_cap):
    logits = jnp.dot(normed, router_cols, preferred_element_type=jnp.float32)
    affinity = jax.nn.sigmoid(logits)
    weights = jnp.take_along_axis(affinity, routing, axis=1)
    flat_ids = routing.reshape(-1)
    onehot = (flat_ids[:, None] == jnp.arange(expert_count, dtype=jnp.int32)[None, :]).astype(
        jnp.int32
    )
    before = jnp.cumsum(onehot, axis=0) - onehot
    slot_ids = jnp.sum(before * onehot, axis=1).reshape(routing.shape)
    expert_hit = (
        routing[:, :, None] == jnp.arange(expert_count, dtype=jnp.int32)[None, None, :]
    ).astype(jnp.float32)
    slot_hit = (
        slot_ids[:, :, None] == jnp.arange(slot_cap, dtype=jnp.int32)[None, None, :]
    ).astype(jnp.float32)
    scatter_map = jnp.einsum("rke,rkc->ecr", expert_hit, slot_hit).astype(jnp.bfloat16)
    flat_slot = routing * slot_cap + slot_ids
    return (scatter_map, weights, flat_slot)


def run_experts(received, gate_cols, up_cols, down_rows):
    sources, slot_count, features = received.shape
    flat_rows = received.reshape(sources * slot_count, features)
    gate_pre = jnp.dot(flat_rows, gate_cols, preferred_element_type=jnp.float32)
    up_pre = jnp.dot(flat_rows, up_cols, preferred_element_type=jnp.float32)
    hidden = (jax.nn.silu(gate_pre) * up_pre).astype(jnp.bfloat16)
    partial_value = jnp.dot(hidden, down_rows, preferred_element_type=jnp.float32).astype(
        jnp.bfloat16
    )
    partial_value = partial_value.reshape(sources, slot_count, features)
    return lax.all_to_all(partial_value, "expert", split_axis=0, concat_axis=0, tiled=True)


def mix_rows(token_rows, weights, flat_slot, outputs):
    picked = outputs[flat_slot]
    return token_rows.astype(jnp.float32) + jnp.sum(weights[:, :, None] * picked, axis=1)


def shards(
    up_state,
    down_state,
    entering_up,
    entering_down,
    up_route,
    down_route,
    norm_gain,
    router,
    w_gate,
    w_up,
    w_down,
):
    gate_cols = w_gate[0]
    up_cols = w_up[0]
    down_rows = w_down[0]
    gain_row = norm_gain[0]
    router_cols = router[0]
    group_size = max(1, lax.axis_size("expert") // 8)
    expert_count = lax.axis_size("expert") // group_size
    segment_id = lax.axis_index("pipe")
    last_segment = lax.axis_size("pipe") - 1
    up_now = up_state[0]
    down_now = down_state[0]
    features = up_now.shape[1]
    slot_cap = up_now.shape[0] * TOP // expert_count
    up_done = up_now
    down_done = down_now
    for tick_id in range(TICKS):
        up_normed = normalize(up_now, gain_row)
        down_normed = normalize(down_now, gain_row)
        up_scatter, up_weights, up_slot = routing_tables(
            up_normed, up_route[tick_id, 0], router_cols, expert_count, slot_cap
        )
        down_scatter, down_weights, down_slot = routing_tables(
            down_normed, down_route[tick_id, 0], router_cols, expert_count, slot_cap
        )
        up_send = jnp.einsum(
            "ecr,rd->ecd", up_scatter, up_normed, preferred_element_type=jnp.float32
        ).astype(jnp.bfloat16)
        down_send = jnp.einsum(
            "ecr,rd->ecd", down_scatter, down_normed, preferred_element_type=jnp.float32
        ).astype(jnp.bfloat16)
        outbound = jnp.concatenate([up_send, down_send], axis=1)
        outgoing = jnp.broadcast_to(
            outbound[:, None], (expert_count, group_size, 2 * slot_cap, features)
        ).reshape(expert_count * group_size, 2 * slot_cap, features)
        returned = run_experts(
            lax.all_to_all(outgoing, "expert", split_axis=0, concat_axis=0, tiled=True),
            gate_cols,
            up_cols,
            down_rows,
        )
        summed = jnp.sum(
            returned.reshape(expert_count, group_size, 2 * slot_cap, features).astype(jnp.float32),
            axis=1,
        )
        up_outputs = summed[:, :slot_cap].reshape(expert_count * slot_cap, features)
        down_outputs = summed[:, slot_cap:].reshape(expert_count * slot_cap, features)
        up_done = mix_rows(up_now, up_weights, up_slot, up_outputs).astype(jnp.bfloat16)
        down_done = mix_rows(down_now, down_weights, down_slot, down_outputs).astype(jnp.bfloat16)
        if tick_id + 1 < TICKS:
            up_moved = shifted(up_done, "pipe", 1)
            down_moved = shifted(down_done, "pipe", -1)
            up_now = jnp.where(segment_id == 0, entering_up, up_moved)
            down_now = jnp.where(segment_id == last_segment, entering_down, down_moved)
    return (up_done[None], down_done[None])


def solution(mesh):
    return jax.shard_map(
        shards,
        mesh=mesh,
        in_specs=(
            P("pipe", "expert", None),
            P("pipe", "expert", None),
            P("expert", None),
            P("expert", None),
            P(None, "pipe", "expert", None),
            P(None, "pipe", "expert", None),
            P("pipe", None),
            P("pipe", None, None),
            P("pipe", None, "expert"),
            P("pipe", None, "expert"),
            P("pipe", "expert", None),
        ),
        out_specs=(P("pipe", "expert", None), P("pipe", "expert", None)),
        check_vma=False,
    )
```

profile of v0, /device:TPU:0, one launch (start us, length us, event | category | flops | bytes accessed | tf_op | source)
XLA Modules:
  0.0 95.5 jit_solution(16662208910313448494)
XLA Ops:
  0.6 1.1 %fusion.52 = f32[16]{0:T(128)S(1)} fusion(bf16[1,16,3584]{2,1,0:T(8,128)(2,1)} %param.13), kind=kLoop, calls=%fused_computation.62 | loop fusion | flops 172016 | bytes 114752 | tf_op jit(solution)/shard_map/reduce_sum | solution.py:21
  1.7 1.0 %fusion.58 = f32[16]{0:T(128)S(1)} fusion(bf16[1,16,3584]{2,1,0:T(8,128)(2,1)} %param.14), kind=kLoop, calls=%fused_computation.68 | loop fusion | flops 172016 | bytes 114752 | tf_op jit(solution)/shard_map/reduce_sum | solution.py:21
  2.8 0.7 slice_bitcast_fusion.1
  3.4 0.7 slice_bitcast_fusion
  4.1 0.1 fusion.113
  4.2 0.1 fusion.117
  4.3 0.2 select_reduce_fusion
  4.5 0.1 copy.24
  4.6 0.1 fusion.115
  4.7 0.1 fusion.119
  4.8 0.2 select_reduce_fusion.1
  5.1 0.8 reduce
  5.8 1.1 %convolution_convert_fusion.3 = bf16[8,2,3584]{2,0,1:T(8,128)(2,1)S(1)} fusion(bf16[1,16,3584]{2,1,0:T(8,128)(2,1)} %param.13, f32[3584]{0:T(1024)S(1)} %reduce, f32[16]{0:T(128)S(1)} %add_rsqrt_fusion.3, f32[16,8]{0,1:T(8,128)S(1)} %copy.23, f32[16,2]{0,1:T(2,128)S(1)} %compare_convert_fusion.3), kind=kOutput, calls=%fused_computation.25 | convolution fusion | flops 2122240 | bytes 244416 | tf_op jit(solution)/shard_map/ecr,rd->ecd/dot_general | solution.py:101
  7.0 1.1 %convolution_convert_fusion.2 = bf16[8,2,3584]{2,0,1:T(8,128)(2,1)S(1)} fusion(bf16[1,16,3584]{2,1,0:T(8,128)(2,1)} %param.14, f32[16]{0:T(128)S(1)} %add_rsqrt_fusion.2, f32[3584]{0:T(1024)S(1)} %reduce, f32[16,8]{0,1:T(8,128)S(1)} %copy.24, f32[16,2]{0,1:T(2,128)S(1)} %compare_convert_fusion.2), kind=kOutput, calls=%fused_computation.24 | convolution fusion | flops 2122240 | bytes 244416 | tf_op jit(solution)/shard_map/ecr,rd->ecd/dot_general | solution.py:104
  8.1 0.8 copy.25
  8.9 5.2 %all-to-all-start = ((bf16[8,4,3584]{2,1,0:T(4,128)(2,1)}), bf16[8,4,3584]{2,1,0:T(4,128)(2,1)S(1)}, u32[]{:S(2)}, u32[]{:S(2)}) async-start(bf16[8,4,3584]{2,1,0:T(4,128)(2,1)} %copy.25), calls=%async_computation | async-start | bytes 458752 | tf_op jit(solution)/shard_map/all_to_all | solution.py:112
  14.1 0.7 fusion.151
  14.8 0.7 fusion.153
  15.5 1.1 %fusion.35 = f32[16,8]{0,1:T(8,128)S(1)} fusion(bf16[1,16,3584]{2,1,0:T(8,128)(2,1)} %param.14, f32[16]{0:T(128)S(1)} %add_rsqrt_fusion.2, f32[3584]{0:T(1024)S(1)} %reduce, bf16[1,3584,8]{1,2,0:T(8,128)(2,1)S(1)} %copy-done), kind=kOutput, calls=%fused_computation.37 | convolution fusion | flops 1147264 | bytes 186944 | tf_op jit(solution)/shard_map/dot_general | solution.py:26
  16.6 1.1 %fusion.41 = f32[16,8]{0,1:T(8,128)S(1)} fusion(bf16[1,16,3584]{2,1,0:T(8,128)(2,1)} %param.13, f32[3584]{0:T(1024)S(1)} %reduce, f32[16]{0:T(128)S(1)} %add_rsqrt_fusion.3, bf16[1,3584,8]{1,2,0:T(8,128)(2,1)S(1)} %copy-done), kind=kOutput, calls=%fused_computation.45 | convolution fusion | flops 1147264 | bytes 186944 | tf_op jit(solution)/shard_map/dot_general | solution.py:26
  17.7 0.7 fusion.143
  18.4 0.7 fusion.142
  19.3 0.6 gather_fusion.6
  20.0 0.6 gather_fusion.4
  20.6 0.7 fusion.146
  21.4 4.4 %fusion.10 = f32[32,1024]{1,0:T(8,128)S(1)} fusion(bf16[32,3584]{1,0:T(8,128)(2,1)S(1)} %reshape.444, bf16[1,3584,1024]{2,1,0:T(8,128)(2,1)} %param.21), kind=kOutput, calls=%fused_computation.18 | convolution fusion | flops 234881024 | bytes 7700480 | tf_op jit(solution)/shard_map/dot_general | solution.py:49
  25.8 7.8 %fusion.12 = bf16[32,3584]{1,0:T(8,128)(2,1)S(1)} fusion(bf16[1,1024,3584]{2,1,0:T(8,128)(2,1)} %param.23, bf16[32,3584]{1,0:T(8,128)(2,1)S(1)} %reshape.444, bf16[1,3584,1024]{2,1,0:T(8,128)(2,1)} %param.22, f32[32,1024]{1,0:T(8,128)S(1)} %fusion.10), kind=kOutput, calls=%fused_computation.20 | convolution fusion | flops 470073344 | bytes 15269888 | tf_op jit(solution)/shard_map/dot_general | solution.py:52
  33.7 0.7 reshape.445
  34.4 4.2 %all-to-all-start.1 = ((bf16[8,4,3584]{2,1,0:T(4,128)(2,1)}), bf16[8,4,3584]{2,1,0:T(4,128)(2,1)S(1)}, u32[]{:S(2)}, u32[]{:S(2)}) async-start(bf16[8,4,3584]{2,1,0:T(4,128)(2,1)} %reshape.445), calls=%async_computation.1 | async-start | bytes 458752 | tf_op jit(solution)/shard_map/all_to_all | solution.py:56
  38.7 6.6 %all-to-all-done.1 = bf16[8,4,3584]{2,1,0:T(4,128)(2,1)S(1)} async-done(((bf16[8,4,3584]{2,1,0:T(4,128)(2,1)}), bf16[8,4,3584]{2,1,0:T(4,128)(2,1)S(1)}, u32[]{:S(2)}, u32[]{:S(2)}) %all-to-all-start.1) | async-done | bytes 229408 | tf_op jit(solution)/shard_map/all_to_all | solution.py:56
  45.2 0.2 fusion.155
  45.4 0.2 reshape.446
  45.6 0.6 gather_fusion
  46.2 0.1 fusion.55
  46.3 3.5 %collective-permute-start = (bf16[16,3584]{1,0:T(8,128)(2,1)S(1)}, bf16[16,3584]{1,0:T(8,128)(2,1)S(1)}, u32[]{:S(2)}, u32[]{:S(2)}) collective-permute-start(bf16[16,3584]{1,0:T(8,128)(2,1)S(1)} %fusion.55), channel_id=1, source_target_pairs={{0,8},{8,16},{16,24},{1,9},{9,17},{17,25},{2,10},{10,18},{18,26},{... | collective-permute-start | bytes 344072 | tf_op jit(solution)/shard_map/ppermute | solution.py:16
  49.8 0.2 reshape.447
  50.0 0.6 gather_fusion.1
  50.6 0.1 fusion.61
  50.7 1.3 %collective-permute-start.1 = (bf16[16,3584]{1,0:T(8,128)(2,1)S(1)}, bf16[16,3584]{1,0:T(8,128)(2,1)S(1)}, u32[]{:S(2)}, u32[]{:S(2)}) collective-permute-start(bf16[16,3584]{1,0:T(8,128)(2,1)S(1)} %fusion.61), channel_id=1, source_target_pairs={{8,0},{16,8},{24,16},{9,1},{17,9},{25,17},{10,2},{18,10},{26,18},{... | collective-permute-start | bytes 344072 | tf_op jit(solution)/shard_map/ppermute | solution.py:16
  52.0 0.1 collective-permute-done
  52.1 0.2 fusion.64
  52.3 5.1 %collective-permute-done.1 = bf16[16,3584]{1,0:T(8,128)(2,1)S(1)} collective-permute-done((bf16[16,3584]{1,0:T(8,128)(2,1)S(1)}, bf16[16,3584]{1,0:T(8,128)(2,1)S(1)}, u32[]{:S(2)}, u32[]{:S(2)}) %collective-permute-start.1) | collective-permute-done | bytes 114720 | tf_op jit(solution)/shard_map/ppermute | solution.py:16
  57.4 0.2 fusion.68
  57.6 0.2 fusion.38
  57.8 0.2 convolution_convert_fusion.1
  58.1 0.2 fusion.32
  58.3 0.2 convolution_convert_fusion
  58.6 0.8 copy.28
  59.3 3.4 %all-to-all-start.2 = ((bf16[8,4,3584]{2,1,0:T(4,128)(2,1)}), bf16[8,4,3584]{2,1,0:T(4,128)(2,1)S(1)}, u32[]{:S(2)}, u32[]{:S(2)}) async-start(bf16[8,4,3584]{2,1,0:T(4,128)(2,1)} %copy.28), calls=%async_computation.2 | async-start | bytes 458752 | tf_op jit(solution)/shard_map/all_to_all | solution.py:112
  62.8 0.6 gather_fusion.5
  63.4 0.6 gather_fusion.7
  64.1 5.2 %all-to-all-done.2 = bf16[8,4,3584]{2,1,0:T(4,128)(2,1)S(1)} async-done(((bf16[8,4,3584]{2,1,0:T(4,128)(2,1)}), bf16[8,4,3584]{2,1,0:T(4,128)(2,1)S(1)}, u32[]{:S(2)}, u32[]{:S(2)}) %all-to-all-start.2) | async-done | bytes 229408 | tf_op jit(solution)/shard_map/all_to_all | solution.py:112
  69.3 4.4 %fusion.8 = f32[32,1024]{1,0:T(8,128)S(1)} fusion(bf16[32,3584]{1,0:T(8,128)(2,1)S(1)} %reshape.448, bf16[1,3584,1024]{2,1,0:T(8,128)(2,1)} %param.21), kind=kOutput, calls=%fused_computation.16 | convolution fusion | flops 234881024 | bytes 7700480 | tf_op jit(solution)/shard_map/dot_general | solution.py:49
  73.8 7.8 %fusion.15 = bf16[32,3584]{1,0:T(8,128)(2,1)S(1)} fusion(bf16[1,1024,3584]{2,1,0:T(8,128)(2,1)} %param.23, bf16[32,3584]{1,0:T(8,128)(2,1)S(1)} %reshape.448, bf16[1,3584,1024]{2,1,0:T(8,128)(2,1)} %param.22, f32[32,1024]{1,0:T(8,128)S(1)} %fusion.8), kind=kOutput, calls=%fused_computation.21 | convolution fusion | flops 470073344 | bytes 15269888 | tf_op jit(solution)/shard_map/dot_general | solution.py:52
  81.6 0.7 reshape.449
  82.4 3.4 %all-to-all-start.3 = ((bf16[8,4,3584]{2,1,0:T(4,128)(2,1)}), bf16[8,4,3584]{2,1,0:T(4,128)(2,1)S(1)}, u32[]{:S(2)}, u32[]{:S(2)}) async-start(bf16[8,4,3584]{2,1,0:T(4,128)(2,1)} %reshape.449), calls=%async_computation.3 | async-start | bytes 458752 | tf_op jit(solution)/shard_map/all_to_all | solution.py:56
  85.8 6.5 %all-to-all-done.3 = bf16[8,4,3584]{2,1,0:T(4,128)(2,1)S(1)} async-done(((bf16[8,4,3584]{2,1,0:T(4,128)(2,1)}), bf16[8,4,3584]{2,1,0:T(4,128)(2,1)S(1)}, u32[]{:S(2)}, u32[]{:S(2)}) %all-to-all-start.3) | async-done | bytes 229408 | tf_op jit(solution)/shard_map/all_to_all | solution.py:56
  92.3 0.2 fusion.154
  92.4 0.2 reshape.451
  92.6 0.2 reshape.450
  92.8 0.6 gather_fusion.3
  93.4 0.7 fusion.82
  94.2 0.6 gather_fusion.2
  94.8 0.7 fusion.83
  (45 shorter events, 0.7 us)
Async XLA Ops:
  0.6 14.8 %copy-start = (bf16[1,3584,8]{1,2,0:T(8,128)(2,1)S(1)}, bf16[1,3584,8]{1,2,0:T(8,128)(2,1)}, u32[]{:S(2)}) copy-start(bf16[1,3584,8]{1,2,0:T(8,128)(2,1)} %param.20) | copy-start | bytes 172036
  8.9 12.4 %all-to-all-start = ((bf16[8,4,3584]{2,1,0:T(4,128)(2,1)}), bf16[8,4,3584]{2,1,0:T(4,128)(2,1)S(1)}, u32[]{:S(2)}, u32[]{:S(2)}) async-start(bf16[8,4,3584]{2,1,0:T(4,128)(2,1)} %copy.25), calls=%async_computation | async-start | bytes 458752 | tf_op jit(solution)/shard_map/all_to_all | solution.py:112
  25.8 12.8 %copy-start.5 = (s32[2,1,16,1]{2,3,1,0:T(1,128)S(1)}, s32[2,1,16,1]{2,3,1,0:T(1,128)}, u32[]{:S(2)}) copy-start(s32[2,1,16,1]{2,3,1,0:T(1,128)} %param.17) | copy-start | bytes 388
  25.8 20.4 %copy-start.1 = (bf16[1,16,3584]{2,1,0:T(8,128)(2,1)S(1)}, bf16[1,16,3584]{2,1,0:T(8,128)(2,1)}, u32[]{:S(2)}) copy-start(bf16[1,16,3584]{2,1,0:T(8,128)(2,1)} %param.13) | copy-start | bytes 344068
  33.7 16.9 %copy-start.2 = (bf16[1,16,3584]{2,1,0:T(8,128)(2,1)S(1)}, bf16[1,16,3584]{2,1,0:T(8,128)(2,1)}, u32[]{:S(2)}) copy-start(bf16[1,16,3584]{2,1,0:T(8,128)(2,1)} %param.14) | copy-start | bytes 344068
  33.7 18.5 %copy-start.3 = (bf16[16,3584]{1,0:T(8,128)(2,1)S(1)}, bf16[16,3584]{1,0:T(8,128)(2,1)}, u32[]{:S(2)}) copy-start(bf16[16,3584]{1,0:T(8,128)(2,1)} %param.15) | copy-start | bytes 344068
  33.7 23.7 %copy-start.4 = (bf16[16,3584]{1,0:T(8,128)(2,1)S(1)}, bf16[16,3584]{1,0:T(8,128)(2,1)}, u32[]{:S(2)}) copy-start(bf16[16,3584]{1,0:T(8,128)(2,1)} %param.16) | copy-start | bytes 344068
  34.4 10.8 %all-to-all-start.1 = ((bf16[8,4,3584]{2,1,0:T(4,128)(2,1)}), bf16[8,4,3584]{2,1,0:T(4,128)(2,1)S(1)}, u32[]{:S(2)}, u32[]{:S(2)}) async-start(bf16[8,4,3584]{2,1,0:T(4,128)(2,1)} %reshape.445), calls=%async_computation.1 | async-start | bytes 458752 | tf_op jit(solution)/shard_map/all_to_all | solution.py:56
  46.3 5.8 %collective-permute-start = (bf16[16,3584]{1,0:T(8,128)(2,1)S(1)}, bf16[16,3584]{1,0:T(8,128)(2,1)S(1)}, u32[]{:S(2)}, u32[]{:S(2)}) collective-permute-start(bf16[16,3584]{1,0:T(8,128)(2,1)S(1)} %fusion.55), channel_id=1, source_target_pairs={{0,8},{8,16},{16,24},{1,9},{9,17},{17,25},{2,10},{10,18},{18,26},{... | collective-permute-start | bytes 344072 | tf_op jit(solution)/shard_map/ppermute | solution.py:16
  50.7 6.7 %collective-permute-start.1 = (bf16[16,3584]{1,0:T(8,128)(2,1)S(1)}, bf16[16,3584]{1,0:T(8,128)(2,1)S(1)}, u32[]{:S(2)}, u32[]{:S(2)}) collective-permute-start(bf16[16,3584]{1,0:T(8,128)(2,1)S(1)} %fusion.61), channel_id=1, source_target_pairs={{8,0},{16,8},{24,16},{9,1},{17,9},{25,17},{10,2},{18,10},{26,18},{... | collective-permute-start | bytes 344072 | tf_op jit(solution)/shard_map/ppermute | solution.py:16
  59.3 9.9 %all-to-all-start.2 = ((bf16[8,4,3584]{2,1,0:T(4,128)(2,1)}), bf16[8,4,3584]{2,1,0:T(4,128)(2,1)S(1)}, u32[]{:S(2)}, u32[]{:S(2)}) async-start(bf16[8,4,3584]{2,1,0:T(4,128)(2,1)} %copy.28), calls=%async_computation.2 | async-start | bytes 458752 | tf_op jit(solution)/shard_map/all_to_all | solution.py:112
  73.8 12.0 %copy-start.6 = (s32[2,1,16,1]{2,3,1,0:T(1,128)S(1)}, s32[2,1,16,1]{2,3,1,0:T(1,128)}, u32[]{:S(2)}) copy-start(s32[2,1,16,1]{2,3,1,0:T(1,128)} %param.18) | copy-start | bytes 388
  82.4 9.9 %all-to-all-start.3 = ((bf16[8,4,3584]{2,1,0:T(4,128)(2,1)}), bf16[8,4,3584]{2,1,0:T(4,128)(2,1)S(1)}, u32[]{:S(2)}, u32[]{:S(2)}) async-start(bf16[8,4,3584]{2,1,0:T(4,128)(2,1)} %reshape.449), calls=%async_computation.3 | async-start | bytes 458752 | tf_op jit(solution)/shard_map/all_to_all | solution.py:56
where the time goes:
time: 96.4 us; the launch traced here: 95.5 us
  matrix products  30 us (31%)
  waiting for transfers between devices  23.5 us (24%)
  starting transfers between devices  21 us (22%)
  local copies, waits for them, and re-layouts  10.9 us (11%)
  other arithmetic  9.2 us (10%)
  between operations  0.98 us (1%)
    dot_general x2, matrix products, run_experts(): jnp.dot(hidden, down_rows, preferred_element_type=jnp.float32)  15.7 us
    all_to_all x2, waiting for transfers between devices, run_experts(): lax.all_to_all(partial_value, 'expert', split_axis=0, concat_axis=0, tile...  13.1 us
    dot_general x2, matrix products, run_experts(): gate_pre = jnp.dot(flat_rows, gate_cols, preferred_element_type=jnp.float32)  8.89 us
    all_to_all x2, starting transfers between devices, shards(): lax.all_to_all(outgoing, 'expert', split_axis=0, concat_axis=0, tiled=True)  8.57 us
    all_to_all x2, starting transfers between devices, run_experts(): lax.all_to_all(partial_value, 'expert', split_axis=0, concat_axis=0, tile...  7.6 us
    all_to_all x2, waiting for transfers between devices, shards(): lax.all_to_all(outgoing, 'expert', split_axis=0, concat_axis=0, tiled=True)  5.22 us
    ppermute x2, waiting for transfers between devices, shifted(): return lax.ppermute(value, axis, pairs)  5.21 us
    ppermute x2, starting transfers between devices, shifted(): return lax.ppermute(value, axis, pairs)  4.78 us
  transfers between devices with their start and end apart: 6, of which 5 were waited for; matrix products, arithmetic and copies ran while one was open for 10% of the time, Pallas kernels for 0%

commit v1 on v0

--- a/solution.py
+++ b/solution.py
@@ -1,10 +1,17 @@
+import functools
+
 import jax
 import jax.numpy as jnp
 from jax import lax
+from jax.experimental import pallas as pl
+from jax.experimental.pallas import tpu as pltpu
 from jax.sharding import PartitionSpec as P
 
 TOP = 1
 TICKS = 2
+EXPERTS = 8
+LANES = 128
+SUBLANES = 16
 
 
 norm_eps = 1e-06
@@ -61,7 +68,7 @@
     return token_rows.astype(jnp.float32) + jnp.sum(weights[:, :, None] * picked, axis=1)
 
 
-def shards(
+def grouped_shards(
     up_state,
     down_state,
     entering_up,
@@ -79,7 +86,7 @@
     down_rows = w_down[0]
     gain_row = norm_gain[0]
     router_cols = router[0]
-    group_size = max(1, lax.axis_size("expert") // 8)
+    group_size = max(1, lax.axis_size("expert") // EXPERTS)
     expert_count = lax.axis_size("expert") // group_size
     segment_id = lax.axis_index("pipe")
     last_segment = lax.axis_size("pipe") - 1
@@ -130,6 +137,338 @@
     return (up_done[None], down_done[None])
 
 
+def iota(shape, axis):
+    return lax.broadcasted_iota(jnp.int32, shape, axis)
+
+
+def slot_map(up_ids, down_ids, parts, slot_cap):
+    rows = up_ids.shape[1]
+    span = 2 * rows * parts
+    diagonal = iota((rows, rows), 0) == iota((rows, rows), 1)
+    up_ids = jnp.sum(jnp.where(diagonal, up_ids, 0), axis=1, keepdims=True)
+    down_ids = jnp.sum(jnp.where(diagonal, down_ids, 0), axis=1, keepdims=True)
+    lane = iota((rows, span), 1)
+    row = iota((rows, span), 0)
+    own = lane % rows
+    way = lane // rows % 2
+    ids = jnp.where(way == 0, up_ids, down_ids)
+    chosen = jnp.sum(jnp.where(row == own, ids, 0), axis=0, keepdims=True)
+    rank = jnp.sum(jnp.where((ids == chosen) & (row < own), 1, 0), axis=0, keepdims=True)
+    lane = iota((1, span), 1)
+    piece = lane // (2 * rows)
+    way = lane // rows % 2
+    target = chosen * SUBLANES + piece * (2 * slot_cap) + way * slot_cap + rank
+    return jnp.where(iota((span, span), 0) == target, 1.0, 0.0)
+
+
+def block_map(parts, slot_cap, span):
+    wide = 2 * slot_cap
+    rows = span // parts
+    lane = iota((span, span), 1)
+    block, within = lane // SUBLANES, lane % SUBLANES
+    target = within // wide * rows + block * wide + within % wide
+    return jnp.where(iota((span, span), 0) == target, 1.0, 0.0)
+
+
+def moved(onehot, rows):
+    return jnp.dot(
+        onehot.astype(jnp.bfloat16), rows, preferred_element_type=jnp.float32
+    ).astype(jnp.bfloat16)
+
+
+def pack_rows(onehot, up_rows, down_rows, parts):
+    width = up_rows.shape[1] // parts
+    pieces = []
+    for q in range(parts):
+        pieces += [up_rows[:, q * width : (q + 1) * width], down_rows[:, q * width : (q + 1) * width]]
+    return moved(onehot, jnp.concatenate(pieces, axis=0))
+
+
+def started(sources, targets, sems, first=0):
+    copies = [
+        pltpu.make_async_copy(source, target, sems.at[first + i])
+        for i, (source, target) in enumerate(zip(sources, targets))
+    ]
+    for copy in copies:
+        copy.start()
+    return copies
+
+
+def row_chunks(source, target, count):
+    step = target.shape[0] // count
+    ranges = [pl.ds(i * step, step) for i in range(count)]
+    return [source.at[r] for r in ranges], [target.at[r] for r in ranges]
+
+
+def prepare_kernel(
+    parts,
+    slot_cap,
+    ticks,
+    early,
+    up,
+    down,
+    up_ids,
+    down_ids,
+    enter_up,
+    enter_down,
+    gain,
+    router,
+    w_down,
+    out_ref,
+    maps_ref,
+    backs_ref,
+    enter_up_v,
+    enter_down_v,
+    gain_v,
+    router_v,
+    early_v,
+    up_v,
+    down_v,
+    up_i,
+    down_i,
+    cols_v,
+    sems,
+):
+    sources = (up_ids, down_ids, up.at[0], down.at[0], router.at[0], gain, enter_up, enter_down)
+    targets = (up_i, down_i, up_v, down_v, cols_v, gain_v, enter_up_v, enter_down_v)
+    copies = started(sources, targets, sems)
+    rows = early_v.shape[0] // early
+    ranges = [pl.ds(i * rows, rows) for i in range(early)]
+    late = started(
+        [w_down.at[0, r] for r in ranges], [early_v.at[r] for r in ranges], sems, len(copies)
+    )
+    copies[0].wait()
+    copies[1].wait()
+    onehots = [slot_map(up_i[t, 0], down_i[t, 0], parts, slot_cap) for t in range(ticks)]
+    copies[2].wait()
+    copies[3].wait()
+    out_ref[...] = pack_rows(onehots[0], up_v[...], down_v[...], parts)
+    for t in range(ticks):
+        maps_ref[t] = onehots[t].astype(jnp.bfloat16)
+        backs_ref[t] = onehots[t].T.astype(jnp.bfloat16)
+    copies[4].wait()
+    cols = cols_v[...].astype(jnp.float32)
+    mine = iota(cols.shape, 0) == lax.axis_index("expert")
+    router_v[...] = jnp.sum(jnp.where(mine, cols, 0.0), axis=0, keepdims=True)
+    for copy in copies[5:] + late:
+        copy.wait()
+
+
+def resend_kernel(parts, pipe, tick_id, even_ref, odd_ref, enter_up_ref, enter_down_ref, maps_ref, out_ref):
+    place = lax.axis_index("pipe")
+    is_even = place % 2 == 0
+    even, odd = even_ref[...], odd_ref[...]
+    up_rows = jnp.where(is_even, odd, even)
+    down_rows = jnp.where(is_even, even, odd)
+    up_rows = jnp.where(place == 0, enter_up_ref[...], up_rows)
+    down_rows = jnp.where(place == pipe - 1, enter_down_ref[...], down_rows)
+    out_ref[...] = pack_rows(maps_ref[tick_id], up_rows, down_rows, parts)
+
+
+def unpack_kernel(tick_id, by_parity, in_ref, backs_ref, first_ref, second_ref):
+    rows = first_ref.shape[0]
+    width = in_ref.shape[1]
+    back = moved(backs_ref[tick_id], in_ref[...])
+    swap = lax.axis_index("pipe") % 2 == 1 if by_parity else None
+    for q in range(first_ref.shape[1] // width):
+        up_piece = back[2 * q * rows : (2 * q + 1) * rows]
+        down_piece = back[(2 * q + 1) * rows : (2 * q + 2) * rows]
+        if by_parity:
+            up_piece, down_piece = (
+                jnp.where(swap, down_piece, up_piece),
+                jnp.where(swap, up_piece, down_piece),
+            )
+        first_ref[:, q * width : (q + 1) * width] = up_piece
+        second_ref[:, q * width : (q + 1) * width] = down_piece
+
+
+def expert_rows(parts, slot_cap, in_ref, gain_ref, router_ref, out_ref, x_ref, inner, outer):
+    span, width = in_ref.shape
+    rows = span // parts
+    onehot = block_map(parts, slot_cap, span)
+    spread = moved(onehot, in_ref[...])
+    for q in range(parts):
+        x_ref[:, q * width : (q + 1) * width] = spread[q * rows : (q + 1) * rows]
+    widened = x_ref[...].astype(jnp.float32)
+    inverse = lax.rsqrt(jnp.mean(widened * widened, axis=1, keepdims=True) + norm_eps)
+    normed = (widened * inverse * gain_ref[...]).astype(jnp.bfloat16)
+    logit = jnp.sum(normed.astype(jnp.float32) * router_ref[...], axis=1, keepdims=True)
+    weight = jax.nn.sigmoid(logit)
+    gate_pre = up_pre = part = 0.0
+    start = 0
+    for gate, up, copies in inner:
+        for copy in copies:
+            copy.wait()
+        piece = normed[:, start : start + gate.shape[0]]
+        gate_pre += jnp.dot(piece, gate[...], preferred_element_type=jnp.float32)
+        up_pre += jnp.dot(piece, up[...], preferred_element_type=jnp.float32)
+        start += gate.shape[0]
+    hidden = (jax.nn.silu(gate_pre) * up_pre).astype(jnp.bfloat16)
+    start = 0
+    for down, copies in outer:
+        for copy in copies:
+            copy.wait()
+        piece = hidden[:, start : start + down.shape[0]]
+        part += jnp.dot(piece, down[...], preferred_element_type=jnp.float32)
+        start += down.shape[0]
+    part = part.astype(jnp.bfloat16).astype(jnp.float32)
+    done = (x_ref[...].astype(jnp.float32) + weight * part).astype(jnp.bfloat16)
+    pieces = [done[:, q * width : (q + 1) * width] for q in range(parts)]
+    out_ref[...] = moved(onehot.T, jnp.concatenate(pieces, axis=0))
+
+
+def first_kernel(
+    parts,
+    slot_cap,
+    chunks,
+    in_ref,
+    gain_ref,
+    router_ref,
+    early_ref,
+    gate,
+    up,
+    down,
+    out_ref,
+    gate_v,
+    up_v,
+    late_v,
+    x_ref,
+    sems,
+):
+    step = gate_v.shape[0] // chunks
+    inner = []
+    for i in range(chunks):
+        r = pl.ds(i * step, step)
+        copies = started((gate.at[0, r], up.at[0, r]), (gate_v.at[r], up_v.at[r]), sems, 2 * i)
+        inner.append((gate_v.at[r], up_v.at[r], copies))
+    early = early_ref.shape[0]
+    step = late_v.shape[0] // 2
+    ranges = [(pl.ds(i * step, step), pl.ds(early + i * step, step)) for i in range(2)]
+    copies = started(
+        [down.at[0, s] for _, s in ranges], [late_v.at[r] for r, _ in ranges], sems, 2 * chunks
+    )
+    outer = [(early_ref, [])] + [(late_v.at[r], [c]) for (r, _), c in zip(ranges, copies)]
+    expert_rows(parts, slot_cap, in_ref, gain_ref, router_ref, out_ref, x_ref, inner, outer)
+
+
+def later_kernel(
+    parts, slot_cap, in_ref, gain_ref, router_ref, early_ref, gate_ref, up_ref, late_ref, out_ref, x_ref
+):
+    inner = [(gate_ref, up_ref, [])]
+    outer = [(early_ref, []), (late_ref, [])]
+    expert_rows(parts, slot_cap, in_ref, gain_ref, router_ref, out_ref, x_ref, inner, outer)
+
+
+VMEM_SPEC = pl.BlockSpec(memory_space=pltpu.VMEM)
+HBM_SPEC = pl.BlockSpec(memory_space=pltpu.HBM)
+
+
+def local_call(kernel, out_shapes, near, far=(), scratch=(), limit=8 << 20):
+    far = [pltpu.with_memory_space_constraint(x, pltpu.HBM) for x in far]
+    return pl.pallas_call(
+        kernel,
+        out_shape=out_shapes,
+        in_specs=[VMEM_SPEC] * len(near) + [HBM_SPEC] * len(far),
+        out_specs=jax.tree.map(lambda _: VMEM_SPEC, out_shapes),
+        scratch_shapes=list(scratch),
+        compiler_params=pltpu.CompilerParams(vmem_limit_bytes=limit),
+    )(*near, *far)
+
+
+def exchanged(blocks):
+    return lax.all_to_all(blocks, "expert", split_axis=0, concat_axis=0, tiled=True)
+
+
+EARLY_COPIES = 4
+CHUNKS = 7
+
+
+def single_shards(
+    up_state,
+    down_state,
+    entering_up,
+    entering_down,
+    up_route,
+    down_route,
+    norm_gain,
+    router,
+    w_gate,
+    w_up,
+    w_down,
+):
+    pipe = lax.axis_size("pipe")
+    experts = lax.axis_size("expert")
+    rows, features = up_state.shape[1:]
+    hidden = w_gate.shape[2]
+    slot_cap = rows * TOP // experts
+    parts = SUBLANES // (2 * slot_cap)
+    span = experts * SUBLANES
+    early = hidden // 2
+    blocks = pltpu.VMEM((span, features // parts), jnp.bfloat16)
+    batch = pltpu.VMEM((rows, features), jnp.bfloat16)
+    ids_v = pltpu.VMEM((TICKS, 1, 1, rows), jnp.int32)
+    row_v = pltpu.VMEM((1, features), jnp.float32)
+    x_v = pltpu.VMEM((span // parts, features), jnp.bfloat16)
+    maps_v = pltpu.VMEM((TICKS, span, span), jnp.bfloat16)
+    inner_v = pltpu.VMEM((features, hidden), jnp.bfloat16)
+    sent, maps, backs, enter_up, enter_down, gain, column, early_down = local_call(
+        functools.partial(prepare_kernel, parts, slot_cap, TICKS, EARLY_COPIES),
+        (blocks, maps_v, maps_v, batch, batch, row_v, row_v, pltpu.VMEM((early, features), jnp.bfloat16)),
+        (),
+        (
+            up_state,
+            down_state,
+            up_route.transpose(0, 1, 3, 2),
+            down_route.transpose(0, 1, 3, 2),
+            entering_up,
+            entering_down,
+            norm_gain,
+            router.transpose(0, 2, 1),
+            w_down,
+        ),
+        [
+            batch,
+            batch,
+            ids_v,
+            ids_v,
+            pltpu.VMEM(router.shape[:0:-1], router.dtype),
+            pltpu.SemaphoreType.DMA((8 + EARLY_COPIES,)),
+        ],
+    )
+    done, gate, up, late_down = local_call(
+        functools.partial(first_kernel, parts, slot_cap, CHUNKS),
+        (blocks, inner_v, inner_v, pltpu.VMEM((hidden - early, features), jnp.bfloat16)),
+        (exchanged(sent), gain, column, early_down),
+        (w_gate, w_up, w_down),
+        [x_v, pltpu.SemaphoreType.DMA((2 * CHUNKS + 2,))],
+    )
+    even_pairs = [(i, i ^ 1) for i in range(pipe) if i ^ 1 < pipe]
+    odd_pairs = [(i, ((i + 1) ^ 1) - 1) for i in range(pipe) if 0 <= ((i + 1) ^ 1) - 1 < pipe]
+    for tick_id in range(1, TICKS):
+        kernel = functools.partial(unpack_kernel, tick_id - 1, True)
+        first, second = local_call(kernel, (batch, batch), (exchanged(done), backs))
+        first = lax.ppermute(first, "pipe", even_pairs)
+        second = lax.ppermute(second, "pipe", odd_pairs)
+        kernel = functools.partial(resend_kernel, parts, pipe, tick_id)
+        sent = local_call(kernel, blocks, (first, second, enter_up, enter_down, maps))
+        kernel = functools.partial(later_kernel, parts, slot_cap)
+        args = (exchanged(sent), gain, column, early_down, gate, up, late_down)
+        done = local_call(kernel, blocks, args, (), [x_v])
+    batch = jax.ShapeDtypeStruct((rows, features), jnp.bfloat16)
+    kernel = functools.partial(unpack_kernel, TICKS - 1, False)
+    first, second = local_call(kernel, (batch, batch), (exchanged(done), backs))
+    return (first[None], second[None])
+
+
+def shards(*args):
+    rows, features = args[0].shape[1:]
+    experts = lax.axis_size("expert")
+    slot_cap = rows * TOP // EXPERTS
+    fits = experts == EXPERTS and rows % SUBLANES == 0 and SUBLANES % (2 * slot_cap) == 0
+    fits = fits and features % (SUBLANES // (2 * slot_cap) * LANES) == 0
+    return single_shards(*args) if fits else grouped_shards(*args)
+
+
 def solution(mesh):
     return jax.shard_map(
         shards,

time: 96.4 us -> 62.3 us (0.65)
  the two profiles are of different devices: /device:TPU:0 before, /device:TPU:16 now
where the time goes in v1:
time: 62.3 us; the launch traced here: 62 us
  blocking collectives  37.1 us (60%)
  Pallas kernels  16 us (26%)
  waiting for transfers between devices  4.76 us (8%)
  starting transfers between devices  3.55 us (6%)
  between operations  0.68 us (1%)
    all_to_all x4, blocking collectives, exchanged(): lax.all_to_all(blocks, 'expert', split_axis=0, concat_axis=0, tiled=True)  37.1 us
    pallas_call x6, Pallas kernels, local_call(): pl.pallas_call(kernel, out_shape=out_shapes, in_specs=[VMEM_SPEC] * len(n...  16 us
    ppermute x1, waiting for transfers between devices, single_shards(): second = lax.ppermute(second, 'pipe', odd_pairs)  3.46 us
    ppermute x1, starting transfers between devices, single_shards(): second = lax.ppermute(second, 'pipe', odd_pairs)  1.91 us
    ppermute x1, starting transfers between devices, single_shards(): first = lax.ppermute(first, 'pipe', even_pairs)  1.64 us
    ppermute x1, waiting for transfers between devices, single_shards(): first = lax.ppermute(first, 'pipe', even_pairs)  1.3 us
  transfers between devices with their start and end apart: 2, of which 2 were waited for; matrix products, arithmetic and copies ran while one was open for 0% of the time, Pallas kernels for 0%

profile of v1, /device:TPU:16, one launch (start us, length us, event | category | flops | bytes accessed | tf_op | source)
XLA Modules:
  0.0 62.0 jit_solution(5919236130129832410)
XLA Ops:
  0.6 2.4 %shard_map.122 = (bf16[128,896]{1,0:T(8,128)(2,1)S(1)}, bf16[2,128,128]{2,1,0:T(8,128)(2,1)S(1)}, bf16[2,128,128]{2,1,0:T(8,128)(2,1)S(1)}, bf16[16,3584]{1,0:T(...) custom-call(bf16[1,16,3584]{2,1,0:T(8,128)(2,1)} %up.2, ...), custom_call_target="tpu_custom_call" | custom-call | tf_op jit(solution)/shard_map/pallas_call | solution.py:368
  3.1 10.1 %all_to_all.44 = bf16[8,16,896]{2,1,0:T(8,128)(2,1)S(1)} all-to-all(bf16[8,16,896]{2,1,0:T(8,128)(2,1)S(1)} %bitcast.23), channel_id=1, replica_groups=mesh['pipe'=4,'expert'=8] {'expert'}, dimensions={0} | all-to-all | bytes 458752 | tf_op jit(solution)/shard_map/all_to_all | solution.py:379
  13.2 7.7 %shard_map.123 = (bf16[128,896]{1,0:T(8,128)(2,1)S(1)}, bf16[3584,1024]{1,0:T(8,128)(2,1)S(1)}, bf16[3584,1024]{1,0:T(8,128)(2,1)S(1)}, bf16[512,3584]{1,0:T(8,128)(2,1)S(1)}) custom-call(bf16[128,896]{1,0:T(8,128)(2,1)S(1)} %bitcast.19, f32[1,3584]{1,0:T(1,128)S(1)} %get-tuple-element.19.gain_ref, f32[1,3584]{1,0:T(1,128)S(1)} %get-tuple-element.20.router_ref, ...), custom_call_target="tpu_custom_call" | custom-call | tf_op jit(solution)/shard_map/pallas_call | solution.py:368
  20.9 9.0 %all_to_all.45 = bf16[8,16,896]{2,1,0:T(8,128)(2,1)S(1)} all-to-all(bf16[8,16,896]{2,1,0:T(8,128)(2,1)S(1)} %bitcast.24), channel_id=1, replica_groups=mesh['pipe'=4,'expert'=8] {'expert'}, dimensions={0} | all-to-all | bytes 458752 | tf_op jit(solution)/shard_map/all_to_all | solution.py:379
  29.9 0.2 shard_map.124
  30.1 1.6 %collective-permute-start = (bf16[16,3584]{1,0:T(8,128)(2,1)S(1)}, bf16[16,3584]{1,0:T(8,128)(2,1)S(1)}, u32[]{:S(2)}, u32[]{:S(2)}) collective-permute-start(bf16[16,3584]{1,0:T(8,128)(2,1)S(1)} %get-tuple-element.24), channel_id=1, source_target_pairs={{0,8},{8,0},{16,24},{24,16},{1,9},{9,1},{17,25},{25,17},{2,10},{10... | collective-permute-start | bytes 344072 | tf_op jit(solution)/shard_map/ppermute | solution.py:450
  31.8 1.9 %collective-permute-start.1 = (bf16[16,3584]{1,0:T(8,128)(2,1)S(1)}, bf16[16,3584]{1,0:T(8,128)(2,1)S(1)}, u32[]{:S(2)}, u32[]{:S(2)}) collective-permute-start(bf16[16,3584]{1,0:T(8,128)(2,1)S(1)} %get-tuple-element.25), channel_id=1, source_target_pairs={{8,16},{16,8},{9,17},{17,9},{10,18},{18,10},{11,19},{19,11},{12,20... | collective-permute-start | bytes 344072 | tf_op jit(solution)/shard_map/ppermute | solution.py:451
  33.7 1.3 %collective-permute-done.even_ref = bf16[16,3584]{1,0:T(8,128)(2,1)S(1)} collective-permute-done((bf16[16,3584]{1,0:T(8,128)(2,1)S(1)}, bf16[16,3584]{1,0:T(8,128)(2,1)S(1)}, u32[]{:S(2)}, u32[]{:S(2)}) %collective-permute-start) | collective-permute-done | bytes 114720 | tf_op jit(solution)/shard_map/ppermute | solution.py:450
  35.0 3.5 %collective-permute-done.1.odd_ref = bf16[16,3584]{1,0:T(8,128)(2,1)S(1)} collective-permute-done((bf16[16,3584]{1,0:T(8,128)(2,1)S(1)}, bf16[16,3584]{1,0:T(8,128)(2,1)S(1)}, u32[]{:S(2)}, u32[]{:S(2)}) %collective-permute-start.1) | collective-permute-done | bytes 114720 | tf_op jit(solution)/shard_map/ppermute | solution.py:451
  38.4 0.2 shard_map.125
  38.7 9.0 %all_to_all.46 = bf16[8,16,896]{2,1,0:T(8,128)(2,1)S(1)} all-to-all(bf16[8,16,896]{2,1,0:T(8,128)(2,1)S(1)} %bitcast.22), channel_id=1, replica_groups=mesh['pipe'=4,'expert'=8] {'expert'}, dimensions={0} | all-to-all | bytes 458752 | tf_op jit(solution)/shard_map/all_to_all | solution.py:379
  47.6 4.5 %shard_map.126 = bf16[128,896]{1,0:T(8,128)(2,1)S(1)} custom-call(bf16[128,896]{1,0:T(8,128)(2,1)S(1)} %bitcast.17, f32[1,3584]{1,0:T(1,128)S(1)} %get-tuple-element.19.gain_ref, f32[1,3584]{1,0:T(1,128)S(1)} %get-tuple-element.20.router_ref, bf16[512,3584]{1,0:T(8,128)(2,1)S(1)} %get-tuple-element.21.early_ref, ...), custom_call_target="tpu_custom_call" | custom-call | tf_op jit(solution)/shard_map/pallas_call | solution.py:368
  52.1 9.0 %all_to_all.47 = bf16[8,16,896]{2,1,0:T(8,128)(2,1)S(1)} all-to-all(bf16[8,16,896]{2,1,0:T(8,128)(2,1)S(1)} %bitcast.18), channel_id=1, replica_groups=mesh['pipe'=4,'expert'=8] {'expert'}, dimensions={0} | all-to-all | bytes 458752 | tf_op jit(solution)/shard_map/all_to_all | solution.py:379
  61.1 0.9 %shard_map.127 = (bf16[16,3584]{1,0:T(8,128)(2,1)}, bf16[16,3584]{1,0:T(8,128)(2,1)}) custom-call(bf16[128,896]{1,0:T(8,128)(2,1)S(1)} %bitcast.20, bf16[2,128,128]{2,1,0:T(8,128)(2,1)S(1)} %get-tuple-element.23.backs_ref), custom_call_target="tpu_custom_call" | custom-call | tf_op jit(solution)/shard_map/pallas_call | solution.py:368
Async XLA Ops:
  30.1 4.9 %collective-permute-start = (bf16[16,3584]{1,0:T(8,128)(2,1)S(1)}, bf16[16,3584]{1,0:T(8,128)(2,1)S(1)}, u32[]{:S(2)}, u32[]{:S(2)}) collective-permute-start(bf16[16,3584]{1,0:T(8,128)(2,1)S(1)} %get-tuple-element.24), channel_id=1, source_target_pairs={{0,8},{8,0},{16,24},{24,16},{1,9},{9,1},{17,25},{25,17},{2,10},{10... | collective-permute-start | bytes 344072 | tf_op jit(solution)/shard_map/ppermute | solution.py:450
  31.8 6.7 %collective-permute-start.1 = (bf16[16,3584]{1,0:T(8,128)(2,1)S(1)}, bf16[16,3584]{1,0:T(8,128)(2,1)S(1)}, u32[]{:S(2)}, u32[]{:S(2)}) collective-permute-start(bf16[16,3584]{1,0:T(8,128)(2,1)S(1)} %get-tuple-element.25), channel_id=1, source_target_pairs={{8,16},{16,8},{9,17},{17,9},{10,18},{18,10},{11,19},{19,11},{12,20... | collective-permute-start | bytes 344072 | tf_op jit(solution)/shard_map/ppermute | solution.py:451

commit v2 on v1

--- a/solution.py
+++ b/solution.py
@@ -141,39 +141,67 @@
     return lax.broadcasted_iota(jnp.int32, shape, axis)
 
 
-def slot_map(up_ids, down_ids, parts, slot_cap):
+def place():
+    index = lax.axis_index("expert")
+    return index // 2, index % 2
+
+
+def one_hot(rows, target):
+    return jnp.where(iota((rows, target.shape[1]), 0) == target, 1.0, 0.0)
+
+
+def row_maps(up_ids, down_ids, parts, slot_cap, span):
     rows = up_ids.shape[1]
-    span = 2 * rows * parts
+    width = 2 * rows * parts
     diagonal = iota((rows, rows), 0) == iota((rows, rows), 1)
     up_ids = jnp.sum(jnp.where(diagonal, up_ids, 0), axis=1, keepdims=True)
     down_ids = jnp.sum(jnp.where(diagonal, down_ids, 0), axis=1, keepdims=True)
-    lane = iota((rows, span), 1)
-    row = iota((rows, span), 0)
+    lane = iota((rows, width), 1)
+    row = iota((rows, width), 0)
     own = lane % rows
-    way = lane // rows % 2
-    ids = jnp.where(way == 0, up_ids, down_ids)
+    ids = jnp.where(lane // rows % 2 == 0, up_ids, down_ids)
     chosen = jnp.sum(jnp.where(row == own, ids, 0), axis=0, keepdims=True)
     rank = jnp.sum(jnp.where((ids == chosen) & (row < own), 1, 0), axis=0, keepdims=True)
-    lane = iota((1, span), 1)
-    piece = lane // (2 * rows)
-    way = lane // rows % 2
-    target = chosen * SUBLANES + piece * (2 * slot_cap) + way * slot_cap + rank
-    return jnp.where(iota((span, span), 0) == target, 1.0, 0.0)
-
-
-def block_map(parts, slot_cap, span):
+    lane = iota((1, width), 1)
+    within = lane // (2 * rows) * (2 * slot_cap) + lane // rows % 2 * slot_cap + rank
+    chip, core = place()
+    across = (chosen // 2) ^ chip ^ (span // (2 * SUBLANES) - 1)
+    to_core = chosen % 2
+    sent = (across * 2 + to_core) * SUBLANES + within
+    array = across + jnp.where(to_core == core, 0, span // (2 * SUBLANES))
+    received = (array * 2 + core) * SUBLANES + within
+    return one_hot(span, sent), one_hot(2 * span, received)
+
+
+def expert_maps(parts, slot_cap, span):
     wide = 2 * slot_cap
     rows = span // parts
-    lane = iota((span, span), 1)
-    block, within = lane // SUBLANES, lane % SUBLANES
-    target = within // wide * rows + block * wide + within % wide
-    return jnp.where(iota((span, span), 0) == target, 1.0, 0.0)
+    chips = span // (2 * SUBLANES)
+    _, core = place()
+    lane = iota((1, 2 * span), 1)
+    array, to_core, within = lane // (2 * SUBLANES), lane // SUBLANES % 2, lane % SUBLANES
+    row = within // wide * rows + array * wide + within % wide
+    received = one_hot(span, jnp.where(to_core == core, row, -1))
+    lane = iota((1, span), 1)
+    array, to_core, within = lane // (2 * SUBLANES), lane // SUBLANES % 2, lane % SUBLANES
+    array = array + jnp.where(to_core == core, 0, chips)
+    return received, one_hot(span, within // wide * rows + array * wide + within % wide)
 
 
 def moved(onehot, rows):
     return jnp.dot(
         onehot.astype(jnp.bfloat16), rows, preferred_element_type=jnp.float32
     ).astype(jnp.bfloat16)
+
+
+def stacked(refs):
+    return jnp.concatenate([ref[...] for ref in refs], axis=0)
+
+
+def put(value, refs):
+    rows = refs[0].shape[0]
+    for i, ref in enumerate(refs):
+        ref[...] = value[i * rows : (i + 1) * rows]
 
 
 def pack_rows(onehot, up_rows, down_rows, parts):
@@ -194,10 +222,9 @@
     return copies
 
 
-def row_chunks(source, target, count):
-    step = target.shape[0] // count
-    ranges = [pl.ds(i * step, step) for i in range(count)]
-    return [source.at[r] for r in ranges], [target.at[r] for r in ranges]
+def cut(rows, count):
+    step = rows // count
+    return [pl.ds(i * step, step) for i in range(count)]
 
 
 def prepare_kernel(
@@ -213,8 +240,8 @@
     enter_down,
     gain,
     router,
-    w_down,
-    out_ref,
+    w_up,
+    out_refs,
     maps_ref,
     backs_ref,
     enter_up_v,
@@ -232,20 +259,20 @@
     sources = (up_ids, down_ids, up.at[0], down.at[0], router.at[0], gain, enter_up, enter_down)
     targets = (up_i, down_i, up_v, down_v, cols_v, gain_v, enter_up_v, enter_down_v)
     copies = started(sources, targets, sems)
-    rows = early_v.shape[0] // early
-    ranges = [pl.ds(i * rows, rows) for i in range(early)]
+    ranges = cut(early_v.shape[0], early)
     late = started(
-        [w_down.at[0, r] for r in ranges], [early_v.at[r] for r in ranges], sems, len(copies)
+        [w_up.at[0, r] for r in ranges], [early_v.at[r] for r in ranges], sems, len(copies)
     )
     copies[0].wait()
     copies[1].wait()
-    onehots = [slot_map(up_i[t, 0], down_i[t, 0], parts, slot_cap) for t in range(ticks)]
+    span = maps_ref.shape[1]
+    maps = [row_maps(up_i[t, 0], down_i[t, 0], parts, slot_cap, span) for t in range(ticks)]
     copies[2].wait()
     copies[3].wait()
-    out_ref[...] = pack_rows(onehots[0], up_v[...], down_v[...], parts)
+    put(pack_rows(maps[0][0], up_v[...], down_v[...], parts), out_refs)
     for t in range(ticks):
-        maps_ref[t] = onehots[t].astype(jnp.bfloat16)
-        backs_ref[t] = onehots[t].T.astype(jnp.bfloat16)
+        maps_ref[t] = maps[t][0].astype(jnp.bfloat16)
+        backs_ref[t] = maps[t][1].T.astype(jnp.bfloat16)
     copies[4].wait()
     cols = cols_v[...].astype(jnp.float32)
     mine = iota(cols.shape, 0) == lax.axis_index("expert")
@@ -254,21 +281,21 @@
         copy.wait()
 
 
-def resend_kernel(parts, pipe, tick_id, even_ref, odd_ref, enter_up_ref, enter_down_ref, maps_ref, out_ref):
-    place = lax.axis_index("pipe")
-    is_even = place % 2 == 0
+def resend_kernel(parts, pipe, tick_id, even_ref, odd_ref, enter_up_ref, enter_down_ref, maps_ref, out_refs):
+    section = lax.axis_index("pipe")
+    is_even = section % 2 == 0
     even, odd = even_ref[...], odd_ref[...]
     up_rows = jnp.where(is_even, odd, even)
     down_rows = jnp.where(is_even, even, odd)
-    up_rows = jnp.where(place == 0, enter_up_ref[...], up_rows)
-    down_rows = jnp.where(place == pipe - 1, enter_down_ref[...], down_rows)
-    out_ref[...] = pack_rows(maps_ref[tick_id], up_rows, down_rows, parts)
-
-
-def unpack_kernel(tick_id, by_parity, in_ref, backs_ref, first_ref, second_ref):
+    up_rows = jnp.where(section == 0, enter_up_ref[...], up_rows)
+    down_rows = jnp.where(section == pipe - 1, enter_down_ref[...], down_rows)
+    put(pack_rows(maps_ref[tick_id], up_rows, down_rows, parts), out_refs)
+
+
+def unpack_kernel(tick_id, by_parity, in_refs, backs_ref, first_ref, second_ref):
     rows = first_ref.shape[0]
-    width = in_ref.shape[1]
-    back = moved(backs_ref[tick_id], in_ref[...])
+    width = in_refs[0].shape[1]
+    back = moved(backs_ref[tick_id], stacked(in_refs))
     swap = lax.axis_index("pipe") % 2 == 1 if by_parity else None
     for q in range(first_ref.shape[1] // width):
         up_piece = back[2 * q * rows : (2 * q + 1) * rows]
@@ -282,11 +309,12 @@
         second_ref[:, q * width : (q + 1) * width] = down_piece
 
 
-def expert_rows(parts, slot_cap, in_ref, gain_ref, router_ref, out_ref, x_ref, inner, outer):
-    span, width = in_ref.shape
+def expert_rows(parts, slot_cap, in_refs, gain_ref, router_ref, out_refs, x_ref, gates, ups, downs):
+    span = sum(ref.shape[0] for ref in out_refs)
+    width = in_refs[0].shape[1]
     rows = span // parts
-    onehot = block_map(parts, slot_cap, span)
-    spread = moved(onehot, in_ref[...])
+    received, sent = expert_maps(parts, slot_cap, span)
+    spread = moved(received, stacked(in_refs))
     for q in range(parts):
         x_ref[:, q * width : (q + 1) * width] = spread[q * rows : (q + 1) * rows]
     widened = x_ref[...].astype(jnp.float32)
@@ -294,93 +322,122 @@
     normed = (widened * inverse * gain_ref[...]).astype(jnp.bfloat16)
     logit = jnp.sum(normed.astype(jnp.float32) * router_ref[...], axis=1, keepdims=True)
     weight = jax.nn.sigmoid(logit)
-    gate_pre = up_pre = part = 0.0
-    start = 0
-    for gate, up, copies in inner:
-        for copy in copies:
-            copy.wait()
-        piece = normed[:, start : start + gate.shape[0]]
-        gate_pre += jnp.dot(piece, gate[...], preferred_element_type=jnp.float32)
-        up_pre += jnp.dot(piece, up[...], preferred_element_type=jnp.float32)
-        start += gate.shape[0]
-    hidden = (jax.nn.silu(gate_pre) * up_pre).astype(jnp.bfloat16)
-    start = 0
-    for down, copies in outer:
-        for copy in copies:
-            copy.wait()
-        piece = hidden[:, start : start + down.shape[0]]
-        part += jnp.dot(piece, down[...], preferred_element_type=jnp.float32)
-        start += down.shape[0]
-    part = part.astype(jnp.bfloat16).astype(jnp.float32)
+
+    def product(left, pieces):
+        total, start = 0.0, 0
+        for ref, copies in pieces:
+            for copy in copies:
+                copy.wait()
+            part = left[:, start : start + ref.shape[0]]
+            total += jnp.dot(part, ref[...], preferred_element_type=jnp.float32)
+            start += ref.shape[0]
+        return total
+
+    gate_pre = product(normed, gates)
+    hidden = (jax.nn.silu(gate_pre) * product(normed, ups)).astype(jnp.bfloat16)
+    part = product(hidden, downs).astype(jnp.bfloat16).astype(jnp.float32)
     done = (x_ref[...].astype(jnp.float32) + weight * part).astype(jnp.bfloat16)
     pieces = [done[:, q * width : (q + 1) * width] for q in range(parts)]
-    out_ref[...] = moved(onehot.T, jnp.concatenate(pieces, axis=0))
+    put(moved(sent.T, jnp.concatenate(pieces, axis=0)), out_refs)
+
+
+def load_kernel(after_ref, source, target, sems):
+    del after_ref
+    ranges = cut(target.shape[0], sems.shape[0])
+    for copy in started([source.at[0, r] for r in ranges], [target.at[r] for r in ranges], sems):
+        copy.wait()
 
 
 def first_kernel(
     parts,
     slot_cap,
-    chunks,
-    in_ref,
+    in_refs,
     gain_ref,
     router_ref,
+    gate_ref,
     early_ref,
-    gate,
+    down_ref,
     up,
-    down,
-    out_ref,
-    gate_v,
-    up_v,
+    out_refs,
     late_v,
     x_ref,
     sems,
 ):
-    step = gate_v.shape[0] // chunks
-    inner = []
-    for i in range(chunks):
-        r = pl.ds(i * step, step)
-        copies = started((gate.at[0, r], up.at[0, r]), (gate_v.at[r], up_v.at[r]), sems, 2 * i)
-        inner.append((gate_v.at[r], up_v.at[r], copies))
     early = early_ref.shape[0]
-    step = late_v.shape[0] // 2
-    ranges = [(pl.ds(i * step, step), pl.ds(early + i * step, step)) for i in range(2)]
-    copies = started(
-        [down.at[0, s] for _, s in ranges], [late_v.at[r] for r, _ in ranges], sems, 2 * chunks
-    )
-    outer = [(early_ref, [])] + [(late_v.at[r], [c]) for (r, _), c in zip(ranges, copies)]
-    expert_rows(parts, slot_cap, in_ref, gain_ref, router_ref, out_ref, x_ref, inner, outer)
+    step = late_v.shape[0] // sems.shape[0]
+    ranges = cut(late_v.shape[0], sems.shape[0])
+    sources = [up.at[0, pl.ds(early + i * step, step)] for i in range(len(ranges))]
+    copies = started(sources, [late_v.at[r] for r in ranges], sems)
+    ups = [(early_ref, [])] + [(late_v.at[r], [c]) for r, c in zip(ranges, copies)]
+    expert_rows(
+        parts, slot_cap, in_refs, gain_ref, router_ref, out_refs, x_ref, [(gate_ref, [])], ups, [(down_ref, [])]
+    )
 
 
 def later_kernel(
-    parts, slot_cap, in_ref, gain_ref, router_ref, early_ref, gate_ref, up_ref, late_ref, out_ref, x_ref
+    parts, slot_cap, in_refs, gain_ref, router_ref, gate_ref, early_ref, down_ref, late_ref, out_refs, x_ref
 ):
-    inner = [(gate_ref, up_ref, [])]
-    outer = [(early_ref, []), (late_ref, [])]
-    expert_rows(parts, slot_cap, in_ref, gain_ref, router_ref, out_ref, x_ref, inner, outer)
+    ups = [(early_ref, []), (late_ref, [])]
+    expert_rows(
+        parts, slot_cap, in_refs, gain_ref, router_ref, out_refs, x_ref, [(gate_ref, [])], ups, [(down_ref, [])]
+    )
 
 
 VMEM_SPEC = pl.BlockSpec(memory_space=pltpu.VMEM)
 HBM_SPEC = pl.BlockSpec(memory_space=pltpu.HBM)
 
 
-def local_call(kernel, out_shapes, near, far=(), scratch=(), limit=8 << 20):
+def local_call(kernel, out_shapes, near, far=(), scratch=(), limit=8 << 20, cost=None):
     far = [pltpu.with_memory_space_constraint(x, pltpu.HBM) for x in far]
-    return pl.pallas_call(
-        kernel,
-        out_shape=out_shapes,
-        in_specs=[VMEM_SPEC] * len(near) + [HBM_SPEC] * len(far),
-        out_specs=jax.tree.map(lambda _: VMEM_SPEC, out_shapes),
+    close, near_tree = jax.tree.flatten(tuple(near))
+    outs, out_tree = jax.tree.flatten(out_shapes)
+
+    def body(*refs):
+        refs = iter(refs)
+        take = lambda count: [next(refs) for _ in range(count)]
+        args = [*near_tree.unflatten(take(len(close))), *take(len(far))]
+        results = out_tree.unflatten(take(len(outs)))
+        kernel(*args, *(results if isinstance(results, tuple) else (results,)), *refs)
+
+    results = pl.pallas_call(
+        body,
+        out_shape=outs,
+        in_specs=[VMEM_SPEC] * len(close) + [HBM_SPEC] * len(far),
+        out_specs=[VMEM_SPEC] * len(outs),
         scratch_shapes=list(scratch),
         compiler_params=pltpu.CompilerParams(vmem_limit_bytes=limit),
-    )(*near, *far)
-
-
-def exchanged(blocks):
-    return lax.all_to_all(blocks, "expert", split_axis=0, concat_axis=0, tiled=True)
+        cost_estimate=cost,
+    )(*close, *far)
+    return out_tree.unflatten(results)
+
+
+def exchanged(arrays, beside=None):
+    last = len(arrays) - 1
+    devices = range(2 * len(arrays))
+    arrived = [
+        lax.ppermute(arrays[j], "expert", [(i, i ^ (2 * (last - j))) for i in devices])
+        for j in range(last)
+    ]
+    if beside is not None:
+        arrived, beside = lax.optimization_barrier((arrived, beside))
+    arrived.append(arrays[last])
+    passed = [lax.ppermute(x, "expert", [(i, i ^ 1) for i in devices]) for x in arrived]
+    return tuple(arrived + passed), beside
+
+
+def section_pairs(parity, pipe, experts):
+    pairs = []
+    for section in range(pipe):
+        other = ((section + parity) ^ 1) - parity
+        for i in range(experts):
+            target = (other, i) if 0 <= other < pipe else (section, i ^ 1)
+            pairs.append((section * experts + i, target[0] * experts + target[1]))
+    return pairs
 
 
 EARLY_COPIES = 4
-CHUNKS = 7
+LATE_COPIES = 4
+LOAD_COPIES = 4
 
 
 def single_shards(
@@ -403,17 +460,24 @@
     slot_cap = rows * TOP // experts
     parts = SUBLANES // (2 * slot_cap)
     span = experts * SUBLANES
-    early = hidden // 2
-    blocks = pltpu.VMEM((span, features // parts), jnp.bfloat16)
+    early = features // 2
+    blocks = (pltpu.VMEM((2 * SUBLANES, features // parts), jnp.bfloat16),) * (experts // 2)
     batch = pltpu.VMEM((rows, features), jnp.bfloat16)
     ids_v = pltpu.VMEM((TICKS, 1, 1, rows), jnp.int32)
     row_v = pltpu.VMEM((1, features), jnp.float32)
     x_v = pltpu.VMEM((span // parts, features), jnp.bfloat16)
-    maps_v = pltpu.VMEM((TICKS, span, span), jnp.bfloat16)
-    inner_v = pltpu.VMEM((features, hidden), jnp.bfloat16)
-    sent, maps, backs, enter_up, enter_down, gain, column, early_down = local_call(
+    sent, maps, backs, enter_up, enter_down, gain, column, early_up = local_call(
         functools.partial(prepare_kernel, parts, slot_cap, TICKS, EARLY_COPIES),
-        (blocks, maps_v, maps_v, batch, batch, row_v, row_v, pltpu.VMEM((early, features), jnp.bfloat16)),
+        (
+            blocks,
+            pltpu.VMEM((TICKS, span, span), jnp.bfloat16),
+            pltpu.VMEM((TICKS, span, 2 * span), jnp.bfloat16),
+            batch,
+            batch,
+            row_v,
+            row_v,
+            pltpu.VMEM((early, hidden), jnp.bfloat16),
+        ),
         (),
         (
             up_state,
@@ -424,7 +488,7 @@
             entering_down,
             norm_gain,
             router.transpose(0, 2, 1),
-            w_down,
+            w_up,
         ),
         [
             batch,
@@ -435,28 +499,35 @@
             pltpu.SemaphoreType.DMA((8 + EARLY_COPIES,)),
         ],
     )
-    done, gate, up, late_down = local_call(
-        functools.partial(first_kernel, parts, slot_cap, CHUNKS),
-        (blocks, inner_v, inner_v, pltpu.VMEM((hidden - early, features), jnp.bfloat16)),
-        (exchanged(sent), gain, column, early_down),
-        (w_gate, w_up, w_down),
-        [x_v, pltpu.SemaphoreType.DMA((2 * CHUNKS + 2,))],
-    )
-    even_pairs = [(i, i ^ 1) for i in range(pipe) if i ^ 1 < pipe]
-    odd_pairs = [(i, ((i + 1) ^ 1) - 1) for i in range(pipe) if 0 <= ((i + 1) ^ 1) - 1 < pipe]
+    gate = local_call(
+        load_kernel,
+        pltpu.VMEM((features, hidden), jnp.bfloat16),
+        (sent[0],),
+        (w_gate,),
+        [pltpu.SemaphoreType.DMA((LOAD_COPIES,))],
+        cost=pl.CostEstimate(flops=0, transcendentals=0, bytes_accessed=4 * features * hidden),
+    )
+    received, gate = exchanged(sent, gate)
+    done, late_up = local_call(
+        functools.partial(first_kernel, parts, slot_cap),
+        (blocks, pltpu.VMEM((features - early, hidden), jnp.bfloat16)),
+        (received, gain, column, gate, early_up, w_down[0]),
+        (w_up,),
+        [x_v, pltpu.SemaphoreType.DMA((LATE_COPIES,))],
+    )
     for tick_id in range(1, TICKS):
         kernel = functools.partial(unpack_kernel, tick_id - 1, True)
-        first, second = local_call(kernel, (batch, batch), (exchanged(done), backs))
-        first = lax.ppermute(first, "pipe", even_pairs)
-        second = lax.ppermute(second, "pipe", odd_pairs)
+        first, second = local_call(kernel, (batch, batch), (exchanged(done)[0], backs))
+        first = lax.ppermute(first, ("pipe", "expert"), section_pairs(0, pipe, experts))
+        second = lax.ppermute(second, ("pipe", "expert"), section_pairs(1, pipe, experts))
         kernel = functools.partial(resend_kernel, parts, pipe, tick_id)
-        sent = local_call(kernel, blocks, (first, second, enter_up, enter_down, maps))
+        (sent,) = local_call(kernel, (blocks,), (first, second, enter_up, enter_down, maps))
         kernel = functools.partial(later_kernel, parts, slot_cap)
-        args = (exchanged(sent), gain, column, early_down, gate, up, late_down)
-        done = local_call(kernel, blocks, args, (), [x_v])
+        args = (exchanged(sent)[0], gain, column, gate, early_up, w_down[0], late_up)
+        (done,) = local_call(kernel, (blocks,), args, (), [x_v])
     batch = jax.ShapeDtypeStruct((rows, features), jnp.bfloat16)
     kernel = functools.partial(unpack_kernel, TICKS - 1, False)
-    first, second = local_call(kernel, (batch, batch), (exchanged(done), backs))
+    first, second = local_call(kernel, (batch, batch), (exchanged(done)[0], backs))
     return (first[None], second[None])
 
 

time: 62.3 us -> 54.6 us (0.88)
  the two profiles are of different devices: /device:TPU:16 before, /device:TPU:0 now
where the time goes in v2:
time: 54.6 us; the launch traced here: 54.3 us
  waiting for transfers between devices  19.2 us (35%)
  starting transfers between devices  17.9 us (33%)
  Pallas kernels  16.4 us (30%)
  between operations  0.73 us (1%)
    pallas_call x7, Pallas kernels, local_call(): pl.pallas_call(body, out_shape=outs, in_specs=[VMEM_SPEC] * len(close) +...  16.4 us
    ppermute x12, starting transfers between devices, exchanged(): lax.ppermute(arrays[j], 'expert', [(i, i ^ 2 * (last - j)) for i in devic...  15.2 us
    ppermute x12, waiting for transfers between devices, exchanged(): lax.ppermute(arrays[j], 'expert', [(i, i ^ 2 * (last - j)) for i in devic...  10.9 us
    ppermute x16, waiting for transfers between devices, exchanged(): lax.ppermute(x, 'expert', [(i, i ^ 1) for i in devices])  4.65 us
    ppermute x1, waiting for transfers between devices, single_shards(): lax.ppermute(first, ('pipe', 'expert'), section_pairs(0, pipe, experts))  3.66 us
    ppermute x1, starting transfers between devices, single_shards(): lax.ppermute(first, ('pipe', 'expert'), section_pairs(0, pipe, experts))  1.65 us
  transfers between devices with their start and end apart: 30, of which 21 were waited for; matrix products, arithmetic and copies ran while one was open for 0% of the time, Pallas kernels for 6%

profile of v2, /device:TPU:0, one launch (start us, length us, event | category | flops | bytes accessed | tf_op | source)
XLA Modules:
  0.0 54.3 jit_solution(5730215828891926243)
XLA Ops:
  0.6 2.4 %shard_map.122 = (bf16[32,896]{1,0:T(8,128)(2,1)S(1)}, bf16[32,896]{1,0:T(8,128)(2,1)S(1)}, bf16[32,896]{1,0:T(8,128)(2,1)S(1)}, bf16[32,896]{1,0:T(8,128)(2,1)S...) custom-call(bf16[1,16,3584]{2,1,0:T(8,128)(2,1)} %refs_0_.1, ...), custom_call_target="tpu_custom_call" | custom-call | tf_op jit(solution)/shard_map/pallas_call | solution.py:402
  3.1 3.0 %collective-permute-start.1 = (bf16[32,896]{1,0:T(8,128)(2,1)S(1)}, bf16[32,896]{1,0:T(8,128)(2,1)S(1)}, u32[]{:S(2)}, u32[]{:S(2)}) collective-permute-start(bf16[32,896]{1,0:T(8,128)(2,1)S(1)} %get-tuple-element.35), channel_id=1, source_target_pairs={{0,4},{1,5},{2,6},{3,7},{4,0},{5,1},{6,2},{7,3},{8,12},{9,13},{10,... | collective-permute-start | bytes 172040 | tf_op jit(solution)/shard_map/ppermute | solution.py:418
  6.1 1.5 %collective-permute-start.2 = (bf16[32,896]{1,0:T(8,128)(2,1)S(1)}, bf16[32,896]{1,0:T(8,128)(2,1)S(1)}, u32[]{:S(2)}, u32[]{:S(2)}) collective-permute-start(bf16[32,896]{1,0:T(8,128)(2,1)S(1)} %get-tuple-element.36), channel_id=1, source_target_pairs={{0,2},{1,3},{2,0},{3,1},{4,6},{5,7},{6,4},{7,5},{8,10},{9,11},{10,... | collective-permute-start | bytes 172040 | tf_op jit(solution)/shard_map/ppermute | solution.py:418
  7.6 0.0 collective-permute-start
  7.6 0.0 collective-permute-start.6
  7.6 3.3 %shard_map.123.refs_10_ = bf16[3584,1024]{1,0:T(8,128)(2,1)S(1)} custom-call(bf16[32,896]{1,0:T(8,128)(2,1)S(1)} %get-tuple-element.34.refs_0_, bf16[1,3584,1024]{2,1,0:T(8,128)(2,1)} %refs_1_.3), custom_call_target="tpu_custom_call" | custom-call | bytes 14680064 | tf_op jit(solution)/shard_map/pallas_call | solution.py:402
  11.0 0.0 collective-permute-done.1.refs_1_
  11.0 0.0 collective-permute-done.2.refs_2_
  11.0 1.7 %collective-permute-done.refs_0_ = bf16[32,896]{1,0:T(8,128)(2,1)S(1)} collective-permute-done((bf16[32,896]{1,0:T(8,128)(2,1)S(1)}, bf16[32,896]{1,0:T(8,128)(2,1)S(1)}, u32[]{:S(2)}, u32[]{:S(2)}) %collective-permute-start) | collective-permute-done | bytes 57376 | tf_op jit(solution)/shard_map/ppermute | solution.py:418
  12.7 0.0 collective-permute-start.3
  12.7 0.5 collective-permute-start.4
  13.2 0.0 collective-permute-start.5
  13.2 0.0 collective-permute-done.6.refs_7_
  13.2 0.7 %collective-permute-done.3.refs_4_ = bf16[32,896]{1,0:T(8,128)(2,1)S(1)} collective-permute-done((bf16[32,896]{1,0:T(8,128)(2,1)S(1)}, bf16[32,896]{1,0:T(8,128)(2,1)S(1)}, u32[]{:S(2)}, u32[]{:S(2)}) %collective-permute-start.3) | collective-permute-done | bytes 57376 | tf_op jit(solution)/shard_map/ppermute | solution.py:424
  13.9 0.2 collective-permute-done.4.refs_5_
  14.1 0.4 collective-permute-done.5.refs_6_
  14.4 4.8 %shard_map.124 = (bf16[32,896]{1,0:T(8,128)(2,1)S(1)}, bf16[32,896]{1,0:T(8,128)(2,1)S(1)}, bf16[32,896]{1,0:T(8,128)(2,1)S(1)}, bf16[32,896]{1,0:T(8,128)(2,1)S(1)}, bf16[1792,1024]{1,0:T(8,128)(2,1)S(1)}) custom-call(bf16[32,896]{1,0:T(8,128)(2,1)S(1)} %collective-permute-done.refs_0_, bf16[32,896]{1,0:T(8,128)(2,1)S(1)} %collective-permute-done.1.refs_1_, ...), custom_call_target="tpu_custom_call" | custom-call | tf_op jit(solution)/shard_map/pallas_call | solution.py:402
  19.3 2.0 %collective-permute-start.7 = (bf16[32,896]{1,0:T(8,128)(2,1)S(1)}, bf16[32,896]{1,0:T(8,128)(2,1)S(1)}, u32[]{:S(2)}, u32[]{:S(2)}) collective-permute-start(bf16[32,896]{1,0:T(8,128)(2,1)S(1)} %get-tuple-element.45), channel_id=1, source_target_pairs={{0,6},{1,7},{2,4},{3,5},{4,2},{5,3},{6,0},{7,1},{8,14},{9,15},{10,... | collective-permute-start | bytes 172040 | tf_op jit(solution)/shard_map/ppermute | solution.py:418
  21.3 0.5 collective-permute-start.8
  21.8 1.1 %collective-permute-start.9 = (bf16[32,896]{1,0:T(8,128)(2,1)S(1)}, bf16[32,896]{1,0:T(8,128)(2,1)S(1)}, u32[]{:S(2)}, u32[]{:S(2)}) collective-permute-start(bf16[32,896]{1,0:T(8,128)(2,1)S(1)} %get-tuple-element.47), channel_id=1, source_target_pairs={{0,2},{1,3},{2,0},{3,1},{4,6},{5,7},{6,4},{7,5},{8,10},{9,11},{10,... | collective-permute-start | bytes 172040 | tf_op jit(solution)/shard_map/ppermute | solution.py:418
  22.8 0.0 collective-permute-start.13
  22.8 1.6 %collective-permute-done.7.refs_0_ = bf16[32,896]{1,0:T(8,128)(2,1)S(1)} collective-permute-done((bf16[32,896]{1,0:T(8,128)(2,1)S(1)}, bf16[32,896]{1,0:T(8,128)(2,1)S(1)}, u32[]{:S(2)}, u32[]{:S(2)}) %collective-permute-start.7) | collective-permute-done | bytes 57376 | tf_op jit(solution)/shard_map/ppermute | solution.py:418
  24.5 0.0 collective-permute-start.10
  24.5 1.2 %collective-permute-done.8.refs_1_ = bf16[32,896]{1,0:T(8,128)(2,1)S(1)} collective-permute-done((bf16[32,896]{1,0:T(8,128)(2,1)S(1)}, bf16[32,896]{1,0:T(8,128)(2,1)S(1)}, u32[]{:S(2)}, u32[]{:S(2)}) %collective-permute-start.8) | collective-permute-done | bytes 57376 | tf_op jit(solution)/shard_map/ppermute | solution.py:418
  25.6 0.0 collective-permute-start.11
  25.7 0.3 collective-permute-done.9.refs_2_
  26.0 0.2 collective-permute-start.12
  26.2 0.0 collective-permute-done.13.refs_7_
  26.2 0.0 collective-permute-done.10.refs_4_
  26.2 0.7 %collective-permute-done.11.refs_5_ = bf16[32,896]{1,0:T(8,128)(2,1)S(1)} collective-permute-done((bf16[32,896]{1,0:T(8,128)(2,1)S(1)}, bf16[32,896]{1,0:T(8,128)(2,1)S(1)}, u32[]{:S(2)}, u32[]{:S(2)}) %collective-permute-start.11) | collective-permute-done | bytes 57376 | tf_op jit(solution)/shard_map/ppermute | solution.py:424
  26.9 0.3 collective-permute-done.12.refs_6_
  27.2 0.2 shard_map.125
  27.4 1.6 %collective-permute-start.14 = (bf16[16,3584]{1,0:T(8,128)(2,1)S(1)}, bf16[16,3584]{1,0:T(8,128)(2,1)S(1)}, u32[]{:S(2)}, u32[]{:S(2)}) collective-permute-start(bf16[16,3584]{1,0:T(8,128)(2,1)S(1)} %get-tuple-element.50), channel_id=1, source_target_pairs={{0,8},{1,9},{2,10},{3,11},{4,12},{5,13},{6,14},{7,15},{8,0},{9,1},... | collective-permute-start | bytes 344072 | tf_op jit(solution)/shard_map/ppermute | solution.py:521
  29.1 0.0 collective-permute-start.15
  29.1 3.7 %collective-permute-done.14.refs_0_ = bf16[16,3584]{1,0:T(8,128)(2,1)S(1)} collective-permute-done((bf16[16,3584]{1,0:T(8,128)(2,1)S(1)}, bf16[16,3584]{1,0:T(8,128)(2,1)S(1)}, u32[]{:S(2)}, u32[]{:S(2)}) %collective-permute-start.14) | collective-permute-done | bytes 114720 | tf_op jit(solution)/shard_map/ppermute | solution.py:521
  32.8 0.2 shard_map.126
  33.0 1.6 %collective-permute-start.16 = (bf16[32,896]{1,0:T(8,128)(2,1)S(1)}, bf16[32,896]{1,0:T(8,128)(2,1)S(1)}, u32[]{:S(2)}, u32[]{:S(2)}) collective-permute-start(bf16[32,896]{1,0:T(8,128)(2,1)S(1)} %get-tuple-element.55), channel_id=1, source_target_pairs={{0,6},{1,7},{2,4},{3,5},{4,2},{5,3},{6,0},{7,1},{8,14},{9,15},{10,... | collective-permute-start | bytes 172040 | tf_op jit(solution)/shard_map/ppermute | solution.py:418
  34.6 0.9 %collective-permute-start.17 = (bf16[32,896]{1,0:T(8,128)(2,1)S(1)}, bf16[32,896]{1,0:T(8,128)(2,1)S(1)}, u32[]{:S(2)}, u32[]{:S(2)}) collective-permute-start(bf16[32,896]{1,0:T(8,128)(2,1)S(1)} %get-tuple-element.56), channel_id=1, source_target_pairs={{0,4},{1,5},{2,6},{3,7},{4,0},{5,1},{6,2},{7,3},{8,12},{9,13},{10,... | collective-permute-start | bytes 172040 | tf_op jit(solution)/shard_map/ppermute | solution.py:418
  35.5 1.0 %collective-permute-start.18 = (bf16[32,896]{1,0:T(8,128)(2,1)S(1)}, bf16[32,896]{1,0:T(8,128)(2,1)S(1)}, u32[]{:S(2)}, u32[]{:S(2)}) collective-permute-start(bf16[32,896]{1,0:T(8,128)(2,1)S(1)} %get-tuple-element.57), channel_id=1, source_target_pairs={{0,2},{1,3},{2,0},{3,1},{4,6},{5,7},{6,4},{7,5},{8,10},{9,11},{10,... | collective-permute-start | bytes 172040 | tf_op jit(solution)/shard_map/ppermute | solution.py:418
  36.6 0.0 collective-permute-start.22
  36.6 2.2 %collective-permute-done.16.refs_0_ = bf16[32,896]{1,0:T(8,128)(2,1)S(1)} collective-permute-done((bf16[32,896]{1,0:T(8,128)(2,1)S(1)}, bf16[32,896]{1,0:T(8,128)(2,1)S(1)}, u32[]{:S(2)}, u32[]{:S(2)}) %collective-permute-start.16) | collective-permute-done | bytes 57376 | tf_op jit(solution)/shard_map/ppermute | solution.py:418
  38.7 0.0 collective-permute-start.19
  38.7 0.3 collective-permute-done.17.refs_1_
  39.1 0.2 collective-permute-start.20
  39.3 0.5 collective-permute-done.18.refs_2_
  39.7 0.0 collective-permute-done.22.refs_7_
  39.7 0.3 collective-permute-done.19.refs_4_
  40.0 0.3 collective-permute-done.20.refs_5_
  40.3 0.6 %collective-permute-done.21.refs_6_ = bf16[32,896]{1,0:T(8,128)(2,1)S(1)} collective-permute-done((bf16[32,896]{1,0:T(8,128)(2,1)S(1)}, bf16[32,896]{1,0:T(8,128)(2,1)S(1)}, u32[]{:S(2)}, u32[]{:S(2)}) %collective-permute-start.21) | collective-permute-done | bytes 57376 | tf_op jit(solution)/shard_map/ppermute | solution.py:424
  41.0 4.5 %shard_map.127 = (bf16[32,896]{1,0:T(8,128)(2,1)S(1)}, bf16[32,896]{1,0:T(8,128)(2,1)S(1)}, bf16[32,896]{1,0:T(8,128)(2,1)S(1)}, bf16[32,896]{1,0:T(8,128)(2,1)S(1)}) custom-call(bf16[32,896]{1,0:T(8,128)(2,1)S(1)} %collective-permute-done.16.refs_0_, bf16[32,896]{1,0:T(8,128)(2,1)S(1)} %collective-permute-done.17.refs_1_, ...), custom_call_target="tpu_custom_call" | custom-call | tf_op jit(solution)/shard_map/pallas_call | solution.py:402
  45.4 2.0 %collective-permute-start.23 = (bf16[32,896]{1,0:T(8,128)(2,1)S(1)}, bf16[32,896]{1,0:T(8,128)(2,1)S(1)}, u32[]{:S(2)}, u32[]{:S(2)}) collective-permute-start(bf16[32,896]{1,0:T(8,128)(2,1)S(1)} %get-tuple-element.60), channel_id=1, source_target_pairs={{0,6},{1,7},{2,4},{3,5},{4,2},{5,3},{6,0},{7,1},{8,14},{9,15},{10,... | collective-permute-start | bytes 172040 | tf_op jit(solution)/shard_map/ppermute | solution.py:418
  47.4 0.6 %collective-permute-start.24 = (bf16[32,896]{1,0:T(8,128)(2,1)S(1)}, bf16[32,896]{1,0:T(8,128)(2,1)S(1)}, u32[]{:S(2)}, u32[]{:S(2)}) collective-permute-start(bf16[32,896]{1,0:T(8,128)(2,1)S(1)} %get-tuple-element.61), channel_id=1, source_target_pairs={{0,4},{1,5},{2,6},{3,7},{4,0},{5,1},{6,2},{7,3},{8,12},{9,13},{10,... | collective-permute-start | bytes 172040 | tf_op jit(solution)/shard_map/ppermute | solution.py:418
  48.0 1.0 %collective-permute-start.25 = (bf16[32,896]{1,0:T(8,128)(2,1)S(1)}, bf16[32,896]{1,0:T(8,128)(2,1)S(1)}, u32[]{:S(2)}, u32[]{:S(2)}) collective-permute-start(bf16[32,896]{1,0:T(8,128)(2,1)S(1)} %get-tuple-element.62), channel_id=1, source_target_pairs={{0,2},{1,3},{2,0},{3,1},{4,6},{5,7},{6,4},{7,5},{8,10},{9,11},{10,... | collective-permute-start | bytes 172040 | tf_op jit(solution)/shard_map/ppermute | solution.py:418
  49.0 1.7 %collective-permute-done.23.refs_0_ = bf16[32,896]{1,0:T(8,128)(2,1)S(1)} collective-permute-done((bf16[32,896]{1,0:T(8,128)(2,1)S(1)}, bf16[32,896]{1,0:T(8,128)(2,1)S(1)}, u32[]{:S(2)}, u32[]{:S(2)}) %collective-permute-start.23) | collective-permute-done | bytes 57376 | tf_op jit(solution)/shard_map/ppermute | solution.py:418
  50.7 0.0 collective-permute-start.26
  50.7 1.1 %collective-permute-done.24.refs_1_ = bf16[32,896]{1,0:T(8,128)(2,1)S(1)} collective-permute-done((bf16[32,896]{1,0:T(8,128)(2,1)S(1)}, bf16[32,896]{1,0:T(8,128)(2,1)S(1)}, u32[]{:S(2)}, u32[]{:S(2)}) %collective-permute-start.24) | collective-permute-done | bytes 57376 | tf_op jit(solution)/shard_map/ppermute | solution.py:418
  51.7 0.0 collective-permute-start.27
  51.7 0.4 collective-permute-done.25.refs_2_
  52.1 0.1 collective-permute-start.28
  52.3 0.0 collective-permute-done.29.refs_7_
  52.3 0.0 collective-permute-done.26.refs_4_
  52.3 0.7 %collective-permute-done.27.refs_5_ = bf16[32,896]{1,0:T(8,128)(2,1)S(1)} collective-permute-done((bf16[32,896]{1,0:T(8,128)(2,1)S(1)}, bf16[32,896]{1,0:T(8,128)(2,1)S(1)}, u32[]{:S(2)}, u32[]{:S(2)}) %collective-permute-start.27) | collective-permute-done | bytes 57376 | tf_op jit(solution)/shard_map/ppermute | solution.py:424
  53.0 0.4 collective-permute-done.28.refs_6_
  53.4 0.9 %shard_map.128 = (bf16[16,3584]{1,0:T(8,128)(2,1)}, bf16[16,3584]{1,0:T(8,128)(2,1)}) custom-call(bf16[32,896]{1,0:T(8,128)(2,1)S(1)} %collective-permute-done.23.refs_0_, bf16[32,896]{1,0:T(8,128)(2,1)S(1)} %collective-permute-done.24.refs_1_, bf16[32,896]{1,0:T(8,128)(2,1)S(1)} %collective-permute-done.25.refs_2_, ...), custom_call_target="tpu_custom_call" | custom-call | tf_op jit(solution)/shard_map/pallas_call | solution.py:402
  (8 shorter events, 0.0 us)
Async XLA Ops:
  3.1 7.9 %collective-permute-start.1 = (bf16[32,896]{1,0:T(8,128)(2,1)S(1)}, bf16[32,896]{1,0:T(8,128)(2,1)S(1)}, u32[]{:S(2)}, u32[]{:S(2)}) collective-permute-start(bf16[32,896]{1,0:T(8,128)(2,1)S(1)} %get-tuple-element.35), channel_id=1, source_target_pairs={{0,4},{1,5},{2,6},{3,7},{4,0},{5,1},{6,2},{7,3},{8,12},{9,13},{10,... | collective-permute-start | bytes 172040 | tf_op jit(solution)/shard_map/ppermute | solution.py:418
  6.1 4.9 %collective-permute-start.2 = (bf16[32,896]{1,0:T(8,128)(2,1)S(1)}, bf16[32,896]{1,0:T(8,128)(2,1)S(1)}, u32[]{:S(2)}, u32[]{:S(2)}) collective-permute-start(bf16[32,896]{1,0:T(8,128)(2,1)S(1)} %get-tuple-element.36), channel_id=1, source_target_pairs={{0,2},{1,3},{2,0},{3,1},{4,6},{5,7},{6,4},{7,5},{8,10},{9,11},{10,... | collective-permute-start | bytes 172040 | tf_op jit(solution)/shard_map/ppermute | solution.py:418
  7.6 5.1 %collective-permute-start = (bf16[32,896]{1,0:T(8,128)(2,1)S(1)}, bf16[32,896]{1,0:T(8,128)(2,1)S(1)}, u32[]{:S(2)}, u32[]{:S(2)}) collective-permute-start(bf16[32,896]{1,0:T(8,128)(2,1)S(1)} %get-tuple-element.34.refs_0_), channel_id=1, source_target_pairs={{0,6},{1,7},{2,4},{3,5},{4,2},{5,3},{6,0},{7,1},{8,14},{9,15},{10,... | collective-permute-start | bytes 172040 | tf_op jit(solution)/shard_map/ppermute | solution.py:418
  7.6 6.8 %slice-start = ((s8[7340032]{0:T(1024)(128)(4,1)}), s8[4194304]{0:T(1024)(128)(4,1)S(1)}, s32[]{:S(2)}) async-start(s8[7340032]{0:T(1024)(128)(4,1)} %bitcast.10), calls=%async_computation | async-start | bytes 8388608
  7.6 6.8 %slice-start.1 = ((s8[7340032]{0:T(1024)(128)(4,1)}), s8[3145728]{0:T(1024)(128)(4,1)S(1)}, s32[]{:S(2)}) async-start(s8[7340032]{0:T(1024)(128)(4,1)} %bitcast.10), calls=%async_computation.1 | async-start | bytes 6291456
  7.6 5.5 %collective-permute-start.6 = (bf16[32,896]{1,0:T(8,128)(2,1)S(1)}, bf16[32,896]{1,0:T(8,128)(2,1)S(1)}, u32[]{:S(2)}, u32[]{:S(2)}) collective-permute-start(bf16[32,896]{1,0:T(8,128)(2,1)S(1)} %get-tuple-element.40.refs_3_), channel_id=1, source_target_pairs={{0,1},{1,0},{2,3},{3,2},{4,5},{5,4},{6,7},{7,6},{8,9},{9,8},{10,11... | collective-permute-start | bytes 172040 | tf_op jit(solution)/shard_map/ppermute | solution.py:424
  12.7 1.2 %collective-permute-start.3 = (bf16[32,896]{1,0:T(8,128)(2,1)S(1)}, bf16[32,896]{1,0:T(8,128)(2,1)S(1)}, u32[]{:S(2)}, u32[]{:S(2)}) collective-permute-start(bf16[32,896]{1,0:T(8,128)(2,1)S(1)} %collective-permute-done.refs_0_), channel_id=1, source_target_pairs={{0,1},{1,0},{2,3},{3,2},{4,5},{5,4},{6,7},{7,6},{8,9},{9,8},{10,11... | collective-permute-start | bytes 172040 | tf_op jit(solution)/shard_map/ppermute | solution.py:424
  12.7 1.4 %collective-permute-start.4 = (bf16[32,896]{1,0:T(8,128)(2,1)S(1)}, bf16[32,896]{1,0:T(8,128)(2,1)S(1)}, u32[]{:S(2)}, u32[]{:S(2)}) collective-permute-start(bf16[32,896]{1,0:T(8,128)(2,1)S(1)} %collective-permute-done.1.refs_1_), channel_id=1, source_target_pairs={{0,1},{1,0},{2,3},{3,2},{4,5},{5,4},{6,7},{7,6},{8,9},{9,8},{10,11... | collective-permute-start | bytes 172040 | tf_op jit(solution)/shard_map/ppermute | solution.py:424
  13.2 1.2 %collective-permute-start.5 = (bf16[32,896]{1,0:T(8,128)(2,1)S(1)}, bf16[32,896]{1,0:T(8,128)(2,1)S(1)}, u32[]{:S(2)}, u32[]{:S(2)}) collective-permute-start(bf16[32,896]{1,0:T(8,128)(2,1)S(1)} %collective-permute-done.2.refs_2_), channel_id=1, source_target_pairs={{0,1},{1,0},{2,3},{3,2},{4,5},{5,4},{6,7},{7,6},{8,9},{9,8},{10,11... | collective-permute-start | bytes 172040 | tf_op jit(solution)/shard_map/ppermute | solution.py:424
  19.3 5.2 %collective-permute-start.7 = (bf16[32,896]{1,0:T(8,128)(2,1)S(1)}, bf16[32,896]{1,0:T(8,128)(2,1)S(1)}, u32[]{:S(2)}, u32[]{:S(2)}) collective-permute-start(bf16[32,896]{1,0:T(8,128)(2,1)S(1)} %get-tuple-element.45), channel_id=1, source_target_pairs={{0,6},{1,7},{2,4},{3,5},{4,2},{5,3},{6,0},{7,1},{8,14},{9,15},{10,... | collective-permute-start | bytes 172040 | tf_op jit(solution)/shard_map/ppermute | solution.py:418
  21.3 4.4 %collective-permute-start.8 = (bf16[32,896]{1,0:T(8,128)(2,1)S(1)}, bf16[32,896]{1,0:T(8,128)(2,1)S(1)}, u32[]{:S(2)}, u32[]{:S(2)}) collective-permute-start(bf16[32,896]{1,0:T(8,128)(2,1)S(1)} %get-tuple-element.46), channel_id=1, source_target_pairs={{0,4},{1,5},{2,6},{3,7},{4,0},{5,1},{6,2},{7,3},{8,12},{9,13},{10,... | collective-permute-start | bytes 172040 | tf_op jit(solution)/shard_map/ppermute | solution.py:418
  21.8 4.2 %collective-permute-start.9 = (bf16[32,896]{1,0:T(8,128)(2,1)S(1)}, bf16[32,896]{1,0:T(8,128)(2,1)S(1)}, u32[]{:S(2)}, u32[]{:S(2)}) collective-permute-start(bf16[32,896]{1,0:T(8,128)(2,1)S(1)} %get-tuple-element.47), channel_id=1, source_target_pairs={{0,2},{1,3},{2,0},{3,1},{4,6},{5,7},{6,4},{7,5},{8,10},{9,11},{10,... | collective-permute-start | bytes 172040 | tf_op jit(solution)/shard_map/ppermute | solution.py:418
  22.8 3.3 %collective-permute-start.13 = (bf16[32,896]{1,0:T(8,128)(2,1)S(1)}, bf16[32,896]{1,0:T(8,128)(2,1)S(1)}, u32[]{:S(2)}, u32[]{:S(2)}) collective-permute-start(bf16[32,896]{1,0:T(8,128)(2,1)S(1)} %get-tuple-element.48.refs_3_), channel_id=1, source_target_pairs={{0,1},{1,0},{2,3},{3,2},{4,5},{5,4},{6,7},{7,6},{8,9},{9,8},{10,11... | collective-permute-start | bytes 172040 | tf_op jit(solution)/shard_map/ppermute | solution.py:424
  24.5 1.7 %collective-permute-start.10 = (bf16[32,896]{1,0:T(8,128)(2,1)S(1)}, bf16[32,896]{1,0:T(8,128)(2,1)S(1)}, u32[]{:S(2)}, u32[]{:S(2)}) collective-permute-start(bf16[32,896]{1,0:T(8,128)(2,1)S(1)} %collective-permute-done.7.refs_0_), channel_id=1, source_target_pairs={{0,1},{1,0},{2,3},{3,2},{4,5},{5,4},{6,7},{7,6},{8,9},{9,8},{10,11... | collective-permute-start | bytes 172040 | tf_op jit(solution)/shard_map/ppermute | solution.py:424
  25.6 1.2 %collective-permute-start.11 = (bf16[32,896]{1,0:T(8,128)(2,1)S(1)}, bf16[32,896]{1,0:T(8,128)(2,1)S(1)}, u32[]{:S(2)}, u32[]{:S(2)}) collective-permute-start(bf16[32,896]{1,0:T(8,128)(2,1)S(1)} %collective-permute-done.8.refs_1_), channel_id=1, source_target_pairs={{0,1},{1,0},{2,3},{3,2},{4,5},{5,4},{6,7},{7,6},{8,9},{9,8},{10,11... | collective-permute-start | bytes 172040 | tf_op jit(solution)/shard_map/ppermute | solution.py:424
  26.0 1.2 %collective-permute-start.12 = (bf16[32,896]{1,0:T(8,128)(2,1)S(1)}, bf16[32,896]{1,0:T(8,128)(2,1)S(1)}, u32[]{:S(2)}, u32[]{:S(2)}) collective-permute-start(bf16[32,896]{1,0:T(8,128)(2,1)S(1)} %collective-permute-done.9.refs_2_), channel_id=1, source_target_pairs={{0,1},{1,0},{2,3},{3,2},{4,5},{5,4},{6,7},{7,6},{8,9},{9,8},{10,11... | collective-permute-start | bytes 172040 | tf_op jit(solution)/shard_map/ppermute | solution.py:424
  27.4 5.3 %collective-permute-start.14 = (bf16[16,3584]{1,0:T(8,128)(2,1)S(1)}, bf16[16,3584]{1,0:T(8,128)(2,1)S(1)}, u32[]{:S(2)}, u32[]{:S(2)}) collective-permute-start(bf16[16,3584]{1,0:T(8,128)(2,1)S(1)} %get-tuple-element.50), channel_id=1, source_target_pairs={{0,8},{1,9},{2,10},{3,11},{4,12},{5,13},{6,14},{7,15},{8,0},{9,1},... | collective-permute-start | bytes 344072 | tf_op jit(solution)/shard_map/ppermute | solution.py:521
  29.1 3.7 %collective-permute-start.15 = (bf16[16,3584]{1,0:T(8,128)(2,1)S(1)}, bf16[16,3584]{1,0:T(8,128)(2,1)S(1)}, u32[]{:S(2)}, u32[]{:S(2)}) collective-permute-start(bf16[16,3584]{1,0:T(8,128)(2,1)S(1)} %get-tuple-element.51), channel_id=1, source_target_pairs={{0,1},{1,0},{2,3},{3,2},{4,5},{5,4},{6,7},{7,6},{8,16},{9,17},{10,... | collective-permute-start | bytes 344072 | tf_op jit(solution)/shard_map/ppermute | solution.py:522
  33.0 5.7 %collective-permute-start.16 = (bf16[32,896]{1,0:T(8,128)(2,1)S(1)}, bf16[32,896]{1,0:T(8,128)(2,1)S(1)}, u32[]{:S(2)}, u32[]{:S(2)}) collective-permute-start(bf16[32,896]{1,0:T(8,128)(2,1)S(1)} %get-tuple-element.55), channel_id=1, source_target_pairs={{0,6},{1,7},{2,4},{3,5},{4,2},{5,3},{6,0},{7,1},{8,14},{9,15},{10,... | collective-permute-start | bytes 172040 | tf_op jit(solution)/shard_map/ppermute | solution.py:418
  34.6 4.5 %collective-permute-start.17 = (bf16[32,896]{1,0:T(8,128)(2,1)S(1)}, bf16[32,896]{1,0:T(8,128)(2,1)S(1)}, u32[]{:S(2)}, u32[]{:S(2)}) collective-permute-start(bf16[32,896]{1,0:T(8,128)(2,1)S(1)} %get-tuple-element.56), channel_id=1, source_target_pairs={{0,4},{1,5},{2,6},{3,7},{4,0},{5,1},{6,2},{7,3},{8,12},{9,13},{10,... | collective-permute-start | bytes 172040 | tf_op jit(solution)/shard_map/ppermute | solution.py:418
  35.5 4.2 %collective-permute-start.18 = (bf16[32,896]{1,0:T(8,128)(2,1)S(1)}, bf16[32,896]{1,0:T(8,128)(2,1)S(1)}, u32[]{:S(2)}, u32[]{:S(2)}) collective-permute-start(bf16[32,896]{1,0:T(8,128)(2,1)S(1)} %get-tuple-element.57), channel_id=1, source_target_pairs={{0,2},{1,3},{2,0},{3,1},{4,6},{5,7},{6,4},{7,5},{8,10},{9,11},{10,... | collective-permute-start | bytes 172040 | tf_op jit(solution)/shard_map/ppermute | solution.py:418
  36.6 3.2 %collective-permute-start.22 = (bf16[32,896]{1,0:T(8,128)(2,1)S(1)}, bf16[32,896]{1,0:T(8,128)(2,1)S(1)}, u32[]{:S(2)}, u32[]{:S(2)}) collective-permute-start(bf16[32,896]{1,0:T(8,128)(2,1)S(1)} %get-tuple-element.58.refs_3_), channel_id=1, source_target_pairs={{0,1},{1,0},{2,3},{3,2},{4,5},{5,4},{6,7},{7,6},{8,9},{9,8},{10,11... | collective-permute-start | bytes 172040 | tf_op jit(solution)/shard_map/ppermute | solution.py:424
  38.7 1.2 %collective-permute-start.19 = (bf16[32,896]{1,0:T(8,128)(2,1)S(1)}, bf16[32,896]{1,0:T(8,128)(2,1)S(1)}, u32[]{:S(2)}, u32[]{:S(2)}) collective-permute-start(bf16[32,896]{1,0:T(8,128)(2,1)S(1)} %collective-permute-done.16.refs_0_), channel_id=1, source_target_pairs={{0,1},{1,0},{2,3},{3,2},{4,5},{5,4},{6,7},{7,6},{8,9},{9,8},{10,11... | collective-permute-start | bytes 172040 | tf_op jit(solution)/shard_map/ppermute | solution.py:424
  39.1 1.2 %collective-permute-start.20 = (bf16[32,896]{1,0:T(8,128)(2,1)S(1)}, bf16[32,896]{1,0:T(8,128)(2,1)S(1)}, u32[]{:S(2)}, u32[]{:S(2)}) collective-permute-start(bf16[32,896]{1,0:T(8,128)(2,1)S(1)} %collective-permute-done.17.refs_1_), channel_id=1, source_target_pairs={{0,1},{1,0},{2,3},{3,2},{4,5},{5,4},{6,7},{7,6},{8,9},{9,8},{10,11... | collective-permute-start | bytes 172040 | tf_op jit(solution)/shard_map/ppermute | solution.py:424
  39.7 1.2 %collective-permute-start.21 = (bf16[32,896]{1,0:T(8,128)(2,1)S(1)}, bf16[32,896]{1,0:T(8,128)(2,1)S(1)}, u32[]{:S(2)}, u32[]{:S(2)}) collective-permute-start(bf16[32,896]{1,0:T(8,128)(2,1)S(1)} %collective-permute-done.18.refs_2_), channel_id=1, source_target_pairs={{0,1},{1,0},{2,3},{3,2},{4,5},{5,4},{6,7},{7,6},{8,9},{9,8},{10,11... | collective-permute-start | bytes 172040 | tf_op jit(solution)/shard_map/ppermute | solution.py:424
  45.4 5.2 %collective-permute-start.23 = (bf16[32,896]{1,0:T(8,128)(2,1)S(1)}, bf16[32,896]{1,0:T(8,128)(2,1)S(1)}, u32[]{:S(2)}, u32[]{:S(2)}) collective-permute-start(bf16[32,896]{1,0:T(8,128)(2,1)S(1)} %get-tuple-element.60), channel_id=1, source_target_pairs={{0,6},{1,7},{2,4},{3,5},{4,2},{5,3},{6,0},{7,1},{8,14},{9,15},{10,... | collective-permute-start | bytes 172040 | tf_op jit(solution)/shard_map/ppermute | solution.py:418
  47.4 4.3 %collective-permute-start.24 = (bf16[32,896]{1,0:T(8,128)(2,1)S(1)}, bf16[32,896]{1,0:T(8,128)(2,1)S(1)}, u32[]{:S(2)}, u32[]{:S(2)}) collective-permute-start(bf16[32,896]{1,0:T(8,128)(2,1)S(1)} %get-tuple-element.61), channel_id=1, source_target_pairs={{0,4},{1,5},{2,6},{3,7},{4,0},{5,1},{6,2},{7,3},{8,12},{9,13},{10,... | collective-permute-start | bytes 172040 | tf_op jit(solution)/shard_map/ppermute | solution.py:418
  48.0 4.2 %collective-permute-start.25 = (bf16[32,896]{1,0:T(8,128)(2,1)S(1)}, bf16[32,896]{1,0:T(8,128)(2,1)S(1)}, u32[]{:S(2)}, u32[]{:S(2)}) collective-permute-start(bf16[32,896]{1,0:T(8,128)(2,1)S(1)} %get-tuple-element.62), channel_id=1, source_target_pairs={{0,2},{1,3},{2,0},{3,1},{4,6},{5,7},{6,4},{7,5},{8,10},{9,11},{10,... | collective-permute-start | bytes 172040 | tf_op jit(solution)/shard_map/ppermute | solution.py:418
  49.0 3.3 %collective-permute-start.29 = (bf16[32,896]{1,0:T(8,128)(2,1)S(1)}, bf16[32,896]{1,0:T(8,128)(2,1)S(1)}, u32[]{:S(2)}, u32[]{:S(2)}) collective-permute-start(bf16[32,896]{1,0:T(8,128)(2,1)S(1)} %get-tuple-element.63.refs_3_), channel_id=1, source_target_pairs={{0,1},{1,0},{2,3},{3,2},{4,5},{5,4},{6,7},{7,6},{8,9},{9,8},{10,11... | collective-permute-start | bytes 172040 | tf_op jit(solution)/shard_map/ppermute | solution.py:424
  50.7 1.6 %collective-permute-start.26 = (bf16[32,896]{1,0:T(8,128)(2,1)S(1)}, bf16[32,896]{1,0:T(8,128)(2,1)S(1)}, u32[]{:S(2)}, u32[]{:S(2)}) collective-permute-start(bf16[32,896]{1,0:T(8,128)(2,1)S(1)} %collective-permute-done.23.refs_0_), channel_id=1, source_target_pairs={{0,1},{1,0},{2,3},{3,2},{4,5},{5,4},{6,7},{7,6},{8,9},{9,8},{10,11... | collective-permute-start | bytes 172040 | tf_op jit(solution)/shard_map/ppermute | solution.py:424
  51.7 1.2 %collective-permute-start.27 = (bf16[32,896]{1,0:T(8,128)(2,1)S(1)}, bf16[32,896]{1,0:T(8,128)(2,1)S(1)}, u32[]{:S(2)}, u32[]{:S(2)}) collective-permute-start(bf16[32,896]{1,0:T(8,128)(2,1)S(1)} %collective-permute-done.24.refs_1_), channel_id=1, source_target_pairs={{0,1},{1,0},{2,3},{3,2},{4,5},{5,4},{6,7},{7,6},{8,9},{9,8},{10,11... | collective-permute-start | bytes 172040 | tf_op jit(solution)/shard_map/ppermute | solution.py:424
  52.1 1.2 %collective-permute-start.28 = (bf16[32,896]{1,0:T(8,128)(2,1)S(1)}, bf16[32,896]{1,0:T(8,128)(2,1)S(1)}, u32[]{:S(2)}, u32[]{:S(2)}) collective-permute-start(bf16[32,896]{1,0:T(8,128)(2,1)S(1)} %collective-permute-done.25.refs_2_), channel_id=1, source_target_pairs={{0,1},{1,0},{2,3},{3,2},{4,5},{5,4},{6,7},{7,6},{8,9},{9,8},{10,11... | collective-permute-start | bytes 172040 | tf_op jit(solution)/shard_map/ppermute | solution.py:424

commit v3 on v2

--- a/solution.py
+++ b/solution.py
@@ -141,7 +141,7 @@
     return lax.broadcasted_iota(jnp.int32, shape, axis)
 
 
-def place():
+def chip_and_core():
     index = lax.axis_index("expert")
     return index // 2, index % 2
 
@@ -150,42 +150,77 @@
     return jnp.where(iota((rows, target.shape[1]), 0) == target, 1.0, 0.0)
 
 
-def row_maps(up_ids, down_ids, parts, slot_cap, span):
-    rows = up_ids.shape[1]
+def upright(ids):
+    rows = ids.shape[1]
+    diagonal = iota((rows, rows), 0) == iota((rows, rows), 1)
+    return jnp.sum(jnp.where(diagonal, ids, 0), axis=1, keepdims=True)
+
+
+def slots(first_ids, second_ids, parts):
+    rows = first_ids.shape[1]
     width = 2 * rows * parts
-    diagonal = iota((rows, rows), 0) == iota((rows, rows), 1)
-    up_ids = jnp.sum(jnp.where(diagonal, up_ids, 0), axis=1, keepdims=True)
-    down_ids = jnp.sum(jnp.where(diagonal, down_ids, 0), axis=1, keepdims=True)
     lane = iota((rows, width), 1)
     row = iota((rows, width), 0)
     own = lane % rows
-    ids = jnp.where(lane // rows % 2 == 0, up_ids, down_ids)
+    ids = jnp.where(lane // rows % 2 == 0, upright(first_ids), upright(second_ids))
     chosen = jnp.sum(jnp.where(row == own, ids, 0), axis=0, keepdims=True)
     rank = jnp.sum(jnp.where((ids == chosen) & (row < own), 1, 0), axis=0, keepdims=True)
     lane = iota((1, width), 1)
-    within = lane // (2 * rows) * (2 * slot_cap) + lane // rows % 2 * slot_cap + rank
-    chip, core = place()
-    across = (chosen // 2) ^ chip ^ (span // (2 * SUBLANES) - 1)
-    to_core = chosen % 2
-    sent = (across * 2 + to_core) * SUBLANES + within
-    array = across + jnp.where(to_core == core, 0, span // (2 * SUBLANES))
-    received = (array * 2 + core) * SUBLANES + within
-    return one_hot(span, sent), one_hot(2 * span, received)
-
-
-def expert_maps(parts, slot_cap, span):
+    return chosen, rank, lane // (2 * rows), lane // rows % 2
+
+
+def sending_map(first_ids, second_ids, parts, slot_cap, span):
+    chosen, rank, piece, group = slots(first_ids, second_ids, parts)
+    chip, _ = chip_and_core()
+    array = (chosen // 2) ^ chip ^ (span // (2 * SUBLANES) - 1)
+    within = piece * (2 * slot_cap) + group * slot_cap + rank
+    return one_hot(span, (array * 2 + chosen % 2) * SUBLANES + within)
+
+
+def returning_map(up_ids, down_ids, parts, slot_cap, span):
+    chosen, rank, piece, group = slots(up_ids, down_ids, parts)
+    chip, core = chip_and_core()
+    chips = span // (2 * SUBLANES)
+    array = (chosen // 2) ^ chip ^ (chips - 1)
+    array = array + jnp.where(chosen % 2 == core, 0, chips)
+    sender = (lax.axis_index("pipe") + 1 + group) % 2
+    within = piece * (2 * slot_cap) + sender * slot_cap + rank
+    return one_hot(2 * span, (array * 2 + core) * SUBLANES + within)
+
+
+def arriving_map(parts, slot_cap, span):
     wide = 2 * slot_cap
-    rows = span // parts
-    chips = span // (2 * SUBLANES)
-    _, core = place()
+    _, core = chip_and_core()
     lane = iota((1, 2 * span), 1)
     array, to_core, within = lane // (2 * SUBLANES), lane // SUBLANES % 2, lane % SUBLANES
-    row = within // wide * rows + array * wide + within % wide
-    received = one_hot(span, jnp.where(to_core == core, row, -1))
+    row = within // wide * (span // parts) + array * wide + within % wide
+    return one_hot(span, jnp.where(to_core == core, row, -1))
+
+
+def relaying_map(parts, slot_cap, span):
+    wide = 2 * slot_cap
+    chips = span // (2 * SUBLANES)
+    _, core = chip_and_core()
+    lane = iota((1, span), 1)
+    half = lane // (span // 2)
+    array, within = lane % (span // 2) // SUBLANES, lane % SUBLANES
+    piece, row = within // wide, within % wide
+    array = array + jnp.where(row // slot_cap == core, 0, chips)
+    way = (half + core + lax.axis_index("pipe")) % 2
+    row = way * slot_cap + row % slot_cap
+    return one_hot(span, piece * (span // parts) + array * wide + row)
+
+
+def closing_map(parts, slot_cap, span):
+    wide = 2 * slot_cap
+    chips = span // (2 * SUBLANES)
+    _, core = chip_and_core()
     lane = iota((1, span), 1)
     array, to_core, within = lane // (2 * SUBLANES), lane // SUBLANES % 2, lane % SUBLANES
-    array = array + jnp.where(to_core == core, 0, chips)
-    return received, one_hot(span, within // wide * rows + array * wide + within % wide)
+    piece, row = within // wide, within % wide
+    array = array + jnp.where(row // slot_cap == core, 0, chips)
+    row = to_core * slot_cap + row % slot_cap
+    return one_hot(span, piece * (span // parts) + array * wide + row)
 
 
 def moved(onehot, rows):
@@ -230,8 +265,6 @@
 def prepare_kernel(
     parts,
     slot_cap,
-    ticks,
-    early,
     up,
     down,
     up_ids,
@@ -240,17 +273,18 @@
     enter_down,
     gain,
     router,
+    w_gate,
     w_up,
+    w_down,
     out_refs,
-    maps_ref,
-    backs_ref,
+    aside_ref,
+    back_ref,
+    gain_v,
+    router_v,
+    up_v,
+    down_v,
     enter_up_v,
     enter_down_v,
-    gain_v,
-    router_v,
-    early_v,
-    up_v,
-    down_v,
     up_i,
     down_i,
     cols_v,
@@ -259,64 +293,92 @@
     sources = (up_ids, down_ids, up.at[0], down.at[0], router.at[0], gain, enter_up, enter_down)
     targets = (up_i, down_i, up_v, down_v, cols_v, gain_v, enter_up_v, enter_down_v)
     copies = started(sources, targets, sems)
-    ranges = cut(early_v.shape[0], early)
-    late = started(
-        [w_up.at[0, r] for r in ranges], [early_v.at[r] for r in ranges], sems, len(copies)
-    )
     copies[0].wait()
     copies[1].wait()
-    span = maps_ref.shape[1]
-    maps = [row_maps(up_i[t, 0], down_i[t, 0], parts, slot_cap, span) for t in range(ticks)]
+    span = back_ref.shape[0]
+    rows, features = up_v.shape
+    width = features // parts
+    sending = sending_map(up_i[0, 0], down_i[0, 0], parts, slot_cap, span)
+    numbers = (iota((span, LANES), 0) % rows).astype(jnp.float32).astype(jnp.bfloat16)
     copies[2].wait()
     copies[3].wait()
-    put(pack_rows(maps[0][0], up_v[...], down_v[...], parts), out_refs)
-    for t in range(ticks):
-        maps_ref[t] = maps[t][0].astype(jnp.bfloat16)
-        backs_ref[t] = maps[t][1].T.astype(jnp.bfloat16)
+    packed = pack_rows(sending, up_v[...], down_v[...], parts)
+    put(packed, [ref.at[:, :width] for ref in out_refs])
+    put(moved(sending, numbers), [ref.at[:, width:] for ref in out_refs])
+    last = up_i.shape[0] - 1
+    back_ref[...] = returning_map(up_i[last, 0], down_i[last, 0], parts, slot_cap, span).T.astype(jnp.bfloat16)
+    ids = jnp.where(iota((rows, LANES), 0) == iota((rows, LANES), 1), 1, 0)
+    up_line = jnp.sum(ids * upright(up_i[last, 0]), axis=0, keepdims=True)
+    down_line = jnp.sum(ids * upright(down_i[last, 0]), axis=0, keepdims=True)
+    row = iota((rows, LANES), 0)
+    lines = jnp.where(row == 0, up_line, jnp.where(row == 1, down_line, 0))
+    aside_ref[rows:] = jnp.zeros((rows, features), jnp.bfloat16)
+    aside_ref[rows:, :LANES] = lines.astype(jnp.float32).astype(jnp.bfloat16)
     copies[4].wait()
     cols = cols_v[...].astype(jnp.float32)
     mine = iota(cols.shape, 0) == lax.axis_index("expert")
     router_v[...] = jnp.sum(jnp.where(mine, cols, 0.0), axis=0, keepdims=True)
-    for copy in copies[5:] + late:
+    for copy in copies[5:]:
         copy.wait()
-
-
-def resend_kernel(parts, pipe, tick_id, even_ref, odd_ref, enter_up_ref, enter_down_ref, maps_ref, out_refs):
+    aside_ref[:rows] = jnp.where(lax.axis_index("pipe") == 0, enter_up_v[...], enter_down_v[...])
+
+
+def merge_kernel(kept_ref, passed_ref, out_refs):
+    for j, ref in enumerate(out_refs):
+        ref[:SUBLANES] = kept_ref[j * SUBLANES : (j + 1) * SUBLANES]
+        ref[SUBLANES:] = passed_ref[j * SUBLANES : (j + 1) * SUBLANES]
+
+
+def turn_kernel(parts, slot_cap, pipe, in_refs, aside_ref, other_ref, out_refs):
     section = lax.axis_index("pipe")
-    is_even = section % 2 == 0
-    even, odd = even_ref[...], odd_ref[...]
-    up_rows = jnp.where(is_even, odd, even)
-    down_rows = jnp.where(is_even, even, odd)
-    up_rows = jnp.where(section == 0, enter_up_ref[...], up_rows)
-    down_rows = jnp.where(section == pipe - 1, enter_down_ref[...], down_rows)
-    put(pack_rows(maps_ref[tick_id], up_rows, down_rows, parts), out_refs)
-
-
-def unpack_kernel(tick_id, by_parity, in_refs, backs_ref, first_ref, second_ref):
-    rows = first_ref.shape[0]
+    _, core = chip_and_core()
+    wide = 2 * slot_cap
+    rows = aside_ref.shape[0] // 2
+    width = out_refs[0].shape[1]
+    span = sum(ref.shape[0] for ref in out_refs)
+    own, other = aside_ref[...], other_ref[...]
+    first = jnp.where(core == 0, own, other)
+    second = jnp.where(core == 0, other, own)
+    line = (section + core + 1) % 2
+    picked = iota((rows, LANES), 0) == line
+
+    def ids(aside):
+        lines = jnp.where(picked, aside[rows:, :LANES].astype(jnp.float32), 0.0)
+        return jnp.sum(lines, axis=0, keepdims=True)[:, :rows].astype(jnp.int32)
+
+    sending = sending_map(ids(first), ids(second), parts, slot_cap, span)
+    received = stacked(in_refs)
+    numbers = received[:, width:].astype(jnp.float32).astype(jnp.int32)[:, :span]
+    sublane = iota((span, span), 0)
+    within = sublane % SUBLANES
+    place = within // wide * (2 * rows) + within % wide // slot_cap * rows
+    sorting = jnp.where(iota((span, span), 1) == place + numbers[:, :1], 1.0, 0.0).T
+    sorted_rows = moved(sorting, received[:, :width])
+    entering = []
+    for q in range(parts):
+        entering += [x[:rows, q * width : (q + 1) * width] for x in (first, second)]
+    partner = ((section + core) ^ 1) - core
+    enters = (partner < 0) | (partner >= pipe)
+    sorted_rows = jnp.where(enters, jnp.concatenate(entering, axis=0), sorted_rows)
+    put(moved(sending, sorted_rows), out_refs)
+
+
+def unpack_kernel(in_refs, back_ref, up_ref, down_ref):
+    rows = up_ref.shape[0]
     width = in_refs[0].shape[1]
-    back = moved(backs_ref[tick_id], stacked(in_refs))
-    swap = lax.axis_index("pipe") % 2 == 1 if by_parity else None
-    for q in range(first_ref.shape[1] // width):
-        up_piece = back[2 * q * rows : (2 * q + 1) * rows]
-        down_piece = back[(2 * q + 1) * rows : (2 * q + 2) * rows]
-        if by_parity:
-            up_piece, down_piece = (
-                jnp.where(swap, down_piece, up_piece),
-                jnp.where(swap, up_piece, down_piece),
-            )
-        first_ref[:, q * width : (q + 1) * width] = up_piece
-        second_ref[:, q * width : (q + 1) * width] = down_piece
-
-
-def expert_rows(parts, slot_cap, in_refs, gain_ref, router_ref, out_refs, x_ref, gates, ups, downs):
-    span = sum(ref.shape[0] for ref in out_refs)
-    width = in_refs[0].shape[1]
+    back = moved(back_ref[...], stacked(in_refs))
+    for q in range(up_ref.shape[1] // width):
+        up_ref[:, q * width : (q + 1) * width] = back[2 * q * rows : (2 * q + 1) * rows]
+        down_ref[:, q * width : (q + 1) * width] = back[(2 * q + 1) * rows : (2 * q + 2) * rows]
+
+
+def expert_rows(parts, slot_cap, in_refs, gain_ref, router_ref, x_ref, gates, ups, downs):
+    span = in_refs[0].shape[0] * len(in_refs) // 2
     rows = span // parts
-    received, sent = expert_maps(parts, slot_cap, span)
-    spread = moved(received, stacked(in_refs))
+    width = x_ref.shape[1] // parts
+    spread = moved(arriving_map(parts, slot_cap, span), stacked(in_refs))
     for q in range(parts):
-        x_ref[:, q * width : (q + 1) * width] = spread[q * rows : (q + 1) * rows]
+        x_ref[:, q * width : (q + 1) * width] = spread[q * rows : (q + 1) * rows, :width]
     widened = x_ref[...].astype(jnp.float32)
     inverse = lax.rsqrt(jnp.mean(widened * widened, axis=1, keepdims=True) + norm_eps)
     normed = (widened * inverse * gain_ref[...]).astype(jnp.bfloat16)
@@ -337,50 +399,25 @@
     hidden = (jax.nn.silu(gate_pre) * product(normed, ups)).astype(jnp.bfloat16)
     part = product(hidden, downs).astype(jnp.bfloat16).astype(jnp.float32)
     done = (x_ref[...].astype(jnp.float32) + weight * part).astype(jnp.bfloat16)
-    pieces = [done[:, q * width : (q + 1) * width] for q in range(parts)]
-    put(moved(sent.T, jnp.concatenate(pieces, axis=0)), out_refs)
-
-
-def load_kernel(after_ref, source, target, sems):
-    del after_ref
-    ranges = cut(target.shape[0], sems.shape[0])
-    for copy in started([source.at[0, r] for r in ranges], [target.at[r] for r in ranges], sems):
-        copy.wait()
+    done = jnp.concatenate([done[:, q * width : (q + 1) * width] for q in range(parts)], axis=0)
+    return done, spread[:, width:]
 
 
 def first_kernel(
-    parts,
-    slot_cap,
-    in_refs,
-    gain_ref,
-    router_ref,
-    gate_ref,
-    early_ref,
-    down_ref,
-    up,
-    out_refs,
-    late_v,
-    x_ref,
-    sems,
+    parts, slot_cap, in_refs, gain_ref, router_ref, gate_ref, up_ref, down_ref, kept_ref, passed_ref, x_ref
 ):
-    early = early_ref.shape[0]
-    step = late_v.shape[0] // sems.shape[0]
-    ranges = cut(late_v.shape[0], sems.shape[0])
-    sources = [up.at[0, pl.ds(early + i * step, step)] for i in range(len(ranges))]
-    copies = started(sources, [late_v.at[r] for r in ranges], sems)
-    ups = [(early_ref, [])] + [(late_v.at[r], [c]) for r, c in zip(ranges, copies)]
-    expert_rows(
-        parts, slot_cap, in_refs, gain_ref, router_ref, out_refs, x_ref, [(gate_ref, [])], ups, [(down_ref, [])]
-    )
-
-
-def later_kernel(
-    parts, slot_cap, in_refs, gain_ref, router_ref, gate_ref, early_ref, down_ref, late_ref, out_refs, x_ref
-):
-    ups = [(early_ref, []), (late_ref, [])]
-    expert_rows(
-        parts, slot_cap, in_refs, gain_ref, router_ref, out_refs, x_ref, [(gate_ref, [])], ups, [(down_ref, [])]
-    )
+    done, numbers = expert_rows(
+        parts, slot_cap, in_refs, gain_ref, router_ref, x_ref, [(gate_ref, [])], [(up_ref, [])], [(down_ref, [])]
+    )
+    onehot = relaying_map(parts, slot_cap, done.shape[0]).T
+    put(moved(onehot, jnp.concatenate([done, numbers], axis=1)), (kept_ref, passed_ref))
+
+
+def later_kernel(parts, slot_cap, in_refs, gain_ref, router_ref, gate_ref, up_ref, down_ref, out_refs, x_ref):
+    done, _ = expert_rows(
+        parts, slot_cap, in_refs, gain_ref, router_ref, x_ref, [(gate_ref, [])], [(up_ref, [])], [(down_ref, [])]
+    )
+    put(moved(closing_map(parts, slot_cap, done.shape[0]).T, done), out_refs)
 
 
 VMEM_SPEC = pl.BlockSpec(memory_space=pltpu.VMEM)
@@ -425,12 +462,12 @@
     return tuple(arrived + passed), beside
 
 
-def section_pairs(parity, pipe, experts):
+def relay_pairs(k, pipe, experts):
     pairs = []
     for section in range(pipe):
-        other = ((section + parity) ^ 1) - parity
         for i in range(experts):
-            target = (other, i) if 0 <= other < pipe else (section, i ^ 1)
+            other = ((section + i % 2) ^ 1) - i % 2
+            target = (other, i ^ (2 * k)) if 0 <= other < pipe else (section, i ^ (2 * (k or 1)))
             pairs.append((section * experts + i, target[0] * experts + target[1]))
     return pairs
 
@@ -460,23 +497,25 @@
     slot_cap = rows * TOP // experts
     parts = SUBLANES // (2 * slot_cap)
     span = experts * SUBLANES
+    chips = experts // 2
+    width = features // parts
     early = features // 2
-    blocks = (pltpu.VMEM((2 * SUBLANES, features // parts), jnp.bfloat16),) * (experts // 2)
+    numbered = (pltpu.VMEM((2 * SUBLANES, width + LANES), jnp.bfloat16),) * chips
+    blocks = (pltpu.VMEM((2 * SUBLANES, width), jnp.bfloat16),) * chips
+    half = pltpu.VMEM((span // 2, width + LANES), jnp.bfloat16)
     batch = pltpu.VMEM((rows, features), jnp.bfloat16)
     ids_v = pltpu.VMEM((TICKS, 1, 1, rows), jnp.int32)
     row_v = pltpu.VMEM((1, features), jnp.float32)
     x_v = pltpu.VMEM((span // parts, features), jnp.bfloat16)
-    sent, maps, backs, enter_up, enter_down, gain, column, early_up = local_call(
-        functools.partial(prepare_kernel, parts, slot_cap, TICKS, EARLY_COPIES),
+    sibling = [(i, i ^ 1) for i in range(experts)]
+    sent, aside, back, gain, column = local_call(
+        functools.partial(prepare_kernel, parts, slot_cap),
         (
-            blocks,
-            pltpu.VMEM((TICKS, span, span), jnp.bfloat16),
-            pltpu.VMEM((TICKS, span, 2 * span), jnp.bfloat16),
-            batch,
-            batch,
+            numbered,
+            pltpu.VMEM((2 * rows, features), jnp.bfloat16),
+            pltpu.VMEM((span, 2 * span), jnp.bfloat16),
             row_v,
             row_v,
-            pltpu.VMEM((early, hidden), jnp.bfloat16),
         ),
         (),
         (
@@ -488,47 +527,48 @@
             entering_down,
             norm_gain,
             router.transpose(0, 2, 1),
+            w_gate,
             w_up,
+            w_down,
         ),
         [
+            batch,
+            batch,
             batch,
             batch,
             ids_v,
             ids_v,
             pltpu.VMEM(router.shape[:0:-1], router.dtype),
-            pltpu.SemaphoreType.DMA((8 + EARLY_COPIES,)),
+            pltpu.SemaphoreType.DMA((8,)),
         ],
     )
-    gate = local_call(
-        load_kernel,
-        pltpu.VMEM((features, hidden), jnp.bfloat16),
-        (sent[0],),
-        (w_gate,),
-        [pltpu.SemaphoreType.DMA((LOAD_COPIES,))],
-        cost=pl.CostEstimate(flops=0, transcendentals=0, bytes_accessed=4 * features * hidden),
-    )
-    received, gate = exchanged(sent, gate)
-    done, late_up = local_call(
+    received, _ = exchanged(sent)
+    gate, up, down = w_gate[0], w_up[0], w_down[0]
+    kept, passed = local_call(
         functools.partial(first_kernel, parts, slot_cap),
-        (blocks, pltpu.VMEM((features - early, hidden), jnp.bfloat16)),
-        (received, gain, column, gate, early_up, w_down[0]),
-        (w_up,),
-        [x_v, pltpu.SemaphoreType.DMA((LATE_COPIES,))],
-    )
-    for tick_id in range(1, TICKS):
-        kernel = functools.partial(unpack_kernel, tick_id - 1, True)
-        first, second = local_call(kernel, (batch, batch), (exchanged(done)[0], backs))
-        first = lax.ppermute(first, ("pipe", "expert"), section_pairs(0, pipe, experts))
-        second = lax.ppermute(second, ("pipe", "expert"), section_pairs(1, pipe, experts))
-        kernel = functools.partial(resend_kernel, parts, pipe, tick_id)
-        (sent,) = local_call(kernel, (blocks,), (first, second, enter_up, enter_down, maps))
-        kernel = functools.partial(later_kernel, parts, slot_cap)
-        args = (exchanged(sent)[0], gain, column, gate, early_up, w_down[0], late_up)
-        (done,) = local_call(kernel, (blocks,), args, (), [x_v])
+        (half, half),
+        (received, gain, column, gate, up, down),
+        (),
+        [x_v],
+    )
+    other = lax.ppermute(aside, "expert", sibling)
+    passed = lax.ppermute(passed, "expert", sibling)
+    (merged,) = local_call(merge_kernel, (numbered,), (kept, passed))
+    relayed = tuple(
+        lax.ppermute(x, ("pipe", "expert"), relay_pairs(chips - 1 - j, pipe, experts))
+        for j, x in enumerate(merged)
+    )
+    kernel = functools.partial(turn_kernel, parts, slot_cap, pipe)
+    relayed = relayed[chips // 2 :] + relayed[: chips // 2]
+    (sent,) = local_call(kernel, (blocks,), (relayed, aside, other))
+    received, _ = exchanged(sent)
+    kernel = functools.partial(later_kernel, parts, slot_cap)
+    args = (received, gain, column, gate, up, down)
+    (done,) = local_call(kernel, (blocks,), args, (), [x_v])
     batch = jax.ShapeDtypeStruct((rows, features), jnp.bfloat16)
-    kernel = functools.partial(unpack_kernel, TICKS - 1, False)
-    first, second = local_call(kernel, (batch, batch), (exchanged(done)[0], backs))
-    return (first[None], second[None])
+    received, _ = exchanged(done)
+    up_done, down_done = local_call(unpack_kernel, (batch, batch), (received, back))
+    return (up_done[None], down_done[None])
 
 
 def shards(*args):
@@ -536,6 +576,7 @@
     experts = lax.axis_size("expert")
     slot_cap = rows * TOP // EXPERTS
     fits = experts == EXPERTS and rows % SUBLANES == 0 and SUBLANES % (2 * slot_cap) == 0
+    fits = fits and TICKS == 2 and lax.axis_size("pipe") > 1
     fits = fits and features % (SUBLANES // (2 * slot_cap) * LANES) == 0
     return single_shards(*args) if fits else grouped_shards(*args)
 

time: 54.6 us -> 51 us (0.934)
  Pallas kernels: 16.4 us -> 11.9 us
  starting transfers between devices: 17.9 us -> 18.9 us
    ppermute x2 -> x6, starting transfers between devices: 1.65 us -> 6.64 us  [the longest x4 5.91 us: single_shards(): lax.ppermute(x, ('pipe', 'expert'), relay_pairs(chips - 1 - j, pipe, expe...]
    pallas_call x7 -> x6, Pallas kernels: 16.4 us -> 11.9 us  [local_call(): pl.pallas_call(body, out_shape=outs, in_specs=[VMEM_SPEC] * len(close) +...]
    ppermute x12 -> x9, starting transfers between devices: 15.2 us -> 11.7 us  [exchanged(): lax.ppermute(arrays[j], 'expert', [(i, i ^ 2 * (last - j)) for i in devic...]
    ppermute x2 -> x6, waiting for transfers between devices: 3.67 us -> 6.17 us  [the longest x4 4.97 us: single_shards(): lax.ppermute(x, ('pipe', 'expert'), relay_pairs(chips - 1 - j, pipe, expe...]
    ppermute x16 -> x12, waiting for transfers between devices: 4.65 us -> 3.21 us  [exchanged(): lax.ppermute(x, 'expert', [(i, i ^ 1) for i in devices])]
    ppermute x12 -> x9, waiting for transfers between devices: 10.9 us -> 9.92 us  [exchanged(): lax.ppermute(arrays[j], 'expert', [(i, i ^ 2 * (last - j)) for i in devic...]
  transfers between devices with their start and end apart: 30 -> 27, of which waited for: 21 -> 17; matrix products, arithmetic and copies ran while one was open for 0% -> 0% of each run, Pallas kernels for 6% -> 9%
where the time goes in v3:
time: 51 us; the launch traced here: 50.8 us
  waiting for transfers between devices  19.3 us (38%)
  starting transfers between devices  18.9 us (37%)
  Pallas kernels  11.9 us (23%)
  between operations  0.74 us (1%)
    pallas_call x6, Pallas kernels, local_call(): pl.pallas_call(body, out_shape=outs, in_specs=[VMEM_SPEC] * len(close) +...  11.9 us
    ppermute x9, starting transfers between devices, exchanged(): lax.ppermute(arrays[j], 'expert', [(i, i ^ 2 * (last - j)) for i in devic...  11.7 us
    ppermute x9, waiting for transfers between devices, exchanged(): lax.ppermute(arrays[j], 'expert', [(i, i ^ 2 * (last - j)) for i in devic...  9.92 us
    ppermute x4, starting transfers between devices, single_shards(): lax.ppermute(x, ('pipe', 'expert'), relay_pairs(chips - 1 - j, pipe, expe...  5.91 us
    ppermute x4, waiting for transfers between devices, single_shards(): lax.ppermute(x, ('pipe', 'expert'), relay_pairs(chips - 1 - j, pipe, expe...  4.97 us
    ppermute x12, waiting for transfers between devices, exchanged(): lax.ppermute(x, 'expert', [(i, i ^ 1) for i in devices])  3.21 us
    ppermute x1, waiting for transfers between devices, single_shards(): passed = lax.ppermute(passed, 'expert', sibling)  1.2 us
  transfers between devices with their start and end apart: 27, of which 17 were waited for; matrix products, arithmetic and copies ran while one was open for 0% of the time, Pallas kernels for 9%

profile of v3, /device:TPU:0, one launch (start us, length us, event | category | flops | bytes accessed | tf_op | source)
XLA Modules:
  0.0 50.8 jit_solution(15729306892991036412)
XLA Ops:
  0.6 0.0 copy-start
  0.6 0.0 copy-start.1
  0.7 0.0 copy-start.2
  0.7 1.5 %shard_map.122 = (bf16[32,1024]{1,0:T(8,128)(2,1)S(1)}, bf16[32,1024]{1,0:T(8,128)(2,1)S(1)}, bf16[32,1024]{1,0:T(8,128)(2,1)S(1)}, bf16[32,1024]{1,0:T(8,128)(2...) custom-call(bf16[1,16,3584]{2,1,0:T(8,128)(2,1)} %refs_0_.1, ...), custom_call_target="tpu_custom_call" | custom-call | tf_op jit(solution)/shard_map/pallas_call | solution.py:439
  2.2 4.0 %collective-permute-start = (bf16[32,1024]{1,0:T(8,128)(2,1)S(1)}, bf16[32,1024]{1,0:T(8,128)(2,1)S(1)}, u32[]{:S(2)}, u32[]{:S(2)}) collective-permute-start(bf16[32,1024]{1,0:T(8,128)(2,1)S(1)} %get-tuple-element.26), channel_id=1, source_target_pairs={{0,6},{1,7},{2,4},{3,5},{4,2},{5,3},{6,0},{7,1},{8,14},{9,15},{10,... | collective-permute-start | bytes 196616 | tf_op jit(solution)/shard_map/ppermute | solution.py:455
  6.1 0.5 collective-permute-start.1
  6.7 0.1 collective-permute-start.2
  6.8 0.0 collective-permute-start.6
  6.8 1.6 %collective-permute-done.refs_0_ = bf16[32,1024]{1,0:T(8,128)(2,1)S(1)} collective-permute-done((bf16[32,1024]{1,0:T(8,128)(2,1)S(1)}, bf16[32,1024]{1,0:T(8,128)(2,1)S(1)}, u32[]{:S(2)}, u32[]{:S(2)}) %collective-permute-start) | collective-permute-done | bytes 65568 | tf_op jit(solution)/shard_map/ppermute | solution.py:455
  8.4 0.0 collective-permute-start.3
  8.4 2.0 %collective-permute-done.1.refs_1_ = bf16[32,1024]{1,0:T(8,128)(2,1)S(1)} collective-permute-done((bf16[32,1024]{1,0:T(8,128)(2,1)S(1)}, bf16[32,1024]{1,0:T(8,128)(2,1)S(1)}, u32[]{:S(2)}, u32[]{:S(2)}) %collective-permute-start.1) | collective-permute-done | bytes 65568 | tf_op jit(solution)/shard_map/ppermute | solution.py:455
  10.4 0.0 collective-permute-start.4
  10.4 0.5 collective-permute-done.2.refs_2_
  10.9 0.0 collective-permute-start.5
  10.9 0.5 collective-permute-start.12
  11.4 0.0 collective-permute-done.6.refs_7_
  11.4 0.0 collective-permute-done.3.refs_4_
  11.4 0.2 collective-permute-done.4.refs_5_
  11.7 0.5 collective-permute-done.5.refs_6_
  12.2 0.0 copy-done
  12.2 0.0 copy-done.1
  12.2 4.5 %shard_map.123 = (bf16[64,1024]{1,0:T(8,128)(2,1)S(1)}, bf16[64,1024]{1,0:T(8,128)(2,1)S(1)}) custom-call(bf16[32,1024]{1,0:T(8,128)(2,1)S(1)} %collective-permute-done.refs_0_, bf16[32,1024]{1,0:T(8,128)(2,1)S(1)} %collective-permute-done.1.refs_1_, bf16[32,1024]{1,0:T(8,128)(2,1)S(1)} %collective-permute-done.2.refs_2_, ...), custom_call_target="tpu_custom_call" | custom-call | tf_op jit(solution)/shard_map/pallas_call | solution.py:439
  16.7 0.2 collective-permute-start.7
  16.9 1.2 %collective-permute-done.7.refs_1_ = bf16[64,1024]{1,0:T(8,128)(2,1)S(1)} collective-permute-done((bf16[64,1024]{1,0:T(8,128)(2,1)S(1)}, bf16[64,1024]{1,0:T(8,128)(2,1)S(1)}, u32[]{:S(2)}, u32[]{:S(2)}) %collective-permute-start.7) | collective-permute-done | bytes 131104 | tf_op jit(solution)/shard_map/ppermute | solution.py:555
  18.1 1.6 %collective-permute-start.8 = (bf16[32,1024]{1,0:T(8,128)(2,1)S(1)}, bf16[32,1024]{1,0:T(8,128)(2,1)S(1)}, u32[]{:S(2)}, u32[]{:S(2)}) collective-permute-start(bf16[32,1024]{1,0:T(8,128)(2,1)S(1)} %get-tuple-element.34), channel_id=1, source_target_pairs={{0,10},{1,3},{2,8},{3,1},{4,14},{5,7},{6,12},{7,5},{8,2},{9,19},{1... | collective-permute-start | bytes 196616 | tf_op jit(solution)/shard_map/ppermute | solution.py:558
  19.8 0.4 collective-permute-start.9
  20.2 3.4 %collective-permute-start.10 = (bf16[32,1024]{1,0:T(8,128)(2,1)S(1)}, bf16[32,1024]{1,0:T(8,128)(2,1)S(1)}, u32[]{:S(2)}, u32[]{:S(2)}) collective-permute-start(bf16[32,1024]{1,0:T(8,128)(2,1)S(1)} %get-tuple-element.36), channel_id=1, source_target_pairs={{0,14},{1,7},{2,12},{3,5},{4,10},{5,3},{6,8},{7,1},{8,6},{9,23},{1... | collective-permute-start | bytes 196616 | tf_op jit(solution)/shard_map/ppermute | solution.py:558
  23.6 0.4 collective-permute-start.11
  24.0 0.0 collective-permute-done.12.refs_5_
  24.0 0.0 collective-permute-done.8.refs_0_
  24.0 0.0 collective-permute-done.9.refs_1_
  24.0 2.5 %collective-permute-done.10.refs_2_ = bf16[32,1024]{1,0:T(8,128)(2,1)S(1)} collective-permute-done((bf16[32,1024]{1,0:T(8,128)(2,1)S(1)}, bf16[32,1024]{1,0:T(8,128)(2,1)S(1)}, u32[]{:S(2)}, u32[]{:S(2)}) %collective-permute-start.10) | collective-permute-done | bytes 65568 | tf_op jit(solution)/shard_map/ppermute | solution.py:558
  26.6 2.4 %collective-permute-done.11.refs_3_ = bf16[32,1024]{1,0:T(8,128)(2,1)S(1)} collective-permute-done((bf16[32,1024]{1,0:T(8,128)(2,1)S(1)}, bf16[32,1024]{1,0:T(8,128)(2,1)S(1)}, u32[]{:S(2)}, u32[]{:S(2)}) %collective-permute-start.11) | collective-permute-done | bytes 65568 | tf_op jit(solution)/shard_map/ppermute | solution.py:558
  29.0 0.5 shard_map.125
  29.5 0.4 collective-permute-start.13
  30.0 1.4 %collective-permute-start.14 = (bf16[32,896]{1,0:T(8,128)(2,1)S(1)}, bf16[32,896]{1,0:T(8,128)(2,1)S(1)}, u32[]{:S(2)}, u32[]{:S(2)}) collective-permute-start(bf16[32,896]{1,0:T(8,128)(2,1)S(1)} %get-tuple-element.40), channel_id=1, source_target_pairs={{0,4},{1,5},{2,6},{3,7},{4,0},{5,1},{6,2},{7,3},{8,12},{9,13},{10,... | collective-permute-start | bytes 172040 | tf_op jit(solution)/shard_map/ppermute | solution.py:455
  31.4 1.7 %collective-permute-start.15 = (bf16[32,896]{1,0:T(8,128)(2,1)S(1)}, bf16[32,896]{1,0:T(8,128)(2,1)S(1)}, u32[]{:S(2)}, u32[]{:S(2)}) collective-permute-start(bf16[32,896]{1,0:T(8,128)(2,1)S(1)} %get-tuple-element.41), channel_id=1, source_target_pairs={{0,2},{1,3},{2,0},{3,1},{4,6},{5,7},{6,4},{7,5},{8,10},{9,11},{10,... | collective-permute-start | bytes 172040 | tf_op jit(solution)/shard_map/ppermute | solution.py:455
  33.1 0.0 collective-permute-start.19
  33.1 1.7 %collective-permute-done.13.refs_0_ = bf16[32,896]{1,0:T(8,128)(2,1)S(1)} collective-permute-done((bf16[32,896]{1,0:T(8,128)(2,1)S(1)}, bf16[32,896]{1,0:T(8,128)(2,1)S(1)}, u32[]{:S(2)}, u32[]{:S(2)}) %collective-permute-start.13) | collective-permute-done | bytes 57376 | tf_op jit(solution)/shard_map/ppermute | solution.py:455
  34.8 0.0 collective-permute-start.16
  34.8 0.0 collective-permute-done.14.refs_1_
  34.8 0.5 collective-permute-start.17
  35.3 0.3 collective-permute-done.15.refs_2_
  35.5 0.0 collective-permute-start.18
  35.5 0.0 collective-permute-done.19.refs_7_
  35.6 0.4 collective-permute-done.16.refs_4_
  36.0 0.2 collective-permute-done.17.refs_5_
  36.2 0.6 %collective-permute-done.18.refs_6_ = bf16[32,896]{1,0:T(8,128)(2,1)S(1)} collective-permute-done((bf16[32,896]{1,0:T(8,128)(2,1)S(1)}, bf16[32,896]{1,0:T(8,128)(2,1)S(1)}, u32[]{:S(2)}, u32[]{:S(2)}) %collective-permute-start.18) | collective-permute-done | bytes 57376 | tf_op jit(solution)/shard_map/ppermute | solution.py:461
  36.8 4.5 %shard_map.126 = (bf16[32,896]{1,0:T(8,128)(2,1)S(1)}, bf16[32,896]{1,0:T(8,128)(2,1)S(1)}, bf16[32,896]{1,0:T(8,128)(2,1)S(1)}, bf16[32,896]{1,0:T(8,128)(2,1)S(1)}) custom-call(bf16[32,896]{1,0:T(8,128)(2,1)S(1)} %collective-permute-done.13.refs_0_, bf16[32,896]{1,0:T(8,128)(2,1)S(1)} %collective-permute-done.14.refs_1_, ...), custom_call_target="tpu_custom_call" | custom-call | tf_op jit(solution)/shard_map/pallas_call | solution.py:439
  41.3 1.5 %collective-permute-start.20 = (bf16[32,896]{1,0:T(8,128)(2,1)S(1)}, bf16[32,896]{1,0:T(8,128)(2,1)S(1)}, u32[]{:S(2)}, u32[]{:S(2)}) collective-permute-start(bf16[32,896]{1,0:T(8,128)(2,1)S(1)} %get-tuple-element.43), channel_id=1, source_target_pairs={{0,6},{1,7},{2,4},{3,5},{4,2},{5,3},{6,0},{7,1},{8,14},{9,15},{10,... | collective-permute-start | bytes 172040 | tf_op jit(solution)/shard_map/ppermute | solution.py:455
  42.8 1.7 %collective-permute-start.21 = (bf16[32,896]{1,0:T(8,128)(2,1)S(1)}, bf16[32,896]{1,0:T(8,128)(2,1)S(1)}, u32[]{:S(2)}, u32[]{:S(2)}) collective-permute-start(bf16[32,896]{1,0:T(8,128)(2,1)S(1)} %get-tuple-element.44), channel_id=1, source_target_pairs={{0,4},{1,5},{2,6},{3,7},{4,0},{5,1},{6,2},{7,3},{8,12},{9,13},{10,... | collective-permute-start | bytes 172040 | tf_op jit(solution)/shard_map/ppermute | solution.py:455
  44.5 0.3 collective-permute-start.22
  44.8 0.0 collective-permute-start.26
  44.8 1.6 %collective-permute-done.20.refs_0_ = bf16[32,896]{1,0:T(8,128)(2,1)S(1)} collective-permute-done((bf16[32,896]{1,0:T(8,128)(2,1)S(1)}, bf16[32,896]{1,0:T(8,128)(2,1)S(1)}, u32[]{:S(2)}, u32[]{:S(2)}) %collective-permute-start.20) | collective-permute-done | bytes 57376 | tf_op jit(solution)/shard_map/ppermute | solution.py:455
  46.5 0.0 collective-permute-start.23
  46.5 1.0 %collective-permute-done.21.refs_1_ = bf16[32,896]{1,0:T(8,128)(2,1)S(1)} collective-permute-done((bf16[32,896]{1,0:T(8,128)(2,1)S(1)}, bf16[32,896]{1,0:T(8,128)(2,1)S(1)}, u32[]{:S(2)}, u32[]{:S(2)}) %collective-permute-start.21) | collective-permute-done | bytes 57376 | tf_op jit(solution)/shard_map/ppermute | solution.py:455
  47.4 0.0 collective-permute-start.24
  47.4 1.2 %collective-permute-done.22.refs_2_ = bf16[32,896]{1,0:T(8,128)(2,1)S(1)} collective-permute-done((bf16[32,896]{1,0:T(8,128)(2,1)S(1)}, bf16[32,896]{1,0:T(8,128)(2,1)S(1)}, u32[]{:S(2)}, u32[]{:S(2)}) %collective-permute-start.22) | collective-permute-done | bytes 57376 | tf_op jit(solution)/shard_map/ppermute | solution.py:455
  48.7 0.0 collective-permute-start.25
  48.7 0.0 collective-permute-done.26.refs_7_
  48.7 0.0 collective-permute-done.23.refs_4_
  48.7 0.0 collective-permute-done.24.refs_5_
  48.7 1.2 %collective-permute-done.25.refs_6_ = bf16[32,896]{1,0:T(8,128)(2,1)S(1)} collective-permute-done((bf16[32,896]{1,0:T(8,128)(2,1)S(1)}, bf16[32,896]{1,0:T(8,128)(2,1)S(1)}, u32[]{:S(2)}, u32[]{:S(2)}) %collective-permute-start.25) | collective-permute-done | bytes 57376 | tf_op jit(solution)/shard_map/ppermute | solution.py:461
  49.9 0.9 %shard_map.127 = (bf16[16,3584]{1,0:T(8,128)(2,1)}, bf16[16,3584]{1,0:T(8,128)(2,1)}) custom-call(bf16[32,896]{1,0:T(8,128)(2,1)S(1)} %collective-permute-done.20.refs_0_, bf16[32,896]{1,0:T(8,128)(2,1)S(1)} %collective-permute-done.21.refs_1_, bf16[32,896]{1,0:T(8,128)(2,1)S(1)} %collective-permute-done.22.refs_2_, ...), custom_call_target="tpu_custom_call" | custom-call | tf_op jit(solution)/shard_map/pallas_call | solution.py:439
  (2 shorter events, 0.0 us)
Async XLA Ops:
  0.6 11.5 %copy-start = (bf16[1,3584,1024]{2,1,0:T(8,128)(2,1)S(1)}, bf16[1,3584,1024]{2,1,0:T(8,128)(2,1)}, u32[]{:S(2)}) copy-start(bf16[1,3584,1024]{2,1,0:T(8,128)(2,1)} %refs_8_.1) | copy-start | bytes 22020100
  0.6 11.5 %copy-start.1 = (bf16[1,3584,1024]{2,1,0:T(8,128)(2,1)S(1)}, bf16[1,3584,1024]{2,1,0:T(8,128)(2,1)}, u32[]{:S(2)}) copy-start(bf16[1,3584,1024]{2,1,0:T(8,128)(2,1)} %refs_9_.1) | copy-start | bytes 22020100
  0.7 11.5 %copy-start.2 = (bf16[1,1024,3584]{2,1,0:T(8,128)(2,1)S(1)}, bf16[1,1024,3584]{2,1,0:T(8,128)(2,1)}, u32[]{:S(2)}) copy-start(bf16[1,1024,3584]{2,1,0:T(8,128)(2,1)} %refs_10_.1) | copy-start | bytes 22020100
  2.2 6.2 %collective-permute-start = (bf16[32,1024]{1,0:T(8,128)(2,1)S(1)}, bf16[32,1024]{1,0:T(8,128)(2,1)S(1)}, u32[]{:S(2)}, u32[]{:S(2)}) collective-permute-start(bf16[32,1024]{1,0:T(8,128)(2,1)S(1)} %get-tuple-element.26), channel_id=1, source_target_pairs={{0,6},{1,7},{2,4},{3,5},{4,2},{5,3},{6,0},{7,1},{8,14},{9,15},{10,... | collective-permute-start | bytes 196616 | tf_op jit(solution)/shard_map/ppermute | solution.py:455
  6.1 4.3 %collective-permute-start.1 = (bf16[32,1024]{1,0:T(8,128)(2,1)S(1)}, bf16[32,1024]{1,0:T(8,128)(2,1)S(1)}, u32[]{:S(2)}, u32[]{:S(2)}) collective-permute-start(bf16[32,1024]{1,0:T(8,128)(2,1)S(1)} %get-tuple-element.27), channel_id=1, source_target_pairs={{0,4},{1,5},{2,6},{3,7},{4,0},{5,1},{6,2},{7,3},{8,12},{9,13},{10,... | collective-permute-start | bytes 196616 | tf_op jit(solution)/shard_map/ppermute | solution.py:455
  6.7 4.3 %collective-permute-start.2 = (bf16[32,1024]{1,0:T(8,128)(2,1)S(1)}, bf16[32,1024]{1,0:T(8,128)(2,1)S(1)}, u32[]{:S(2)}, u32[]{:S(2)}) collective-permute-start(bf16[32,1024]{1,0:T(8,128)(2,1)S(1)} %get-tuple-element.28), channel_id=1, source_target_pairs={{0,2},{1,3},{2,0},{3,1},{4,6},{5,7},{6,4},{7,5},{8,10},{9,11},{10,... | collective-permute-start | bytes 196616 | tf_op jit(solution)/shard_map/ppermute | solution.py:455
  6.8 4.6 %collective-permute-start.6 = (bf16[32,1024]{1,0:T(8,128)(2,1)S(1)}, bf16[32,1024]{1,0:T(8,128)(2,1)S(1)}, u32[]{:S(2)}, u32[]{:S(2)}) collective-permute-start(bf16[32,1024]{1,0:T(8,128)(2,1)S(1)} %get-tuple-element.29.refs_3_), channel_id=1, source_target_pairs={{0,1},{1,0},{2,3},{3,2},{4,5},{5,4},{6,7},{7,6},{8,9},{9,8},{10,11... | collective-permute-start | bytes 196616 | tf_op jit(solution)/shard_map/ppermute | solution.py:461
  8.4 3.0 %collective-permute-start.3 = (bf16[32,1024]{1,0:T(8,128)(2,1)S(1)}, bf16[32,1024]{1,0:T(8,128)(2,1)S(1)}, u32[]{:S(2)}, u32[]{:S(2)}) collective-permute-start(bf16[32,1024]{1,0:T(8,128)(2,1)S(1)} %collective-permute-done.refs_0_), channel_id=1, source_target_pairs={{0,1},{1,0},{2,3},{3,2},{4,5},{5,4},{6,7},{7,6},{8,9},{9,8},{10,11... | collective-permute-start | bytes 196616 | tf_op jit(solution)/shard_map/ppermute | solution.py:461
  10.4 1.3 %collective-permute-start.4 = (bf16[32,1024]{1,0:T(8,128)(2,1)S(1)}, bf16[32,1024]{1,0:T(8,128)(2,1)S(1)}, u32[]{:S(2)}, u32[]{:S(2)}) collective-permute-start(bf16[32,1024]{1,0:T(8,128)(2,1)S(1)} %collective-permute-done.1.refs_1_), channel_id=1, source_target_pairs={{0,1},{1,0},{2,3},{3,2},{4,5},{5,4},{6,7},{7,6},{8,9},{9,8},{10,11... | collective-permute-start | bytes 196616 | tf_op jit(solution)/shard_map/ppermute | solution.py:461
  10.9 1.3 %collective-permute-start.5 = (bf16[32,1024]{1,0:T(8,128)(2,1)S(1)}, bf16[32,1024]{1,0:T(8,128)(2,1)S(1)}, u32[]{:S(2)}, u32[]{:S(2)}) collective-permute-start(bf16[32,1024]{1,0:T(8,128)(2,1)S(1)} %collective-permute-done.2.refs_2_), channel_id=1, source_target_pairs={{0,1},{1,0},{2,3},{3,2},{4,5},{5,4},{6,7},{7,6},{8,9},{9,8},{10,11... | collective-permute-start | bytes 196616 | tf_op jit(solution)/shard_map/ppermute | solution.py:461
  10.9 13.1 %collective-permute-start.12 = (bf16[32,3584]{1,0:T(8,128)(2,1)S(1)}, bf16[32,3584]{1,0:T(8,128)(2,1)S(1)}, u32[]{:S(2)}, u32[]{:S(2)}) collective-permute-start(bf16[32,3584]{1,0:T(8,128)(2,1)S(1)} %get-tuple-element.38.refs_4_), channel_id=1, source_target_pairs={{0,1},{1,0},{2,3},{3,2},{4,5},{5,4},{6,7},{7,6},{8,9},{9,8},{10,11... | collective-permute-start | bytes 688136 | tf_op jit(solution)/shard_map/ppermute | solution.py:554
  16.7 1.4 %collective-permute-start.7 = (bf16[64,1024]{1,0:T(8,128)(2,1)S(1)}, bf16[64,1024]{1,0:T(8,128)(2,1)S(1)}, u32[]{:S(2)}, u32[]{:S(2)}) collective-permute-start(bf16[64,1024]{1,0:T(8,128)(2,1)S(1)} %get-tuple-element.33), channel_id=1, source_target_pairs={{0,1},{1,0},{2,3},{3,2},{4,5},{5,4},{6,7},{7,6},{8,9},{9,8},{10,11... | collective-permute-start | bytes 393224 | tf_op jit(solution)/shard_map/ppermute | solution.py:555
  18.1 5.9 %collective-permute-start.8 = (bf16[32,1024]{1,0:T(8,128)(2,1)S(1)}, bf16[32,1024]{1,0:T(8,128)(2,1)S(1)}, u32[]{:S(2)}, u32[]{:S(2)}) collective-permute-start(bf16[32,1024]{1,0:T(8,128)(2,1)S(1)} %get-tuple-element.34), channel_id=1, source_target_pairs={{0,10},{1,3},{2,8},{3,1},{4,14},{5,7},{6,12},{7,5},{8,2},{9,19},{1... | collective-permute-start | bytes 196616 | tf_op jit(solution)/shard_map/ppermute | solution.py:558
  19.8 4.3 %collective-permute-start.9 = (bf16[32,1024]{1,0:T(8,128)(2,1)S(1)}, bf16[32,1024]{1,0:T(8,128)(2,1)S(1)}, u32[]{:S(2)}, u32[]{:S(2)}) collective-permute-start(bf16[32,1024]{1,0:T(8,128)(2,1)S(1)} %get-tuple-element.35), channel_id=1, source_target_pairs={{0,8},{1,3},{2,10},{3,1},{4,12},{5,7},{6,14},{7,5},{8,0},{9,17},{1... | collective-permute-start | bytes 196616 | tf_op jit(solution)/shard_map/ppermute | solution.py:558
  20.2 6.4 %collective-permute-start.10 = (bf16[32,1024]{1,0:T(8,128)(2,1)S(1)}, bf16[32,1024]{1,0:T(8,128)(2,1)S(1)}, u32[]{:S(2)}, u32[]{:S(2)}) collective-permute-start(bf16[32,1024]{1,0:T(8,128)(2,1)S(1)} %get-tuple-element.36), channel_id=1, source_target_pairs={{0,14},{1,7},{2,12},{3,5},{4,10},{5,3},{6,8},{7,1},{8,6},{9,23},{1... | collective-permute-start | bytes 196616 | tf_op jit(solution)/shard_map/ppermute | solution.py:558
  23.6 5.4 %collective-permute-start.11 = (bf16[32,1024]{1,0:T(8,128)(2,1)S(1)}, bf16[32,1024]{1,0:T(8,128)(2,1)S(1)}, u32[]{:S(2)}, u32[]{:S(2)}) collective-permute-start(bf16[32,1024]{1,0:T(8,128)(2,1)S(1)} %get-tuple-element.37), channel_id=1, source_target_pairs={{0,12},{1,5},{2,14},{3,7},{4,8},{5,1},{6,10},{7,3},{8,4},{9,21},{1... | collective-permute-start | bytes 196616 | tf_op jit(solution)/shard_map/ppermute | solution.py:558
  29.5 5.2 %collective-permute-start.13 = (bf16[32,896]{1,0:T(8,128)(2,1)S(1)}, bf16[32,896]{1,0:T(8,128)(2,1)S(1)}, u32[]{:S(2)}, u32[]{:S(2)}) collective-permute-start(bf16[32,896]{1,0:T(8,128)(2,1)S(1)} %get-tuple-element.39), channel_id=1, source_target_pairs={{0,6},{1,7},{2,4},{3,5},{4,2},{5,3},{6,0},{7,1},{8,14},{9,15},{10,... | collective-permute-start | bytes 172040 | tf_op jit(solution)/shard_map/ppermute | solution.py:455
  30.0 4.8 %collective-permute-start.14 = (bf16[32,896]{1,0:T(8,128)(2,1)S(1)}, bf16[32,896]{1,0:T(8,128)(2,1)S(1)}, u32[]{:S(2)}, u32[]{:S(2)}) collective-permute-start(bf16[32,896]{1,0:T(8,128)(2,1)S(1)} %get-tuple-element.40), channel_id=1, source_target_pairs={{0,4},{1,5},{2,6},{3,7},{4,0},{5,1},{6,2},{7,3},{8,12},{9,13},{10,... | collective-permute-start | bytes 172040 | tf_op jit(solution)/shard_map/ppermute | solution.py:455
  31.4 4.2 %collective-permute-start.15 = (bf16[32,896]{1,0:T(8,128)(2,1)S(1)}, bf16[32,896]{1,0:T(8,128)(2,1)S(1)}, u32[]{:S(2)}, u32[]{:S(2)}) collective-permute-start(bf16[32,896]{1,0:T(8,128)(2,1)S(1)} %get-tuple-element.41), channel_id=1, source_target_pairs={{0,2},{1,3},{2,0},{3,1},{4,6},{5,7},{6,4},{7,5},{8,10},{9,11},{10,... | collective-permute-start | bytes 172040 | tf_op jit(solution)/shard_map/ppermute | solution.py:455
  33.1 2.5 %collective-permute-start.19 = (bf16[32,896]{1,0:T(8,128)(2,1)S(1)}, bf16[32,896]{1,0:T(8,128)(2,1)S(1)}, u32[]{:S(2)}, u32[]{:S(2)}) collective-permute-start(bf16[32,896]{1,0:T(8,128)(2,1)S(1)} %get-tuple-element.42.refs_3_), channel_id=1, source_target_pairs={{0,1},{1,0},{2,3},{3,2},{4,5},{5,4},{6,7},{7,6},{8,9},{9,8},{10,11... | collective-permute-start | bytes 172040 | tf_op jit(solution)/shard_map/ppermute | solution.py:461
  34.8 1.2 %collective-permute-start.16 = (bf16[32,896]{1,0:T(8,128)(2,1)S(1)}, bf16[32,896]{1,0:T(8,128)(2,1)S(1)}, u32[]{:S(2)}, u32[]{:S(2)}) collective-permute-start(bf16[32,896]{1,0:T(8,128)(2,1)S(1)} %collective-permute-done.13.refs_0_), channel_id=1, source_target_pairs={{0,1},{1,0},{2,3},{3,2},{4,5},{5,4},{6,7},{7,6},{8,9},{9,8},{10,11... | collective-permute-start | bytes 172040 | tf_op jit(solution)/shard_map/ppermute | solution.py:461
  34.8 1.4 %collective-permute-start.17 = (bf16[32,896]{1,0:T(8,128)(2,1)S(1)}, bf16[32,896]{1,0:T(8,128)(2,1)S(1)}, u32[]{:S(2)}, u32[]{:S(2)}) collective-permute-start(bf16[32,896]{1,0:T(8,128)(2,1)S(1)} %collective-permute-done.14.refs_1_), channel_id=1, source_target_pairs={{0,1},{1,0},{2,3},{3,2},{4,5},{5,4},{6,7},{7,6},{8,9},{9,8},{10,11... | collective-permute-start | bytes 172040 | tf_op jit(solution)/shard_map/ppermute | solution.py:461
  35.5 1.2 %collective-permute-start.18 = (bf16[32,896]{1,0:T(8,128)(2,1)S(1)}, bf16[32,896]{1,0:T(8,128)(2,1)S(1)}, u32[]{:S(2)}, u32[]{:S(2)}) collective-permute-start(bf16[32,896]{1,0:T(8,128)(2,1)S(1)} %collective-permute-done.15.refs_2_), channel_id=1, source_target_pairs={{0,1},{1,0},{2,3},{3,2},{4,5},{5,4},{6,7},{7,6},{8,9},{9,8},{10,11... | collective-permute-start | bytes 172040 | tf_op jit(solution)/shard_map/ppermute | solution.py:461
  41.3 5.2 %collective-permute-start.20 = (bf16[32,896]{1,0:T(8,128)(2,1)S(1)}, bf16[32,896]{1,0:T(8,128)(2,1)S(1)}, u32[]{:S(2)}, u32[]{:S(2)}) collective-permute-start(bf16[32,896]{1,0:T(8,128)(2,1)S(1)} %get-tuple-element.43), channel_id=1, source_target_pairs={{0,6},{1,7},{2,4},{3,5},{4,2},{5,3},{6,0},{7,1},{8,14},{9,15},{10,... | collective-permute-start | bytes 172040 | tf_op jit(solution)/shard_map/ppermute | solution.py:455
  42.8 4.7 %collective-permute-start.21 = (bf16[32,896]{1,0:T(8,128)(2,1)S(1)}, bf16[32,896]{1,0:T(8,128)(2,1)S(1)}, u32[]{:S(2)}, u32[]{:S(2)}) collective-permute-start(bf16[32,896]{1,0:T(8,128)(2,1)S(1)} %get-tuple-element.44), channel_id=1, source_target_pairs={{0,4},{1,5},{2,6},{3,7},{4,0},{5,1},{6,2},{7,3},{8,12},{9,13},{10,... | collective-permute-start | bytes 172040 | tf_op jit(solution)/shard_map/ppermute | solution.py:455
  44.5 4.2 %collective-permute-start.22 = (bf16[32,896]{1,0:T(8,128)(2,1)S(1)}, bf16[32,896]{1,0:T(8,128)(2,1)S(1)}, u32[]{:S(2)}, u32[]{:S(2)}) collective-permute-start(bf16[32,896]{1,0:T(8,128)(2,1)S(1)} %get-tuple-element.45), channel_id=1, source_target_pairs={{0,2},{1,3},{2,0},{3,1},{4,6},{5,7},{6,4},{7,5},{8,10},{9,11},{10,... | collective-permute-start | bytes 172040 | tf_op jit(solution)/shard_map/ppermute | solution.py:455
  44.8 3.9 %collective-permute-start.26 = (bf16[32,896]{1,0:T(8,128)(2,1)S(1)}, bf16[32,896]{1,0:T(8,128)(2,1)S(1)}, u32[]{:S(2)}, u32[]{:S(2)}) collective-permute-start(bf16[32,896]{1,0:T(8,128)(2,1)S(1)} %get-tuple-element.46.refs_3_), channel_id=1, source_target_pairs={{0,1},{1,0},{2,3},{3,2},{4,5},{5,4},{6,7},{7,6},{8,9},{9,8},{10,11... | collective-permute-start | bytes 172040 | tf_op jit(solution)/shard_map/ppermute | solution.py:461
  46.5 2.2 %collective-permute-start.23 = (bf16[32,896]{1,0:T(8,128)(2,1)S(1)}, bf16[32,896]{1,0:T(8,128)(2,1)S(1)}, u32[]{:S(2)}, u32[]{:S(2)}) collective-permute-start(bf16[32,896]{1,0:T(8,128)(2,1)S(1)} %collective-permute-done.20.refs_0_), channel_id=1, source_target_pairs={{0,1},{1,0},{2,3},{3,2},{4,5},{5,4},{6,7},{7,6},{8,9},{9,8},{10,11... | collective-permute-start | bytes 172040 | tf_op jit(solution)/shard_map/ppermute | solution.py:461
  47.4 1.3 %collective-permute-start.24 = (bf16[32,896]{1,0:T(8,128)(2,1)S(1)}, bf16[32,896]{1,0:T(8,128)(2,1)S(1)}, u32[]{:S(2)}, u32[]{:S(2)}) collective-permute-start(bf16[32,896]{1,0:T(8,128)(2,1)S(1)} %collective-permute-done.21.refs_1_), channel_id=1, source_target_pairs={{0,1},{1,0},{2,3},{3,2},{4,5},{5,4},{6,7},{7,6},{8,9},{9,8},{10,11... | collective-permute-start | bytes 172040 | tf_op jit(solution)/shard_map/ppermute | solution.py:461
  48.7 1.2 %collective-permute-start.25 = (bf16[32,896]{1,0:T(8,128)(2,1)S(1)}, bf16[32,896]{1,0:T(8,128)(2,1)S(1)}, u32[]{:S(2)}, u32[]{:S(2)}) collective-permute-start(bf16[32,896]{1,0:T(8,128)(2,1)S(1)} %collective-permute-done.22.refs_2_), channel_id=1, source_target_pairs={{0,1},{1,0},{2,3},{3,2},{4,5},{5,4},{6,7},{7,6},{8,9},{9,8},{10,11... | collective-permute-start | bytes 172040 | tf_op jit(solution)/shard_map/ppermute | solution.py:461

commit v4 on v3

--- a/solution.py
+++ b/solution.py
@@ -257,12 +257,7 @@
     return copies
 
 
-def cut(rows, count):
-    step = rows // count
-    return [pl.ds(i * step, step) for i in range(count)]
-
-
-def prepare_kernel(
+def send_kernel(
     parts,
     slot_cap,
     up,
@@ -271,56 +266,85 @@
     down_ids,
     enter_up,
     enter_down,
-    gain,
-    router,
     w_gate,
     w_up,
     w_down,
     out_refs,
-    aside_ref,
+    up_v,
+    down_v,
+    up_i,
+    down_i,
+    enter_up_v,
+    enter_down_v,
+    sems,
+):
+    del w_gate, w_up, w_down
+    sources = (up_ids, down_ids, up.at[0], down.at[0], enter_up, enter_down)
+    copies = started(sources, (up_i, down_i, up_v, down_v, enter_up_v, enter_down_v), sems)
+    copies[0].wait()
+    copies[1].wait()
+    blocks = [ref.at[: 2 * SUBLANES] for ref in out_refs]
+    span = 2 * SUBLANES * len(blocks)
+    rows, features = up_v.shape
+    width = features // parts
+    sending = sending_map(up_i[0, 0], down_i[0, 0], parts, slot_cap, span)
+    last = up_i.shape[0] - 1
+    square = jnp.where(iota((rows, LANES), 0) == iota((rows, LANES), 1), 1, 0)
+    up_line = jnp.sum(square * upright(up_i[last, 0]), axis=0, keepdims=True)
+    down_line = jnp.sum(square * upright(down_i[last, 0]), axis=0, keepdims=True)
+    row = iota((rows, LANES), 0)
+    lines = jnp.where(row == 0, up_line, jnp.where(row == 1, down_line, 0))
+    aside = out_refs[-1].at[2 * SUBLANES :]
+    aside[parts * rows :, :LANES] = lines.astype(jnp.float32).astype(jnp.bfloat16)
+    numbers = (iota((span, LANES), 0) % rows).astype(jnp.float32).astype(jnp.bfloat16)
+    put(moved(sending, numbers), [ref.at[:, width:] for ref in blocks])
+    copies[2].wait()
+    copies[3].wait()
+    packed = pack_rows(sending, up_v[...], down_v[...], parts)
+    put(packed, [ref.at[:, :width] for ref in blocks])
+    copies[4].wait()
+    copies[5].wait()
+    for q in range(parts):
+        cols = slice(q * width, (q + 1) * width)
+        entering = jnp.where(lax.axis_index("pipe") == 0, enter_up_v[:, cols], enter_down_v[:, cols])
+        aside[q * rows : (q + 1) * rows, :width] = entering
+
+
+def plan_kernel(
+    parts,
+    slot_cap,
+    after_ref,
+    up_ids,
+    down_ids,
+    gain,
+    router,
     back_ref,
+    arriving_ref,
+    relaying_ref,
+    closing_ref,
     gain_v,
     router_v,
-    up_v,
-    down_v,
-    enter_up_v,
-    enter_down_v,
     up_i,
     down_i,
     cols_v,
     sems,
 ):
-    sources = (up_ids, down_ids, up.at[0], down.at[0], router.at[0], gain, enter_up, enter_down)
-    targets = (up_i, down_i, up_v, down_v, cols_v, gain_v, enter_up_v, enter_down_v)
-    copies = started(sources, targets, sems)
+    del after_ref
+    last = up_ids.shape[0] - 1
+    sources = (up_ids.at[last, 0], down_ids.at[last, 0], router.at[0], gain)
+    copies = started(sources, (up_i, down_i, cols_v, gain_v), sems)
+    span = back_ref.shape[0]
+    arriving_ref[...] = arriving_map(parts, slot_cap, span).astype(jnp.bfloat16)
+    relaying_ref[...] = relaying_map(parts, slot_cap, span).T.astype(jnp.bfloat16)
+    closing_ref[...] = closing_map(parts, slot_cap, span).T.astype(jnp.bfloat16)
     copies[0].wait()
     copies[1].wait()
-    span = back_ref.shape[0]
-    rows, features = up_v.shape
-    width = features // parts
-    sending = sending_map(up_i[0, 0], down_i[0, 0], parts, slot_cap, span)
-    numbers = (iota((span, LANES), 0) % rows).astype(jnp.float32).astype(jnp.bfloat16)
+    back_ref[...] = returning_map(up_i[...], down_i[...], parts, slot_cap, span).T.astype(jnp.bfloat16)
     copies[2].wait()
-    copies[3].wait()
-    packed = pack_rows(sending, up_v[...], down_v[...], parts)
-    put(packed, [ref.at[:, :width] for ref in out_refs])
-    put(moved(sending, numbers), [ref.at[:, width:] for ref in out_refs])
-    last = up_i.shape[0] - 1
-    back_ref[...] = returning_map(up_i[last, 0], down_i[last, 0], parts, slot_cap, span).T.astype(jnp.bfloat16)
-    ids = jnp.where(iota((rows, LANES), 0) == iota((rows, LANES), 1), 1, 0)
-    up_line = jnp.sum(ids * upright(up_i[last, 0]), axis=0, keepdims=True)
-    down_line = jnp.sum(ids * upright(down_i[last, 0]), axis=0, keepdims=True)
-    row = iota((rows, LANES), 0)
-    lines = jnp.where(row == 0, up_line, jnp.where(row == 1, down_line, 0))
-    aside_ref[rows:] = jnp.zeros((rows, features), jnp.bfloat16)
-    aside_ref[rows:, :LANES] = lines.astype(jnp.float32).astype(jnp.bfloat16)
-    copies[4].wait()
     cols = cols_v[...].astype(jnp.float32)
     mine = iota(cols.shape, 0) == lax.axis_index("expert")
     router_v[...] = jnp.sum(jnp.where(mine, cols, 0.0), axis=0, keepdims=True)
-    for copy in copies[5:]:
-        copy.wait()
-    aside_ref[:rows] = jnp.where(lax.axis_index("pipe") == 0, enter_up_v[...], enter_down_v[...])
+    copies[3].wait()
 
 
 def merge_kernel(kept_ref, passed_ref, out_refs):
@@ -329,38 +353,45 @@
         ref[SUBLANES:] = passed_ref[j * SUBLANES : (j + 1) * SUBLANES]
 
 
-def turn_kernel(parts, slot_cap, pipe, in_refs, aside_ref, other_ref, out_refs):
+def turn_plan_kernel(parts, slot_cap, own_ref, other_ref, sending_ref, entering_ref):
+    section = lax.axis_index("pipe")
+    _, core = chip_and_core()
+    span, width = entering_ref.shape
+    rows = span // (2 * parts)
+    own, other = own_ref[2 * SUBLANES :], other_ref[2 * SUBLANES :]
+    first = jnp.where(core == 0, own, other)
+    second = jnp.where(core == 0, other, own)
+    picked = iota((rows, LANES), 0) == (section + core + 1) % 2
+
+    def ids(aside):
+        lines = jnp.where(picked, aside[parts * rows :, :LANES].astype(jnp.float32), 0.0)
+        return jnp.sum(lines, axis=0, keepdims=True)[:, :rows].astype(jnp.int32)
+
+    sending = sending_map(ids(first), ids(second), parts, slot_cap, span)
+    sending_ref[...] = sending.astype(jnp.bfloat16)
+    pieces = []
+    for q in range(parts):
+        pieces += [x[q * rows : (q + 1) * rows, :width] for x in (first, second)]
+    entering_ref[...] = moved(sending, jnp.concatenate(pieces, axis=0))
+
+
+def turn_kernel(parts, slot_cap, pipe, in_refs, sending_ref, entering_ref, out_refs):
     section = lax.axis_index("pipe")
     _, core = chip_and_core()
     wide = 2 * slot_cap
-    rows = aside_ref.shape[0] // 2
-    width = out_refs[0].shape[1]
-    span = sum(ref.shape[0] for ref in out_refs)
-    own, other = aside_ref[...], other_ref[...]
-    first = jnp.where(core == 0, own, other)
-    second = jnp.where(core == 0, other, own)
-    line = (section + core + 1) % 2
-    picked = iota((rows, LANES), 0) == line
-
-    def ids(aside):
-        lines = jnp.where(picked, aside[rows:, :LANES].astype(jnp.float32), 0.0)
-        return jnp.sum(lines, axis=0, keepdims=True)[:, :rows].astype(jnp.int32)
-
-    sending = sending_map(ids(first), ids(second), parts, slot_cap, span)
+    span, width = entering_ref.shape
+    rows = span // (2 * parts)
     received = stacked(in_refs)
     numbers = received[:, width:].astype(jnp.float32).astype(jnp.int32)[:, :span]
     sublane = iota((span, span), 0)
     within = sublane % SUBLANES
     place = within // wide * (2 * rows) + within % wide // slot_cap * rows
-    sorting = jnp.where(iota((span, span), 1) == place + numbers[:, :1], 1.0, 0.0).T
-    sorted_rows = moved(sorting, received[:, :width])
-    entering = []
-    for q in range(parts):
-        entering += [x[:rows, q * width : (q + 1) * width] for x in (first, second)]
+    sorting = jnp.where(iota((span, span), 1) == place + numbers, 1.0, 0.0).astype(jnp.bfloat16)
+    across = (((1,), (1,)), ((), ()))
+    sending = lax.dot_general(sending_ref[...], sorting, across, preferred_element_type=jnp.float32)
     partner = ((section + core) ^ 1) - core
     enters = (partner < 0) | (partner >= pipe)
-    sorted_rows = jnp.where(enters, jnp.concatenate(entering, axis=0), sorted_rows)
-    put(moved(sending, sorted_rows), out_refs)
+    put(jnp.where(enters, entering_ref[...], moved(sending, received[:, :width])), out_refs)
 
 
 def unpack_kernel(in_refs, back_ref, up_ref, down_ref):
@@ -372,11 +403,20 @@
         down_ref[:, q * width : (q + 1) * width] = back[(2 * q + 1) * rows : (2 * q + 2) * rows]
 
 
-def expert_rows(parts, slot_cap, in_refs, gain_ref, router_ref, x_ref, gates, ups, downs):
-    span = in_refs[0].shape[0] * len(in_refs) // 2
-    rows = span // parts
+MXU_ROWS = 128
+
+
+def product(left, weight):
+    rows = left.shape[0]
+    spare = jnp.zeros((max(0, MXU_ROWS - rows), left.shape[1]), left.dtype)
+    left = jnp.concatenate([left, spare], axis=0)
+    return jnp.dot(left, weight, preferred_element_type=jnp.float32)[:rows]
+
+
+def expert_rows(parts, in_refs, arriving_ref, gain_ref, router_ref, gate_ref, up_ref, down_ref, x_ref):
+    rows = x_ref.shape[0]
     width = x_ref.shape[1] // parts
-    spread = moved(arriving_map(parts, slot_cap, span), stacked(in_refs))
+    spread = moved(arriving_ref[...], stacked([ref.at[: 2 * SUBLANES] for ref in in_refs]))
     for q in range(parts):
         x_ref[:, q * width : (q + 1) * width] = spread[q * rows : (q + 1) * rows, :width]
     widened = x_ref[...].astype(jnp.float32)
@@ -384,47 +424,31 @@
     normed = (widened * inverse * gain_ref[...]).astype(jnp.bfloat16)
     logit = jnp.sum(normed.astype(jnp.float32) * router_ref[...], axis=1, keepdims=True)
     weight = jax.nn.sigmoid(logit)
-
-    def product(left, pieces):
-        total, start = 0.0, 0
-        for ref, copies in pieces:
-            for copy in copies:
-                copy.wait()
-            part = left[:, start : start + ref.shape[0]]
-            total += jnp.dot(part, ref[...], preferred_element_type=jnp.float32)
-            start += ref.shape[0]
-        return total
-
-    gate_pre = product(normed, gates)
-    hidden = (jax.nn.silu(gate_pre) * product(normed, ups)).astype(jnp.bfloat16)
-    part = product(hidden, downs).astype(jnp.bfloat16).astype(jnp.float32)
+    gate_pre = product(normed, gate_ref[...])
+    hidden = (jax.nn.silu(gate_pre) * product(normed, up_ref[...])).astype(jnp.bfloat16)
+    part = product(hidden, down_ref[...]).astype(jnp.bfloat16).astype(jnp.float32)
     done = (x_ref[...].astype(jnp.float32) + weight * part).astype(jnp.bfloat16)
     done = jnp.concatenate([done[:, q * width : (q + 1) * width] for q in range(parts)], axis=0)
     return done, spread[:, width:]
 
 
-def first_kernel(
-    parts, slot_cap, in_refs, gain_ref, router_ref, gate_ref, up_ref, down_ref, kept_ref, passed_ref, x_ref
-):
-    done, numbers = expert_rows(
-        parts, slot_cap, in_refs, gain_ref, router_ref, x_ref, [(gate_ref, [])], [(up_ref, [])], [(down_ref, [])]
-    )
-    onehot = relaying_map(parts, slot_cap, done.shape[0]).T
-    put(moved(onehot, jnp.concatenate([done, numbers], axis=1)), (kept_ref, passed_ref))
-
-
-def later_kernel(parts, slot_cap, in_refs, gain_ref, router_ref, gate_ref, up_ref, down_ref, out_refs, x_ref):
-    done, _ = expert_rows(
-        parts, slot_cap, in_refs, gain_ref, router_ref, x_ref, [(gate_ref, [])], [(up_ref, [])], [(down_ref, [])]
-    )
-    put(moved(closing_map(parts, slot_cap, done.shape[0]).T, done), out_refs)
+def first_kernel(parts, in_refs, leaving_ref, *refs):
+    *ins, kept_ref, passed_ref, x_ref = refs
+    done, numbers = expert_rows(parts, in_refs, *ins, x_ref)
+    put(moved(leaving_ref[...], jnp.concatenate([done, numbers], axis=1)), (kept_ref, passed_ref))
+
+
+def later_kernel(parts, in_refs, leaving_ref, *refs):
+    *ins, out_refs, x_ref = refs
+    done, _ = expert_rows(parts, in_refs, *ins, x_ref)
+    put(moved(leaving_ref[...], done), out_refs)
 
 
 VMEM_SPEC = pl.BlockSpec(memory_space=pltpu.VMEM)
 HBM_SPEC = pl.BlockSpec(memory_space=pltpu.HBM)
 
 
-def local_call(kernel, out_shapes, near, far=(), scratch=(), limit=8 << 20, cost=None):
+def local_call(kernel, out_shapes, near, far=(), scratch=()):
     far = [pltpu.with_memory_space_constraint(x, pltpu.HBM) for x in far]
     close, near_tree = jax.tree.flatten(tuple(near))
     outs, out_tree = jax.tree.flatten(out_shapes)
@@ -442,24 +466,21 @@
         in_specs=[VMEM_SPEC] * len(close) + [HBM_SPEC] * len(far),
         out_specs=[VMEM_SPEC] * len(outs),
         scratch_shapes=list(scratch),
-        compiler_params=pltpu.CompilerParams(vmem_limit_bytes=limit),
-        cost_estimate=cost,
+        compiler_params=pltpu.CompilerParams(vmem_limit_bytes=8 << 20),
     )(*close, *far)
     return out_tree.unflatten(results)
 
 
-def exchanged(arrays, beside=None):
+def exchanged(arrays):
     last = len(arrays) - 1
     devices = range(2 * len(arrays))
     arrived = [
         lax.ppermute(arrays[j], "expert", [(i, i ^ (2 * (last - j))) for i in devices])
         for j in range(last)
     ]
-    if beside is not None:
-        arrived, beside = lax.optimization_barrier((arrived, beside))
     arrived.append(arrays[last])
     passed = [lax.ppermute(x, "expert", [(i, i ^ 1) for i in devices]) for x in arrived]
-    return tuple(arrived + passed), beside
+    return tuple(arrived + passed)
 
 
 def relay_pairs(k, pipe, experts):
@@ -470,11 +491,6 @@
             target = (other, i ^ (2 * k)) if 0 <= other < pipe else (section, i ^ (2 * (k or 1)))
             pairs.append((section * experts + i, target[0] * experts + target[1]))
     return pairs
-
-
-EARLY_COPIES = 4
-LATE_COPIES = 4
-LOAD_COPIES = 4
 
 
 def single_shards(
@@ -493,81 +509,70 @@
     pipe = lax.axis_size("pipe")
     experts = lax.axis_size("expert")
     rows, features = up_state.shape[1:]
-    hidden = w_gate.shape[2]
     slot_cap = rows * TOP // experts
     parts = SUBLANES // (2 * slot_cap)
     span = experts * SUBLANES
     chips = experts // 2
     width = features // parts
-    early = features // 2
     numbered = (pltpu.VMEM((2 * SUBLANES, width + LANES), jnp.bfloat16),) * chips
     blocks = (pltpu.VMEM((2 * SUBLANES, width), jnp.bfloat16),) * chips
     half = pltpu.VMEM((span // 2, width + LANES), jnp.bfloat16)
     batch = pltpu.VMEM((rows, features), jnp.bfloat16)
-    ids_v = pltpu.VMEM((TICKS, 1, 1, rows), jnp.int32)
+    ids_v = pltpu.VMEM((1, rows), jnp.int32)
+    all_ids_v = pltpu.VMEM((TICKS, 1, 1, rows), jnp.int32)
     row_v = pltpu.VMEM((1, features), jnp.float32)
     x_v = pltpu.VMEM((span // parts, features), jnp.bfloat16)
+    map_v = pltpu.VMEM((span, span), jnp.bfloat16)
+    wide_map_v = pltpu.VMEM((span, 2 * span), jnp.bfloat16)
     sibling = [(i, i ^ 1) for i in range(experts)]
-    sent, aside, back, gain, column = local_call(
-        functools.partial(prepare_kernel, parts, slot_cap),
-        (
-            numbered,
-            pltpu.VMEM((2 * rows, features), jnp.bfloat16),
-            pltpu.VMEM((span, 2 * span), jnp.bfloat16),
-            row_v,
-            row_v,
-        ),
+    ids = (up_route.transpose(0, 1, 3, 2), down_route.transpose(0, 1, 3, 2))
+    kept_back = pltpu.VMEM((2 * SUBLANES + (parts + 1) * rows, width + LANES), jnp.bfloat16)
+    (sent,) = local_call(
+        functools.partial(send_kernel, parts, slot_cap),
+        (numbered[1:] + (kept_back,),),
         (),
-        (
-            up_state,
-            down_state,
-            up_route.transpose(0, 1, 3, 2),
-            down_route.transpose(0, 1, 3, 2),
-            entering_up,
-            entering_down,
-            norm_gain,
-            router.transpose(0, 2, 1),
-            w_gate,
-            w_up,
-            w_down,
-        ),
-        [
-            batch,
-            batch,
-            batch,
-            batch,
-            ids_v,
-            ids_v,
-            pltpu.VMEM(router.shape[:0:-1], router.dtype),
-            pltpu.SemaphoreType.DMA((8,)),
-        ],
-    )
-    received, _ = exchanged(sent)
-    gate, up, down = w_gate[0], w_up[0], w_down[0]
+        (up_state, down_state, *ids, entering_up, entering_down, w_gate, w_up, w_down),
+        [batch, batch, all_ids_v, all_ids_v, batch, batch, pltpu.SemaphoreType.DMA((6,))],
+    )
+    back, arriving, relaying, closing, gain, column = local_call(
+        functools.partial(plan_kernel, parts, slot_cap),
+        (wide_map_v, wide_map_v, map_v, map_v, row_v, row_v),
+        (sent[-1],),
+        (*ids, norm_gain, router.transpose(0, 2, 1)),
+        [ids_v, ids_v, pltpu.VMEM(router.shape[:0:-1], router.dtype), pltpu.SemaphoreType.DMA((4,))],
+    )
+    layer = (arriving, gain, column, w_gate[0], w_up[0], w_down[0])
+    received = exchanged(sent)
+    sending, entering = local_call(
+        functools.partial(turn_plan_kernel, parts, slot_cap),
+        (map_v, pltpu.VMEM((span, width), jnp.bfloat16)),
+        (sent[-1], received[-1]),
+    )
     kept, passed = local_call(
-        functools.partial(first_kernel, parts, slot_cap),
+        functools.partial(first_kernel, parts),
         (half, half),
-        (received, gain, column, gate, up, down),
+        (received, relaying, *layer),
         (),
         [x_v],
     )
-    other = lax.ppermute(aside, "expert", sibling)
     passed = lax.ppermute(passed, "expert", sibling)
     (merged,) = local_call(merge_kernel, (numbered,), (kept, passed))
     relayed = tuple(
         lax.ppermute(x, ("pipe", "expert"), relay_pairs(chips - 1 - j, pipe, experts))
         for j, x in enumerate(merged)
     )
-    kernel = functools.partial(turn_kernel, parts, slot_cap, pipe)
-    relayed = relayed[chips // 2 :] + relayed[: chips // 2]
-    (sent,) = local_call(kernel, (blocks,), (relayed, aside, other))
-    received, _ = exchanged(sent)
-    kernel = functools.partial(later_kernel, parts, slot_cap)
-    args = (received, gain, column, gate, up, down)
-    (done,) = local_call(kernel, (blocks,), args, (), [x_v])
-    batch = jax.ShapeDtypeStruct((rows, features), jnp.bfloat16)
-    received, _ = exchanged(done)
-    up_done, down_done = local_call(unpack_kernel, (batch, batch), (received, back))
+    (sent,) = local_call(
+        functools.partial(turn_kernel, parts, slot_cap, pipe), (blocks,), (relayed, sending, entering)
+    )
+    (done,) = local_call(
+        functools.partial(later_kernel, parts),
+        (blocks,),
+        (exchanged(sent), closing, *layer),
+        (),
+        [x_v],
+    )
+    result = jax.ShapeDtypeStruct((rows, features), jnp.bfloat16)
+    up_done, down_done = local_call(unpack_kernel, (result, result), (exchanged(done), back))
     return (up_done[None], down_done[None])
 
 

time: 51 us -> 48.1 us (0.943)
  waiting for transfers between devices: 19.3 us -> 17.4 us
    ppermute x4, waiting for transfers between devices: 4.97 us -> 3.48 us  [single_shards(): lax.ppermute(x, ('pipe', 'expert'), relay_pairs(chips - 1 - j, pipe, expe...]
    ppermute x12, waiting for transfers between devices: 3.21 us -> 2.41 us  [exchanged(): lax.ppermute(x, 'expert', [(i, i ^ 1) for i in devices])]
    pallas_call x6 -> x8, Pallas kernels: 11.9 us -> 11.4 us  [local_call(): pl.pallas_call(body, out_shape=outs, in_specs=[VMEM_SPEC] * len(close) +...]
  transfers between devices with their start and end apart: 27 -> 26, of which waited for: 17 -> 17; matrix products, arithmetic and copies ran while one was open for 0% -> 0% of each run, Pallas kernels for 9% -> 3%
where the time goes in v4:
time: 48.1 us; the launch traced here: 47.9 us
  starting transfers between devices  18.4 us (38%)
  waiting for transfers between devices  17.4 us (36%)
  Pallas kernels  11.4 us (24%)
  between operations  0.77 us (2%)
    pallas_call x8, Pallas kernels, local_call(): pl.pallas_call(body, out_shape=outs, in_specs=[VMEM_SPEC] * len(close) +...  11.4 us
    ppermute x9, starting transfers between devices, exchanged(): lax.ppermute(arrays[j], 'expert', [(i, i ^ 2 * (last - j)) for i in devic...  11.3 us
    ppermute x9, waiting for transfers between devices, exchanged(): lax.ppermute(arrays[j], 'expert', [(i, i ^ 2 * (last - j)) for i in devic...  10.4 us
    ppermute x4, starting transfers between devices, single_shards(): lax.ppermute(x, ('pipe', 'expert'), relay_pairs(chips - 1 - j, pipe, expe...  5.91 us
    ppermute x4, waiting for transfers between devices, single_shards(): lax.ppermute(x, ('pipe', 'expert'), relay_pairs(chips - 1 - j, pipe, expe...  3.48 us
    ppermute x12, waiting for transfers between devices, exchanged(): lax.ppermute(x, 'expert', [(i, i ^ 1) for i in devices])  2.41 us
    ppermute x1, waiting for transfers between devices, single_shards(): passed = lax.ppermute(passed, 'expert', sibling)  1.03 us
  transfers between devices with their start and end apart: 26, of which 17 were waited for; matrix products, arithmetic and copies ran while one was open for 0% of the time, Pallas kernels for 3%

profile of v4, /device:TPU:0, one launch (start us, length us, event | category | flops | bytes accessed | tf_op | source)
XLA Modules:
  0.0 47.9 jit_solution(14197816399452613444)
XLA Ops:
  0.6 0.0 copy-start
  0.6 0.0 copy-start.1
  0.7 0.0 copy-start.2
  0.7 1.4 %shard_map.122 = (bf16[32,1024]{1,0:T(8,128)(2,1)S(1)}, bf16[32,1024]{1,0:T(8,128)(2,1)S(1)}, bf16[32,1024]{1,0:T(8,128)(2,1)S(1)}, bf16[112,1024]{1,0:T(8,128)(2,1)S(1)}) custom-call(bf16[1,16,3584]{2,1,0:T(8,128)(2,1)} %refs_0_.1, bf16[1,16,3584]{2,1,0:T(8,128)(2,1)} %refs_1_.1, s32[2,1,1,16]{3,2,1,0:T(1,128)} %bitcast.19, s32[2,1,1,16]{3,2,1,0:T(1,128)} %bitcast.21, ...), custom_call_target="tpu_custom_call" | custom-call | tf_op jit(solution)/shard_map/pallas_call | solution.py:463
  2.1 0.5 %collective-permute-start.6 = (bf16[112,1024]{1,0:T(8,128)(2,1)S(1)}, bf16[112,1024]{1,0:T(8,128)(2,1)S(1)}, u32[]{:S(2)}, u32[]{:S(2)}) collective-permute-start(bf16[112,1024]{1,0:T(8,128)(2,1)S(1)} %get-tuple-element.33.refs_0_.refs_3_), channel_id=1, source_target_pairs={{0,1},{1,0},{2,3},{3,2},{4,5},{5,4},{6,7},{7,6},{8,9},{9,8},{10,11... | collective-permute-start | bytes 688136 | tf_op jit(solution)/shard_map/ppermute | solution.py:482
  2.6 3.5 %collective-permute-start = (bf16[32,1024]{1,0:T(8,128)(2,1)S(1)}, bf16[32,1024]{1,0:T(8,128)(2,1)S(1)}, u32[]{:S(2)}, u32[]{:S(2)}) collective-permute-start(bf16[32,1024]{1,0:T(8,128)(2,1)S(1)} %get-tuple-element.30), channel_id=1, source_target_pairs={{0,6},{1,7},{2,4},{3,5},{4,2},{5,3},{6,0},{7,1},{8,14},{9,15},{10,... | collective-permute-start | bytes 196616 | tf_op jit(solution)/shard_map/ppermute | solution.py:478
  6.1 0.5 %collective-permute-start.1 = (bf16[32,1024]{1,0:T(8,128)(2,1)S(1)}, bf16[32,1024]{1,0:T(8,128)(2,1)S(1)}, u32[]{:S(2)}, u32[]{:S(2)}) collective-permute-start(bf16[32,1024]{1,0:T(8,128)(2,1)S(1)} %get-tuple-element.31), channel_id=1, source_target_pairs={{0,4},{1,5},{2,6},{3,7},{4,0},{5,1},{6,2},{7,3},{8,12},{9,13},{10,... | collective-permute-start | bytes 196616 | tf_op jit(solution)/shard_map/ppermute | solution.py:478
  6.6 0.1 collective-permute-start.2
  6.8 2.0 %collective-permute-done.refs_0_ = bf16[32,1024]{1,0:T(8,128)(2,1)S(1)} collective-permute-done((bf16[32,1024]{1,0:T(8,128)(2,1)S(1)}, bf16[32,1024]{1,0:T(8,128)(2,1)S(1)}, u32[]{:S(2)}, u32[]{:S(2)}) %collective-permute-start) | collective-permute-done | bytes 65568 | tf_op jit(solution)/shard_map/ppermute | solution.py:478
  8.8 0.0 collective-permute-start.3
  8.8 1.6 %collective-permute-done.1.refs_1_ = bf16[32,1024]{1,0:T(8,128)(2,1)S(1)} collective-permute-done((bf16[32,1024]{1,0:T(8,128)(2,1)S(1)}, bf16[32,1024]{1,0:T(8,128)(2,1)S(1)}, u32[]{:S(2)}, u32[]{:S(2)}) %collective-permute-start.1) | collective-permute-done | bytes 65568 | tf_op jit(solution)/shard_map/ppermute | solution.py:478
  10.4 0.0 collective-permute-start.4
  10.4 0.5 %collective-permute-done.2.refs_2_ = bf16[32,1024]{1,0:T(8,128)(2,1)S(1)} collective-permute-done((bf16[32,1024]{1,0:T(8,128)(2,1)S(1)}, bf16[32,1024]{1,0:T(8,128)(2,1)S(1)}, u32[]{:S(2)}, u32[]{:S(2)}) %collective-permute-start.2) | collective-permute-done | bytes 65568 | tf_op jit(solution)/shard_map/ppermute | solution.py:478
  10.9 0.0 collective-permute-start.5
  10.9 1.0 %shard_map.123 = (bf16[128,256]{1,0:T(8,128)(2,1)S(1)}, bf16[128,256]{1,0:T(8,128)(2,1)S(1)}, bf16[128,128]{1,0:T(8,128)(2,1)S(1)}, bf16[128,128]{1,0:T(8,128)(2...) custom-call(bf16[112,1024]{1,0:T(8,128)(2,1)S(1)} %get-tuple-element.33.refs_0_.refs_3_, s32[2,1,1,16]{3,2,1,0:T(1,128)} %bitcast.20, ...), custom_call_target="tpu_custom_call" | custom-call | tf_op jit(solution)/shard_map/pallas_call | solution.py:463
  11.9 0.0 collective-permute-done.3.refs_4_
  11.9 0.0 collective-permute-done.4.refs_5_
  11.9 0.2 collective-permute-done.5.refs_6_
  12.2 0.0 collective-permute-done.6.refs_7_.refs_1_
  12.2 0.0 copy-done
  12.2 0.0 copy-done.2
  12.2 3.7 %shard_map.124 = (bf16[64,1024]{1,0:T(8,128)(2,1)S(1)}, bf16[64,1024]{1,0:T(8,128)(2,1)S(1)}) custom-call(bf16[32,1024]{1,0:T(8,128)(2,1)S(1)} %collective-permute-done.refs_0_, bf16[32,1024]{1,0:T(8,128)(2,1)S(1)} %collective-permute-done.1.refs_1_, bf16[32,1024]{1,0:T(8,128)(2,1)S(1)} %collective-permute-done.2.refs_2_, ...), custom_call_target="tpu_custom_call" | custom-call | tf_op jit(solution)/shard_map/pallas_call | solution.py:463
  15.9 0.4 collective-permute-start.7
  16.2 1.0 %collective-permute-done.7.refs_1_ = bf16[64,1024]{1,0:T(8,128)(2,1)S(1)} collective-permute-done((bf16[64,1024]{1,0:T(8,128)(2,1)S(1)}, bf16[64,1024]{1,0:T(8,128)(2,1)S(1)}, u32[]{:S(2)}, u32[]{:S(2)}) %collective-permute-start.7) | collective-permute-done | bytes 131104 | tf_op jit(solution)/shard_map/ppermute | solution.py:558
  17.3 2.7 %collective-permute-start.8 = (bf16[32,1024]{1,0:T(8,128)(2,1)S(1)}, bf16[32,1024]{1,0:T(8,128)(2,1)S(1)}, u32[]{:S(2)}, u32[]{:S(2)}) collective-permute-start(bf16[32,1024]{1,0:T(8,128)(2,1)S(1)} %get-tuple-element.40), channel_id=1, source_target_pairs={{0,14},{1,7},{2,12},{3,5},{4,10},{5,3},{6,8},{7,1},{8,6},{9,23},{1... | collective-permute-start | bytes 196616 | tf_op jit(solution)/shard_map/ppermute | solution.py:561
  20.0 1.1 %collective-permute-start.9 = (bf16[32,1024]{1,0:T(8,128)(2,1)S(1)}, bf16[32,1024]{1,0:T(8,128)(2,1)S(1)}, u32[]{:S(2)}, u32[]{:S(2)}) collective-permute-start(bf16[32,1024]{1,0:T(8,128)(2,1)S(1)} %get-tuple-element.41), channel_id=1, source_target_pairs={{0,12},{1,5},{2,14},{3,7},{4,8},{5,1},{6,10},{7,3},{8,4},{9,21},{1... | collective-permute-start | bytes 196616 | tf_op jit(solution)/shard_map/ppermute | solution.py:561
  21.1 1.7 %collective-permute-start.10 = (bf16[32,1024]{1,0:T(8,128)(2,1)S(1)}, bf16[32,1024]{1,0:T(8,128)(2,1)S(1)}, u32[]{:S(2)}, u32[]{:S(2)}) collective-permute-start(bf16[32,1024]{1,0:T(8,128)(2,1)S(1)} %get-tuple-element.42), channel_id=1, source_target_pairs={{0,10},{1,3},{2,8},{3,1},{4,14},{5,7},{6,12},{7,5},{8,2},{9,19},{1... | collective-permute-start | bytes 196616 | tf_op jit(solution)/shard_map/ppermute | solution.py:561
  22.8 0.4 collective-permute-start.11
  23.2 0.3 shard_map.126
  23.5 0.0 collective-permute-done.8.refs_0_
  23.5 1.6 %collective-permute-done.9.refs_1_ = bf16[32,1024]{1,0:T(8,128)(2,1)S(1)} collective-permute-done((bf16[32,1024]{1,0:T(8,128)(2,1)S(1)}, bf16[32,1024]{1,0:T(8,128)(2,1)S(1)}, u32[]{:S(2)}, u32[]{:S(2)}) %collective-permute-start.9) | collective-permute-done | bytes 65568 | tf_op jit(solution)/shard_map/ppermute | solution.py:561
  25.1 1.1 %collective-permute-done.10.refs_2_ = bf16[32,1024]{1,0:T(8,128)(2,1)S(1)} collective-permute-done((bf16[32,1024]{1,0:T(8,128)(2,1)S(1)}, bf16[32,1024]{1,0:T(8,128)(2,1)S(1)}, u32[]{:S(2)}, u32[]{:S(2)}) %collective-permute-start.10) | collective-permute-done | bytes 65568 | tf_op jit(solution)/shard_map/ppermute | solution.py:561
  26.2 0.8 %collective-permute-done.11.refs_3_ = bf16[32,1024]{1,0:T(8,128)(2,1)S(1)} collective-permute-done((bf16[32,1024]{1,0:T(8,128)(2,1)S(1)}, bf16[32,1024]{1,0:T(8,128)(2,1)S(1)}, u32[]{:S(2)}, u32[]{:S(2)}) %collective-permute-start.11) | collective-permute-done | bytes 65568 | tf_op jit(solution)/shard_map/ppermute | solution.py:561
  27.0 0.4 shard_map.127
  27.4 1.7 %collective-permute-start.12 = (bf16[32,896]{1,0:T(8,128)(2,1)S(1)}, bf16[32,896]{1,0:T(8,128)(2,1)S(1)}, u32[]{:S(2)}, u32[]{:S(2)}) collective-permute-start(bf16[32,896]{1,0:T(8,128)(2,1)S(1)} %get-tuple-element.46), channel_id=1, source_target_pairs={{0,6},{1,7},{2,4},{3,5},{4,2},{5,3},{6,0},{7,1},{8,14},{9,15},{10,... | collective-permute-start | bytes 172040 | tf_op jit(solution)/shard_map/ppermute | solution.py:478
  29.1 1.2 %collective-permute-start.13 = (bf16[32,896]{1,0:T(8,128)(2,1)S(1)}, bf16[32,896]{1,0:T(8,128)(2,1)S(1)}, u32[]{:S(2)}, u32[]{:S(2)}) collective-permute-start(bf16[32,896]{1,0:T(8,128)(2,1)S(1)} %get-tuple-element.47), channel_id=1, source_target_pairs={{0,4},{1,5},{2,6},{3,7},{4,0},{5,1},{6,2},{7,3},{8,12},{9,13},{10,... | collective-permute-start | bytes 172040 | tf_op jit(solution)/shard_map/ppermute | solution.py:478
  30.3 0.7 %collective-permute-start.14 = (bf16[32,896]{1,0:T(8,128)(2,1)S(1)}, bf16[32,896]{1,0:T(8,128)(2,1)S(1)}, u32[]{:S(2)}, u32[]{:S(2)}) collective-permute-start(bf16[32,896]{1,0:T(8,128)(2,1)S(1)} %get-tuple-element.48), channel_id=1, source_target_pairs={{0,2},{1,3},{2,0},{3,1},{4,6},{5,7},{6,4},{7,5},{8,10},{9,11},{10,... | collective-permute-start | bytes 172040 | tf_op jit(solution)/shard_map/ppermute | solution.py:478
  31.0 0.0 collective-permute-start.18
  31.0 1.6 %collective-permute-done.12.refs_0_ = bf16[32,896]{1,0:T(8,128)(2,1)S(1)} collective-permute-done((bf16[32,896]{1,0:T(8,128)(2,1)S(1)}, bf16[32,896]{1,0:T(8,128)(2,1)S(1)}, u32[]{:S(2)}, u32[]{:S(2)}) %collective-permute-start.12) | collective-permute-done | bytes 57376 | tf_op jit(solution)/shard_map/ppermute | solution.py:478
  32.6 0.0 collective-permute-start.15
  32.6 0.7 %collective-permute-done.13.refs_1_ = bf16[32,896]{1,0:T(8,128)(2,1)S(1)} collective-permute-done((bf16[32,896]{1,0:T(8,128)(2,1)S(1)}, bf16[32,896]{1,0:T(8,128)(2,1)S(1)}, u32[]{:S(2)}, u32[]{:S(2)}) %collective-permute-start.13) | collective-permute-done | bytes 57376 | tf_op jit(solution)/shard_map/ppermute | solution.py:478
  33.2 0.0 collective-permute-start.16
  33.2 1.2 %collective-permute-done.14.refs_2_ = bf16[32,896]{1,0:T(8,128)(2,1)S(1)} collective-permute-done((bf16[32,896]{1,0:T(8,128)(2,1)S(1)}, bf16[32,896]{1,0:T(8,128)(2,1)S(1)}, u32[]{:S(2)}, u32[]{:S(2)}) %collective-permute-start.14) | collective-permute-done | bytes 57376 | tf_op jit(solution)/shard_map/ppermute | solution.py:478
  34.5 0.0 collective-permute-start.17
  34.5 0.0 collective-permute-done.18.refs_7_
  34.5 0.0 collective-permute-done.15.refs_4_
  34.5 0.0 collective-permute-done.16.refs_5_
  34.5 1.2 %collective-permute-done.17.refs_6_ = bf16[32,896]{1,0:T(8,128)(2,1)S(1)} collective-permute-done((bf16[32,896]{1,0:T(8,128)(2,1)S(1)}, bf16[32,896]{1,0:T(8,128)(2,1)S(1)}, u32[]{:S(2)}, u32[]{:S(2)}) %collective-permute-start.17) | collective-permute-done | bytes 57376 | tf_op jit(solution)/shard_map/ppermute | solution.py:482
  35.7 3.7 %shard_map.128 = (bf16[32,896]{1,0:T(8,128)(2,1)S(1)}, bf16[32,896]{1,0:T(8,128)(2,1)S(1)}, bf16[32,896]{1,0:T(8,128)(2,1)S(1)}, bf16[32,896]{1,0:T(8,128)(2,1)S(1)}) custom-call(bf16[32,896]{1,0:T(8,128)(2,1)S(1)} %collective-permute-done.12.refs_0_, bf16[32,896]{1,0:T(8,128)(2,1)S(1)} %collective-permute-done.13.refs_1_, ...), custom_call_target="tpu_custom_call" | custom-call | tf_op jit(solution)/shard_map/pallas_call | solution.py:463
  39.4 1.7 %collective-permute-start.19 = (bf16[32,896]{1,0:T(8,128)(2,1)S(1)}, bf16[32,896]{1,0:T(8,128)(2,1)S(1)}, u32[]{:S(2)}, u32[]{:S(2)}) collective-permute-start(bf16[32,896]{1,0:T(8,128)(2,1)S(1)} %get-tuple-element.51), channel_id=1, source_target_pairs={{0,6},{1,7},{2,4},{3,5},{4,2},{5,3},{6,0},{7,1},{8,14},{9,15},{10,... | collective-permute-start | bytes 172040 | tf_op jit(solution)/shard_map/ppermute | solution.py:478
  41.1 0.5 %collective-permute-start.20 = (bf16[32,896]{1,0:T(8,128)(2,1)S(1)}, bf16[32,896]{1,0:T(8,128)(2,1)S(1)}, u32[]{:S(2)}, u32[]{:S(2)}) collective-permute-start(bf16[32,896]{1,0:T(8,128)(2,1)S(1)} %get-tuple-element.52), channel_id=1, source_target_pairs={{0,4},{1,5},{2,6},{3,7},{4,0},{5,1},{6,2},{7,3},{8,12},{9,13},{10,... | collective-permute-start | bytes 172040 | tf_op jit(solution)/shard_map/ppermute | solution.py:478
  41.6 1.3 %collective-permute-start.21 = (bf16[32,896]{1,0:T(8,128)(2,1)S(1)}, bf16[32,896]{1,0:T(8,128)(2,1)S(1)}, u32[]{:S(2)}, u32[]{:S(2)}) collective-permute-start(bf16[32,896]{1,0:T(8,128)(2,1)S(1)} %get-tuple-element.53), channel_id=1, source_target_pairs={{0,2},{1,3},{2,0},{3,1},{4,6},{5,7},{6,4},{7,5},{8,10},{9,11},{10,... | collective-permute-start | bytes 172040 | tf_op jit(solution)/shard_map/ppermute | solution.py:478
  42.9 0.0 collective-permute-start.25
  42.9 1.6 %collective-permute-done.19.refs_0_ = bf16[32,896]{1,0:T(8,128)(2,1)S(1)} collective-permute-done((bf16[32,896]{1,0:T(8,128)(2,1)S(1)}, bf16[32,896]{1,0:T(8,128)(2,1)S(1)}, u32[]{:S(2)}, u32[]{:S(2)}) %collective-permute-start.19) | collective-permute-done | bytes 57376 | tf_op jit(solution)/shard_map/ppermute | solution.py:478
  44.6 0.0 collective-permute-start.22
  44.6 1.0 %collective-permute-done.20.refs_1_ = bf16[32,896]{1,0:T(8,128)(2,1)S(1)} collective-permute-done((bf16[32,896]{1,0:T(8,128)(2,1)S(1)}, bf16[32,896]{1,0:T(8,128)(2,1)S(1)}, u32[]{:S(2)}, u32[]{:S(2)}) %collective-permute-start.20) | collective-permute-done | bytes 57376 | tf_op jit(solution)/shard_map/ppermute | solution.py:478
  45.5 0.0 collective-permute-start.23
  45.5 0.2 collective-permute-done.21.refs_2_
  45.8 0.3 collective-permute-start.24
  46.0 0.0 collective-permute-done.25.refs_7_
  46.0 0.0 collective-permute-done.22.refs_4_
  46.0 0.7 %collective-permute-done.23.refs_5_ = bf16[32,896]{1,0:T(8,128)(2,1)S(1)} collective-permute-done((bf16[32,896]{1,0:T(8,128)(2,1)S(1)}, bf16[32,896]{1,0:T(8,128)(2,1)S(1)}, u32[]{:S(2)}, u32[]{:S(2)}) %collective-permute-start.23) | collective-permute-done | bytes 57376 | tf_op jit(solution)/shard_map/ppermute | solution.py:482
  46.8 0.2 collective-permute-done.24.refs_6_
  47.0 0.9 %shard_map.129 = (bf16[16,3584]{1,0:T(8,128)(2,1)}, bf16[16,3584]{1,0:T(8,128)(2,1)}) custom-call(bf16[32,896]{1,0:T(8,128)(2,1)S(1)} %collective-permute-done.19.refs_0_, bf16[32,896]{1,0:T(8,128)(2,1)S(1)} %collective-permute-done.20.refs_1_, bf16[32,896]{1,0:T(8,128)(2,1)S(1)} %collective-permute-done.21.refs_2_, ...), custom_call_target="tpu_custom_call" | custom-call | tf_op jit(solution)/shard_map/pallas_call | solution.py:463
  (2 shorter events, 0.0 us)
Async XLA Ops:
  0.6 11.5 %copy-start = (bf16[1,3584,1024]{2,1,0:T(8,128)(2,1)S(1)}, bf16[1,3584,1024]{2,1,0:T(8,128)(2,1)}, u32[]{:S(2)}) copy-start(bf16[1,3584,1024]{2,1,0:T(8,128)(2,1)} %refs_6_.1) | copy-start | bytes 22020100
  0.6 11.5 %copy-start.1 = (bf16[1,3584,1024]{2,1,0:T(8,128)(2,1)S(1)}, bf16[1,3584,1024]{2,1,0:T(8,128)(2,1)}, u32[]{:S(2)}) copy-start(bf16[1,3584,1024]{2,1,0:T(8,128)(2,1)} %refs_7_.1) | copy-start | bytes 22020100
  0.7 11.5 %copy-start.2 = (bf16[1,1024,3584]{2,1,0:T(8,128)(2,1)S(1)}, bf16[1,1024,3584]{2,1,0:T(8,128)(2,1)}, u32[]{:S(2)}) copy-start(bf16[1,1024,3584]{2,1,0:T(8,128)(2,1)} %refs_8_.1) | copy-start | bytes 22020100
  2.1 10.1 %collective-permute-start.6 = (bf16[112,1024]{1,0:T(8,128)(2,1)S(1)}, bf16[112,1024]{1,0:T(8,128)(2,1)S(1)}, u32[]{:S(2)}, u32[]{:S(2)}) collective-permute-start(bf16[112,1024]{1,0:T(8,128)(2,1)S(1)} %get-tuple-element.33.refs_0_.refs_3_), channel_id=1, source_target_pairs={{0,1},{1,0},{2,3},{3,2},{4,5},{5,4},{6,7},{7,6},{8,9},{9,8},{10,11... | collective-permute-start | bytes 688136 | tf_op jit(solution)/shard_map/ppermute | solution.py:482
  2.6 6.2 %collective-permute-start = (bf16[32,1024]{1,0:T(8,128)(2,1)S(1)}, bf16[32,1024]{1,0:T(8,128)(2,1)S(1)}, u32[]{:S(2)}, u32[]{:S(2)}) collective-permute-start(bf16[32,1024]{1,0:T(8,128)(2,1)S(1)} %get-tuple-element.30), channel_id=1, source_target_pairs={{0,6},{1,7},{2,4},{3,5},{4,2},{5,3},{6,0},{7,1},{8,14},{9,15},{10,... | collective-permute-start | bytes 196616 | tf_op jit(solution)/shard_map/ppermute | solution.py:478
  6.1 4.3 %collective-permute-start.1 = (bf16[32,1024]{1,0:T(8,128)(2,1)S(1)}, bf16[32,1024]{1,0:T(8,128)(2,1)S(1)}, u32[]{:S(2)}, u32[]{:S(2)}) collective-permute-start(bf16[32,1024]{1,0:T(8,128)(2,1)S(1)} %get-tuple-element.31), channel_id=1, source_target_pairs={{0,4},{1,5},{2,6},{3,7},{4,0},{5,1},{6,2},{7,3},{8,12},{9,13},{10,... | collective-permute-start | bytes 196616 | tf_op jit(solution)/shard_map/ppermute | solution.py:478
  6.6 4.3 %collective-permute-start.2 = (bf16[32,1024]{1,0:T(8,128)(2,1)S(1)}, bf16[32,1024]{1,0:T(8,128)(2,1)S(1)}, u32[]{:S(2)}, u32[]{:S(2)}) collective-permute-start(bf16[32,1024]{1,0:T(8,128)(2,1)S(1)} %get-tuple-element.32), channel_id=1, source_target_pairs={{0,2},{1,3},{2,0},{3,1},{4,6},{5,7},{6,4},{7,5},{8,10},{9,11},{10,... | collective-permute-start | bytes 196616 | tf_op jit(solution)/shard_map/ppermute | solution.py:478
  8.8 3.1 %collective-permute-start.3 = (bf16[32,1024]{1,0:T(8,128)(2,1)S(1)}, bf16[32,1024]{1,0:T(8,128)(2,1)S(1)}, u32[]{:S(2)}, u32[]{:S(2)}) collective-permute-start(bf16[32,1024]{1,0:T(8,128)(2,1)S(1)} %collective-permute-done.refs_0_), channel_id=1, source_target_pairs={{0,1},{1,0},{2,3},{3,2},{4,5},{5,4},{6,7},{7,6},{8,9},{9,8},{10,11... | collective-permute-start | bytes 196616 | tf_op jit(solution)/shard_map/ppermute | solution.py:482
  10.4 1.5 %collective-permute-start.4 = (bf16[32,1024]{1,0:T(8,128)(2,1)S(1)}, bf16[32,1024]{1,0:T(8,128)(2,1)S(1)}, u32[]{:S(2)}, u32[]{:S(2)}) collective-permute-start(bf16[32,1024]{1,0:T(8,128)(2,1)S(1)} %collective-permute-done.1.refs_1_), channel_id=1, source_target_pairs={{0,1},{1,0},{2,3},{3,2},{4,5},{5,4},{6,7},{7,6},{8,9},{9,8},{10,11... | collective-permute-start | bytes 196616 | tf_op jit(solution)/shard_map/ppermute | solution.py:482
  10.9 1.3 %collective-permute-start.5 = (bf16[32,1024]{1,0:T(8,128)(2,1)S(1)}, bf16[32,1024]{1,0:T(8,128)(2,1)S(1)}, u32[]{:S(2)}, u32[]{:S(2)}) collective-permute-start(bf16[32,1024]{1,0:T(8,128)(2,1)S(1)} %collective-permute-done.2.refs_2_), channel_id=1, source_target_pairs={{0,1},{1,0},{2,3},{3,2},{4,5},{5,4},{6,7},{7,6},{8,9},{9,8},{10,11... | collective-permute-start | bytes 196616 | tf_op jit(solution)/shard_map/ppermute | solution.py:482
  15.9 1.4 %collective-permute-start.7 = (bf16[64,1024]{1,0:T(8,128)(2,1)S(1)}, bf16[64,1024]{1,0:T(8,128)(2,1)S(1)}, u32[]{:S(2)}, u32[]{:S(2)}) collective-permute-start(bf16[64,1024]{1,0:T(8,128)(2,1)S(1)} %get-tuple-element.39), channel_id=1, source_target_pairs={{0,1},{1,0},{2,3},{3,2},{4,5},{5,4},{6,7},{7,6},{8,9},{9,8},{10,11... | collective-permute-start | bytes 393224 | tf_op jit(solution)/shard_map/ppermute | solution.py:558
  17.3 6.2 %collective-permute-start.8 = (bf16[32,1024]{1,0:T(8,128)(2,1)S(1)}, bf16[32,1024]{1,0:T(8,128)(2,1)S(1)}, u32[]{:S(2)}, u32[]{:S(2)}) collective-permute-start(bf16[32,1024]{1,0:T(8,128)(2,1)S(1)} %get-tuple-element.40), channel_id=1, source_target_pairs={{0,14},{1,7},{2,12},{3,5},{4,10},{5,3},{6,8},{7,1},{8,6},{9,23},{1... | collective-permute-start | bytes 196616 | tf_op jit(solution)/shard_map/ppermute | solution.py:561
  20.0 5.2 %collective-permute-start.9 = (bf16[32,1024]{1,0:T(8,128)(2,1)S(1)}, bf16[32,1024]{1,0:T(8,128)(2,1)S(1)}, u32[]{:S(2)}, u32[]{:S(2)}) collective-permute-start(bf16[32,1024]{1,0:T(8,128)(2,1)S(1)} %get-tuple-element.41), channel_id=1, source_target_pairs={{0,12},{1,5},{2,14},{3,7},{4,8},{5,1},{6,10},{7,3},{8,4},{9,21},{1... | collective-permute-start | bytes 196616 | tf_op jit(solution)/shard_map/ppermute | solution.py:561
  21.1 5.2 %collective-permute-start.10 = (bf16[32,1024]{1,0:T(8,128)(2,1)S(1)}, bf16[32,1024]{1,0:T(8,128)(2,1)S(1)}, u32[]{:S(2)}, u32[]{:S(2)}) collective-permute-start(bf16[32,1024]{1,0:T(8,128)(2,1)S(1)} %get-tuple-element.42), channel_id=1, source_target_pairs={{0,10},{1,3},{2,8},{3,1},{4,14},{5,7},{6,12},{7,5},{8,2},{9,19},{1... | collective-permute-start | bytes 196616 | tf_op jit(solution)/shard_map/ppermute | solution.py:561
  22.8 4.3 %collective-permute-start.11 = (bf16[32,1024]{1,0:T(8,128)(2,1)S(1)}, bf16[32,1024]{1,0:T(8,128)(2,1)S(1)}, u32[]{:S(2)}, u32[]{:S(2)}) collective-permute-start(bf16[32,1024]{1,0:T(8,128)(2,1)S(1)} %get-tuple-element.43), channel_id=1, source_target_pairs={{0,8},{1,3},{2,10},{3,1},{4,12},{5,7},{6,14},{7,5},{8,0},{9,17},{1... | collective-permute-start | bytes 196616 | tf_op jit(solution)/shard_map/ppermute | solution.py:561
  27.4 5.1 %collective-permute-start.12 = (bf16[32,896]{1,0:T(8,128)(2,1)S(1)}, bf16[32,896]{1,0:T(8,128)(2,1)S(1)}, u32[]{:S(2)}, u32[]{:S(2)}) collective-permute-start(bf16[32,896]{1,0:T(8,128)(2,1)S(1)} %get-tuple-element.46), channel_id=1, source_target_pairs={{0,6},{1,7},{2,4},{3,5},{4,2},{5,3},{6,0},{7,1},{8,14},{9,15},{10,... | collective-permute-start | bytes 172040 | tf_op jit(solution)/shard_map/ppermute | solution.py:478
  29.1 4.2 %collective-permute-start.13 = (bf16[32,896]{1,0:T(8,128)(2,1)S(1)}, bf16[32,896]{1,0:T(8,128)(2,1)S(1)}, u32[]{:S(2)}, u32[]{:S(2)}) collective-permute-start(bf16[32,896]{1,0:T(8,128)(2,1)S(1)} %get-tuple-element.47), channel_id=1, source_target_pairs={{0,4},{1,5},{2,6},{3,7},{4,0},{5,1},{6,2},{7,3},{8,12},{9,13},{10,... | collective-permute-start | bytes 172040 | tf_op jit(solution)/shard_map/ppermute | solution.py:478
  30.3 4.2 %collective-permute-start.14 = (bf16[32,896]{1,0:T(8,128)(2,1)S(1)}, bf16[32,896]{1,0:T(8,128)(2,1)S(1)}, u32[]{:S(2)}, u32[]{:S(2)}) collective-permute-start(bf16[32,896]{1,0:T(8,128)(2,1)S(1)} %get-tuple-element.48), channel_id=1, source_target_pairs={{0,2},{1,3},{2,0},{3,1},{4,6},{5,7},{6,4},{7,5},{8,10},{9,11},{10,... | collective-permute-start | bytes 172040 | tf_op jit(solution)/shard_map/ppermute | solution.py:478
  31.0 3.5 %collective-permute-start.18 = (bf16[32,896]{1,0:T(8,128)(2,1)S(1)}, bf16[32,896]{1,0:T(8,128)(2,1)S(1)}, u32[]{:S(2)}, u32[]{:S(2)}) collective-permute-start(bf16[32,896]{1,0:T(8,128)(2,1)S(1)} %get-tuple-element.49.refs_3_), channel_id=1, source_target_pairs={{0,1},{1,0},{2,3},{3,2},{4,5},{5,4},{6,7},{7,6},{8,9},{9,8},{10,11... | collective-permute-start | bytes 172040 | tf_op jit(solution)/shard_map/ppermute | solution.py:482
  32.6 1.9 %collective-permute-start.15 = (bf16[32,896]{1,0:T(8,128)(2,1)S(1)}, bf16[32,896]{1,0:T(8,128)(2,1)S(1)}, u32[]{:S(2)}, u32[]{:S(2)}) collective-permute-start(bf16[32,896]{1,0:T(8,128)(2,1)S(1)} %collective-permute-done.12.refs_0_), channel_id=1, source_target_pairs={{0,1},{1,0},{2,3},{3,2},{4,5},{5,4},{6,7},{7,6},{8,9},{9,8},{10,11... | collective-permute-start | bytes 172040 | tf_op jit(solution)/shard_map/ppermute | solution.py:482
  33.2 1.2 %collective-permute-start.16 = (bf16[32,896]{1,0:T(8,128)(2,1)S(1)}, bf16[32,896]{1,0:T(8,128)(2,1)S(1)}, u32[]{:S(2)}, u32[]{:S(2)}) collective-permute-start(bf16[32,896]{1,0:T(8,128)(2,1)S(1)} %collective-permute-done.13.refs_1_), channel_id=1, source_target_pairs={{0,1},{1,0},{2,3},{3,2},{4,5},{5,4},{6,7},{7,6},{8,9},{9,8},{10,11... | collective-permute-start | bytes 172040 | tf_op jit(solution)/shard_map/ppermute | solution.py:482
  34.5 1.2 %collective-permute-start.17 = (bf16[32,896]{1,0:T(8,128)(2,1)S(1)}, bf16[32,896]{1,0:T(8,128)(2,1)S(1)}, u32[]{:S(2)}, u32[]{:S(2)}) collective-permute-start(bf16[32,896]{1,0:T(8,128)(2,1)S(1)} %collective-permute-done.14.refs_2_), channel_id=1, source_target_pairs={{0,1},{1,0},{2,3},{3,2},{4,5},{5,4},{6,7},{7,6},{8,9},{9,8},{10,11... | collective-permute-start | bytes 172040 | tf_op jit(solution)/shard_map/ppermute | solution.py:482
  39.4 5.2 %collective-permute-start.19 = (bf16[32,896]{1,0:T(8,128)(2,1)S(1)}, bf16[32,896]{1,0:T(8,128)(2,1)S(1)}, u32[]{:S(2)}, u32[]{:S(2)}) collective-permute-start(bf16[32,896]{1,0:T(8,128)(2,1)S(1)} %get-tuple-element.51), channel_id=1, source_target_pairs={{0,6},{1,7},{2,4},{3,5},{4,2},{5,3},{6,0},{7,1},{8,14},{9,15},{10,... | collective-permute-start | bytes 172040 | tf_op jit(solution)/shard_map/ppermute | solution.py:478
  41.1 4.5 %collective-permute-start.20 = (bf16[32,896]{1,0:T(8,128)(2,1)S(1)}, bf16[32,896]{1,0:T(8,128)(2,1)S(1)}, u32[]{:S(2)}, u32[]{:S(2)}) collective-permute-start(bf16[32,896]{1,0:T(8,128)(2,1)S(1)} %get-tuple-element.52), channel_id=1, source_target_pairs={{0,4},{1,5},{2,6},{3,7},{4,0},{5,1},{6,2},{7,3},{8,12},{9,13},{10,... | collective-permute-start | bytes 172040 | tf_op jit(solution)/shard_map/ppermute | solution.py:478
  41.6 4.2 %collective-permute-start.21 = (bf16[32,896]{1,0:T(8,128)(2,1)S(1)}, bf16[32,896]{1,0:T(8,128)(2,1)S(1)}, u32[]{:S(2)}, u32[]{:S(2)}) collective-permute-start(bf16[32,896]{1,0:T(8,128)(2,1)S(1)} %get-tuple-element.53), channel_id=1, source_target_pairs={{0,2},{1,3},{2,0},{3,1},{4,6},{5,7},{6,4},{7,5},{8,10},{9,11},{10,... | collective-permute-start | bytes 172040 | tf_op jit(solution)/shard_map/ppermute | solution.py:478
  42.9 3.1 %collective-permute-start.25 = (bf16[32,896]{1,0:T(8,128)(2,1)S(1)}, bf16[32,896]{1,0:T(8,128)(2,1)S(1)}, u32[]{:S(2)}, u32[]{:S(2)}) collective-permute-start(bf16[32,896]{1,0:T(8,128)(2,1)S(1)} %get-tuple-element.54.refs_3_), channel_id=1, source_target_pairs={{0,1},{1,0},{2,3},{3,2},{4,5},{5,4},{6,7},{7,6},{8,9},{9,8},{10,11... | collective-permute-start | bytes 172040 | tf_op jit(solution)/shard_map/ppermute | solution.py:482
  44.6 1.5 %collective-permute-start.22 = (bf16[32,896]{1,0:T(8,128)(2,1)S(1)}, bf16[32,896]{1,0:T(8,128)(2,1)S(1)}, u32[]{:S(2)}, u32[]{:S(2)}) collective-permute-start(bf16[32,896]{1,0:T(8,128)(2,1)S(1)} %collective-permute-done.19.refs_0_), channel_id=1, source_target_pairs={{0,1},{1,0},{2,3},{3,2},{4,5},{5,4},{6,7},{7,6},{8,9},{9,8},{10,11... | collective-permute-start | bytes 172040 | tf_op jit(solution)/shard_map/ppermute | solution.py:482
  45.5 1.2 %collective-permute-start.23 = (bf16[32,896]{1,0:T(8,128)(2,1)S(1)}, bf16[32,896]{1,0:T(8,128)(2,1)S(1)}, u32[]{:S(2)}, u32[]{:S(2)}) collective-permute-start(bf16[32,896]{1,0:T(8,128)(2,1)S(1)} %collective-permute-done.20.refs_1_), channel_id=1, source_target_pairs={{0,1},{1,0},{2,3},{3,2},{4,5},{5,4},{6,7},{7,6},{8,9},{9,8},{10,11... | collective-permute-start | bytes 172040 | tf_op jit(solution)/shard_map/ppermute | solution.py:482
  45.8 1.2 %collective-permute-start.24 = (bf16[32,896]{1,0:T(8,128)(2,1)S(1)}, bf16[32,896]{1,0:T(8,128)(2,1)S(1)}, u32[]{:S(2)}, u32[]{:S(2)}) collective-permute-start(bf16[32,896]{1,0:T(8,128)(2,1)S(1)} %collective-permute-done.21.refs_2_), channel_id=1, source_target_pairs={{0,1},{1,0},{2,3},{3,2},{4,5},{5,4},{6,7},{7,6},{8,9},{9,8},{10,11... | collective-permute-start | bytes 172040 | tf_op jit(solution)/shard_map/ppermute | solution.py:482

commit v5 on v4

--- a/solution.py
+++ b/solution.py
@@ -183,7 +183,7 @@
     chips = span // (2 * SUBLANES)
     array = (chosen // 2) ^ chip ^ (chips - 1)
     array = array + jnp.where(chosen % 2 == core, 0, chips)
-    sender = (lax.axis_index("pipe") + 1 + group) % 2
+    sender = (lax.axis_index("pipe") + group) % 2
     within = piece * (2 * slot_cap) + sender * slot_cap + rank
     return one_hot(2 * span, (array * 2 + core) * SUBLANES + within)
 
@@ -270,6 +270,7 @@
     w_up,
     w_down,
     out_refs,
+    aside_ref,
     up_v,
     down_v,
     up_i,
@@ -283,8 +284,7 @@
     copies = started(sources, (up_i, down_i, up_v, down_v, enter_up_v, enter_down_v), sems)
     copies[0].wait()
     copies[1].wait()
-    blocks = [ref.at[: 2 * SUBLANES] for ref in out_refs]
-    span = 2 * SUBLANES * len(blocks)
+    span = sum(ref.shape[0] for ref in out_refs)
     rows, features = up_v.shape
     width = features // parts
     sending = sending_map(up_i[0, 0], down_i[0, 0], parts, slot_cap, span)
@@ -294,20 +294,19 @@
     down_line = jnp.sum(square * upright(down_i[last, 0]), axis=0, keepdims=True)
     row = iota((rows, LANES), 0)
     lines = jnp.where(row == 0, up_line, jnp.where(row == 1, down_line, 0))
-    aside = out_refs[-1].at[2 * SUBLANES :]
-    aside[parts * rows :, :LANES] = lines.astype(jnp.float32).astype(jnp.bfloat16)
+    aside_ref[parts * rows :, :LANES] = lines.astype(jnp.float32).astype(jnp.bfloat16)
     numbers = (iota((span, LANES), 0) % rows).astype(jnp.float32).astype(jnp.bfloat16)
-    put(moved(sending, numbers), [ref.at[:, width:] for ref in blocks])
+    put(moved(sending, numbers), [ref.at[:, width:] for ref in out_refs])
     copies[2].wait()
     copies[3].wait()
     packed = pack_rows(sending, up_v[...], down_v[...], parts)
-    put(packed, [ref.at[:, :width] for ref in blocks])
+    put(packed, [ref.at[:, :width] for ref in out_refs])
     copies[4].wait()
     copies[5].wait()
     for q in range(parts):
         cols = slice(q * width, (q + 1) * width)
         entering = jnp.where(lax.axis_index("pipe") == 0, enter_up_v[:, cols], enter_down_v[:, cols])
-        aside[q * rows : (q + 1) * rows, :width] = entering
+        aside_ref[q * rows : (q + 1) * rows, :width] = entering
 
 
 def plan_kernel(
@@ -353,15 +352,16 @@
         ref[SUBLANES:] = passed_ref[j * SUBLANES : (j + 1) * SUBLANES]
 
 
-def turn_plan_kernel(parts, slot_cap, own_ref, other_ref, sending_ref, entering_ref):
+def turn_plan_kernel(parts, slot_cap, after_ref, own_ref, other_ref, sending_ref, entering_ref):
+    del after_ref
     section = lax.axis_index("pipe")
     _, core = chip_and_core()
     span, width = entering_ref.shape
     rows = span // (2 * parts)
-    own, other = own_ref[2 * SUBLANES :], other_ref[2 * SUBLANES :]
+    own, other = own_ref[...], other_ref[...]
     first = jnp.where(core == 0, own, other)
     second = jnp.where(core == 0, other, own)
-    picked = iota((rows, LANES), 0) == (section + core + 1) % 2
+    picked = iota((rows, LANES), 0) == (section + core) % 2
 
     def ids(aside):
         lines = jnp.where(picked, aside[parts * rows :, :LANES].astype(jnp.float32), 0.0)
@@ -389,7 +389,7 @@
     sorting = jnp.where(iota((span, span), 1) == place + numbers, 1.0, 0.0).astype(jnp.bfloat16)
     across = (((1,), (1,)), ((), ()))
     sending = lax.dot_general(sending_ref[...], sorting, across, preferred_element_type=jnp.float32)
-    partner = ((section + core) ^ 1) - core
+    partner = ((section + 1 - core) ^ 1) - (1 - core)
     enters = (partner < 0) | (partner >= pipe)
     put(jnp.where(enters, entering_ref[...], moved(sending, received[:, :width])), out_refs)
 
@@ -416,7 +416,7 @@
 def expert_rows(parts, in_refs, arriving_ref, gain_ref, router_ref, gate_ref, up_ref, down_ref, x_ref):
     rows = x_ref.shape[0]
     width = x_ref.shape[1] // parts
-    spread = moved(arriving_ref[...], stacked([ref.at[: 2 * SUBLANES] for ref in in_refs]))
+    spread = moved(arriving_ref[...], stacked(in_refs))
     for q in range(parts):
         x_ref[:, q * width : (q + 1) * width] = spread[q * rows : (q + 1) * rows, :width]
     widened = x_ref[...].astype(jnp.float32)
@@ -474,13 +474,13 @@
 def exchanged(arrays):
     last = len(arrays) - 1
     devices = range(2 * len(arrays))
+    sibling = [(i, i ^ 1) for i in devices]
     arrived = [
-        lax.ppermute(arrays[j], "expert", [(i, i ^ (2 * (last - j))) for i in devices])
+        lax.ppermute(arrays[j], "expert", [(i, i ^ (2 * (last - j)) ^ 1) for i in devices])
         for j in range(last)
     ]
-    arrived.append(arrays[last])
-    passed = [lax.ppermute(x, "expert", [(i, i ^ 1) for i in devices]) for x in arrived]
-    return tuple(arrived + passed)
+    passed = [lax.ppermute(x, "expert", sibling) for x in arrived + [arrays[last]]]
+    return tuple(passed[:last] + [arrays[last]] + arrived + passed[last:])
 
 
 def relay_pairs(k, pipe, experts):
@@ -488,8 +488,8 @@
     for section in range(pipe):
         for i in range(experts):
             other = ((section + i % 2) ^ 1) - i % 2
-            target = (other, i ^ (2 * k)) if 0 <= other < pipe else (section, i ^ (2 * (k or 1)))
-            pairs.append((section * experts + i, target[0] * experts + target[1]))
+            other = other if 0 <= other < pipe else section
+            pairs.append((section * experts + i, other * experts + (i ^ (2 * k) ^ 1)))
     return pairs
 
 
@@ -526,10 +526,10 @@
     wide_map_v = pltpu.VMEM((span, 2 * span), jnp.bfloat16)
     sibling = [(i, i ^ 1) for i in range(experts)]
     ids = (up_route.transpose(0, 1, 3, 2), down_route.transpose(0, 1, 3, 2))
-    kept_back = pltpu.VMEM((2 * SUBLANES + (parts + 1) * rows, width + LANES), jnp.bfloat16)
-    (sent,) = local_call(
+    aside_v = pltpu.VMEM(((parts + 1) * rows, width), jnp.bfloat16)
+    sent, aside = local_call(
         functools.partial(send_kernel, parts, slot_cap),
-        (numbered[1:] + (kept_back,),),
+        (numbered, aside_v),
         (),
         (up_state, down_state, *ids, entering_up, entering_down, w_gate, w_up, w_down),
         [batch, batch, all_ids_v, all_ids_v, batch, batch, pltpu.SemaphoreType.DMA((6,))],
@@ -543,11 +543,6 @@
     )
     layer = (arriving, gain, column, w_gate[0], w_up[0], w_down[0])
     received = exchanged(sent)
-    sending, entering = local_call(
-        functools.partial(turn_plan_kernel, parts, slot_cap),
-        (map_v, pltpu.VMEM((span, width), jnp.bfloat16)),
-        (sent[-1], received[-1]),
-    )
     kept, passed = local_call(
         functools.partial(first_kernel, parts),
         (half, half),
@@ -555,12 +550,18 @@
         (),
         [x_v],
     )
+    sending, entering = local_call(
+        functools.partial(turn_plan_kernel, parts, slot_cap),
+        (map_v, pltpu.VMEM((span, width), jnp.bfloat16)),
+        (kept, aside, lax.ppermute(aside, "expert", sibling)),
+    )
     passed = lax.ppermute(passed, "expert", sibling)
     (merged,) = local_call(merge_kernel, (numbered,), (kept, passed))
     relayed = tuple(
         lax.ppermute(x, ("pipe", "expert"), relay_pairs(chips - 1 - j, pipe, experts))
         for j, x in enumerate(merged)
     )
+    relayed = relayed[chips // 2 :] + relayed[: chips // 2]
     (sent,) = local_call(
         functools.partial(turn_kernel, parts, slot_cap, pipe), (blocks,), (relayed, sending, entering)
     )

time: 48.1 us -> 46.7 us (0.971)
  waiting for transfers between devices: 17.4 us -> 13.6 us
  starting transfers between devices: 18.4 us -> 20.8 us
    ppermute x21 -> x22, waiting for transfers between devices: 12.8 us -> 10.6 us  [the longest x9 8.72 us: exchanged(): lax.ppermute(arrays[j], 'expert', [(i, i ^ 2 * (last - j) ^ 1) for i in d...]
    ppermute x21 -> x22, starting transfers between devices: 12.1 us -> 13.8 us  [the longest x9 10.5 us: exchanged(): lax.ppermute(arrays[j], 'expert', [(i, i ^ 2 * (last - j) ^ 1) for i in d...]
    ppermute x4, waiting for transfers between devices: 3.48 us -> 2.18 us  [single_shards(): lax.ppermute(x, ('pipe', 'expert'), relay_pairs(chips - 1 - j, pipe, expe...]
    ppermute x4, starting transfers between devices: 5.91 us -> 6.58 us  [single_shards(): lax.ppermute(x, ('pipe', 'expert'), relay_pairs(chips - 1 - j, pipe, expe...]
  transfers between devices with their start and end apart: 26 -> 27, of which waited for: 17 -> 15; matrix products, arithmetic and copies ran while one was open for 0% -> 0% of each run, Pallas kernels for 3% -> 3%
where the time goes in v5:
time: 46.7 us; the launch traced here: 46.6 us
  starting transfers between devices  20.8 us (45%)
  waiting for transfers between devices  13.6 us (29%)
  Pallas kernels  11.4 us (24%)
  between operations  0.76 us (2%)
    pallas_call x8, Pallas kernels, local_call(): pl.pallas_call(body, out_shape=outs, in_specs=[VMEM_SPEC] * len(close) +...  11.4 us
    ppermute x9, starting transfers between devices, exchanged(): lax.ppermute(arrays[j], 'expert', [(i, i ^ 2 * (last - j) ^ 1) for i in d...  10.5 us
    ppermute x9, waiting for transfers between devices, exchanged(): lax.ppermute(arrays[j], 'expert', [(i, i ^ 2 * (last - j) ^ 1) for i in d...  8.72 us
    ppermute x4, starting transfers between devices, single_shards(): lax.ppermute(x, ('pipe', 'expert'), relay_pairs(chips - 1 - j, pipe, expe...  6.58 us
    ppermute x12, starting transfers between devices, exchanged(): lax.ppermute(x, 'expert', sibling)  3.11 us
    ppermute x4, waiting for transfers between devices, single_shards(): lax.ppermute(x, ('pipe', 'expert'), relay_pairs(chips - 1 - j, pipe, expe...  2.18 us
    ppermute x12, waiting for transfers between devices, exchanged(): lax.ppermute(x, 'expert', sibling)  1.89 us
  transfers between devices with their start and end apart: 27, of which 15 were waited for; matrix products, arithmetic and copies ran while one was open for 0% of the time, Pallas kernels for 3%

profile of v5, /device:TPU:0, one launch (start us, length us, event | category | flops | bytes accessed | tf_op | source)
XLA Modules:
  0.0 46.6 jit_solution(11350758526803890197)
XLA Ops:
  0.6 0.0 copy-start
  0.6 0.0 copy-start.1
  0.7 1.4 %shard_map.122 = (bf16[32,1024]{1,0:T(8,128)(2,1)S(1)}, bf16[32,1024]{1,0:T(8,128)(2,1)S(1)}, bf16[32,1024]{1,0:T(8,128)(2,1)S(1)}, bf16[32,1024]{1,0:T(8,128)(2,1)S(1)}, bf16[80,896]{1,0:T(8,128)(2,1)S(1)}) custom-call(bf16[1,16,3584]{2,1,0:T(8,128)(2,1)} %refs_0_.1, bf16[1,16,3584]{2,1,0:T(8,128)(2,1)} %refs_1_.1, s32[2,1,1,16]{3,2,1,0:T(1,128)} %bitcast.19, ...), custom_call_target="tpu_custom_call" | custom-call | tf_op jit(solution)/shard_map/pallas_call | solution.py:463
  2.1 3.4 %collective-permute-start = (bf16[32,1024]{1,0:T(8,128)(2,1)S(1)}, bf16[32,1024]{1,0:T(8,128)(2,1)S(1)}, u32[]{:S(2)}, u32[]{:S(2)}) collective-permute-start(bf16[32,1024]{1,0:T(8,128)(2,1)S(1)} %get-tuple-element.31), channel_id=1, source_target_pairs={{0,7},{1,6},{2,5},{3,4},{4,3},{5,2},{6,1},{7,0},{8,15},{9,14},{10,... | collective-permute-start | bytes 196616 | tf_op jit(solution)/shard_map/ppermute | solution.py:479
  5.5 0.8 %collective-permute-start.2 = (bf16[32,1024]{1,0:T(8,128)(2,1)S(1)}, bf16[32,1024]{1,0:T(8,128)(2,1)S(1)}, u32[]{:S(2)}, u32[]{:S(2)}) collective-permute-start(bf16[32,1024]{1,0:T(8,128)(2,1)S(1)} %get-tuple-element.32), channel_id=1, source_target_pairs={{0,5},{1,4},{2,7},{3,6},{4,1},{5,0},{6,3},{7,2},{8,13},{9,12},{10,... | collective-permute-start | bytes 196616 | tf_op jit(solution)/shard_map/ppermute | solution.py:479
  6.3 0.1 collective-permute-start.4
  6.4 0.0 collective-permute-start.6
  6.4 1.6 %collective-permute-done.refs_4_ = bf16[32,1024]{1,0:T(8,128)(2,1)S(1)} collective-permute-done((bf16[32,1024]{1,0:T(8,128)(2,1)S(1)}, bf16[32,1024]{1,0:T(8,128)(2,1)S(1)}, u32[]{:S(2)}, u32[]{:S(2)}) %collective-permute-start) | collective-permute-done | bytes 65568 | tf_op jit(solution)/shard_map/ppermute | solution.py:479
  8.0 0.1 collective-permute-start.1
  8.1 1.2 %collective-permute-done.2.refs_5_ = bf16[32,1024]{1,0:T(8,128)(2,1)S(1)} collective-permute-done((bf16[32,1024]{1,0:T(8,128)(2,1)S(1)}, bf16[32,1024]{1,0:T(8,128)(2,1)S(1)}, u32[]{:S(2)}, u32[]{:S(2)}) %collective-permute-start.2) | collective-permute-done | bytes 65568 | tf_op jit(solution)/shard_map/ppermute | solution.py:479
  9.4 0.8 %collective-permute-start.3 = (bf16[32,1024]{1,0:T(8,128)(2,1)S(1)}, bf16[32,1024]{1,0:T(8,128)(2,1)S(1)}, u32[]{:S(2)}, u32[]{:S(2)}) collective-permute-start(bf16[32,1024]{1,0:T(8,128)(2,1)S(1)} %collective-permute-done.2.refs_5_), channel_id=1, source_target_pairs={{0,1},{1,0},{2,3},{3,2},{4,5},{5,4},{6,7},{7,6},{8,9},{9,8},{10,11... | collective-permute-start | bytes 196616 | tf_op jit(solution)/shard_map/ppermute | solution.py:482
  10.2 0.4 collective-permute-done.4.refs_6_
  10.6 0.1 collective-permute-start.5
  10.7 1.0 %shard_map.123 = (bf16[128,256]{1,0:T(8,128)(2,1)S(1)}, bf16[128,256]{1,0:T(8,128)(2,1)S(1)}, bf16[128,128]{1,0:T(8,128)(2,1)S(1)}, bf16[128,128]{1,0:T(8,128)(2...) custom-call(bf16[32,1024]{1,0:T(8,128)(2,1)S(1)} %get-tuple-element.34.refs_0_.refs_3_, s32[2,1,1,16]{3,2,1,0:T(1,128)} %bitcast.20, ...), custom_call_target="tpu_custom_call" | custom-call | tf_op jit(solution)/shard_map/pallas_call | solution.py:463
  11.7 0.0 collective-permute-done.6.refs_7_
  11.7 0.0 collective-permute-done.1.refs_0_
  11.7 0.0 collective-permute-done.3.refs_1_
  11.8 0.1 collective-permute-done.5.refs_2_
  11.9 0.0 copy-done.2
  11.9 3.7 %shard_map.124 = (bf16[64,1024]{1,0:T(8,128)(2,1)S(1)}, bf16[64,1024]{1,0:T(8,128)(2,1)S(1)}) custom-call(bf16[32,1024]{1,0:T(8,128)(2,1)S(1)} %collective-permute-done.1.refs_0_, bf16[32,1024]{1,0:T(8,128)(2,1)S(1)} %collective-permute-done.3.refs_1_, bf16[32,1024]{1,0:T(8,128)(2,1)S(1)} %collective-permute-done.5.refs_2_, ...), custom_call_target="tpu_custom_call" | custom-call | tf_op jit(solution)/shard_map/pallas_call | solution.py:463
  15.5 0.4 collective-permute-start.7
  15.9 0.2 collective-permute-start.12
  16.1 0.8 %collective-permute-done.7.refs_1_ = bf16[64,1024]{1,0:T(8,128)(2,1)S(1)} collective-permute-done((bf16[64,1024]{1,0:T(8,128)(2,1)S(1)}, bf16[64,1024]{1,0:T(8,128)(2,1)S(1)}, u32[]{:S(2)}, u32[]{:S(2)}) %collective-permute-start.7) | collective-permute-done | bytes 131104 | tf_op jit(solution)/shard_map/ppermute | solution.py:558
  17.0 2.5 %collective-permute-start.10 = (bf16[32,1024]{1,0:T(8,128)(2,1)S(1)}, bf16[32,1024]{1,0:T(8,128)(2,1)S(1)}, u32[]{:S(2)}, u32[]{:S(2)}) collective-permute-start(bf16[32,1024]{1,0:T(8,128)(2,1)S(1)} %get-tuple-element.43), channel_id=1, source_target_pairs={{0,15},{1,6},{2,13},{3,4},{4,11},{5,2},{6,9},{7,0},{8,7},{9,22},{1... | collective-permute-start | bytes 196616 | tf_op jit(solution)/shard_map/ppermute | solution.py:561
  19.5 2.2 %collective-permute-start.11 = (bf16[32,1024]{1,0:T(8,128)(2,1)S(1)}, bf16[32,1024]{1,0:T(8,128)(2,1)S(1)}, u32[]{:S(2)}, u32[]{:S(2)}) collective-permute-start(bf16[32,1024]{1,0:T(8,128)(2,1)S(1)} %get-tuple-element.44), channel_id=1, source_target_pairs={{0,13},{1,4},{2,15},{3,6},{4,9},{5,0},{6,11},{7,2},{8,5},{9,20},{1... | collective-permute-start | bytes 196616 | tf_op jit(solution)/shard_map/ppermute | solution.py:561
  21.7 1.5 %collective-permute-start.8 = (bf16[32,1024]{1,0:T(8,128)(2,1)S(1)}, bf16[32,1024]{1,0:T(8,128)(2,1)S(1)}, u32[]{:S(2)}, u32[]{:S(2)}) collective-permute-start(bf16[32,1024]{1,0:T(8,128)(2,1)S(1)} %get-tuple-element.41), channel_id=1, source_target_pairs={{0,11},{1,2},{2,9},{3,0},{4,15},{5,6},{6,13},{7,4},{8,3},{9,18},{1... | collective-permute-start | bytes 196616 | tf_op jit(solution)/shard_map/ppermute | solution.py:561
  23.2 0.4 collective-permute-start.9
  23.6 0.0 collective-permute-done.12.refs_2_
  23.6 0.3 shard_map.126
  23.9 0.0 collective-permute-done.10.refs_2_
  23.9 0.5 %collective-permute-done.11.refs_3_ = bf16[32,1024]{1,0:T(8,128)(2,1)S(1)} collective-permute-done((bf16[32,1024]{1,0:T(8,128)(2,1)S(1)}, bf16[32,1024]{1,0:T(8,128)(2,1)S(1)}, u32[]{:S(2)}, u32[]{:S(2)}) %collective-permute-start.11) | collective-permute-done | bytes 65568 | tf_op jit(solution)/shard_map/ppermute | solution.py:561
  24.4 1.6 %collective-permute-done.8.refs_0_ = bf16[32,1024]{1,0:T(8,128)(2,1)S(1)} collective-permute-done((bf16[32,1024]{1,0:T(8,128)(2,1)S(1)}, bf16[32,1024]{1,0:T(8,128)(2,1)S(1)}, u32[]{:S(2)}, u32[]{:S(2)}) %collective-permute-start.8) | collective-permute-done | bytes 65568 | tf_op jit(solution)/shard_map/ppermute | solution.py:561
  26.1 0.0 collective-permute-done.9.refs_1_
  26.1 0.4 shard_map.127
  26.5 1.4 %collective-permute-start.13 = (bf16[32,896]{1,0:T(8,128)(2,1)S(1)}, bf16[32,896]{1,0:T(8,128)(2,1)S(1)}, u32[]{:S(2)}, u32[]{:S(2)}) collective-permute-start(bf16[32,896]{1,0:T(8,128)(2,1)S(1)} %get-tuple-element.48), channel_id=1, source_target_pairs={{0,7},{1,6},{2,5},{3,4},{4,3},{5,2},{6,1},{7,0},{8,15},{9,14},{10,... | collective-permute-start | bytes 172040 | tf_op jit(solution)/shard_map/ppermute | solution.py:479
  27.8 0.8 %collective-permute-start.15 = (bf16[32,896]{1,0:T(8,128)(2,1)S(1)}, bf16[32,896]{1,0:T(8,128)(2,1)S(1)}, u32[]{:S(2)}, u32[]{:S(2)}) collective-permute-start(bf16[32,896]{1,0:T(8,128)(2,1)S(1)} %get-tuple-element.49), channel_id=1, source_target_pairs={{0,5},{1,4},{2,7},{3,6},{4,1},{5,0},{6,3},{7,2},{8,13},{9,12},{10,... | collective-permute-start | bytes 172040 | tf_op jit(solution)/shard_map/ppermute | solution.py:479
  28.7 0.8 %collective-permute-start.17 = (bf16[32,896]{1,0:T(8,128)(2,1)S(1)}, bf16[32,896]{1,0:T(8,128)(2,1)S(1)}, u32[]{:S(2)}, u32[]{:S(2)}) collective-permute-start(bf16[32,896]{1,0:T(8,128)(2,1)S(1)} %get-tuple-element.50), channel_id=1, source_target_pairs={{0,3},{1,2},{2,1},{3,0},{4,7},{5,6},{6,5},{7,4},{8,11},{9,10},{10,... | collective-permute-start | bytes 172040 | tf_op jit(solution)/shard_map/ppermute | solution.py:479
  29.5 0.4 collective-permute-start.19
  29.9 1.5 %collective-permute-done.13.refs_4_ = bf16[32,896]{1,0:T(8,128)(2,1)S(1)} collective-permute-done((bf16[32,896]{1,0:T(8,128)(2,1)S(1)}, bf16[32,896]{1,0:T(8,128)(2,1)S(1)}, u32[]{:S(2)}, u32[]{:S(2)}) %collective-permute-start.13) | collective-permute-done | bytes 57376 | tf_op jit(solution)/shard_map/ppermute | solution.py:479
  31.4 0.1 collective-permute-start.14
  31.6 1.3 %collective-permute-done.15.refs_5_ = bf16[32,896]{1,0:T(8,128)(2,1)S(1)} collective-permute-done((bf16[32,896]{1,0:T(8,128)(2,1)S(1)}, bf16[32,896]{1,0:T(8,128)(2,1)S(1)}, u32[]{:S(2)}, u32[]{:S(2)}) %collective-permute-start.15) | collective-permute-done | bytes 57376 | tf_op jit(solution)/shard_map/ppermute | solution.py:479
  32.8 0.1 collective-permute-start.16
  32.9 0.0 collective-permute-done.17.refs_6_
  32.9 0.4 collective-permute-start.18
  33.3 0.0 collective-permute-done.19.refs_7_
  33.3 0.0 collective-permute-done.14.refs_0_
  33.3 0.7 %collective-permute-done.16.refs_1_ = bf16[32,896]{1,0:T(8,128)(2,1)S(1)} collective-permute-done((bf16[32,896]{1,0:T(8,128)(2,1)S(1)}, bf16[32,896]{1,0:T(8,128)(2,1)S(1)}, u32[]{:S(2)}, u32[]{:S(2)}) %collective-permute-start.16) | collective-permute-done | bytes 57376 | tf_op jit(solution)/shard_map/ppermute | solution.py:482
  34.1 0.2 collective-permute-done.18.refs_2_
  34.2 3.6 %shard_map.128 = (bf16[32,896]{1,0:T(8,128)(2,1)S(1)}, bf16[32,896]{1,0:T(8,128)(2,1)S(1)}, bf16[32,896]{1,0:T(8,128)(2,1)S(1)}, bf16[32,896]{1,0:T(8,128)(2,1)S(1)}) custom-call(bf16[32,896]{1,0:T(8,128)(2,1)S(1)} %collective-permute-done.14.refs_0_, bf16[32,896]{1,0:T(8,128)(2,1)S(1)} %collective-permute-done.16.refs_1_, ...), custom_call_target="tpu_custom_call" | custom-call | tf_op jit(solution)/shard_map/pallas_call | solution.py:463
  37.9 1.6 %collective-permute-start.20 = (bf16[32,896]{1,0:T(8,128)(2,1)S(1)}, bf16[32,896]{1,0:T(8,128)(2,1)S(1)}, u32[]{:S(2)}, u32[]{:S(2)}) collective-permute-start(bf16[32,896]{1,0:T(8,128)(2,1)S(1)} %get-tuple-element.53), channel_id=1, source_target_pairs={{0,7},{1,6},{2,5},{3,4},{4,3},{5,2},{6,1},{7,0},{8,15},{9,14},{10,... | collective-permute-start | bytes 172040 | tf_op jit(solution)/shard_map/ppermute | solution.py:479
  39.5 0.7 %collective-permute-start.22 = (bf16[32,896]{1,0:T(8,128)(2,1)S(1)}, bf16[32,896]{1,0:T(8,128)(2,1)S(1)}, u32[]{:S(2)}, u32[]{:S(2)}) collective-permute-start(bf16[32,896]{1,0:T(8,128)(2,1)S(1)} %get-tuple-element.54), channel_id=1, source_target_pairs={{0,5},{1,4},{2,7},{3,6},{4,1},{5,0},{6,3},{7,2},{8,13},{9,12},{10,... | collective-permute-start | bytes 172040 | tf_op jit(solution)/shard_map/ppermute | solution.py:479
  40.2 1.0 %collective-permute-start.24 = (bf16[32,896]{1,0:T(8,128)(2,1)S(1)}, bf16[32,896]{1,0:T(8,128)(2,1)S(1)}, u32[]{:S(2)}, u32[]{:S(2)}) collective-permute-start(bf16[32,896]{1,0:T(8,128)(2,1)S(1)} %get-tuple-element.55), channel_id=1, source_target_pairs={{0,3},{1,2},{2,1},{3,0},{4,7},{5,6},{6,5},{7,4},{8,11},{9,10},{10,... | collective-permute-start | bytes 172040 | tf_op jit(solution)/shard_map/ppermute | solution.py:479
  41.1 0.2 collective-permute-start.26
  41.3 1.3 %collective-permute-done.20.refs_4_ = bf16[32,896]{1,0:T(8,128)(2,1)S(1)} collective-permute-done((bf16[32,896]{1,0:T(8,128)(2,1)S(1)}, bf16[32,896]{1,0:T(8,128)(2,1)S(1)}, u32[]{:S(2)}, u32[]{:S(2)}) %collective-permute-start.20) | collective-permute-done | bytes 57376 | tf_op jit(solution)/shard_map/ppermute | solution.py:479
  42.6 0.3 collective-permute-start.21
  42.9 1.3 %collective-permute-done.22.refs_5_ = bf16[32,896]{1,0:T(8,128)(2,1)S(1)} collective-permute-done((bf16[32,896]{1,0:T(8,128)(2,1)S(1)}, bf16[32,896]{1,0:T(8,128)(2,1)S(1)}, u32[]{:S(2)}, u32[]{:S(2)}) %collective-permute-start.22) | collective-permute-done | bytes 57376 | tf_op jit(solution)/shard_map/ppermute | solution.py:479
  44.3 0.1 collective-permute-start.23
  44.4 0.0 collective-permute-done.24.refs_6_
  44.4 0.4 collective-permute-start.25
  44.8 0.0 collective-permute-done.26.refs_7_
  44.8 0.0 collective-permute-done.21.refs_0_
  44.8 0.7 %collective-permute-done.23.refs_1_ = bf16[32,896]{1,0:T(8,128)(2,1)S(1)} collective-permute-done((bf16[32,896]{1,0:T(8,128)(2,1)S(1)}, bf16[32,896]{1,0:T(8,128)(2,1)S(1)}, u32[]{:S(2)}, u32[]{:S(2)}) %collective-permute-start.23) | collective-permute-done | bytes 57376 | tf_op jit(solution)/shard_map/ppermute | solution.py:482
  45.5 0.2 collective-permute-done.25.refs_2_
  45.7 0.9 %shard_map.129 = (bf16[16,3584]{1,0:T(8,128)(2,1)}, bf16[16,3584]{1,0:T(8,128)(2,1)}) custom-call(bf16[32,896]{1,0:T(8,128)(2,1)S(1)} %collective-permute-done.21.refs_0_, bf16[32,896]{1,0:T(8,128)(2,1)S(1)} %collective-permute-done.23.refs_1_, bf16[32,896]{1,0:T(8,128)(2,1)S(1)} %collective-permute-done.25.refs_2_, ...), custom_call_target="tpu_custom_call" | custom-call | tf_op jit(solution)/shard_map/pallas_call | solution.py:463
  (4 shorter events, 0.0 us)
Async XLA Ops:
  0.6 11.2 %copy-start = (bf16[1,3584,1024]{2,1,0:T(8,128)(2,1)S(1)}, bf16[1,3584,1024]{2,1,0:T(8,128)(2,1)}, u32[]{:S(2)}) copy-start(bf16[1,3584,1024]{2,1,0:T(8,128)(2,1)} %refs_6_.1) | copy-start | bytes 22020100
  0.6 11.2 %copy-start.1 = (bf16[1,3584,1024]{2,1,0:T(8,128)(2,1)S(1)}, bf16[1,3584,1024]{2,1,0:T(8,128)(2,1)}, u32[]{:S(2)}) copy-start(bf16[1,3584,1024]{2,1,0:T(8,128)(2,1)} %refs_7_.1) | copy-start | bytes 22020100
  0.7 11.2 %copy-start.2 = (bf16[1,1024,3584]{2,1,0:T(8,128)(2,1)S(1)}, bf16[1,1024,3584]{2,1,0:T(8,128)(2,1)}, u32[]{:S(2)}) copy-start(bf16[1,1024,3584]{2,1,0:T(8,128)(2,1)} %refs_8_.1) | copy-start | bytes 22020100
  2.1 5.9 %collective-permute-start = (bf16[32,1024]{1,0:T(8,128)(2,1)S(1)}, bf16[32,1024]{1,0:T(8,128)(2,1)S(1)}, u32[]{:S(2)}, u32[]{:S(2)}) collective-permute-start(bf16[32,1024]{1,0:T(8,128)(2,1)S(1)} %get-tuple-element.31), channel_id=1, source_target_pairs={{0,7},{1,6},{2,5},{3,4},{4,3},{5,2},{6,1},{7,0},{8,15},{9,14},{10,... | collective-permute-start | bytes 196616 | tf_op jit(solution)/shard_map/ppermute | solution.py:479
  5.5 3.9 %collective-permute-start.2 = (bf16[32,1024]{1,0:T(8,128)(2,1)S(1)}, bf16[32,1024]{1,0:T(8,128)(2,1)S(1)}, u32[]{:S(2)}, u32[]{:S(2)}) collective-permute-start(bf16[32,1024]{1,0:T(8,128)(2,1)S(1)} %get-tuple-element.32), channel_id=1, source_target_pairs={{0,5},{1,4},{2,7},{3,6},{4,1},{5,0},{6,3},{7,2},{8,13},{9,12},{10,... | collective-permute-start | bytes 196616 | tf_op jit(solution)/shard_map/ppermute | solution.py:479
  6.3 4.3 %collective-permute-start.4 = (bf16[32,1024]{1,0:T(8,128)(2,1)S(1)}, bf16[32,1024]{1,0:T(8,128)(2,1)S(1)}, u32[]{:S(2)}, u32[]{:S(2)}) collective-permute-start(bf16[32,1024]{1,0:T(8,128)(2,1)S(1)} %get-tuple-element.33), channel_id=1, source_target_pairs={{0,3},{1,2},{2,1},{3,0},{4,7},{5,6},{6,5},{7,4},{8,11},{9,10},{10,... | collective-permute-start | bytes 196616 | tf_op jit(solution)/shard_map/ppermute | solution.py:479
  6.4 5.3 %collective-permute-start.6 = (bf16[32,1024]{1,0:T(8,128)(2,1)S(1)}, bf16[32,1024]{1,0:T(8,128)(2,1)S(1)}, u32[]{:S(2)}, u32[]{:S(2)}) collective-permute-start(bf16[32,1024]{1,0:T(8,128)(2,1)S(1)} %get-tuple-element.34.refs_0_.refs_3_), channel_id=1, source_target_pairs={{0,1},{1,0},{2,3},{3,2},{4,5},{5,4},{6,7},{7,6},{8,9},{9,8},{10,11... | collective-permute-start | bytes 196616 | tf_op jit(solution)/shard_map/ppermute | solution.py:482
  8.0 3.7 %collective-permute-start.1 = (bf16[32,1024]{1,0:T(8,128)(2,1)S(1)}, bf16[32,1024]{1,0:T(8,128)(2,1)S(1)}, u32[]{:S(2)}, u32[]{:S(2)}) collective-permute-start(bf16[32,1024]{1,0:T(8,128)(2,1)S(1)} %collective-permute-done.refs_4_), channel_id=1, source_target_pairs={{0,1},{1,0},{2,3},{3,2},{4,5},{5,4},{6,7},{7,6},{8,9},{9,8},{10,11... | collective-permute-start | bytes 196616 | tf_op jit(solution)/shard_map/ppermute | solution.py:482
  9.4 2.4 %collective-permute-start.3 = (bf16[32,1024]{1,0:T(8,128)(2,1)S(1)}, bf16[32,1024]{1,0:T(8,128)(2,1)S(1)}, u32[]{:S(2)}, u32[]{:S(2)}) collective-permute-start(bf16[32,1024]{1,0:T(8,128)(2,1)S(1)} %collective-permute-done.2.refs_5_), channel_id=1, source_target_pairs={{0,1},{1,0},{2,3},{3,2},{4,5},{5,4},{6,7},{7,6},{8,9},{9,8},{10,11... | collective-permute-start | bytes 196616 | tf_op jit(solution)/shard_map/ppermute | solution.py:482
  10.6 1.3 %collective-permute-start.5 = (bf16[32,1024]{1,0:T(8,128)(2,1)S(1)}, bf16[32,1024]{1,0:T(8,128)(2,1)S(1)}, u32[]{:S(2)}, u32[]{:S(2)}) collective-permute-start(bf16[32,1024]{1,0:T(8,128)(2,1)S(1)} %collective-permute-done.4.refs_6_), channel_id=1, source_target_pairs={{0,1},{1,0},{2,3},{3,2},{4,5},{5,4},{6,7},{7,6},{8,9},{9,8},{10,11... | collective-permute-start | bytes 196616 | tf_op jit(solution)/shard_map/ppermute | solution.py:482
  15.5 1.4 %collective-permute-start.7 = (bf16[64,1024]{1,0:T(8,128)(2,1)S(1)}, bf16[64,1024]{1,0:T(8,128)(2,1)S(1)}, u32[]{:S(2)}, u32[]{:S(2)}) collective-permute-start(bf16[64,1024]{1,0:T(8,128)(2,1)S(1)} %get-tuple-element.40), channel_id=1, source_target_pairs={{0,1},{1,0},{2,3},{3,2},{4,5},{5,4},{6,7},{7,6},{8,9},{9,8},{10,11... | collective-permute-start | bytes 393224 | tf_op jit(solution)/shard_map/ppermute | solution.py:558
  15.9 7.6 %collective-permute-start.12 = (bf16[80,896]{1,0:T(8,128)(2,1)S(1)}, bf16[80,896]{1,0:T(8,128)(2,1)S(1)}, u32[]{:S(2)}, u32[]{:S(2)}) collective-permute-start(bf16[80,896]{1,0:T(8,128)(2,1)S(1)} %get-tuple-element.45.refs_1_), channel_id=1, source_target_pairs={{0,1},{1,0},{2,3},{3,2},{4,5},{5,4},{6,7},{7,6},{8,9},{9,8},{10,11... | collective-permute-start | bytes 430088 | tf_op jit(solution)/shard_map/ppermute | solution.py:556
  17.0 6.9 %collective-permute-start.10 = (bf16[32,1024]{1,0:T(8,128)(2,1)S(1)}, bf16[32,1024]{1,0:T(8,128)(2,1)S(1)}, u32[]{:S(2)}, u32[]{:S(2)}) collective-permute-start(bf16[32,1024]{1,0:T(8,128)(2,1)S(1)} %get-tuple-element.43), channel_id=1, source_target_pairs={{0,15},{1,6},{2,13},{3,4},{4,11},{5,2},{6,9},{7,0},{8,7},{9,22},{1... | collective-permute-start | bytes 196616 | tf_op jit(solution)/shard_map/ppermute | solution.py:561
  19.5 4.9 %collective-permute-start.11 = (bf16[32,1024]{1,0:T(8,128)(2,1)S(1)}, bf16[32,1024]{1,0:T(8,128)(2,1)S(1)}, u32[]{:S(2)}, u32[]{:S(2)}) collective-permute-start(bf16[32,1024]{1,0:T(8,128)(2,1)S(1)} %get-tuple-element.44), channel_id=1, source_target_pairs={{0,13},{1,4},{2,15},{3,6},{4,9},{5,0},{6,11},{7,2},{8,5},{9,20},{1... | collective-permute-start | bytes 196616 | tf_op jit(solution)/shard_map/ppermute | solution.py:561
  21.7 4.4 %collective-permute-start.8 = (bf16[32,1024]{1,0:T(8,128)(2,1)S(1)}, bf16[32,1024]{1,0:T(8,128)(2,1)S(1)}, u32[]{:S(2)}, u32[]{:S(2)}) collective-permute-start(bf16[32,1024]{1,0:T(8,128)(2,1)S(1)} %get-tuple-element.41), channel_id=1, source_target_pairs={{0,11},{1,2},{2,9},{3,0},{4,15},{5,6},{6,13},{7,4},{8,3},{9,18},{1... | collective-permute-start | bytes 196616 | tf_op jit(solution)/shard_map/ppermute | solution.py:561
  23.2 2.9 %collective-permute-start.9 = (bf16[32,1024]{1,0:T(8,128)(2,1)S(1)}, bf16[32,1024]{1,0:T(8,128)(2,1)S(1)}, u32[]{:S(2)}, u32[]{:S(2)}) collective-permute-start(bf16[32,1024]{1,0:T(8,128)(2,1)S(1)} %get-tuple-element.42), channel_id=1, source_target_pairs={{0,9},{1,0},{2,11},{3,2},{4,13},{5,4},{6,15},{7,6},{8,1},{9,16},{1... | collective-permute-start | bytes 196616 | tf_op jit(solution)/shard_map/ppermute | solution.py:561
  26.5 4.9 %collective-permute-start.13 = (bf16[32,896]{1,0:T(8,128)(2,1)S(1)}, bf16[32,896]{1,0:T(8,128)(2,1)S(1)}, u32[]{:S(2)}, u32[]{:S(2)}) collective-permute-start(bf16[32,896]{1,0:T(8,128)(2,1)S(1)} %get-tuple-element.48), channel_id=1, source_target_pairs={{0,7},{1,6},{2,5},{3,4},{4,3},{5,2},{6,1},{7,0},{8,15},{9,14},{10,... | collective-permute-start | bytes 172040 | tf_op jit(solution)/shard_map/ppermute | solution.py:479
  27.8 5.0 %collective-permute-start.15 = (bf16[32,896]{1,0:T(8,128)(2,1)S(1)}, bf16[32,896]{1,0:T(8,128)(2,1)S(1)}, u32[]{:S(2)}, u32[]{:S(2)}) collective-permute-start(bf16[32,896]{1,0:T(8,128)(2,1)S(1)} %get-tuple-element.49), channel_id=1, source_target_pairs={{0,5},{1,4},{2,7},{3,6},{4,1},{5,0},{6,3},{7,2},{8,13},{9,12},{10,... | collective-permute-start | bytes 172040 | tf_op jit(solution)/shard_map/ppermute | solution.py:479
  28.7 4.3 %collective-permute-start.17 = (bf16[32,896]{1,0:T(8,128)(2,1)S(1)}, bf16[32,896]{1,0:T(8,128)(2,1)S(1)}, u32[]{:S(2)}, u32[]{:S(2)}) collective-permute-start(bf16[32,896]{1,0:T(8,128)(2,1)S(1)} %get-tuple-element.50), channel_id=1, source_target_pairs={{0,3},{1,2},{2,1},{3,0},{4,7},{5,6},{6,5},{7,4},{8,11},{9,10},{10,... | collective-permute-start | bytes 172040 | tf_op jit(solution)/shard_map/ppermute | solution.py:479
  29.5 3.9 %collective-permute-start.19 = (bf16[32,896]{1,0:T(8,128)(2,1)S(1)}, bf16[32,896]{1,0:T(8,128)(2,1)S(1)}, u32[]{:S(2)}, u32[]{:S(2)}) collective-permute-start(bf16[32,896]{1,0:T(8,128)(2,1)S(1)} %get-tuple-element.51.refs_3_), channel_id=1, source_target_pairs={{0,1},{1,0},{2,3},{3,2},{4,5},{5,4},{6,7},{7,6},{8,9},{9,8},{10,11... | collective-permute-start | bytes 172040 | tf_op jit(solution)/shard_map/ppermute | solution.py:482
  31.4 1.9 %collective-permute-start.14 = (bf16[32,896]{1,0:T(8,128)(2,1)S(1)}, bf16[32,896]{1,0:T(8,128)(2,1)S(1)}, u32[]{:S(2)}, u32[]{:S(2)}) collective-permute-start(bf16[32,896]{1,0:T(8,128)(2,1)S(1)} %collective-permute-done.13.refs_4_), channel_id=1, source_target_pairs={{0,1},{1,0},{2,3},{3,2},{4,5},{5,4},{6,7},{7,6},{8,9},{9,8},{10,11... | collective-permute-start | bytes 172040 | tf_op jit(solution)/shard_map/ppermute | solution.py:482
  32.8 1.2 %collective-permute-start.16 = (bf16[32,896]{1,0:T(8,128)(2,1)S(1)}, bf16[32,896]{1,0:T(8,128)(2,1)S(1)}, u32[]{:S(2)}, u32[]{:S(2)}) collective-permute-start(bf16[32,896]{1,0:T(8,128)(2,1)S(1)} %collective-permute-done.15.refs_5_), channel_id=1, source_target_pairs={{0,1},{1,0},{2,3},{3,2},{4,5},{5,4},{6,7},{7,6},{8,9},{9,8},{10,11... | collective-permute-start | bytes 172040 | tf_op jit(solution)/shard_map/ppermute | solution.py:482
  32.9 1.3 %collective-permute-start.18 = (bf16[32,896]{1,0:T(8,128)(2,1)S(1)}, bf16[32,896]{1,0:T(8,128)(2,1)S(1)}, u32[]{:S(2)}, u32[]{:S(2)}) collective-permute-start(bf16[32,896]{1,0:T(8,128)(2,1)S(1)} %collective-permute-done.17.refs_6_), channel_id=1, source_target_pairs={{0,1},{1,0},{2,3},{3,2},{4,5},{5,4},{6,7},{7,6},{8,9},{9,8},{10,11... | collective-permute-start | bytes 172040 | tf_op jit(solution)/shard_map/ppermute | solution.py:482
  37.9 4.7 %collective-permute-start.20 = (bf16[32,896]{1,0:T(8,128)(2,1)S(1)}, bf16[32,896]{1,0:T(8,128)(2,1)S(1)}, u32[]{:S(2)}, u32[]{:S(2)}) collective-permute-start(bf16[32,896]{1,0:T(8,128)(2,1)S(1)} %get-tuple-element.53), channel_id=1, source_target_pairs={{0,7},{1,6},{2,5},{3,4},{4,3},{5,2},{6,1},{7,0},{8,15},{9,14},{10,... | collective-permute-start | bytes 172040 | tf_op jit(solution)/shard_map/ppermute | solution.py:479
  39.5 4.8 %collective-permute-start.22 = (bf16[32,896]{1,0:T(8,128)(2,1)S(1)}, bf16[32,896]{1,0:T(8,128)(2,1)S(1)}, u32[]{:S(2)}, u32[]{:S(2)}) collective-permute-start(bf16[32,896]{1,0:T(8,128)(2,1)S(1)} %get-tuple-element.54), channel_id=1, source_target_pairs={{0,5},{1,4},{2,7},{3,6},{4,1},{5,0},{6,3},{7,2},{8,13},{9,12},{10,... | collective-permute-start | bytes 172040 | tf_op jit(solution)/shard_map/ppermute | solution.py:479
  40.2 4.2 %collective-permute-start.24 = (bf16[32,896]{1,0:T(8,128)(2,1)S(1)}, bf16[32,896]{1,0:T(8,128)(2,1)S(1)}, u32[]{:S(2)}, u32[]{:S(2)}) collective-permute-start(bf16[32,896]{1,0:T(8,128)(2,1)S(1)} %get-tuple-element.55), channel_id=1, source_target_pairs={{0,3},{1,2},{2,1},{3,0},{4,7},{5,6},{6,5},{7,4},{8,11},{9,10},{10,... | collective-permute-start | bytes 172040 | tf_op jit(solution)/shard_map/ppermute | solution.py:479
  41.1 3.7 %collective-permute-start.26 = (bf16[32,896]{1,0:T(8,128)(2,1)S(1)}, bf16[32,896]{1,0:T(8,128)(2,1)S(1)}, u32[]{:S(2)}, u32[]{:S(2)}) collective-permute-start(bf16[32,896]{1,0:T(8,128)(2,1)S(1)} %get-tuple-element.56.refs_3_), channel_id=1, source_target_pairs={{0,1},{1,0},{2,3},{3,2},{4,5},{5,4},{6,7},{7,6},{8,9},{9,8},{10,11... | collective-permute-start | bytes 172040 | tf_op jit(solution)/shard_map/ppermute | solution.py:482
  42.6 2.2 %collective-permute-start.21 = (bf16[32,896]{1,0:T(8,128)(2,1)S(1)}, bf16[32,896]{1,0:T(8,128)(2,1)S(1)}, u32[]{:S(2)}, u32[]{:S(2)}) collective-permute-start(bf16[32,896]{1,0:T(8,128)(2,1)S(1)} %collective-permute-done.20.refs_4_), channel_id=1, source_target_pairs={{0,1},{1,0},{2,3},{3,2},{4,5},{5,4},{6,7},{7,6},{8,9},{9,8},{10,11... | collective-permute-start | bytes 172040 | tf_op jit(solution)/shard_map/ppermute | solution.py:482
  44.3 1.2 %collective-permute-start.23 = (bf16[32,896]{1,0:T(8,128)(2,1)S(1)}, bf16[32,896]{1,0:T(8,128)(2,1)S(1)}, u32[]{:S(2)}, u32[]{:S(2)}) collective-permute-start(bf16[32,896]{1,0:T(8,128)(2,1)S(1)} %collective-permute-done.22.refs_5_), channel_id=1, source_target_pairs={{0,1},{1,0},{2,3},{3,2},{4,5},{5,4},{6,7},{7,6},{8,9},{9,8},{10,11... | collective-permute-start | bytes 172040 | tf_op jit(solution)/shard_map/ppermute | solution.py:482
  44.4 1.3 %collective-permute-start.25 = (bf16[32,896]{1,0:T(8,128)(2,1)S(1)}, bf16[32,896]{1,0:T(8,128)(2,1)S(1)}, u32[]{:S(2)}, u32[]{:S(2)}) collective-permute-start(bf16[32,896]{1,0:T(8,128)(2,1)S(1)} %collective-permute-done.24.refs_6_), channel_id=1, source_target_pairs={{0,1},{1,0},{2,3},{3,2},{4,5},{5,4},{6,7},{7,6},{8,9},{9,8},{10,11... | collective-permute-start | bytes 172040 | tf_op jit(solution)/shard_map/ppermute | solution.py:482

commit v6 on v5

--- a/solution.py
+++ b/solution.py
@@ -183,8 +183,7 @@
     chips = span // (2 * SUBLANES)
     array = (chosen // 2) ^ chip ^ (chips - 1)
     array = array + jnp.where(chosen % 2 == core, 0, chips)
-    sender = (lax.axis_index("pipe") + group) % 2
-    within = piece * (2 * slot_cap) + sender * slot_cap + rank
+    within = piece * (2 * slot_cap) + (1 - group) * slot_cap + rank
     return one_hot(2 * span, (array * 2 + core) * SUBLANES + within)
 
 
@@ -206,7 +205,7 @@
     array, within = lane % (span // 2) // SUBLANES, lane % SUBLANES
     piece, row = within // wide, within % wide
     array = array + jnp.where(row // slot_cap == core, 0, chips)
-    way = (half + core + lax.axis_index("pipe")) % 2
+    way = (half + core) % 2
     row = way * slot_cap + row % slot_cap
     return one_hot(span, piece * (span // parts) + array * wide + row)
 
@@ -354,14 +353,13 @@
 
 def turn_plan_kernel(parts, slot_cap, after_ref, own_ref, other_ref, sending_ref, entering_ref):
     del after_ref
-    section = lax.axis_index("pipe")
     _, core = chip_and_core()
     span, width = entering_ref.shape
     rows = span // (2 * parts)
     own, other = own_ref[...], other_ref[...]
     first = jnp.where(core == 0, own, other)
     second = jnp.where(core == 0, other, own)
-    picked = iota((rows, LANES), 0) == (section + core) % 2
+    picked = iota((rows, LANES), 0) == 1 - core
 
     def ids(aside):
         lines = jnp.where(picked, aside[parts * rows :, :LANES].astype(jnp.float32), 0.0)
@@ -389,8 +387,7 @@
     sorting = jnp.where(iota((span, span), 1) == place + numbers, 1.0, 0.0).astype(jnp.bfloat16)
     across = (((1,), (1,)), ((), ()))
     sending = lax.dot_general(sending_ref[...], sorting, across, preferred_element_type=jnp.float32)
-    partner = ((section + 1 - core) ^ 1) - (1 - core)
-    enters = (partner < 0) | (partner >= pipe)
+    enters = section == jnp.where(core == 0, pipe - 1, 0)
     put(jnp.where(enters, entering_ref[...], moved(sending, received[:, :width])), out_refs)
 
 
@@ -487,9 +484,9 @@
     pairs = []
     for section in range(pipe):
         for i in range(experts):
-            other = ((section + i % 2) ^ 1) - i % 2
-            other = other if 0 <= other < pipe else section
-            pairs.append((section * experts + i, other * experts + (i ^ (2 * k) ^ 1)))
+            other = section + 1 - 2 * (i % 2)
+            target = (other, i ^ (2 * k) ^ 1) if 0 <= other < pipe else (section, i ^ (2 * (k or 1)))
+            pairs.append((section * experts + i, target[0] * experts + target[1]))
     return pairs
 
 

time: 46.7 us -> 46.2 us (0.989)
  starting transfers between devices: 20.8 us -> 19.3 us
  waiting for transfers between devices: 13.6 us -> 14.5 us
    ppermute x4, starting transfers between devices: 6.58 us -> 5.35 us  [single_shards(): lax.ppermute(x, ('pipe', 'expert'), relay_pairs(chips - 1 - j, pipe, expe...]
    ppermute x4, waiting for transfers between devices: 2.18 us -> 3.12 us  [single_shards(): lax.ppermute(x, ('pipe', 'expert'), relay_pairs(chips - 1 - j, pipe, expe...]
  transfers between devices with their start and end apart: 27 -> 27, of which waited for: 15 -> 17; matrix products, arithmetic and copies ran while one was open for 0% -> 0% of each run, Pallas kernels for 3% -> 3%
where the time goes in v6:
time: 46.2 us; the launch traced here: 46 us
  starting transfers between devices  19.3 us (42%)
  waiting for transfers between devices  14.5 us (31%)
  Pallas kernels  11.4 us (25%)
  between operations  0.78 us (2%)
    pallas_call x8, Pallas kernels, local_call(): pl.pallas_call(body, out_shape=outs, in_specs=[VMEM_SPEC] * len(close) +...  11.4 us
    ppermute x9, starting transfers between devices, exchanged(): lax.ppermute(arrays[j], 'expert', [(i, i ^ 2 * (last - j) ^ 1) for i in d...  10.2 us
    ppermute x9, waiting for transfers between devices, exchanged(): lax.ppermute(arrays[j], 'expert', [(i, i ^ 2 * (last - j) ^ 1) for i in d...  8.34 us
    ppermute x4, starting transfers between devices, single_shards(): lax.ppermute(x, ('pipe', 'expert'), relay_pairs(chips - 1 - j, pipe, expe...  5.35 us
    ppermute x12, starting transfers between devices, exchanged(): lax.ppermute(x, 'expert', sibling)  3.19 us
    ppermute x4, waiting for transfers between devices, single_shards(): lax.ppermute(x, ('pipe', 'expert'), relay_pairs(chips - 1 - j, pipe, expe...  3.12 us
    ppermute x12, waiting for transfers between devices, exchanged(): lax.ppermute(x, 'expert', sibling)  2.23 us
  transfers between devices with their start and end apart: 27, of which 17 were waited for; matrix products, arithmetic and copies ran while one was open for 0% of the time, Pallas kernels for 3%

profile of v6, /device:TPU:0, one launch (start us, length us, event | category | flops | bytes accessed | tf_op | source)
XLA Modules:
  0.0 46.0 jit_solution(16866110963334689757)
XLA Ops:
  0.6 0.0 copy-start
  0.6 0.0 copy-start.1
  0.7 0.0 copy-start.2
  0.7 1.4 %shard_map.122 = (bf16[32,1024]{1,0:T(8,128)(2,1)S(1)}, bf16[32,1024]{1,0:T(8,128)(2,1)S(1)}, bf16[32,1024]{1,0:T(8,128)(2,1)S(1)}, bf16[32,1024]{1,0:T(8,128)(2,1)S(1)}, bf16[80,896]{1,0:T(8,128)(2,1)S(1)}) custom-call(bf16[1,16,3584]{2,1,0:T(8,128)(2,1)} %refs_0_.1, bf16[1,16,3584]{2,1,0:T(8,128)(2,1)} %refs_1_.1, s32[2,1,1,16]{3,2,1,0:T(1,128)} %bitcast.19, ...), custom_call_target="tpu_custom_call" | custom-call | tf_op jit(solution)/shard_map/pallas_call | solution.py:460
  2.1 3.4 %collective-permute-start = (bf16[32,1024]{1,0:T(8,128)(2,1)S(1)}, bf16[32,1024]{1,0:T(8,128)(2,1)S(1)}, u32[]{:S(2)}, u32[]{:S(2)}) collective-permute-start(bf16[32,1024]{1,0:T(8,128)(2,1)S(1)} %get-tuple-element.31), channel_id=1, source_target_pairs={{0,7},{1,6},{2,5},{3,4},{4,3},{5,2},{6,1},{7,0},{8,15},{9,14},{10,... | collective-permute-start | bytes 196616 | tf_op jit(solution)/shard_map/ppermute | solution.py:476
  5.5 0.8 %collective-permute-start.2 = (bf16[32,1024]{1,0:T(8,128)(2,1)S(1)}, bf16[32,1024]{1,0:T(8,128)(2,1)S(1)}, u32[]{:S(2)}, u32[]{:S(2)}) collective-permute-start(bf16[32,1024]{1,0:T(8,128)(2,1)S(1)} %get-tuple-element.32), channel_id=1, source_target_pairs={{0,5},{1,4},{2,7},{3,6},{4,1},{5,0},{6,3},{7,2},{8,13},{9,12},{10,... | collective-permute-start | bytes 196616 | tf_op jit(solution)/shard_map/ppermute | solution.py:476
  6.3 0.1 collective-permute-start.4
  6.4 0.0 collective-permute-start.6
  6.4 1.6 %collective-permute-done.refs_4_ = bf16[32,1024]{1,0:T(8,128)(2,1)S(1)} collective-permute-done((bf16[32,1024]{1,0:T(8,128)(2,1)S(1)}, bf16[32,1024]{1,0:T(8,128)(2,1)S(1)}, u32[]{:S(2)}, u32[]{:S(2)}) %collective-permute-start) | collective-permute-done | bytes 65568 | tf_op jit(solution)/shard_map/ppermute | solution.py:476
  8.0 0.1 collective-permute-start.1
  8.1 1.2 %collective-permute-done.2.refs_5_ = bf16[32,1024]{1,0:T(8,128)(2,1)S(1)} collective-permute-done((bf16[32,1024]{1,0:T(8,128)(2,1)S(1)}, bf16[32,1024]{1,0:T(8,128)(2,1)S(1)}, u32[]{:S(2)}, u32[]{:S(2)}) %collective-permute-start.2) | collective-permute-done | bytes 65568 | tf_op jit(solution)/shard_map/ppermute | solution.py:476
  9.4 0.8 %collective-permute-start.3 = (bf16[32,1024]{1,0:T(8,128)(2,1)S(1)}, bf16[32,1024]{1,0:T(8,128)(2,1)S(1)}, u32[]{:S(2)}, u32[]{:S(2)}) collective-permute-start(bf16[32,1024]{1,0:T(8,128)(2,1)S(1)} %collective-permute-done.2.refs_5_), channel_id=1, source_target_pairs={{0,1},{1,0},{2,3},{3,2},{4,5},{5,4},{6,7},{7,6},{8,9},{9,8},{10,11... | collective-permute-start | bytes 196616 | tf_op jit(solution)/shard_map/ppermute | solution.py:479
  10.2 0.4 collective-permute-done.4.refs_6_
  10.6 0.1 collective-permute-start.5
  10.7 1.0 %shard_map.123 = (bf16[128,256]{1,0:T(8,128)(2,1)S(1)}, bf16[128,256]{1,0:T(8,128)(2,1)S(1)}, bf16[128,128]{1,0:T(8,128)(2,1)S(1)}, bf16[128,128]{1,0:T(8,128)(2...) custom-call(bf16[32,1024]{1,0:T(8,128)(2,1)S(1)} %get-tuple-element.34.refs_0_.refs_3_, s32[2,1,1,16]{3,2,1,0:T(1,128)} %bitcast.20, ...), custom_call_target="tpu_custom_call" | custom-call | tf_op jit(solution)/shard_map/pallas_call | solution.py:460
  11.7 0.0 collective-permute-done.6.refs_7_
  11.7 0.0 collective-permute-done.1.refs_0_
  11.7 0.0 collective-permute-done.3.refs_1_
  11.8 0.1 collective-permute-done.5.refs_2_
  11.9 3.7 %shard_map.124 = (bf16[64,1024]{1,0:T(8,128)(2,1)S(1)}, bf16[64,1024]{1,0:T(8,128)(2,1)S(1)}) custom-call(bf16[32,1024]{1,0:T(8,128)(2,1)S(1)} %collective-permute-done.1.refs_0_, bf16[32,1024]{1,0:T(8,128)(2,1)S(1)} %collective-permute-done.3.refs_1_, bf16[32,1024]{1,0:T(8,128)(2,1)S(1)} %collective-permute-done.5.refs_2_, ...), custom_call_target="tpu_custom_call" | custom-call | tf_op jit(solution)/shard_map/pallas_call | solution.py:460
  15.5 0.4 collective-permute-start.7
  15.9 0.2 collective-permute-start.12
  16.1 0.8 %collective-permute-done.7.refs_1_ = bf16[64,1024]{1,0:T(8,128)(2,1)S(1)} collective-permute-done((bf16[64,1024]{1,0:T(8,128)(2,1)S(1)}, bf16[64,1024]{1,0:T(8,128)(2,1)S(1)}, u32[]{:S(2)}, u32[]{:S(2)}) %collective-permute-start.7) | collective-permute-done | bytes 131104 | tf_op jit(solution)/shard_map/ppermute | solution.py:555
  17.0 2.5 %collective-permute-start.10 = (bf16[32,1024]{1,0:T(8,128)(2,1)S(1)}, bf16[32,1024]{1,0:T(8,128)(2,1)S(1)}, u32[]{:S(2)}, u32[]{:S(2)}) collective-permute-start(bf16[32,1024]{1,0:T(8,128)(2,1)S(1)} %get-tuple-element.43), channel_id=1, source_target_pairs={{0,15},{1,7},{2,13},{3,5},{4,11},{5,3},{6,9},{7,1},{8,23},{9,6},{1... | collective-permute-start | bytes 196616 | tf_op jit(solution)/shard_map/ppermute | solution.py:558
  19.5 1.1 %collective-permute-start.11 = (bf16[32,1024]{1,0:T(8,128)(2,1)S(1)}, bf16[32,1024]{1,0:T(8,128)(2,1)S(1)}, u32[]{:S(2)}, u32[]{:S(2)}) collective-permute-start(bf16[32,1024]{1,0:T(8,128)(2,1)S(1)} %get-tuple-element.44), channel_id=1, source_target_pairs={{0,13},{1,5},{2,15},{3,7},{4,9},{5,1},{6,11},{7,3},{8,21},{9,4},{1... | collective-permute-start | bytes 196616 | tf_op jit(solution)/shard_map/ppermute | solution.py:558
  20.6 1.5 %collective-permute-start.8 = (bf16[32,1024]{1,0:T(8,128)(2,1)S(1)}, bf16[32,1024]{1,0:T(8,128)(2,1)S(1)}, u32[]{:S(2)}, u32[]{:S(2)}) collective-permute-start(bf16[32,1024]{1,0:T(8,128)(2,1)S(1)} %get-tuple-element.41), channel_id=1, source_target_pairs={{0,11},{1,3},{2,9},{3,1},{4,15},{5,7},{6,13},{7,5},{8,19},{9,2},{1... | collective-permute-start | bytes 196616 | tf_op jit(solution)/shard_map/ppermute | solution.py:558
  22.1 0.2 collective-permute-start.9
  22.3 0.0 collective-permute-done.12.refs_2_
  22.3 0.3 shard_map.126
  22.7 0.0 collective-permute-done.10.refs_2_
  22.7 1.4 %collective-permute-done.11.refs_3_ = bf16[32,1024]{1,0:T(8,128)(2,1)S(1)} collective-permute-done((bf16[32,1024]{1,0:T(8,128)(2,1)S(1)}, bf16[32,1024]{1,0:T(8,128)(2,1)S(1)}, u32[]{:S(2)}, u32[]{:S(2)}) %collective-permute-start.11) | collective-permute-done | bytes 65568 | tf_op jit(solution)/shard_map/ppermute | solution.py:558
  24.1 1.1 %collective-permute-done.8.refs_0_ = bf16[32,1024]{1,0:T(8,128)(2,1)S(1)} collective-permute-done((bf16[32,1024]{1,0:T(8,128)(2,1)S(1)}, bf16[32,1024]{1,0:T(8,128)(2,1)S(1)}, u32[]{:S(2)}, u32[]{:S(2)}) %collective-permute-start.8) | collective-permute-done | bytes 65568 | tf_op jit(solution)/shard_map/ppermute | solution.py:558
  25.2 0.6 %collective-permute-done.9.refs_1_ = bf16[32,1024]{1,0:T(8,128)(2,1)S(1)} collective-permute-done((bf16[32,1024]{1,0:T(8,128)(2,1)S(1)}, bf16[32,1024]{1,0:T(8,128)(2,1)S(1)}, u32[]{:S(2)}, u32[]{:S(2)}) %collective-permute-start.9) | collective-permute-done | bytes 65568 | tf_op jit(solution)/shard_map/ppermute | solution.py:558
  25.8 0.4 shard_map.127
  26.2 0.1 collective-permute-start.13
  26.3 2.5 %collective-permute-start.15 = (bf16[32,896]{1,0:T(8,128)(2,1)S(1)}, bf16[32,896]{1,0:T(8,128)(2,1)S(1)}, u32[]{:S(2)}, u32[]{:S(2)}) collective-permute-start(bf16[32,896]{1,0:T(8,128)(2,1)S(1)} %get-tuple-element.49), channel_id=1, source_target_pairs={{0,5},{1,4},{2,7},{3,6},{4,1},{5,0},{6,3},{7,2},{8,13},{9,12},{10,... | collective-permute-start | bytes 172040 | tf_op jit(solution)/shard_map/ppermute | solution.py:476
  28.7 0.3 collective-permute-start.17
  29.0 0.6 %collective-permute-start.19 = (bf16[32,896]{1,0:T(8,128)(2,1)S(1)}, bf16[32,896]{1,0:T(8,128)(2,1)S(1)}, u32[]{:S(2)}, u32[]{:S(2)}) collective-permute-start(bf16[32,896]{1,0:T(8,128)(2,1)S(1)} %get-tuple-element.51.refs_3_), channel_id=1, source_target_pairs={{0,1},{1,0},{2,3},{3,2},{4,5},{5,4},{6,7},{7,6},{8,9},{9,8},{10,11... | collective-permute-start | bytes 172040 | tf_op jit(solution)/shard_map/ppermute | solution.py:479
  29.6 1.3 %collective-permute-done.13.refs_4_ = bf16[32,896]{1,0:T(8,128)(2,1)S(1)} collective-permute-done((bf16[32,896]{1,0:T(8,128)(2,1)S(1)}, bf16[32,896]{1,0:T(8,128)(2,1)S(1)}, u32[]{:S(2)}, u32[]{:S(2)}) %collective-permute-start.13) | collective-permute-done | bytes 57376 | tf_op jit(solution)/shard_map/ppermute | solution.py:476
  30.8 0.0 collective-permute-start.14
  30.9 0.5 %collective-permute-done.15.refs_5_ = bf16[32,896]{1,0:T(8,128)(2,1)S(1)} collective-permute-done((bf16[32,896]{1,0:T(8,128)(2,1)S(1)}, bf16[32,896]{1,0:T(8,128)(2,1)S(1)}, u32[]{:S(2)}, u32[]{:S(2)}) %collective-permute-start.15) | collective-permute-done | bytes 57376 | tf_op jit(solution)/shard_map/ppermute | solution.py:476
  31.4 0.6 %collective-permute-start.16 = (bf16[32,896]{1,0:T(8,128)(2,1)S(1)}, bf16[32,896]{1,0:T(8,128)(2,1)S(1)}, u32[]{:S(2)}, u32[]{:S(2)}) collective-permute-start(bf16[32,896]{1,0:T(8,128)(2,1)S(1)} %collective-permute-done.15.refs_5_), channel_id=1, source_target_pairs={{0,1},{1,0},{2,3},{3,2},{4,5},{5,4},{6,7},{7,6},{8,9},{9,8},{10,11... | collective-permute-start | bytes 172040 | tf_op jit(solution)/shard_map/ppermute | solution.py:479
  31.9 0.5 collective-permute-done.17.refs_6_
  32.4 0.0 collective-permute-start.18
  32.4 0.0 collective-permute-done.19.refs_7_
  32.4 0.0 collective-permute-done.14.refs_0_
  32.4 0.4 collective-permute-done.16.refs_1_
  32.8 0.8 %collective-permute-done.18.refs_2_ = bf16[32,896]{1,0:T(8,128)(2,1)S(1)} collective-permute-done((bf16[32,896]{1,0:T(8,128)(2,1)S(1)}, bf16[32,896]{1,0:T(8,128)(2,1)S(1)}, u32[]{:S(2)}, u32[]{:S(2)}) %collective-permute-start.18) | collective-permute-done | bytes 57376 | tf_op jit(solution)/shard_map/ppermute | solution.py:479
  33.6 3.7 %shard_map.128 = (bf16[32,896]{1,0:T(8,128)(2,1)S(1)}, bf16[32,896]{1,0:T(8,128)(2,1)S(1)}, bf16[32,896]{1,0:T(8,128)(2,1)S(1)}, bf16[32,896]{1,0:T(8,128)(2,1)S(1)}) custom-call(bf16[32,896]{1,0:T(8,128)(2,1)S(1)} %collective-permute-done.14.refs_0_, bf16[32,896]{1,0:T(8,128)(2,1)S(1)} %collective-permute-done.16.refs_1_, ...), custom_call_target="tpu_custom_call" | custom-call | tf_op jit(solution)/shard_map/pallas_call | solution.py:460
  37.3 1.5 %collective-permute-start.20 = (bf16[32,896]{1,0:T(8,128)(2,1)S(1)}, bf16[32,896]{1,0:T(8,128)(2,1)S(1)}, u32[]{:S(2)}, u32[]{:S(2)}) collective-permute-start(bf16[32,896]{1,0:T(8,128)(2,1)S(1)} %get-tuple-element.53), channel_id=1, source_target_pairs={{0,7},{1,6},{2,5},{3,4},{4,3},{5,2},{6,1},{7,0},{8,15},{9,14},{10,... | collective-permute-start | bytes 172040 | tf_op jit(solution)/shard_map/ppermute | solution.py:476
  38.8 0.9 %collective-permute-start.22 = (bf16[32,896]{1,0:T(8,128)(2,1)S(1)}, bf16[32,896]{1,0:T(8,128)(2,1)S(1)}, u32[]{:S(2)}, u32[]{:S(2)}) collective-permute-start(bf16[32,896]{1,0:T(8,128)(2,1)S(1)} %get-tuple-element.54), channel_id=1, source_target_pairs={{0,5},{1,4},{2,7},{3,6},{4,1},{5,0},{6,3},{7,2},{8,13},{9,12},{10,... | collective-permute-start | bytes 172040 | tf_op jit(solution)/shard_map/ppermute | solution.py:476
  39.7 0.7 %collective-permute-start.24 = (bf16[32,896]{1,0:T(8,128)(2,1)S(1)}, bf16[32,896]{1,0:T(8,128)(2,1)S(1)}, u32[]{:S(2)}, u32[]{:S(2)}) collective-permute-start(bf16[32,896]{1,0:T(8,128)(2,1)S(1)} %get-tuple-element.55), channel_id=1, source_target_pairs={{0,3},{1,2},{2,1},{3,0},{4,7},{5,6},{6,5},{7,4},{8,11},{9,10},{10,... | collective-permute-start | bytes 172040 | tf_op jit(solution)/shard_map/ppermute | solution.py:476
  40.4 0.3 collective-permute-start.26
  40.7 1.5 %collective-permute-done.20.refs_4_ = bf16[32,896]{1,0:T(8,128)(2,1)S(1)} collective-permute-done((bf16[32,896]{1,0:T(8,128)(2,1)S(1)}, bf16[32,896]{1,0:T(8,128)(2,1)S(1)}, u32[]{:S(2)}, u32[]{:S(2)}) %collective-permute-start.20) | collective-permute-done | bytes 57376 | tf_op jit(solution)/shard_map/ppermute | solution.py:476
  42.2 0.2 collective-permute-start.21
  42.4 1.3 %collective-permute-done.22.refs_5_ = bf16[32,896]{1,0:T(8,128)(2,1)S(1)} collective-permute-done((bf16[32,896]{1,0:T(8,128)(2,1)S(1)}, bf16[32,896]{1,0:T(8,128)(2,1)S(1)}, u32[]{:S(2)}, u32[]{:S(2)}) %collective-permute-start.22) | collective-permute-done | bytes 57376 | tf_op jit(solution)/shard_map/ppermute | solution.py:476
  43.7 0.1 collective-permute-start.23
  43.8 0.0 collective-permute-done.24.refs_6_
  43.8 0.4 collective-permute-start.25
  44.2 0.0 collective-permute-done.26.refs_7_
  44.2 0.0 collective-permute-done.21.refs_0_
  44.2 0.7 %collective-permute-done.23.refs_1_ = bf16[32,896]{1,0:T(8,128)(2,1)S(1)} collective-permute-done((bf16[32,896]{1,0:T(8,128)(2,1)S(1)}, bf16[32,896]{1,0:T(8,128)(2,1)S(1)}, u32[]{:S(2)}, u32[]{:S(2)}) %collective-permute-start.23) | collective-permute-done | bytes 57376 | tf_op jit(solution)/shard_map/ppermute | solution.py:479
  44.9 0.2 collective-permute-done.25.refs_2_
  45.1 0.9 %shard_map.129 = (bf16[16,3584]{1,0:T(8,128)(2,1)}, bf16[16,3584]{1,0:T(8,128)(2,1)}) custom-call(bf16[32,896]{1,0:T(8,128)(2,1)S(1)} %collective-permute-done.21.refs_0_, bf16[32,896]{1,0:T(8,128)(2,1)S(1)} %collective-permute-done.23.refs_1_, bf16[32,896]{1,0:T(8,128)(2,1)S(1)} %collective-permute-done.25.refs_2_, ...), custom_call_target="tpu_custom_call" | custom-call | tf_op jit(solution)/shard_map/pallas_call | solution.py:460
  (4 shorter events, 0.0 us)
Async XLA Ops:
  0.6 11.2 %copy-start = (bf16[1,3584,1024]{2,1,0:T(8,128)(2,1)S(1)}, bf16[1,3584,1024]{2,1,0:T(8,128)(2,1)}, u32[]{:S(2)}) copy-start(bf16[1,3584,1024]{2,1,0:T(8,128)(2,1)} %refs_6_.1) | copy-start | bytes 22020100
  0.6 11.2 %copy-start.1 = (bf16[1,3584,1024]{2,1,0:T(8,128)(2,1)S(1)}, bf16[1,3584,1024]{2,1,0:T(8,128)(2,1)}, u32[]{:S(2)}) copy-start(bf16[1,3584,1024]{2,1,0:T(8,128)(2,1)} %refs_7_.1) | copy-start | bytes 22020100
  0.7 11.2 %copy-start.2 = (bf16[1,1024,3584]{2,1,0:T(8,128)(2,1)S(1)}, bf16[1,1024,3584]{2,1,0:T(8,128)(2,1)}, u32[]{:S(2)}) copy-start(bf16[1,1024,3584]{2,1,0:T(8,128)(2,1)} %refs_8_.1) | copy-start | bytes 22020100
  2.1 5.9 %collective-permute-start = (bf16[32,1024]{1,0:T(8,128)(2,1)S(1)}, bf16[32,1024]{1,0:T(8,128)(2,1)S(1)}, u32[]{:S(2)}, u32[]{:S(2)}) collective-permute-start(bf16[32,1024]{1,0:T(8,128)(2,1)S(1)} %get-tuple-element.31), channel_id=1, source_target_pairs={{0,7},{1,6},{2,5},{3,4},{4,3},{5,2},{6,1},{7,0},{8,15},{9,14},{10,... | collective-permute-start | bytes 196616 | tf_op jit(solution)/shard_map/ppermute | solution.py:476
  5.5 3.9 %collective-permute-start.2 = (bf16[32,1024]{1,0:T(8,128)(2,1)S(1)}, bf16[32,1024]{1,0:T(8,128)(2,1)S(1)}, u32[]{:S(2)}, u32[]{:S(2)}) collective-permute-start(bf16[32,1024]{1,0:T(8,128)(2,1)S(1)} %get-tuple-element.32), channel_id=1, source_target_pairs={{0,5},{1,4},{2,7},{3,6},{4,1},{5,0},{6,3},{7,2},{8,13},{9,12},{10,... | collective-permute-start | bytes 196616 | tf_op jit(solution)/shard_map/ppermute | solution.py:476
  6.3 4.3 %collective-permute-start.4 = (bf16[32,1024]{1,0:T(8,128)(2,1)S(1)}, bf16[32,1024]{1,0:T(8,128)(2,1)S(1)}, u32[]{:S(2)}, u32[]{:S(2)}) collective-permute-start(bf16[32,1024]{1,0:T(8,128)(2,1)S(1)} %get-tuple-element.33), channel_id=1, source_target_pairs={{0,3},{1,2},{2,1},{3,0},{4,7},{5,6},{6,5},{7,4},{8,11},{9,10},{10,... | collective-permute-start | bytes 196616 | tf_op jit(solution)/shard_map/ppermute | solution.py:476
  6.4 5.3 %collective-permute-start.6 = (bf16[32,1024]{1,0:T(8,128)(2,1)S(1)}, bf16[32,1024]{1,0:T(8,128)(2,1)S(1)}, u32[]{:S(2)}, u32[]{:S(2)}) collective-permute-start(bf16[32,1024]{1,0:T(8,128)(2,1)S(1)} %get-tuple-element.34.refs_0_.refs_3_), channel_id=1, source_target_pairs={{0,1},{1,0},{2,3},{3,2},{4,5},{5,4},{6,7},{7,6},{8,9},{9,8},{10,11... | collective-permute-start | bytes 196616 | tf_op jit(solution)/shard_map/ppermute | solution.py:479
  8.0 3.7 %collective-permute-start.1 = (bf16[32,1024]{1,0:T(8,128)(2,1)S(1)}, bf16[32,1024]{1,0:T(8,128)(2,1)S(1)}, u32[]{:S(2)}, u32[]{:S(2)}) collective-permute-start(bf16[32,1024]{1,0:T(8,128)(2,1)S(1)} %collective-permute-done.refs_4_), channel_id=1, source_target_pairs={{0,1},{1,0},{2,3},{3,2},{4,5},{5,4},{6,7},{7,6},{8,9},{9,8},{10,11... | collective-permute-start | bytes 196616 | tf_op jit(solution)/shard_map/ppermute | solution.py:479
  9.4 2.4 %collective-permute-start.3 = (bf16[32,1024]{1,0:T(8,128)(2,1)S(1)}, bf16[32,1024]{1,0:T(8,128)(2,1)S(1)}, u32[]{:S(2)}, u32[]{:S(2)}) collective-permute-start(bf16[32,1024]{1,0:T(8,128)(2,1)S(1)} %collective-permute-done.2.refs_5_), channel_id=1, source_target_pairs={{0,1},{1,0},{2,3},{3,2},{4,5},{5,4},{6,7},{7,6},{8,9},{9,8},{10,11... | collective-permute-start | bytes 196616 | tf_op jit(solution)/shard_map/ppermute | solution.py:479
  10.6 1.3 %collective-permute-start.5 = (bf16[32,1024]{1,0:T(8,128)(2,1)S(1)}, bf16[32,1024]{1,0:T(8,128)(2,1)S(1)}, u32[]{:S(2)}, u32[]{:S(2)}) collective-permute-start(bf16[32,1024]{1,0:T(8,128)(2,1)S(1)} %collective-permute-done.4.refs_6_), channel_id=1, source_target_pairs={{0,1},{1,0},{2,3},{3,2},{4,5},{5,4},{6,7},{7,6},{8,9},{9,8},{10,11... | collective-permute-start | bytes 196616 | tf_op jit(solution)/shard_map/ppermute | solution.py:479
  15.5 1.4 %collective-permute-start.7 = (bf16[64,1024]{1,0:T(8,128)(2,1)S(1)}, bf16[64,1024]{1,0:T(8,128)(2,1)S(1)}, u32[]{:S(2)}, u32[]{:S(2)}) collective-permute-start(bf16[64,1024]{1,0:T(8,128)(2,1)S(1)} %get-tuple-element.40), channel_id=1, source_target_pairs={{0,1},{1,0},{2,3},{3,2},{4,5},{5,4},{6,7},{7,6},{8,9},{9,8},{10,11... | collective-permute-start | bytes 393224 | tf_op jit(solution)/shard_map/ppermute | solution.py:555
  15.9 6.4 %collective-permute-start.12 = (bf16[80,896]{1,0:T(8,128)(2,1)S(1)}, bf16[80,896]{1,0:T(8,128)(2,1)S(1)}, u32[]{:S(2)}, u32[]{:S(2)}) collective-permute-start(bf16[80,896]{1,0:T(8,128)(2,1)S(1)} %get-tuple-element.45.refs_1_), channel_id=1, source_target_pairs={{0,1},{1,0},{2,3},{3,2},{4,5},{5,4},{6,7},{7,6},{8,9},{9,8},{10,11... | collective-permute-start | bytes 430088 | tf_op jit(solution)/shard_map/ppermute | solution.py:553
  17.0 5.7 %collective-permute-start.10 = (bf16[32,1024]{1,0:T(8,128)(2,1)S(1)}, bf16[32,1024]{1,0:T(8,128)(2,1)S(1)}, u32[]{:S(2)}, u32[]{:S(2)}) collective-permute-start(bf16[32,1024]{1,0:T(8,128)(2,1)S(1)} %get-tuple-element.43), channel_id=1, source_target_pairs={{0,15},{1,7},{2,13},{3,5},{4,11},{5,3},{6,9},{7,1},{8,23},{9,6},{1... | collective-permute-start | bytes 196616 | tf_op jit(solution)/shard_map/ppermute | solution.py:558
  19.5 4.6 %collective-permute-start.11 = (bf16[32,1024]{1,0:T(8,128)(2,1)S(1)}, bf16[32,1024]{1,0:T(8,128)(2,1)S(1)}, u32[]{:S(2)}, u32[]{:S(2)}) collective-permute-start(bf16[32,1024]{1,0:T(8,128)(2,1)S(1)} %get-tuple-element.44), channel_id=1, source_target_pairs={{0,13},{1,5},{2,15},{3,7},{4,9},{5,1},{6,11},{7,3},{8,21},{9,4},{1... | collective-permute-start | bytes 196616 | tf_op jit(solution)/shard_map/ppermute | solution.py:558
  20.6 4.6 %collective-permute-start.8 = (bf16[32,1024]{1,0:T(8,128)(2,1)S(1)}, bf16[32,1024]{1,0:T(8,128)(2,1)S(1)}, u32[]{:S(2)}, u32[]{:S(2)}) collective-permute-start(bf16[32,1024]{1,0:T(8,128)(2,1)S(1)} %get-tuple-element.41), channel_id=1, source_target_pairs={{0,11},{1,3},{2,9},{3,1},{4,15},{5,7},{6,13},{7,5},{8,19},{9,2},{1... | collective-permute-start | bytes 196616 | tf_op jit(solution)/shard_map/ppermute | solution.py:558
  22.1 3.7 %collective-permute-start.9 = (bf16[32,1024]{1,0:T(8,128)(2,1)S(1)}, bf16[32,1024]{1,0:T(8,128)(2,1)S(1)}, u32[]{:S(2)}, u32[]{:S(2)}) collective-permute-start(bf16[32,1024]{1,0:T(8,128)(2,1)S(1)} %get-tuple-element.42), channel_id=1, source_target_pairs={{0,9},{1,3},{2,11},{3,1},{4,13},{5,7},{6,15},{7,5},{8,17},{9,0},{1... | collective-permute-start | bytes 196616 | tf_op jit(solution)/shard_map/ppermute | solution.py:558
  26.2 4.7 %collective-permute-start.13 = (bf16[32,896]{1,0:T(8,128)(2,1)S(1)}, bf16[32,896]{1,0:T(8,128)(2,1)S(1)}, u32[]{:S(2)}, u32[]{:S(2)}) collective-permute-start(bf16[32,896]{1,0:T(8,128)(2,1)S(1)} %get-tuple-element.48), channel_id=1, source_target_pairs={{0,7},{1,6},{2,5},{3,4},{4,3},{5,2},{6,1},{7,0},{8,15},{9,14},{10,... | collective-permute-start | bytes 172040 | tf_op jit(solution)/shard_map/ppermute | solution.py:476
  26.3 5.1 %collective-permute-start.15 = (bf16[32,896]{1,0:T(8,128)(2,1)S(1)}, bf16[32,896]{1,0:T(8,128)(2,1)S(1)}, u32[]{:S(2)}, u32[]{:S(2)}) collective-permute-start(bf16[32,896]{1,0:T(8,128)(2,1)S(1)} %get-tuple-element.49), channel_id=1, source_target_pairs={{0,5},{1,4},{2,7},{3,6},{4,1},{5,0},{6,3},{7,2},{8,13},{9,12},{10,... | collective-permute-start | bytes 172040 | tf_op jit(solution)/shard_map/ppermute | solution.py:476
  28.7 3.7 %collective-permute-start.17 = (bf16[32,896]{1,0:T(8,128)(2,1)S(1)}, bf16[32,896]{1,0:T(8,128)(2,1)S(1)}, u32[]{:S(2)}, u32[]{:S(2)}) collective-permute-start(bf16[32,896]{1,0:T(8,128)(2,1)S(1)} %get-tuple-element.50), channel_id=1, source_target_pairs={{0,3},{1,2},{2,1},{3,0},{4,7},{5,6},{6,5},{7,4},{8,11},{9,10},{10,... | collective-permute-start | bytes 172040 | tf_op jit(solution)/shard_map/ppermute | solution.py:476
  29.0 3.4 %collective-permute-start.19 = (bf16[32,896]{1,0:T(8,128)(2,1)S(1)}, bf16[32,896]{1,0:T(8,128)(2,1)S(1)}, u32[]{:S(2)}, u32[]{:S(2)}) collective-permute-start(bf16[32,896]{1,0:T(8,128)(2,1)S(1)} %get-tuple-element.51.refs_3_), channel_id=1, source_target_pairs={{0,1},{1,0},{2,3},{3,2},{4,5},{5,4},{6,7},{7,6},{8,9},{9,8},{10,11... | collective-permute-start | bytes 172040 | tf_op jit(solution)/shard_map/ppermute | solution.py:479
  30.8 1.6 %collective-permute-start.14 = (bf16[32,896]{1,0:T(8,128)(2,1)S(1)}, bf16[32,896]{1,0:T(8,128)(2,1)S(1)}, u32[]{:S(2)}, u32[]{:S(2)}) collective-permute-start(bf16[32,896]{1,0:T(8,128)(2,1)S(1)} %collective-permute-done.13.refs_4_), channel_id=1, source_target_pairs={{0,1},{1,0},{2,3},{3,2},{4,5},{5,4},{6,7},{7,6},{8,9},{9,8},{10,11... | collective-permute-start | bytes 172040 | tf_op jit(solution)/shard_map/ppermute | solution.py:479
  31.4 1.5 %collective-permute-start.16 = (bf16[32,896]{1,0:T(8,128)(2,1)S(1)}, bf16[32,896]{1,0:T(8,128)(2,1)S(1)}, u32[]{:S(2)}, u32[]{:S(2)}) collective-permute-start(bf16[32,896]{1,0:T(8,128)(2,1)S(1)} %collective-permute-done.15.refs_5_), channel_id=1, source_target_pairs={{0,1},{1,0},{2,3},{3,2},{4,5},{5,4},{6,7},{7,6},{8,9},{9,8},{10,11... | collective-permute-start | bytes 172040 | tf_op jit(solution)/shard_map/ppermute | solution.py:479
  32.4 1.2 %collective-permute-start.18 = (bf16[32,896]{1,0:T(8,128)(2,1)S(1)}, bf16[32,896]{1,0:T(8,128)(2,1)S(1)}, u32[]{:S(2)}, u32[]{:S(2)}) collective-permute-start(bf16[32,896]{1,0:T(8,128)(2,1)S(1)} %collective-permute-done.17.refs_6_), channel_id=1, source_target_pairs={{0,1},{1,0},{2,3},{3,2},{4,5},{5,4},{6,7},{7,6},{8,9},{9,8},{10,11... | collective-permute-start | bytes 172040 | tf_op jit(solution)/shard_map/ppermute | solution.py:479
  37.3 4.9 %collective-permute-start.20 = (bf16[32,896]{1,0:T(8,128)(2,1)S(1)}, bf16[32,896]{1,0:T(8,128)(2,1)S(1)}, u32[]{:S(2)}, u32[]{:S(2)}) collective-permute-start(bf16[32,896]{1,0:T(8,128)(2,1)S(1)} %get-tuple-element.53), channel_id=1, source_target_pairs={{0,7},{1,6},{2,5},{3,4},{4,3},{5,2},{6,1},{7,0},{8,15},{9,14},{10,... | collective-permute-start | bytes 172040 | tf_op jit(solution)/shard_map/ppermute | solution.py:476
  38.8 4.9 %collective-permute-start.22 = (bf16[32,896]{1,0:T(8,128)(2,1)S(1)}, bf16[32,896]{1,0:T(8,128)(2,1)S(1)}, u32[]{:S(2)}, u32[]{:S(2)}) collective-permute-start(bf16[32,896]{1,0:T(8,128)(2,1)S(1)} %get-tuple-element.54), channel_id=1, source_target_pairs={{0,5},{1,4},{2,7},{3,6},{4,1},{5,0},{6,3},{7,2},{8,13},{9,12},{10,... | collective-permute-start | bytes 172040 | tf_op jit(solution)/shard_map/ppermute | solution.py:476
  39.7 4.1 %collective-permute-start.24 = (bf16[32,896]{1,0:T(8,128)(2,1)S(1)}, bf16[32,896]{1,0:T(8,128)(2,1)S(1)}, u32[]{:S(2)}, u32[]{:S(2)}) collective-permute-start(bf16[32,896]{1,0:T(8,128)(2,1)S(1)} %get-tuple-element.55), channel_id=1, source_target_pairs={{0,3},{1,2},{2,1},{3,0},{4,7},{5,6},{6,5},{7,4},{8,11},{9,10},{10,... | collective-permute-start | bytes 172040 | tf_op jit(solution)/shard_map/ppermute | solution.py:476
  40.4 3.8 %collective-permute-start.26 = (bf16[32,896]{1,0:T(8,128)(2,1)S(1)}, bf16[32,896]{1,0:T(8,128)(2,1)S(1)}, u32[]{:S(2)}, u32[]{:S(2)}) collective-permute-start(bf16[32,896]{1,0:T(8,128)(2,1)S(1)} %get-tuple-element.56.refs_3_), channel_id=1, source_target_pairs={{0,1},{1,0},{2,3},{3,2},{4,5},{5,4},{6,7},{7,6},{8,9},{9,8},{10,11... | collective-permute-start | bytes 172040 | tf_op jit(solution)/shard_map/ppermute | solution.py:479
  42.2 2.0 %collective-permute-start.21 = (bf16[32,896]{1,0:T(8,128)(2,1)S(1)}, bf16[32,896]{1,0:T(8,128)(2,1)S(1)}, u32[]{:S(2)}, u32[]{:S(2)}) collective-permute-start(bf16[32,896]{1,0:T(8,128)(2,1)S(1)} %collective-permute-done.20.refs_4_), channel_id=1, source_target_pairs={{0,1},{1,0},{2,3},{3,2},{4,5},{5,4},{6,7},{7,6},{8,9},{9,8},{10,11... | collective-permute-start | bytes 172040 | tf_op jit(solution)/shard_map/ppermute | solution.py:479
  43.7 1.2 %collective-permute-start.23 = (bf16[32,896]{1,0:T(8,128)(2,1)S(1)}, bf16[32,896]{1,0:T(8,128)(2,1)S(1)}, u32[]{:S(2)}, u32[]{:S(2)}) collective-permute-start(bf16[32,896]{1,0:T(8,128)(2,1)S(1)} %collective-permute-done.22.refs_5_), channel_id=1, source_target_pairs={{0,1},{1,0},{2,3},{3,2},{4,5},{5,4},{6,7},{7,6},{8,9},{9,8},{10,11... | collective-permute-start | bytes 172040 | tf_op jit(solution)/shard_map/ppermute | solution.py:479
  43.8 1.3 %collective-permute-start.25 = (bf16[32,896]{1,0:T(8,128)(2,1)S(1)}, bf16[32,896]{1,0:T(8,128)(2,1)S(1)}, u32[]{:S(2)}, u32[]{:S(2)}) collective-permute-start(bf16[32,896]{1,0:T(8,128)(2,1)S(1)} %collective-permute-done.24.refs_6_), channel_id=1, source_target_pairs={{0,1},{1,0},{2,3},{3,2},{4,5},{5,4},{6,7},{7,6},{8,9},{9,8},{10,11... | collective-permute-start | bytes 172040 | tf_op jit(solution)/shard_map/ppermute | solution.py:479

commit v7 on v6

--- a/solution.py
+++ b/solution.py
@@ -471,13 +471,13 @@
 def exchanged(arrays):
     last = len(arrays) - 1
     devices = range(2 * len(arrays))
-    sibling = [(i, i ^ 1) for i in devices]
-    arrived = [
-        lax.ppermute(arrays[j], "expert", [(i, i ^ (2 * (last - j)) ^ 1) for i in devices])
-        for j in range(last)
-    ]
-    passed = [lax.ppermute(x, "expert", sibling) for x in arrived + [arrays[last]]]
-    return tuple(passed[:last] + [arrays[last]] + arrived + passed[last:])
+
+    def sent(value, flip):
+        return lax.ppermute(value, "expert", [(i, i ^ flip) for i in devices])
+
+    arrived = [sent(x, 2 * (last - j) + 1) for j, x in enumerate(arrays[:last])]
+    passed = [sent(x, 1) for x in arrived[:-1]] + [sent(arrays[last - 1], 2)]
+    return (*passed, arrays[last], *arrived, sent(arrays[last], 1))
 
 
 def relay_pairs(k, pipe, experts):

time: 46.2 us -> 45.6 us (0.987)
  waiting for transfers between devices: 14.5 us -> 9.38 us
  starting transfers between devices: 19.3 us -> 23.9 us
    ppermute x21, waiting for transfers between devices: 10.6 us -> 5.4 us  [sent(): return lax.ppermute(value, 'expert', [(i, i ^ flip) for i in devices])]
    ppermute x21, starting transfers between devices: 13.4 us -> 17.8 us  [sent(): return lax.ppermute(value, 'expert', [(i, i ^ flip) for i in devices])]
  transfers between devices with their start and end apart: 27 -> 27, of which waited for: 17 -> 11; matrix products, arithmetic and copies ran while one was open for 0% -> 0% of each run, Pallas kernels for 3% -> 3%
where the time goes in v7:
time: 45.6 us; the launch traced here: 45.5 us
  starting transfers between devices  23.9 us (52%)
  Pallas kernels  11.4 us (25%)
  waiting for transfers between devices  9.38 us (21%)
  between operations  0.82 us (2%)
    ppermute x21, starting transfers between devices, sent(): return lax.ppermute(value, 'expert', [(i, i ^ flip) for i in devices])  17.8 us
    pallas_call x8, Pallas kernels, local_call(): pl.pallas_call(body, out_shape=outs, in_specs=[VMEM_SPEC] * len(close) +...  11.4 us
    ppermute x4, starting transfers between devices, single_shards(): lax.ppermute(x, ('pipe', 'expert'), relay_pairs(chips - 1 - j, pipe, expe...  5.53 us
    ppermute x21, waiting for transfers between devices, sent(): return lax.ppermute(value, 'expert', [(i, i ^ flip) for i in devices])  5.4 us
    ppermute x4, waiting for transfers between devices, single_shards(): lax.ppermute(x, ('pipe', 'expert'), relay_pairs(chips - 1 - j, pipe, expe...  3.12 us
  transfers between devices with their start and end apart: 27, of which 11 were waited for; matrix products, arithmetic and copies ran while one was open for 0% of the time, Pallas kernels for 3%

profile of v7, /device:TPU:0, one launch (start us, length us, event | category | flops | bytes accessed | tf_op | source)
XLA Modules:
  0.0 45.5 jit_solution(7869334777850608670)
XLA Ops:
  0.6 0.0 copy-start
  0.6 0.0 copy-start.1
  0.7 0.0 copy-start.2
  0.7 1.4 %shard_map.122 = (bf16[32,1024]{1,0:T(8,128)(2,1)S(1)}, bf16[32,1024]{1,0:T(8,128)(2,1)S(1)}, bf16[32,1024]{1,0:T(8,128)(2,1)S(1)}, bf16[32,1024]{1,0:T(8,128)(2,1)S(1)}, bf16[80,896]{1,0:T(8,128)(2,1)S(1)}) custom-call(bf16[1,16,3584]{2,1,0:T(8,128)(2,1)} %refs_0_.1, bf16[1,16,3584]{2,1,0:T(8,128)(2,1)} %refs_1_.1, s32[2,1,1,16]{3,2,1,0:T(1,128)} %bitcast.19, ...), custom_call_target="tpu_custom_call" | custom-call | tf_op jit(solution)/shard_map/pallas_call | solution.py:460
  2.1 3.4 %collective-permute-start = (bf16[32,1024]{1,0:T(8,128)(2,1)S(1)}, bf16[32,1024]{1,0:T(8,128)(2,1)S(1)}, u32[]{:S(2)}, u32[]{:S(2)}) collective-permute-start(bf16[32,1024]{1,0:T(8,128)(2,1)S(1)} %get-tuple-element.31), channel_id=1, source_target_pairs={{0,7},{1,6},{2,5},{3,4},{4,3},{5,2},{6,1},{7,0},{8,15},{9,14},{10,... | collective-permute-start | bytes 196616 | tf_op jit(solution)/shard_map/ppermute | solution.py:476
  5.5 0.8 %collective-permute-start.2 = (bf16[32,1024]{1,0:T(8,128)(2,1)S(1)}, bf16[32,1024]{1,0:T(8,128)(2,1)S(1)}, u32[]{:S(2)}, u32[]{:S(2)}) collective-permute-start(bf16[32,1024]{1,0:T(8,128)(2,1)S(1)} %get-tuple-element.32), channel_id=1, source_target_pairs={{0,5},{1,4},{2,7},{3,6},{4,1},{5,0},{6,3},{7,2},{8,13},{9,12},{10,... | collective-permute-start | bytes 196616 | tf_op jit(solution)/shard_map/ppermute | solution.py:476
  6.3 0.0 collective-permute-start.4
  6.3 1.2 %collective-permute-start.5 = (bf16[32,1024]{1,0:T(8,128)(2,1)S(1)}, bf16[32,1024]{1,0:T(8,128)(2,1)S(1)}, u32[]{:S(2)}, u32[]{:S(2)}) collective-permute-start(bf16[32,1024]{1,0:T(8,128)(2,1)S(1)} %get-tuple-element.33), channel_id=1, source_target_pairs={{0,3},{1,2},{2,1},{3,0},{4,7},{5,6},{6,5},{7,4},{8,11},{9,10},{10,... | collective-permute-start | bytes 196616 | tf_op jit(solution)/shard_map/ppermute | solution.py:476
  7.5 0.9 %collective-permute-start.6 = (bf16[32,1024]{1,0:T(8,128)(2,1)S(1)}, bf16[32,1024]{1,0:T(8,128)(2,1)S(1)}, u32[]{:S(2)}, u32[]{:S(2)}) collective-permute-start(bf16[32,1024]{1,0:T(8,128)(2,1)S(1)} %get-tuple-element.34.refs_0_.refs_3_), channel_id=1, source_target_pairs={{0,1},{1,0},{2,3},{3,2},{4,5},{5,4},{6,7},{7,6},{8,9},{9,8},{10,11... | collective-permute-start | bytes 196616 | tf_op jit(solution)/shard_map/ppermute | solution.py:476
  8.4 0.0 collective-permute-done.refs_4_
  8.4 0.0 collective-permute-start.1
  8.4 0.9 %collective-permute-done.2.refs_5_ = bf16[32,1024]{1,0:T(8,128)(2,1)S(1)} collective-permute-done((bf16[32,1024]{1,0:T(8,128)(2,1)S(1)}, bf16[32,1024]{1,0:T(8,128)(2,1)S(1)}, u32[]{:S(2)}, u32[]{:S(2)}) %collective-permute-start.2) | collective-permute-done | bytes 65568 | tf_op jit(solution)/shard_map/ppermute | solution.py:476
  9.4 0.8 %collective-permute-start.3 = (bf16[32,1024]{1,0:T(8,128)(2,1)S(1)}, bf16[32,1024]{1,0:T(8,128)(2,1)S(1)}, u32[]{:S(2)}, u32[]{:S(2)}) collective-permute-start(bf16[32,1024]{1,0:T(8,128)(2,1)S(1)} %collective-permute-done.2.refs_5_), channel_id=1, source_target_pairs={{0,1},{1,0},{2,3},{3,2},{4,5},{5,4},{6,7},{7,6},{8,9},{9,8},{10,11... | collective-permute-start | bytes 196616 | tf_op jit(solution)/shard_map/ppermute | solution.py:476
  10.2 1.0 %shard_map.123 = (bf16[128,256]{1,0:T(8,128)(2,1)S(1)}, bf16[128,256]{1,0:T(8,128)(2,1)S(1)}, bf16[128,128]{1,0:T(8,128)(2,1)S(1)}, bf16[128,128]{1,0:T(8,128)(2...) custom-call(bf16[32,1024]{1,0:T(8,128)(2,1)S(1)} %get-tuple-element.34.refs_0_.refs_3_, s32[2,1,1,16]{3,2,1,0:T(1,128)} %bitcast.20, ...), custom_call_target="tpu_custom_call" | custom-call | tf_op jit(solution)/shard_map/pallas_call | solution.py:460
  11.2 0.0 collective-permute-done.6.refs_7_
  11.2 0.0 collective-permute-done.4.refs_2_
  11.2 0.0 collective-permute-done.5.refs_6_
  11.2 0.0 collective-permute-done.1.refs_0_
  11.2 0.0 collective-permute-done.3.refs_1_
  11.2 3.7 %shard_map.124 = (bf16[64,1024]{1,0:T(8,128)(2,1)S(1)}, bf16[64,1024]{1,0:T(8,128)(2,1)S(1)}) custom-call(bf16[32,1024]{1,0:T(8,128)(2,1)S(1)} %collective-permute-done.1.refs_0_, bf16[32,1024]{1,0:T(8,128)(2,1)S(1)} %collective-permute-done.3.refs_1_, bf16[32,1024]{1,0:T(8,128)(2,1)S(1)} %collective-permute-done.4.refs_2_, ...), custom_call_target="tpu_custom_call" | custom-call | tf_op jit(solution)/shard_map/pallas_call | solution.py:460
  14.9 0.5 collective-permute-start.7
  15.4 0.1 collective-permute-start.12
  15.5 0.9 %collective-permute-done.7.refs_1_ = bf16[64,1024]{1,0:T(8,128)(2,1)S(1)} collective-permute-done((bf16[64,1024]{1,0:T(8,128)(2,1)S(1)}, bf16[64,1024]{1,0:T(8,128)(2,1)S(1)}, u32[]{:S(2)}, u32[]{:S(2)}) %collective-permute-start.7) | collective-permute-done | bytes 131104 | tf_op jit(solution)/shard_map/ppermute | solution.py:555
  16.4 3.0 %collective-permute-start.10 = (bf16[32,1024]{1,0:T(8,128)(2,1)S(1)}, bf16[32,1024]{1,0:T(8,128)(2,1)S(1)}, u32[]{:S(2)}, u32[]{:S(2)}) collective-permute-start(bf16[32,1024]{1,0:T(8,128)(2,1)S(1)} %get-tuple-element.43), channel_id=1, source_target_pairs={{0,15},{1,7},{2,13},{3,5},{4,11},{5,3},{6,9},{7,1},{8,23},{9,6},{1... | collective-permute-start | bytes 196616 | tf_op jit(solution)/shard_map/ppermute | solution.py:558
  19.4 1.2 %collective-permute-start.11 = (bf16[32,1024]{1,0:T(8,128)(2,1)S(1)}, bf16[32,1024]{1,0:T(8,128)(2,1)S(1)}, u32[]{:S(2)}, u32[]{:S(2)}) collective-permute-start(bf16[32,1024]{1,0:T(8,128)(2,1)S(1)} %get-tuple-element.44), channel_id=1, source_target_pairs={{0,13},{1,5},{2,15},{3,7},{4,9},{5,1},{6,11},{7,3},{8,21},{9,4},{1... | collective-permute-start | bytes 196616 | tf_op jit(solution)/shard_map/ppermute | solution.py:558
  20.6 1.1 %collective-permute-start.8 = (bf16[32,1024]{1,0:T(8,128)(2,1)S(1)}, bf16[32,1024]{1,0:T(8,128)(2,1)S(1)}, u32[]{:S(2)}, u32[]{:S(2)}) collective-permute-start(bf16[32,1024]{1,0:T(8,128)(2,1)S(1)} %get-tuple-element.41), channel_id=1, source_target_pairs={{0,11},{1,3},{2,9},{3,1},{4,15},{5,7},{6,13},{7,5},{8,19},{9,2},{1... | collective-permute-start | bytes 196616 | tf_op jit(solution)/shard_map/ppermute | solution.py:558
  21.7 0.2 collective-permute-start.9
  21.9 0.0 collective-permute-done.12.refs_2_
  21.9 0.3 shard_map.126
  22.2 0.0 collective-permute-done.10.refs_2_
  22.2 1.8 %collective-permute-done.11.refs_3_ = bf16[32,1024]{1,0:T(8,128)(2,1)S(1)} collective-permute-done((bf16[32,1024]{1,0:T(8,128)(2,1)S(1)}, bf16[32,1024]{1,0:T(8,128)(2,1)S(1)}, u32[]{:S(2)}, u32[]{:S(2)}) %collective-permute-start.11) | collective-permute-done | bytes 65568 | tf_op jit(solution)/shard_map/ppermute | solution.py:558
  24.0 1.2 %collective-permute-done.8.refs_0_ = bf16[32,1024]{1,0:T(8,128)(2,1)S(1)} collective-permute-done((bf16[32,1024]{1,0:T(8,128)(2,1)S(1)}, bf16[32,1024]{1,0:T(8,128)(2,1)S(1)}, u32[]{:S(2)}, u32[]{:S(2)}) %collective-permute-start.8) | collective-permute-done | bytes 65568 | tf_op jit(solution)/shard_map/ppermute | solution.py:558
  25.2 0.2 collective-permute-done.9.refs_1_
  25.4 0.4 shard_map.127
  25.7 0.1 collective-permute-start.13
  25.8 2.9 %collective-permute-start.15 = (bf16[32,896]{1,0:T(8,128)(2,1)S(1)}, bf16[32,896]{1,0:T(8,128)(2,1)S(1)}, u32[]{:S(2)}, u32[]{:S(2)}) collective-permute-start(bf16[32,896]{1,0:T(8,128)(2,1)S(1)} %get-tuple-element.49), channel_id=1, source_target_pairs={{0,5},{1,4},{2,7},{3,6},{4,1},{5,0},{6,3},{7,2},{8,13},{9,12},{10,... | collective-permute-start | bytes 172040 | tf_op jit(solution)/shard_map/ppermute | solution.py:476
  28.7 0.3 collective-permute-start.17
  29.0 0.1 collective-permute-start.18
  29.1 1.7 %collective-permute-start.19 = (bf16[32,896]{1,0:T(8,128)(2,1)S(1)}, bf16[32,896]{1,0:T(8,128)(2,1)S(1)}, u32[]{:S(2)}, u32[]{:S(2)}) collective-permute-start(bf16[32,896]{1,0:T(8,128)(2,1)S(1)} %get-tuple-element.51.refs_3_), channel_id=1, source_target_pairs={{0,1},{1,0},{2,3},{3,2},{4,5},{5,4},{6,7},{7,6},{8,9},{9,8},{10,11... | collective-permute-start | bytes 172040 | tf_op jit(solution)/shard_map/ppermute | solution.py:476
  30.8 0.0 collective-permute-done.13.refs_4_
  30.8 0.0 collective-permute-start.14
  30.8 0.3 collective-permute-done.15.refs_5_
  31.2 0.3 collective-permute-start.16
  31.5 1.7 %collective-permute-done.17.refs_2_ = bf16[32,896]{1,0:T(8,128)(2,1)S(1)} collective-permute-done((bf16[32,896]{1,0:T(8,128)(2,1)S(1)}, bf16[32,896]{1,0:T(8,128)(2,1)S(1)}, u32[]{:S(2)}, u32[]{:S(2)}) %collective-permute-start.17) | collective-permute-done | bytes 57376 | tf_op jit(solution)/shard_map/ppermute | solution.py:476
  33.2 0.0 collective-permute-done.18.refs_6_
  33.2 0.0 collective-permute-done.19.refs_7_
  33.2 0.0 collective-permute-done.14.refs_0_
  33.2 0.0 collective-permute-done.16.refs_1_
  33.3 3.7 %shard_map.128 = (bf16[32,896]{1,0:T(8,128)(2,1)S(1)}, bf16[32,896]{1,0:T(8,128)(2,1)S(1)}, bf16[32,896]{1,0:T(8,128)(2,1)S(1)}, bf16[32,896]{1,0:T(8,128)(2,1)S(1)}) custom-call(bf16[32,896]{1,0:T(8,128)(2,1)S(1)} %collective-permute-done.14.refs_0_, bf16[32,896]{1,0:T(8,128)(2,1)S(1)} %collective-permute-done.16.refs_1_, ...), custom_call_target="tpu_custom_call" | custom-call | tf_op jit(solution)/shard_map/pallas_call | solution.py:460
  36.9 1.7 %collective-permute-start.20 = (bf16[32,896]{1,0:T(8,128)(2,1)S(1)}, bf16[32,896]{1,0:T(8,128)(2,1)S(1)}, u32[]{:S(2)}, u32[]{:S(2)}) collective-permute-start(bf16[32,896]{1,0:T(8,128)(2,1)S(1)} %get-tuple-element.53), channel_id=1, source_target_pairs={{0,7},{1,6},{2,5},{3,4},{4,3},{5,2},{6,1},{7,0},{8,15},{9,14},{10,... | collective-permute-start | bytes 172040 | tf_op jit(solution)/shard_map/ppermute | solution.py:476
  38.6 0.7 %collective-permute-start.22 = (bf16[32,896]{1,0:T(8,128)(2,1)S(1)}, bf16[32,896]{1,0:T(8,128)(2,1)S(1)}, u32[]{:S(2)}, u32[]{:S(2)}) collective-permute-start(bf16[32,896]{1,0:T(8,128)(2,1)S(1)} %get-tuple-element.54), channel_id=1, source_target_pairs={{0,5},{1,4},{2,7},{3,6},{4,1},{5,0},{6,3},{7,2},{8,13},{9,12},{10,... | collective-permute-start | bytes 172040 | tf_op jit(solution)/shard_map/ppermute | solution.py:476
  39.4 0.8 %collective-permute-start.24 = (bf16[32,896]{1,0:T(8,128)(2,1)S(1)}, bf16[32,896]{1,0:T(8,128)(2,1)S(1)}, u32[]{:S(2)}, u32[]{:S(2)}) collective-permute-start(bf16[32,896]{1,0:T(8,128)(2,1)S(1)} %get-tuple-element.55), channel_id=1, source_target_pairs={{0,2},{1,3},{2,0},{3,1},{4,6},{5,7},{6,4},{7,5},{8,10},{9,11},{10,... | collective-permute-start | bytes 172040 | tf_op jit(solution)/shard_map/ppermute | solution.py:476
  40.2 0.3 collective-permute-start.25
  40.5 1.0 %collective-permute-start.26 = (bf16[32,896]{1,0:T(8,128)(2,1)S(1)}, bf16[32,896]{1,0:T(8,128)(2,1)S(1)}, u32[]{:S(2)}, u32[]{:S(2)}) collective-permute-start(bf16[32,896]{1,0:T(8,128)(2,1)S(1)} %get-tuple-element.56.refs_3_), channel_id=1, source_target_pairs={{0,1},{1,0},{2,3},{3,2},{4,5},{5,4},{6,7},{7,6},{8,9},{9,8},{10,11... | collective-permute-start | bytes 172040 | tf_op jit(solution)/shard_map/ppermute | solution.py:476
  41.5 0.0 collective-permute-done.20.refs_4_
  41.5 0.5 %collective-permute-start.21 = (bf16[32,896]{1,0:T(8,128)(2,1)S(1)}, bf16[32,896]{1,0:T(8,128)(2,1)S(1)}, u32[]{:S(2)}, u32[]{:S(2)}) collective-permute-start(bf16[32,896]{1,0:T(8,128)(2,1)S(1)} %collective-permute-done.20.refs_4_), channel_id=1, source_target_pairs={{0,1},{1,0},{2,3},{3,2},{4,5},{5,4},{6,7},{7,6},{8,9},{9,8},{10,11... | collective-permute-start | bytes 172040 | tf_op jit(solution)/shard_map/ppermute | solution.py:476
  42.0 1.3 %collective-permute-done.22.refs_5_ = bf16[32,896]{1,0:T(8,128)(2,1)S(1)} collective-permute-done((bf16[32,896]{1,0:T(8,128)(2,1)S(1)}, bf16[32,896]{1,0:T(8,128)(2,1)S(1)}, u32[]{:S(2)}, u32[]{:S(2)}) %collective-permute-start.22) | collective-permute-done | bytes 57376 | tf_op jit(solution)/shard_map/ppermute | solution.py:476
  43.3 0.2 collective-permute-start.23
  43.5 0.4 collective-permute-done.24.refs_2_
  43.9 0.6 %collective-permute-done.25.refs_6_ = bf16[32,896]{1,0:T(8,128)(2,1)S(1)} collective-permute-done((bf16[32,896]{1,0:T(8,128)(2,1)S(1)}, bf16[32,896]{1,0:T(8,128)(2,1)S(1)}, u32[]{:S(2)}, u32[]{:S(2)}) %collective-permute-start.25) | collective-permute-done | bytes 57376 | tf_op jit(solution)/shard_map/ppermute | solution.py:476
  44.4 0.0 collective-permute-done.26.refs_7_
  44.4 0.0 collective-permute-done.21.refs_0_
  44.4 0.1 collective-permute-done.23.refs_1_
  44.5 0.9 %shard_map.129 = (bf16[16,3584]{1,0:T(8,128)(2,1)}, bf16[16,3584]{1,0:T(8,128)(2,1)}) custom-call(bf16[32,896]{1,0:T(8,128)(2,1)S(1)} %collective-permute-done.21.refs_0_, bf16[32,896]{1,0:T(8,128)(2,1)S(1)} %collective-permute-done.23.refs_1_, bf16[32,896]{1,0:T(8,128)(2,1)S(1)} %collective-permute-done.24.refs_2_, ...), custom_call_target="tpu_custom_call" | custom-call | tf_op jit(solution)/shard_map/pallas_call | solution.py:460
  (4 shorter events, 0.0 us)
Async XLA Ops:
  0.6 10.6 %copy-start = (bf16[1,3584,1024]{2,1,0:T(8,128)(2,1)S(1)}, bf16[1,3584,1024]{2,1,0:T(8,128)(2,1)}, u32[]{:S(2)}) copy-start(bf16[1,3584,1024]{2,1,0:T(8,128)(2,1)} %refs_6_.1) | copy-start | bytes 22020100
  0.6 10.6 %copy-start.1 = (bf16[1,3584,1024]{2,1,0:T(8,128)(2,1)S(1)}, bf16[1,3584,1024]{2,1,0:T(8,128)(2,1)}, u32[]{:S(2)}) copy-start(bf16[1,3584,1024]{2,1,0:T(8,128)(2,1)} %refs_7_.1) | copy-start | bytes 22020100
  0.7 10.6 %copy-start.2 = (bf16[1,1024,3584]{2,1,0:T(8,128)(2,1)S(1)}, bf16[1,1024,3584]{2,1,0:T(8,128)(2,1)}, u32[]{:S(2)}) copy-start(bf16[1,1024,3584]{2,1,0:T(8,128)(2,1)} %refs_8_.1) | copy-start | bytes 22020100
  2.1 6.3 %collective-permute-start = (bf16[32,1024]{1,0:T(8,128)(2,1)S(1)}, bf16[32,1024]{1,0:T(8,128)(2,1)S(1)}, u32[]{:S(2)}, u32[]{:S(2)}) collective-permute-start(bf16[32,1024]{1,0:T(8,128)(2,1)S(1)} %get-tuple-element.31), channel_id=1, source_target_pairs={{0,7},{1,6},{2,5},{3,4},{4,3},{5,2},{6,1},{7,0},{8,15},{9,14},{10,... | collective-permute-start | bytes 196616 | tf_op jit(solution)/shard_map/ppermute | solution.py:476
  5.5 3.9 %collective-permute-start.2 = (bf16[32,1024]{1,0:T(8,128)(2,1)S(1)}, bf16[32,1024]{1,0:T(8,128)(2,1)S(1)}, u32[]{:S(2)}, u32[]{:S(2)}) collective-permute-start(bf16[32,1024]{1,0:T(8,128)(2,1)S(1)} %get-tuple-element.32), channel_id=1, source_target_pairs={{0,5},{1,4},{2,7},{3,6},{4,1},{5,0},{6,3},{7,2},{8,13},{9,12},{10,... | collective-permute-start | bytes 196616 | tf_op jit(solution)/shard_map/ppermute | solution.py:476
  6.3 4.9 %collective-permute-start.4 = (bf16[32,1024]{1,0:T(8,128)(2,1)S(1)}, bf16[32,1024]{1,0:T(8,128)(2,1)S(1)}, u32[]{:S(2)}, u32[]{:S(2)}) collective-permute-start(bf16[32,1024]{1,0:T(8,128)(2,1)S(1)} %get-tuple-element.33), channel_id=1, source_target_pairs={{0,2},{1,3},{2,0},{3,1},{4,6},{5,7},{6,4},{7,5},{8,10},{9,11},{10,... | collective-permute-start | bytes 196616 | tf_op jit(solution)/shard_map/ppermute | solution.py:476
  6.3 4.9 %collective-permute-start.5 = (bf16[32,1024]{1,0:T(8,128)(2,1)S(1)}, bf16[32,1024]{1,0:T(8,128)(2,1)S(1)}, u32[]{:S(2)}, u32[]{:S(2)}) collective-permute-start(bf16[32,1024]{1,0:T(8,128)(2,1)S(1)} %get-tuple-element.33), channel_id=1, source_target_pairs={{0,3},{1,2},{2,1},{3,0},{4,7},{5,6},{6,5},{7,4},{8,11},{9,10},{10,... | collective-permute-start | bytes 196616 | tf_op jit(solution)/shard_map/ppermute | solution.py:476
  7.5 3.6 %collective-permute-start.6 = (bf16[32,1024]{1,0:T(8,128)(2,1)S(1)}, bf16[32,1024]{1,0:T(8,128)(2,1)S(1)}, u32[]{:S(2)}, u32[]{:S(2)}) collective-permute-start(bf16[32,1024]{1,0:T(8,128)(2,1)S(1)} %get-tuple-element.34.refs_0_.refs_3_), channel_id=1, source_target_pairs={{0,1},{1,0},{2,3},{3,2},{4,5},{5,4},{6,7},{7,6},{8,9},{9,8},{10,11... | collective-permute-start | bytes 196616 | tf_op jit(solution)/shard_map/ppermute | solution.py:476
  8.4 2.8 %collective-permute-start.1 = (bf16[32,1024]{1,0:T(8,128)(2,1)S(1)}, bf16[32,1024]{1,0:T(8,128)(2,1)S(1)}, u32[]{:S(2)}, u32[]{:S(2)}) collective-permute-start(bf16[32,1024]{1,0:T(8,128)(2,1)S(1)} %collective-permute-done.refs_4_), channel_id=1, source_target_pairs={{0,1},{1,0},{2,3},{3,2},{4,5},{5,4},{6,7},{7,6},{8,9},{9,8},{10,11... | collective-permute-start | bytes 196616 | tf_op jit(solution)/shard_map/ppermute | solution.py:476
  9.4 1.9 %collective-permute-start.3 = (bf16[32,1024]{1,0:T(8,128)(2,1)S(1)}, bf16[32,1024]{1,0:T(8,128)(2,1)S(1)}, u32[]{:S(2)}, u32[]{:S(2)}) collective-permute-start(bf16[32,1024]{1,0:T(8,128)(2,1)S(1)} %collective-permute-done.2.refs_5_), channel_id=1, source_target_pairs={{0,1},{1,0},{2,3},{3,2},{4,5},{5,4},{6,7},{7,6},{8,9},{9,8},{10,11... | collective-permute-start | bytes 196616 | tf_op jit(solution)/shard_map/ppermute | solution.py:476
  14.9 1.4 %collective-permute-start.7 = (bf16[64,1024]{1,0:T(8,128)(2,1)S(1)}, bf16[64,1024]{1,0:T(8,128)(2,1)S(1)}, u32[]{:S(2)}, u32[]{:S(2)}) collective-permute-start(bf16[64,1024]{1,0:T(8,128)(2,1)S(1)} %get-tuple-element.40), channel_id=1, source_target_pairs={{0,1},{1,0},{2,3},{3,2},{4,5},{5,4},{6,7},{7,6},{8,9},{9,8},{10,11... | collective-permute-start | bytes 393224 | tf_op jit(solution)/shard_map/ppermute | solution.py:555
  15.4 6.5 %collective-permute-start.12 = (bf16[80,896]{1,0:T(8,128)(2,1)S(1)}, bf16[80,896]{1,0:T(8,128)(2,1)S(1)}, u32[]{:S(2)}, u32[]{:S(2)}) collective-permute-start(bf16[80,896]{1,0:T(8,128)(2,1)S(1)} %get-tuple-element.45.refs_1_), channel_id=1, source_target_pairs={{0,1},{1,0},{2,3},{3,2},{4,5},{5,4},{6,7},{7,6},{8,9},{9,8},{10,11... | collective-permute-start | bytes 430088 | tf_op jit(solution)/shard_map/ppermute | solution.py:553
  16.4 5.9 %collective-permute-start.10 = (bf16[32,1024]{1,0:T(8,128)(2,1)S(1)}, bf16[32,1024]{1,0:T(8,128)(2,1)S(1)}, u32[]{:S(2)}, u32[]{:S(2)}) collective-permute-start(bf16[32,1024]{1,0:T(8,128)(2,1)S(1)} %get-tuple-element.43), channel_id=1, source_target_pairs={{0,15},{1,7},{2,13},{3,5},{4,11},{5,3},{6,9},{7,1},{8,23},{9,6},{1... | collective-permute-start | bytes 196616 | tf_op jit(solution)/shard_map/ppermute | solution.py:558
  19.4 4.6 %collective-permute-start.11 = (bf16[32,1024]{1,0:T(8,128)(2,1)S(1)}, bf16[32,1024]{1,0:T(8,128)(2,1)S(1)}, u32[]{:S(2)}, u32[]{:S(2)}) collective-permute-start(bf16[32,1024]{1,0:T(8,128)(2,1)S(1)} %get-tuple-element.44), channel_id=1, source_target_pairs={{0,13},{1,5},{2,15},{3,7},{4,9},{5,1},{6,11},{7,3},{8,21},{9,4},{1... | collective-permute-start | bytes 196616 | tf_op jit(solution)/shard_map/ppermute | solution.py:558
  20.6 4.6 %collective-permute-start.8 = (bf16[32,1024]{1,0:T(8,128)(2,1)S(1)}, bf16[32,1024]{1,0:T(8,128)(2,1)S(1)}, u32[]{:S(2)}, u32[]{:S(2)}) collective-permute-start(bf16[32,1024]{1,0:T(8,128)(2,1)S(1)} %get-tuple-element.41), channel_id=1, source_target_pairs={{0,11},{1,3},{2,9},{3,1},{4,15},{5,7},{6,13},{7,5},{8,19},{9,2},{1... | collective-permute-start | bytes 196616 | tf_op jit(solution)/shard_map/ppermute | solution.py:558
  21.7 3.7 %collective-permute-start.9 = (bf16[32,1024]{1,0:T(8,128)(2,1)S(1)}, bf16[32,1024]{1,0:T(8,128)(2,1)S(1)}, u32[]{:S(2)}, u32[]{:S(2)}) collective-permute-start(bf16[32,1024]{1,0:T(8,128)(2,1)S(1)} %get-tuple-element.42), channel_id=1, source_target_pairs={{0,9},{1,3},{2,11},{3,1},{4,13},{5,7},{6,15},{7,5},{8,17},{9,0},{1... | collective-permute-start | bytes 196616 | tf_op jit(solution)/shard_map/ppermute | solution.py:558
  25.7 5.1 %collective-permute-start.13 = (bf16[32,896]{1,0:T(8,128)(2,1)S(1)}, bf16[32,896]{1,0:T(8,128)(2,1)S(1)}, u32[]{:S(2)}, u32[]{:S(2)}) collective-permute-start(bf16[32,896]{1,0:T(8,128)(2,1)S(1)} %get-tuple-element.48), channel_id=1, source_target_pairs={{0,7},{1,6},{2,5},{3,4},{4,3},{5,2},{6,1},{7,0},{8,15},{9,14},{10,... | collective-permute-start | bytes 172040 | tf_op jit(solution)/shard_map/ppermute | solution.py:476
  25.8 5.3 %collective-permute-start.15 = (bf16[32,896]{1,0:T(8,128)(2,1)S(1)}, bf16[32,896]{1,0:T(8,128)(2,1)S(1)}, u32[]{:S(2)}, u32[]{:S(2)}) collective-permute-start(bf16[32,896]{1,0:T(8,128)(2,1)S(1)} %get-tuple-element.49), channel_id=1, source_target_pairs={{0,5},{1,4},{2,7},{3,6},{4,1},{5,0},{6,3},{7,2},{8,13},{9,12},{10,... | collective-permute-start | bytes 172040 | tf_op jit(solution)/shard_map/ppermute | solution.py:476
  28.7 4.5 %collective-permute-start.17 = (bf16[32,896]{1,0:T(8,128)(2,1)S(1)}, bf16[32,896]{1,0:T(8,128)(2,1)S(1)}, u32[]{:S(2)}, u32[]{:S(2)}) collective-permute-start(bf16[32,896]{1,0:T(8,128)(2,1)S(1)} %get-tuple-element.50), channel_id=1, source_target_pairs={{0,2},{1,3},{2,0},{3,1},{4,6},{5,7},{6,4},{7,5},{8,10},{9,11},{10,... | collective-permute-start | bytes 172040 | tf_op jit(solution)/shard_map/ppermute | solution.py:476
  29.0 4.2 %collective-permute-start.18 = (bf16[32,896]{1,0:T(8,128)(2,1)S(1)}, bf16[32,896]{1,0:T(8,128)(2,1)S(1)}, u32[]{:S(2)}, u32[]{:S(2)}) collective-permute-start(bf16[32,896]{1,0:T(8,128)(2,1)S(1)} %get-tuple-element.50), channel_id=1, source_target_pairs={{0,3},{1,2},{2,1},{3,0},{4,7},{5,6},{6,5},{7,4},{8,11},{9,10},{10,... | collective-permute-start | bytes 172040 | tf_op jit(solution)/shard_map/ppermute | solution.py:476
  29.1 4.1 %collective-permute-start.19 = (bf16[32,896]{1,0:T(8,128)(2,1)S(1)}, bf16[32,896]{1,0:T(8,128)(2,1)S(1)}, u32[]{:S(2)}, u32[]{:S(2)}) collective-permute-start(bf16[32,896]{1,0:T(8,128)(2,1)S(1)} %get-tuple-element.51.refs_3_), channel_id=1, source_target_pairs={{0,1},{1,0},{2,3},{3,2},{4,5},{5,4},{6,7},{7,6},{8,9},{9,8},{10,11... | collective-permute-start | bytes 172040 | tf_op jit(solution)/shard_map/ppermute | solution.py:476
  30.8 2.4 %collective-permute-start.14 = (bf16[32,896]{1,0:T(8,128)(2,1)S(1)}, bf16[32,896]{1,0:T(8,128)(2,1)S(1)}, u32[]{:S(2)}, u32[]{:S(2)}) collective-permute-start(bf16[32,896]{1,0:T(8,128)(2,1)S(1)} %collective-permute-done.13.refs_4_), channel_id=1, source_target_pairs={{0,1},{1,0},{2,3},{3,2},{4,5},{5,4},{6,7},{7,6},{8,9},{9,8},{10,11... | collective-permute-start | bytes 172040 | tf_op jit(solution)/shard_map/ppermute | solution.py:476
  31.2 2.1 %collective-permute-start.16 = (bf16[32,896]{1,0:T(8,128)(2,1)S(1)}, bf16[32,896]{1,0:T(8,128)(2,1)S(1)}, u32[]{:S(2)}, u32[]{:S(2)}) collective-permute-start(bf16[32,896]{1,0:T(8,128)(2,1)S(1)} %collective-permute-done.15.refs_5_), channel_id=1, source_target_pairs={{0,1},{1,0},{2,3},{3,2},{4,5},{5,4},{6,7},{7,6},{8,9},{9,8},{10,11... | collective-permute-start | bytes 172040 | tf_op jit(solution)/shard_map/ppermute | solution.py:476
  36.9 4.6 %collective-permute-start.20 = (bf16[32,896]{1,0:T(8,128)(2,1)S(1)}, bf16[32,896]{1,0:T(8,128)(2,1)S(1)}, u32[]{:S(2)}, u32[]{:S(2)}) collective-permute-start(bf16[32,896]{1,0:T(8,128)(2,1)S(1)} %get-tuple-element.53), channel_id=1, source_target_pairs={{0,7},{1,6},{2,5},{3,4},{4,3},{5,2},{6,1},{7,0},{8,15},{9,14},{10,... | collective-permute-start | bytes 172040 | tf_op jit(solution)/shard_map/ppermute | solution.py:476
  38.6 4.7 %collective-permute-start.22 = (bf16[32,896]{1,0:T(8,128)(2,1)S(1)}, bf16[32,896]{1,0:T(8,128)(2,1)S(1)}, u32[]{:S(2)}, u32[]{:S(2)}) collective-permute-start(bf16[32,896]{1,0:T(8,128)(2,1)S(1)} %get-tuple-element.54), channel_id=1, source_target_pairs={{0,5},{1,4},{2,7},{3,6},{4,1},{5,0},{6,3},{7,2},{8,13},{9,12},{10,... | collective-permute-start | bytes 172040 | tf_op jit(solution)/shard_map/ppermute | solution.py:476
  39.4 4.5 %collective-permute-start.24 = (bf16[32,896]{1,0:T(8,128)(2,1)S(1)}, bf16[32,896]{1,0:T(8,128)(2,1)S(1)}, u32[]{:S(2)}, u32[]{:S(2)}) collective-permute-start(bf16[32,896]{1,0:T(8,128)(2,1)S(1)} %get-tuple-element.55), channel_id=1, source_target_pairs={{0,2},{1,3},{2,0},{3,1},{4,6},{5,7},{6,4},{7,5},{8,10},{9,11},{10,... | collective-permute-start | bytes 172040 | tf_op jit(solution)/shard_map/ppermute | solution.py:476
  40.2 4.2 %collective-permute-start.25 = (bf16[32,896]{1,0:T(8,128)(2,1)S(1)}, bf16[32,896]{1,0:T(8,128)(2,1)S(1)}, u32[]{:S(2)}, u32[]{:S(2)}) collective-permute-start(bf16[32,896]{1,0:T(8,128)(2,1)S(1)} %get-tuple-element.55), channel_id=1, source_target_pairs={{0,3},{1,2},{2,1},{3,0},{4,7},{5,6},{6,5},{7,4},{8,11},{9,10},{10,... | collective-permute-start | bytes 172040 | tf_op jit(solution)/shard_map/ppermute | solution.py:476
  40.5 3.9 %collective-permute-start.26 = (bf16[32,896]{1,0:T(8,128)(2,1)S(1)}, bf16[32,896]{1,0:T(8,128)(2,1)S(1)}, u32[]{:S(2)}, u32[]{:S(2)}) collective-permute-start(bf16[32,896]{1,0:T(8,128)(2,1)S(1)} %get-tuple-element.56.refs_3_), channel_id=1, source_target_pairs={{0,1},{1,0},{2,3},{3,2},{4,5},{5,4},{6,7},{7,6},{8,9},{9,8},{10,11... | collective-permute-start | bytes 172040 | tf_op jit(solution)/shard_map/ppermute | solution.py:476
  41.5 2.9 %collective-permute-start.21 = (bf16[32,896]{1,0:T(8,128)(2,1)S(1)}, bf16[32,896]{1,0:T(8,128)(2,1)S(1)}, u32[]{:S(2)}, u32[]{:S(2)}) collective-permute-start(bf16[32,896]{1,0:T(8,128)(2,1)S(1)} %collective-permute-done.20.refs_4_), channel_id=1, source_target_pairs={{0,1},{1,0},{2,3},{3,2},{4,5},{5,4},{6,7},{7,6},{8,9},{9,8},{10,11... | collective-permute-start | bytes 172040 | tf_op jit(solution)/shard_map/ppermute | solution.py:476
  43.3 1.2 %collective-permute-start.23 = (bf16[32,896]{1,0:T(8,128)(2,1)S(1)}, bf16[32,896]{1,0:T(8,128)(2,1)S(1)}, u32[]{:S(2)}, u32[]{:S(2)}) collective-permute-start(bf16[32,896]{1,0:T(8,128)(2,1)S(1)} %collective-permute-done.22.refs_5_), channel_id=1, source_target_pairs={{0,1},{1,0},{2,3},{3,2},{4,5},{5,4},{6,7},{7,6},{8,9},{9,8},{10,11... | collective-permute-start | bytes 172040 | tf_op jit(solution)/shard_map/ppermute | solution.py:476

commit v8 on v7

--- a/solution.py
+++ b/solution.py
@@ -445,15 +445,17 @@
 HBM_SPEC = pl.BlockSpec(memory_space=pltpu.HBM)
 
 
-def local_call(kernel, out_shapes, near, far=(), scratch=()):
+def local_call(kernel, out_shapes, near, far=(), scratch=(), order=()):
     far = [pltpu.with_memory_space_constraint(x, pltpu.HBM) for x in far]
     close, near_tree = jax.tree.flatten(tuple(near))
+    order = list(order) + list(range(len(order), len(close)))
     outs, out_tree = jax.tree.flatten(out_shapes)
 
     def body(*refs):
         refs = iter(refs)
         take = lambda count: [next(refs) for _ in range(count)]
-        args = [*near_tree.unflatten(take(len(close))), *take(len(far))]
+        fed = dict(zip(order, take(len(close))))
+        args = [*near_tree.unflatten([fed[i] for i in range(len(close))]), *take(len(far))]
         results = out_tree.unflatten(take(len(outs)))
         kernel(*args, *(results if isinstance(results, tuple) else (results,)), *refs)
 
@@ -464,7 +466,7 @@
         out_specs=[VMEM_SPEC] * len(outs),
         scratch_shapes=list(scratch),
         compiler_params=pltpu.CompilerParams(vmem_limit_bytes=8 << 20),
-    )(*close, *far)
+    )(*[close[i] for i in order], *far)
     return out_tree.unflatten(results)
 
 
@@ -478,6 +480,11 @@
     arrived = [sent(x, 2 * (last - j) + 1) for j, x in enumerate(arrays[:last])]
     passed = [sent(x, 1) for x in arrived[:-1]] + [sent(arrays[last - 1], 2)]
     return (*passed, arrays[last], *arrived, sent(arrays[last], 1))
+
+
+def start_order(chips):
+    last = chips - 1
+    return [*range(chips, chips + last - 1), last - 1, chips + last - 1, *range(last - 1), last, chips + last]
 
 
 def relay_pairs(k, pipe, experts):
@@ -485,7 +492,7 @@
     for section in range(pipe):
         for i in range(experts):
             other = section + 1 - 2 * (i % 2)
-            target = (other, i ^ (2 * k) ^ 1) if 0 <= other < pipe else (section, i ^ (2 * (k or 1)))
+            target = (other, i ^ (2 * k) ^ 1) if 0 <= other < pipe else (section, i ^ 2)
             pairs.append((section * experts + i, target[0] * experts + target[1]))
     return pairs
 
@@ -546,6 +553,7 @@
         (received, relaying, *layer),
         (),
         [x_v],
+        order=start_order(chips),
     )
     sending, entering = local_call(
         functools.partial(turn_plan_kernel, parts, slot_cap),
@@ -568,9 +576,10 @@
         (exchanged(sent), closing, *layer),
         (),
         [x_v],
+        order=start_order(chips),
     )
     result = jax.ShapeDtypeStruct((rows, features), jnp.bfloat16)
-    up_done, down_done = local_call(unpack_kernel, (result, result), (exchanged(done), back))
+    up_done, down_done = local_call(unpack_kernel, (result, result), (exchanged(done), back), order=start_order(chips))
     return (up_done[None], down_done[None])
 
 

time: 45.6 us -> 45.6 us (level)
  no operation moved by 1% of the time
where the time goes in v8:
time: 45.6 us; the launch traced here: 45.4 us
  starting transfers between devices  23.9 us (52%)
  Pallas kernels  11.4 us (25%)
  waiting for transfers between devices  9.38 us (21%)
  between operations  0.82 us (2%)
    ppermute x21, starting transfers between devices, sent(): return lax.ppermute(value, 'expert', [(i, i ^ flip) for i in devices])  17.8 us
    pallas_call x8, Pallas kernels, local_call(): pl.pallas_call(body, out_shape=outs, in_specs=[VMEM_SPEC] * len(close) +...  11.4 us
    ppermute x4, starting transfers between devices, single_shards(): lax.ppermute(x, ('pipe', 'expert'), relay_pairs(chips - 1 - j, pipe, expe...  5.53 us
    ppermute x21, waiting for transfers between devices, sent(): return lax.ppermute(value, 'expert', [(i, i ^ flip) for i in devices])  5.4 us
    ppermute x4, waiting for transfers between devices, single_shards(): lax.ppermute(x, ('pipe', 'expert'), relay_pairs(chips - 1 - j, pipe, expe...  3.12 us
  transfers between devices with their start and end apart: 27, of which 11 were waited for; matrix products, arithmetic and copies ran while one was open for 0% of the time, Pallas kernels for 3%

profile of v8, /device:TPU:0, one launch (start us, length us, event | category | flops | bytes accessed | tf_op | source)
XLA Modules:
  0.0 45.4 jit_solution(68966978906586769)
XLA Ops:
  0.6 0.0 copy-start
  0.6 0.0 copy-start.1
  0.7 0.0 copy-start.2
  0.7 1.4 %shard_map.122 = (bf16[32,1024]{1,0:T(8,128)(2,1)S(1)}, bf16[32,1024]{1,0:T(8,128)(2,1)S(1)}, bf16[32,1024]{1,0:T(8,128)(2,1)S(1)}, bf16[32,1024]{1,0:T(8,128)(2,1)S(1)}, bf16[80,896]{1,0:T(8,128)(2,1)S(1)}) custom-call(bf16[1,16,3584]{2,1,0:T(8,128)(2,1)} %refs_0_.1, bf16[1,16,3584]{2,1,0:T(8,128)(2,1)} %refs_1_.1, s32[2,1,1,16]{3,2,1,0:T(1,128)} %bitcast.19, ...), custom_call_target="tpu_custom_call" | custom-call | tf_op jit(solution)/shard_map/pallas_call | solution.py:462
  2.1 3.4 %collective-permute-start = (bf16[32,1024]{1,0:T(8,128)(2,1)S(1)}, bf16[32,1024]{1,0:T(8,128)(2,1)S(1)}, u32[]{:S(2)}, u32[]{:S(2)}) collective-permute-start(bf16[32,1024]{1,0:T(8,128)(2,1)S(1)} %get-tuple-element.31), channel_id=1, source_target_pairs={{0,7},{1,6},{2,5},{3,4},{4,3},{5,2},{6,1},{7,0},{8,15},{9,14},{10,... | collective-permute-start | bytes 196616 | tf_op jit(solution)/shard_map/ppermute | solution.py:478
  5.5 0.8 %collective-permute-start.1 = (bf16[32,1024]{1,0:T(8,128)(2,1)S(1)}, bf16[32,1024]{1,0:T(8,128)(2,1)S(1)}, u32[]{:S(2)}, u32[]{:S(2)}) collective-permute-start(bf16[32,1024]{1,0:T(8,128)(2,1)S(1)} %get-tuple-element.32), channel_id=1, source_target_pairs={{0,5},{1,4},{2,7},{3,6},{4,1},{5,0},{6,3},{7,2},{8,13},{9,12},{10,... | collective-permute-start | bytes 196616 | tf_op jit(solution)/shard_map/ppermute | solution.py:478
  6.3 0.0 collective-permute-start.2
  6.3 1.2 %collective-permute-start.3 = (bf16[32,1024]{1,0:T(8,128)(2,1)S(1)}, bf16[32,1024]{1,0:T(8,128)(2,1)S(1)}, u32[]{:S(2)}, u32[]{:S(2)}) collective-permute-start(bf16[32,1024]{1,0:T(8,128)(2,1)S(1)} %get-tuple-element.33), channel_id=1, source_target_pairs={{0,3},{1,2},{2,1},{3,0},{4,7},{5,6},{6,5},{7,4},{8,11},{9,10},{10,... | collective-permute-start | bytes 196616 | tf_op jit(solution)/shard_map/ppermute | solution.py:478
  7.5 0.9 %collective-permute-start.6 = (bf16[32,1024]{1,0:T(8,128)(2,1)S(1)}, bf16[32,1024]{1,0:T(8,128)(2,1)S(1)}, u32[]{:S(2)}, u32[]{:S(2)}) collective-permute-start(bf16[32,1024]{1,0:T(8,128)(2,1)S(1)} %get-tuple-element.34.refs_0_.refs_6_), channel_id=1, source_target_pairs={{0,1},{1,0},{2,3},{3,2},{4,5},{5,4},{6,7},{7,6},{8,9},{9,8},{10,11... | collective-permute-start | bytes 196616 | tf_op jit(solution)/shard_map/ppermute | solution.py:478
  8.4 0.0 collective-permute-done.refs_0_
  8.4 0.0 collective-permute-start.4
  8.4 0.9 %collective-permute-done.1.refs_1_ = bf16[32,1024]{1,0:T(8,128)(2,1)S(1)} collective-permute-done((bf16[32,1024]{1,0:T(8,128)(2,1)S(1)}, bf16[32,1024]{1,0:T(8,128)(2,1)S(1)}, u32[]{:S(2)}, u32[]{:S(2)}) %collective-permute-start.1) | collective-permute-done | bytes 65568 | tf_op jit(solution)/shard_map/ppermute | solution.py:478
  9.4 0.8 %collective-permute-start.5 = (bf16[32,1024]{1,0:T(8,128)(2,1)S(1)}, bf16[32,1024]{1,0:T(8,128)(2,1)S(1)}, u32[]{:S(2)}, u32[]{:S(2)}) collective-permute-start(bf16[32,1024]{1,0:T(8,128)(2,1)S(1)} %collective-permute-done.1.refs_1_), channel_id=1, source_target_pairs={{0,1},{1,0},{2,3},{3,2},{4,5},{5,4},{6,7},{7,6},{8,9},{9,8},{10,11... | collective-permute-start | bytes 196616 | tf_op jit(solution)/shard_map/ppermute | solution.py:478
  10.2 1.0 %shard_map.123 = (bf16[128,256]{1,0:T(8,128)(2,1)S(1)}, bf16[128,256]{1,0:T(8,128)(2,1)S(1)}, bf16[128,128]{1,0:T(8,128)(2,1)S(1)}, bf16[128,128]{1,0:T(8,128)(2...) custom-call(bf16[32,1024]{1,0:T(8,128)(2,1)S(1)} %get-tuple-element.34.refs_0_.refs_6_, s32[2,1,1,16]{3,2,1,0:T(1,128)} %bitcast.20, ...), custom_call_target="tpu_custom_call" | custom-call | tf_op jit(solution)/shard_map/pallas_call | solution.py:462
  11.2 0.0 collective-permute-done.6.refs_7_
  11.2 0.0 collective-permute-done.2.refs_2_
  11.2 0.0 collective-permute-done.3.refs_3_
  11.2 0.0 collective-permute-done.4.refs_4_
  11.2 0.0 collective-permute-done.5.refs_5_
  11.2 3.7 %shard_map.124 = (bf16[64,1024]{1,0:T(8,128)(2,1)S(1)}, bf16[64,1024]{1,0:T(8,128)(2,1)S(1)}) custom-call(bf16[32,1024]{1,0:T(8,128)(2,1)S(1)} %collective-permute-done.refs_0_, bf16[32,1024]{1,0:T(8,128)(2,1)S(1)} %collective-permute-done.1.refs_1_, bf16[32,1024]{1,0:T(8,128)(2,1)S(1)} %collective-permute-done.2.refs_2_, ...), custom_call_target="tpu_custom_call" | custom-call | tf_op jit(solution)/shard_map/pallas_call | solution.py:462
  14.9 0.5 collective-permute-start.7
  15.4 0.1 collective-permute-start.12
  15.5 0.9 %collective-permute-done.7.refs_1_ = bf16[64,1024]{1,0:T(8,128)(2,1)S(1)} collective-permute-done((bf16[64,1024]{1,0:T(8,128)(2,1)S(1)}, bf16[64,1024]{1,0:T(8,128)(2,1)S(1)}, u32[]{:S(2)}, u32[]{:S(2)}) %collective-permute-start.7) | collective-permute-done | bytes 131104 | tf_op jit(solution)/shard_map/ppermute | solution.py:563
  16.4 3.0 %collective-permute-start.10 = (bf16[32,1024]{1,0:T(8,128)(2,1)S(1)}, bf16[32,1024]{1,0:T(8,128)(2,1)S(1)}, u32[]{:S(2)}, u32[]{:S(2)}) collective-permute-start(bf16[32,1024]{1,0:T(8,128)(2,1)S(1)} %get-tuple-element.43), channel_id=1, source_target_pairs={{0,15},{1,3},{2,13},{3,1},{4,11},{5,7},{6,9},{7,5},{8,23},{9,6},{1... | collective-permute-start | bytes 196616 | tf_op jit(solution)/shard_map/ppermute | solution.py:566
  19.4 1.2 %collective-permute-start.11 = (bf16[32,1024]{1,0:T(8,128)(2,1)S(1)}, bf16[32,1024]{1,0:T(8,128)(2,1)S(1)}, u32[]{:S(2)}, u32[]{:S(2)}) collective-permute-start(bf16[32,1024]{1,0:T(8,128)(2,1)S(1)} %get-tuple-element.44), channel_id=1, source_target_pairs={{0,13},{1,3},{2,15},{3,1},{4,9},{5,7},{6,11},{7,5},{8,21},{9,4},{1... | collective-permute-start | bytes 196616 | tf_op jit(solution)/shard_map/ppermute | solution.py:566
  20.6 1.1 %collective-permute-start.8 = (bf16[32,1024]{1,0:T(8,128)(2,1)S(1)}, bf16[32,1024]{1,0:T(8,128)(2,1)S(1)}, u32[]{:S(2)}, u32[]{:S(2)}) collective-permute-start(bf16[32,1024]{1,0:T(8,128)(2,1)S(1)} %get-tuple-element.41), channel_id=1, source_target_pairs={{0,11},{1,3},{2,9},{3,1},{4,15},{5,7},{6,13},{7,5},{8,19},{9,2},{1... | collective-permute-start | bytes 196616 | tf_op jit(solution)/shard_map/ppermute | solution.py:566
  21.7 0.2 collective-permute-start.9
  21.9 0.0 collective-permute-done.12.refs_2_
  21.9 0.3 shard_map.126
  22.2 0.0 collective-permute-done.10.refs_2_
  22.2 1.8 %collective-permute-done.11.refs_3_ = bf16[32,1024]{1,0:T(8,128)(2,1)S(1)} collective-permute-done((bf16[32,1024]{1,0:T(8,128)(2,1)S(1)}, bf16[32,1024]{1,0:T(8,128)(2,1)S(1)}, u32[]{:S(2)}, u32[]{:S(2)}) %collective-permute-start.11) | collective-permute-done | bytes 65568 | tf_op jit(solution)/shard_map/ppermute | solution.py:566
  24.0 1.2 %collective-permute-done.8.refs_0_ = bf16[32,1024]{1,0:T(8,128)(2,1)S(1)} collective-permute-done((bf16[32,1024]{1,0:T(8,128)(2,1)S(1)}, bf16[32,1024]{1,0:T(8,128)(2,1)S(1)}, u32[]{:S(2)}, u32[]{:S(2)}) %collective-permute-start.8) | collective-permute-done | bytes 65568 | tf_op jit(solution)/shard_map/ppermute | solution.py:566
  25.2 0.2 collective-permute-done.9.refs_1_
  25.4 0.4 shard_map.127
  25.7 0.1 collective-permute-start.13
  25.8 2.9 %collective-permute-start.14 = (bf16[32,896]{1,0:T(8,128)(2,1)S(1)}, bf16[32,896]{1,0:T(8,128)(2,1)S(1)}, u32[]{:S(2)}, u32[]{:S(2)}) collective-permute-start(bf16[32,896]{1,0:T(8,128)(2,1)S(1)} %get-tuple-element.49), channel_id=1, source_target_pairs={{0,5},{1,4},{2,7},{3,6},{4,1},{5,0},{6,3},{7,2},{8,13},{9,12},{10,... | collective-permute-start | bytes 172040 | tf_op jit(solution)/shard_map/ppermute | solution.py:478
  28.7 0.3 collective-permute-start.15
  29.0 0.1 collective-permute-start.16
  29.1 1.7 %collective-permute-start.19 = (bf16[32,896]{1,0:T(8,128)(2,1)S(1)}, bf16[32,896]{1,0:T(8,128)(2,1)S(1)}, u32[]{:S(2)}, u32[]{:S(2)}) collective-permute-start(bf16[32,896]{1,0:T(8,128)(2,1)S(1)} %get-tuple-element.51.refs_6_), channel_id=1, source_target_pairs={{0,1},{1,0},{2,3},{3,2},{4,5},{5,4},{6,7},{7,6},{8,9},{9,8},{10,11... | collective-permute-start | bytes 172040 | tf_op jit(solution)/shard_map/ppermute | solution.py:478
  30.8 0.0 collective-permute-done.13.refs_0_
  30.8 0.0 collective-permute-start.17
  30.8 0.3 collective-permute-done.14.refs_1_
  31.2 0.3 collective-permute-start.18
  31.5 1.7 %collective-permute-done.15.refs_2_ = bf16[32,896]{1,0:T(8,128)(2,1)S(1)} collective-permute-done((bf16[32,896]{1,0:T(8,128)(2,1)S(1)}, bf16[32,896]{1,0:T(8,128)(2,1)S(1)}, u32[]{:S(2)}, u32[]{:S(2)}) %collective-permute-start.15) | collective-permute-done | bytes 57376 | tf_op jit(solution)/shard_map/ppermute | solution.py:478
  33.2 0.0 collective-permute-done.16.refs_3_
  33.2 0.0 collective-permute-done.19.refs_7_
  33.2 0.0 collective-permute-done.17.refs_4_
  33.2 0.0 collective-permute-done.18.refs_5_
  33.3 3.7 %shard_map.128 = (bf16[32,896]{1,0:T(8,128)(2,1)S(1)}, bf16[32,896]{1,0:T(8,128)(2,1)S(1)}, bf16[32,896]{1,0:T(8,128)(2,1)S(1)}, bf16[32,896]{1,0:T(8,128)(2,1)S(1)}) custom-call(bf16[32,896]{1,0:T(8,128)(2,1)S(1)} %collective-permute-done.13.refs_0_, bf16[32,896]{1,0:T(8,128)(2,1)S(1)} %collective-permute-done.14.refs_1_, ...), custom_call_target="tpu_custom_call" | custom-call | tf_op jit(solution)/shard_map/pallas_call | solution.py:462
  36.9 1.7 %collective-permute-start.20 = (bf16[32,896]{1,0:T(8,128)(2,1)S(1)}, bf16[32,896]{1,0:T(8,128)(2,1)S(1)}, u32[]{:S(2)}, u32[]{:S(2)}) collective-permute-start(bf16[32,896]{1,0:T(8,128)(2,1)S(1)} %get-tuple-element.53), channel_id=1, source_target_pairs={{0,7},{1,6},{2,5},{3,4},{4,3},{5,2},{6,1},{7,0},{8,15},{9,14},{10,... | collective-permute-start | bytes 172040 | tf_op jit(solution)/shard_map/ppermute | solution.py:478
  38.6 0.7 %collective-permute-start.21 = (bf16[32,896]{1,0:T(8,128)(2,1)S(1)}, bf16[32,896]{1,0:T(8,128)(2,1)S(1)}, u32[]{:S(2)}, u32[]{:S(2)}) collective-permute-start(bf16[32,896]{1,0:T(8,128)(2,1)S(1)} %get-tuple-element.54), channel_id=1, source_target_pairs={{0,5},{1,4},{2,7},{3,6},{4,1},{5,0},{6,3},{7,2},{8,13},{9,12},{10,... | collective-permute-start | bytes 172040 | tf_op jit(solution)/shard_map/ppermute | solution.py:478
  39.4 0.8 %collective-permute-start.22 = (bf16[32,896]{1,0:T(8,128)(2,1)S(1)}, bf16[32,896]{1,0:T(8,128)(2,1)S(1)}, u32[]{:S(2)}, u32[]{:S(2)}) collective-permute-start(bf16[32,896]{1,0:T(8,128)(2,1)S(1)} %get-tuple-element.55), channel_id=1, source_target_pairs={{0,2},{1,3},{2,0},{3,1},{4,6},{5,7},{6,4},{7,5},{8,10},{9,11},{10,... | collective-permute-start | bytes 172040 | tf_op jit(solution)/shard_map/ppermute | solution.py:478
  40.2 0.3 collective-permute-start.23
  40.5 1.0 %collective-permute-start.26 = (bf16[32,896]{1,0:T(8,128)(2,1)S(1)}, bf16[32,896]{1,0:T(8,128)(2,1)S(1)}, u32[]{:S(2)}, u32[]{:S(2)}) collective-permute-start(bf16[32,896]{1,0:T(8,128)(2,1)S(1)} %get-tuple-element.56.refs_6_), channel_id=1, source_target_pairs={{0,1},{1,0},{2,3},{3,2},{4,5},{5,4},{6,7},{7,6},{8,9},{9,8},{10,11... | collective-permute-start | bytes 172040 | tf_op jit(solution)/shard_map/ppermute | solution.py:478
  41.5 0.0 collective-permute-done.20.refs_0_
  41.5 0.5 %collective-permute-start.24 = (bf16[32,896]{1,0:T(8,128)(2,1)S(1)}, bf16[32,896]{1,0:T(8,128)(2,1)S(1)}, u32[]{:S(2)}, u32[]{:S(2)}) collective-permute-start(bf16[32,896]{1,0:T(8,128)(2,1)S(1)} %collective-permute-done.20.refs_0_), channel_id=1, source_target_pairs={{0,1},{1,0},{2,3},{3,2},{4,5},{5,4},{6,7},{7,6},{8,9},{9,8},{10,11... | collective-permute-start | bytes 172040 | tf_op jit(solution)/shard_map/ppermute | solution.py:478
  42.0 1.3 %collective-permute-done.21.refs_1_ = bf16[32,896]{1,0:T(8,128)(2,1)S(1)} collective-permute-done((bf16[32,896]{1,0:T(8,128)(2,1)S(1)}, bf16[32,896]{1,0:T(8,128)(2,1)S(1)}, u32[]{:S(2)}, u32[]{:S(2)}) %collective-permute-start.21) | collective-permute-done | bytes 57376 | tf_op jit(solution)/shard_map/ppermute | solution.py:478
  43.3 0.2 collective-permute-start.25
  43.5 0.4 collective-permute-done.22.refs_2_
  43.9 0.5 %collective-permute-done.23.refs_3_ = bf16[32,896]{1,0:T(8,128)(2,1)S(1)} collective-permute-done((bf16[32,896]{1,0:T(8,128)(2,1)S(1)}, bf16[32,896]{1,0:T(8,128)(2,1)S(1)}, u32[]{:S(2)}, u32[]{:S(2)}) %collective-permute-start.23) | collective-permute-done | bytes 57376 | tf_op jit(solution)/shard_map/ppermute | solution.py:478
  44.4 0.0 collective-permute-done.26.refs_7_
  44.4 0.0 collective-permute-done.24.refs_4_
  44.4 0.1 collective-permute-done.25.refs_5_
  44.5 0.9 %shard_map.129 = (bf16[16,3584]{1,0:T(8,128)(2,1)}, bf16[16,3584]{1,0:T(8,128)(2,1)}) custom-call(bf16[32,896]{1,0:T(8,128)(2,1)S(1)} %collective-permute-done.20.refs_0_, bf16[32,896]{1,0:T(8,128)(2,1)S(1)} %collective-permute-done.21.refs_1_, bf16[32,896]{1,0:T(8,128)(2,1)S(1)} %collective-permute-done.22.refs_2_, ...), custom_call_target="tpu_custom_call" | custom-call | tf_op jit(solution)/shard_map/pallas_call | solution.py:462
  (4 shorter events, 0.0 us)
Async XLA Ops:
  0.6 10.6 %copy-start = (bf16[1,3584,1024]{2,1,0:T(8,128)(2,1)S(1)}, bf16[1,3584,1024]{2,1,0:T(8,128)(2,1)}, u32[]{:S(2)}) copy-start(bf16[1,3584,1024]{2,1,0:T(8,128)(2,1)} %refs_6_.1) | copy-start | bytes 22020100
  0.6 10.6 %copy-start.1 = (bf16[1,3584,1024]{2,1,0:T(8,128)(2,1)S(1)}, bf16[1,3584,1024]{2,1,0:T(8,128)(2,1)}, u32[]{:S(2)}) copy-start(bf16[1,3584,1024]{2,1,0:T(8,128)(2,1)} %refs_7_.1) | copy-start | bytes 22020100
  0.7 10.6 %copy-start.2 = (bf16[1,1024,3584]{2,1,0:T(8,128)(2,1)S(1)}, bf16[1,1024,3584]{2,1,0:T(8,128)(2,1)}, u32[]{:S(2)}) copy-start(bf16[1,1024,3584]{2,1,0:T(8,128)(2,1)} %refs_8_.1) | copy-start | bytes 22020100
  2.1 6.3 %collective-permute-start = (bf16[32,1024]{1,0:T(8,128)(2,1)S(1)}, bf16[32,1024]{1,0:T(8,128)(2,1)S(1)}, u32[]{:S(2)}, u32[]{:S(2)}) collective-permute-start(bf16[32,1024]{1,0:T(8,128)(2,1)S(1)} %get-tuple-element.31), channel_id=1, source_target_pairs={{0,7},{1,6},{2,5},{3,4},{4,3},{5,2},{6,1},{7,0},{8,15},{9,14},{10,... | collective-permute-start | bytes 196616 | tf_op jit(solution)/shard_map/ppermute | solution.py:478
  5.5 3.9 %collective-permute-start.1 = (bf16[32,1024]{1,0:T(8,128)(2,1)S(1)}, bf16[32,1024]{1,0:T(8,128)(2,1)S(1)}, u32[]{:S(2)}, u32[]{:S(2)}) collective-permute-start(bf16[32,1024]{1,0:T(8,128)(2,1)S(1)} %get-tuple-element.32), channel_id=1, source_target_pairs={{0,5},{1,4},{2,7},{3,6},{4,1},{5,0},{6,3},{7,2},{8,13},{9,12},{10,... | collective-permute-start | bytes 196616 | tf_op jit(solution)/shard_map/ppermute | solution.py:478
  6.3 4.9 %collective-permute-start.2 = (bf16[32,1024]{1,0:T(8,128)(2,1)S(1)}, bf16[32,1024]{1,0:T(8,128)(2,1)S(1)}, u32[]{:S(2)}, u32[]{:S(2)}) collective-permute-start(bf16[32,1024]{1,0:T(8,128)(2,1)S(1)} %get-tuple-element.33), channel_id=1, source_target_pairs={{0,2},{1,3},{2,0},{3,1},{4,6},{5,7},{6,4},{7,5},{8,10},{9,11},{10,... | collective-permute-start | bytes 196616 | tf_op jit(solution)/shard_map/ppermute | solution.py:478
  6.3 4.9 %collective-permute-start.3 = (bf16[32,1024]{1,0:T(8,128)(2,1)S(1)}, bf16[32,1024]{1,0:T(8,128)(2,1)S(1)}, u32[]{:S(2)}, u32[]{:S(2)}) collective-permute-start(bf16[32,1024]{1,0:T(8,128)(2,1)S(1)} %get-tuple-element.33), channel_id=1, source_target_pairs={{0,3},{1,2},{2,1},{3,0},{4,7},{5,6},{6,5},{7,4},{8,11},{9,10},{10,... | collective-permute-start | bytes 196616 | tf_op jit(solution)/shard_map/ppermute | solution.py:478
  7.5 3.6 %collective-permute-start.6 = (bf16[32,1024]{1,0:T(8,128)(2,1)S(1)}, bf16[32,1024]{1,0:T(8,128)(2,1)S(1)}, u32[]{:S(2)}, u32[]{:S(2)}) collective-permute-start(bf16[32,1024]{1,0:T(8,128)(2,1)S(1)} %get-tuple-element.34.refs_0_.refs_6_), channel_id=1, source_target_pairs={{0,1},{1,0},{2,3},{3,2},{4,5},{5,4},{6,7},{7,6},{8,9},{9,8},{10,11... | collective-permute-start | bytes 196616 | tf_op jit(solution)/shard_map/ppermute | solution.py:478
  8.4 2.8 %collective-permute-start.4 = (bf16[32,1024]{1,0:T(8,128)(2,1)S(1)}, bf16[32,1024]{1,0:T(8,128)(2,1)S(1)}, u32[]{:S(2)}, u32[]{:S(2)}) collective-permute-start(bf16[32,1024]{1,0:T(8,128)(2,1)S(1)} %collective-permute-done.refs_0_), channel_id=1, source_target_pairs={{0,1},{1,0},{2,3},{3,2},{4,5},{5,4},{6,7},{7,6},{8,9},{9,8},{10,11... | collective-permute-start | bytes 196616 | tf_op jit(solution)/shard_map/ppermute | solution.py:478
  9.4 1.9 %collective-permute-start.5 = (bf16[32,1024]{1,0:T(8,128)(2,1)S(1)}, bf16[32,1024]{1,0:T(8,128)(2,1)S(1)}, u32[]{:S(2)}, u32[]{:S(2)}) collective-permute-start(bf16[32,1024]{1,0:T(8,128)(2,1)S(1)} %collective-permute-done.1.refs_1_), channel_id=1, source_target_pairs={{0,1},{1,0},{2,3},{3,2},{4,5},{5,4},{6,7},{7,6},{8,9},{9,8},{10,11... | collective-permute-start | bytes 196616 | tf_op jit(solution)/shard_map/ppermute | solution.py:478
  14.9 1.4 %collective-permute-start.7 = (bf16[64,1024]{1,0:T(8,128)(2,1)S(1)}, bf16[64,1024]{1,0:T(8,128)(2,1)S(1)}, u32[]{:S(2)}, u32[]{:S(2)}) collective-permute-start(bf16[64,1024]{1,0:T(8,128)(2,1)S(1)} %get-tuple-element.40), channel_id=1, source_target_pairs={{0,1},{1,0},{2,3},{3,2},{4,5},{5,4},{6,7},{7,6},{8,9},{9,8},{10,11... | collective-permute-start | bytes 393224 | tf_op jit(solution)/shard_map/ppermute | solution.py:563
  15.4 6.5 %collective-permute-start.12 = (bf16[80,896]{1,0:T(8,128)(2,1)S(1)}, bf16[80,896]{1,0:T(8,128)(2,1)S(1)}, u32[]{:S(2)}, u32[]{:S(2)}) collective-permute-start(bf16[80,896]{1,0:T(8,128)(2,1)S(1)} %get-tuple-element.45.refs_1_), channel_id=1, source_target_pairs={{0,1},{1,0},{2,3},{3,2},{4,5},{5,4},{6,7},{7,6},{8,9},{9,8},{10,11... | collective-permute-start | bytes 430088 | tf_op jit(solution)/shard_map/ppermute | solution.py:561
  16.4 5.9 %collective-permute-start.10 = (bf16[32,1024]{1,0:T(8,128)(2,1)S(1)}, bf16[32,1024]{1,0:T(8,128)(2,1)S(1)}, u32[]{:S(2)}, u32[]{:S(2)}) collective-permute-start(bf16[32,1024]{1,0:T(8,128)(2,1)S(1)} %get-tuple-element.43), channel_id=1, source_target_pairs={{0,15},{1,3},{2,13},{3,1},{4,11},{5,7},{6,9},{7,5},{8,23},{9,6},{1... | collective-permute-start | bytes 196616 | tf_op jit(solution)/shard_map/ppermute | solution.py:566
  19.4 4.6 %collective-permute-start.11 = (bf16[32,1024]{1,0:T(8,128)(2,1)S(1)}, bf16[32,1024]{1,0:T(8,128)(2,1)S(1)}, u32[]{:S(2)}, u32[]{:S(2)}) collective-permute-start(bf16[32,1024]{1,0:T(8,128)(2,1)S(1)} %get-tuple-element.44), channel_id=1, source_target_pairs={{0,13},{1,3},{2,15},{3,1},{4,9},{5,7},{6,11},{7,5},{8,21},{9,4},{1... | collective-permute-start | bytes 196616 | tf_op jit(solution)/shard_map/ppermute | solution.py:566
  20.6 4.6 %collective-permute-start.8 = (bf16[32,1024]{1,0:T(8,128)(2,1)S(1)}, bf16[32,1024]{1,0:T(8,128)(2,1)S(1)}, u32[]{:S(2)}, u32[]{:S(2)}) collective-permute-start(bf16[32,1024]{1,0:T(8,128)(2,1)S(1)} %get-tuple-element.41), channel_id=1, source_target_pairs={{0,11},{1,3},{2,9},{3,1},{4,15},{5,7},{6,13},{7,5},{8,19},{9,2},{1... | collective-permute-start | bytes 196616 | tf_op jit(solution)/shard_map/ppermute | solution.py:566
  21.7 3.7 %collective-permute-start.9 = (bf16[32,1024]{1,0:T(8,128)(2,1)S(1)}, bf16[32,1024]{1,0:T(8,128)(2,1)S(1)}, u32[]{:S(2)}, u32[]{:S(2)}) collective-permute-start(bf16[32,1024]{1,0:T(8,128)(2,1)S(1)} %get-tuple-element.42), channel_id=1, source_target_pairs={{0,9},{1,3},{2,11},{3,1},{4,13},{5,7},{6,15},{7,5},{8,17},{9,0},{1... | collective-permute-start | bytes 196616 | tf_op jit(solution)/shard_map/ppermute | solution.py:566
  25.7 5.1 %collective-permute-start.13 = (bf16[32,896]{1,0:T(8,128)(2,1)S(1)}, bf16[32,896]{1,0:T(8,128)(2,1)S(1)}, u32[]{:S(2)}, u32[]{:S(2)}) collective-permute-start(bf16[32,896]{1,0:T(8,128)(2,1)S(1)} %get-tuple-element.48), channel_id=1, source_target_pairs={{0,7},{1,6},{2,5},{3,4},{4,3},{5,2},{6,1},{7,0},{8,15},{9,14},{10,... | collective-permute-start | bytes 172040 | tf_op jit(solution)/shard_map/ppermute | solution.py:478
  25.8 5.3 %collective-permute-start.14 = (bf16[32,896]{1,0:T(8,128)(2,1)S(1)}, bf16[32,896]{1,0:T(8,128)(2,1)S(1)}, u32[]{:S(2)}, u32[]{:S(2)}) collective-permute-start(bf16[32,896]{1,0:T(8,128)(2,1)S(1)} %get-tuple-element.49), channel_id=1, source_target_pairs={{0,5},{1,4},{2,7},{3,6},{4,1},{5,0},{6,3},{7,2},{8,13},{9,12},{10,... | collective-permute-start | bytes 172040 | tf_op jit(solution)/shard_map/ppermute | solution.py:478
  28.7 4.5 %collective-permute-start.15 = (bf16[32,896]{1,0:T(8,128)(2,1)S(1)}, bf16[32,896]{1,0:T(8,128)(2,1)S(1)}, u32[]{:S(2)}, u32[]{:S(2)}) collective-permute-start(bf16[32,896]{1,0:T(8,128)(2,1)S(1)} %get-tuple-element.50), channel_id=1, source_target_pairs={{0,2},{1,3},{2,0},{3,1},{4,6},{5,7},{6,4},{7,5},{8,10},{9,11},{10,... | collective-permute-start | bytes 172040 | tf_op jit(solution)/shard_map/ppermute | solution.py:478
  29.0 4.2 %collective-permute-start.16 = (bf16[32,896]{1,0:T(8,128)(2,1)S(1)}, bf16[32,896]{1,0:T(8,128)(2,1)S(1)}, u32[]{:S(2)}, u32[]{:S(2)}) collective-permute-start(bf16[32,896]{1,0:T(8,128)(2,1)S(1)} %get-tuple-element.50), channel_id=1, source_target_pairs={{0,3},{1,2},{2,1},{3,0},{4,7},{5,6},{6,5},{7,4},{8,11},{9,10},{10,... | collective-permute-start | bytes 172040 | tf_op jit(solution)/shard_map/ppermute | solution.py:478
  29.1 4.1 %collective-permute-start.19 = (bf16[32,896]{1,0:T(8,128)(2,1)S(1)}, bf16[32,896]{1,0:T(8,128)(2,1)S(1)}, u32[]{:S(2)}, u32[]{:S(2)}) collective-permute-start(bf16[32,896]{1,0:T(8,128)(2,1)S(1)} %get-tuple-element.51.refs_6_), channel_id=1, source_target_pairs={{0,1},{1,0},{2,3},{3,2},{4,5},{5,4},{6,7},{7,6},{8,9},{9,8},{10,11... | collective-permute-start | bytes 172040 | tf_op jit(solution)/shard_map/ppermute | solution.py:478
  30.8 2.4 %collective-permute-start.17 = (bf16[32,896]{1,0:T(8,128)(2,1)S(1)}, bf16[32,896]{1,0:T(8,128)(2,1)S(1)}, u32[]{:S(2)}, u32[]{:S(2)}) collective-permute-start(bf16[32,896]{1,0:T(8,128)(2,1)S(1)} %collective-permute-done.13.refs_0_), channel_id=1, source_target_pairs={{0,1},{1,0},{2,3},{3,2},{4,5},{5,4},{6,7},{7,6},{8,9},{9,8},{10,11... | collective-permute-start | bytes 172040 | tf_op jit(solution)/shard_map/ppermute | solution.py:478
  31.2 2.1 %collective-permute-start.18 = (bf16[32,896]{1,0:T(8,128)(2,1)S(1)}, bf16[32,896]{1,0:T(8,128)(2,1)S(1)}, u32[]{:S(2)}, u32[]{:S(2)}) collective-permute-start(bf16[32,896]{1,0:T(8,128)(2,1)S(1)} %collective-permute-done.14.refs_1_), channel_id=1, source_target_pairs={{0,1},{1,0},{2,3},{3,2},{4,5},{5,4},{6,7},{7,6},{8,9},{9,8},{10,11... | collective-permute-start | bytes 172040 | tf_op jit(solution)/shard_map/ppermute | solution.py:478
  36.9 4.6 %collective-permute-start.20 = (bf16[32,896]{1,0:T(8,128)(2,1)S(1)}, bf16[32,896]{1,0:T(8,128)(2,1)S(1)}, u32[]{:S(2)}, u32[]{:S(2)}) collective-permute-start(bf16[32,896]{1,0:T(8,128)(2,1)S(1)} %get-tuple-element.53), channel_id=1, source_target_pairs={{0,7},{1,6},{2,5},{3,4},{4,3},{5,2},{6,1},{7,0},{8,15},{9,14},{10,... | collective-permute-start | bytes 172040 | tf_op jit(solution)/shard_map/ppermute | solution.py:478
  38.6 4.7 %collective-permute-start.21 = (bf16[32,896]{1,0:T(8,128)(2,1)S(1)}, bf16[32,896]{1,0:T(8,128)(2,1)S(1)}, u32[]{:S(2)}, u32[]{:S(2)}) collective-permute-start(bf16[32,896]{1,0:T(8,128)(2,1)S(1)} %get-tuple-element.54), channel_id=1, source_target_pairs={{0,5},{1,4},{2,7},{3,6},{4,1},{5,0},{6,3},{7,2},{8,13},{9,12},{10,... | collective-permute-start | bytes 172040 | tf_op jit(solution)/shard_map/ppermute | solution.py:478
  39.4 4.5 %collective-permute-start.22 = (bf16[32,896]{1,0:T(8,128)(2,1)S(1)}, bf16[32,896]{1,0:T(8,128)(2,1)S(1)}, u32[]{:S(2)}, u32[]{:S(2)}) collective-permute-start(bf16[32,896]{1,0:T(8,128)(2,1)S(1)} %get-tuple-element.55), channel_id=1, source_target_pairs={{0,2},{1,3},{2,0},{3,1},{4,6},{5,7},{6,4},{7,5},{8,10},{9,11},{10,... | collective-permute-start | bytes 172040 | tf_op jit(solution)/shard_map/ppermute | solution.py:478
  40.2 4.2 %collective-permute-start.23 = (bf16[32,896]{1,0:T(8,128)(2,1)S(1)}, bf16[32,896]{1,0:T(8,128)(2,1)S(1)}, u32[]{:S(2)}, u32[]{:S(2)}) collective-permute-start(bf16[32,896]{1,0:T(8,128)(2,1)S(1)} %get-tuple-element.55), channel_id=1, source_target_pairs={{0,3},{1,2},{2,1},{3,0},{4,7},{5,6},{6,5},{7,4},{8,11},{9,10},{10,... | collective-permute-start | bytes 172040 | tf_op jit(solution)/shard_map/ppermute | solution.py:478
  40.5 3.9 %collective-permute-start.26 = (bf16[32,896]{1,0:T(8,128)(2,1)S(1)}, bf16[32,896]{1,0:T(8,128)(2,1)S(1)}, u32[]{:S(2)}, u32[]{:S(2)}) collective-permute-start(bf16[32,896]{1,0:T(8,128)(2,1)S(1)} %get-tuple-element.56.refs_6_), channel_id=1, source_target_pairs={{0,1},{1,0},{2,3},{3,2},{4,5},{5,4},{6,7},{7,6},{8,9},{9,8},{10,11... | collective-permute-start | bytes 172040 | tf_op jit(solution)/shard_map/ppermute | solution.py:478
  41.5 2.9 %collective-permute-start.24 = (bf16[32,896]{1,0:T(8,128)(2,1)S(1)}, bf16[32,896]{1,0:T(8,128)(2,1)S(1)}, u32[]{:S(2)}, u32[]{:S(2)}) collective-permute-start(bf16[32,896]{1,0:T(8,128)(2,1)S(1)} %collective-permute-done.20.refs_0_), channel_id=1, source_target_pairs={{0,1},{1,0},{2,3},{3,2},{4,5},{5,4},{6,7},{7,6},{8,9},{9,8},{10,11... | collective-permute-start | bytes 172040 | tf_op jit(solution)/shard_map/ppermute | solution.py:478
  43.3 1.2 %collective-permute-start.25 = (bf16[32,896]{1,0:T(8,128)(2,1)S(1)}, bf16[32,896]{1,0:T(8,128)(2,1)S(1)}, u32[]{:S(2)}, u32[]{:S(2)}) collective-permute-start(bf16[32,896]{1,0:T(8,128)(2,1)S(1)} %collective-permute-done.21.refs_1_), channel_id=1, source_target_pairs={{0,1},{1,0},{2,3},{3,2},{4,5},{5,4},{6,7},{7,6},{8,9},{9,8},{10,11... | collective-permute-start | bytes 172040 | tf_op jit(solution)/shard_map/ppermute | solution.py:478
